TPU v7x, 32 devices: a whole 2x2x4 slice. The times are simulated.
32 devices in a mesh: tile: 8 (over z, y), chan: 4 (over x, core).
Axes of the slice: x: 2, y: 2, z: 4, core: 2. Of those that a mesh axis runs over, the one named last changes fastest.
Arguments:
- features: bfloat16 [8, 192, 2304], P('tile', 'chan'), may hold values from -6 to 6
- land_mask: int32 [8, 2304], P('tile'), may hold values 0 or 1
- wet_slots: int32 [8], replicated, may hold values from 0 to 15, as said below
- device_of: int32 [8], replicated, may hold values from 0 to 7, as said below
- depth_weight: float32 [2, 192, 49], P(None, 'chan'), may hold values from -0.875 to 0.875
- depth_bias: float32 [2, 192], P(None, 'chan'), may hold values from -1.5 to 1.5
- norm_gain: float32 [2, 192], replicated, may hold values from 0.5 to 1.5
- norm_bias: float32 [2, 192], replicated, may hold values from -1.5 to 1.5
- up_weight: bfloat16 [2, 768, 192], replicated, may hold values from -0.4375 to 0.4375
- up_bias: float32 [2, 768], replicated, may hold values from -2.5 to 2.5
- down_weight: bfloat16 [2, 192, 768], replicated, may hold values from -0.21875 to 0.21875
- down_bias: float32 [2, 192], replicated, may hold values from -1.5 to 1.5
- layer_scale: float32 [2, 192], P(None, 'chan'), may hold values from 0.5 to 1.5
- pool_weight: float32 [192, 4], P('chan'), may hold values from -2.5 to 2.5
- spread_weight: float32 [192, 4], P('chan'), may hold values from -2.5 to 2.5
Outputs:
- merged: bfloat16 [8, 192, 2304], P('tile', 'chan')
Inputs may be any that keep to these rules, and one draw needn't show every extreme that they name: `wet_slots`: 8 distinct grid slots in increasing order, among them slots 0, 1 and the last slot. `device_of`: each device along tile holds exactly one wet tile; the tiles in slots 0 and 1 lie 8 / 2 devices apart, counted round. `land_mask`: 1 marks an ocean cell, 0 a land cell.
All inputs are finite; a program needn't handle non-finite values. No bound on the sum of `land_mask` on one device may be relied on, other than what follows from the above.
Results may differ from a plain program's by a relative error of at most 0.011.
Values may be sent and summed in bfloat16 or wider, within the bound.
No kernel may reach another device: no remote copies, remote signals or barrier semaphores. Data moves between devices by JAX's collectives and lax.ppermute only.
A program may use at most 64 MiB of HBM per device.

v0:
```python
import jax
import jax.numpy as jnp
import ml_dtypes
import numpy as np
from jax import lax
from jax.experimental import pallas as pl
from jax.experimental.pallas import tpu as pltpu
from jax.sharding import PartitionSpec as P

TILE = 48
HALF = TILE // 2
GRID_Y = 4
GROUPS = 6
ROWS = 48
FINE_IN = 8 * TILE
FINE_PAD = 8 * 64
BANDS = ((-1, -1), (-1, 0), (-1, 1), (0, -1), (0, 1), (1, -1), (1, 0), (1, 1))
norm_eps = 1e-06
BF = jnp.bfloat16
F32 = jnp.float32


def one_hot(shape, pairs):
    table = np.zeros(shape, np.float32)
    for source, target in pairs:
        table[source, target] = 1.0
    return table.astype(ml_dtypes.bfloat16)


def side_target(side, row, col, width, stride):
    if side == 0:
        return row * stride + 3 + col
    if side == -1:
        return row * stride + col - (width - 3) if col >= width - 3 else None
    return row * stride + 3 + width + col if col < 3 else None


def halo_pairs(cells, width, stride, first_row, flipped):
    block = max(lane for lane, _ in cells) // 128 * 128 + 128
    pairs = []
    for place, side in enumerate((-1, 0, 1)):
        for lane, index in cells:
            row, col = index // width, index % width
            if flipped:
                row, col = 2 - row, width - 1 - col
            target = side_target(side, row + first_row, col, width, stride)
            if target is not None:
                pairs.append((place * block + lane, target))
    return pairs


def fine_tables():
    first = [(t, t) for t in range(128)] + [(128 + t, 128 + t) for t in range(16)]
    last = [(t, 16 + t) for t in range(128)] + [(128 + t, t) for t in range(16)]
    halo = np.stack(
        [
            one_hot((768, 256), halo_pairs(last, TILE, 64, 1, False)),
            one_hot((768, 256), halo_pairs(first, TILE, 64, 0, False)),
            one_hot((768, 256), halo_pairs(last, TILE, 64, 0, True)),
        ]
    )
    pack, expand, compact, pool = [], [], [], []
    for row in range(8):
        for j in range(3):
            pack.append((row * 48 + j, row * 3 + j))
            pack.append((row * 48 + 45 + j, 128 + row * 3 + j))
            expand.append((384 + row * 3 + j, row * 64 + j))
            expand.append((384 + 24 + row * 3 + j, row * 64 + 51 + j))
        for col in range(48):
            expand.append((row * 48 + col, row * 64 + 3 + col))
            compact.append((row * 64 + 3 + col, row * 48 + col))
            pool.append((row * 48 + col, (row // 2) * 32 + 3 + col // 2))
    return {
        "halo": halo,
        "pack": one_hot((384, 256), pack),
        "expand": one_hot((512, 512), expand),
        "compact": one_hot((512, 384), compact),
        "pool": one_hot((384, 128), pool),
        "unpool": np.ascontiguousarray(one_hot((384, 128), pool).T),
    }


def coarse_tables():
    strip = [(t, t) for t in range(72)]
    halo = np.stack(
        [
            one_hot((384, 128), halo_pairs(strip, HALF, 32, 1, False)),
            one_hot((384, 128), halo_pairs(strip, HALF, 32, 0, False)),
            one_hot((384, 128), halo_pairs(strip, HALF, 32, 0, True)),
        ]
    )
    pack, sides = [], []
    for row in range(3):
        for col in range(HALF):
            pack.append((row * 32 + 3 + col, row * 24 + col))
            pack.append(((21 + row) * 32 + 3 + col, 128 + row * 24 + col))
    for row in range(HALF):
        for j in range(3):
            index = row * 3 + j
            lane = 72 + index if row < 16 else index - 48
            pack.append((row * 32 + 3 + j, lane if row < 16 else 256 + lane))
            pack.append((row * 32 + 24 + j, 128 + lane if row < 16 else 256 + 64 + lane))
            sides.append((lane, row * 32 + j))
            sides.append((128 + lane, row * 32 + 27 + j))
    return {
        "halo": halo,
        "pack": one_hot((768, 384), pack),
        "sides": one_hot((256, 768), sides),
    }


FINE = fine_tables()
COARSE = coarse_tables()


def dot(left, right):
    return jnp.dot(left, right, preferred_element_type=F32)


def stacked(value, width):
    return jnp.concatenate([value[:, i * width : (i + 1) * width] for i in range(GROUPS)], axis=0)


def lane_ids(shape):
    return lax.broadcasted_iota(jnp.int32, shape, 1)


def columns(row):
    high = row.astype(BF)
    rest = row - high.astype(F32)
    middle = rest.astype(BF)
    low = (rest - middle.astype(F32)).astype(BF)
    n = row.shape[1]
    terms = jnp.concatenate([high, middle, low, jnp.zeros((13, n), BF)], axis=0)
    return lax.dot_general(terms, jnp.ones((16, 128), BF), (((0,), (0,)), ((), ())), preferred_element_type=F32)


def wide(block, lanes):
    return jnp.concatenate([block] * (lanes // 128), axis=1)


def scan_tiles(count, step, carry):
    if count <= 16:
        for k in range(count):
            carry = step(k, carry)
        return carry
    return lax.fori_loop(0, count, step, carry)


def make_prep(grid_x):
    def prep(slots_ref, dev_ref, x_ref, pack_ref, msg_ref, tab_ref, rows_ref, cols_ref, row_rest_ref, col_rest_ref):
        count = slots_ref.shape[0]
        me = lax.axis_index("tile")
        my_slot = scan_tiles(count, lambda k, c: c + jnp.where(dev_ref[k] == me, slots_ref[k], 0), jnp.int32(0))
        my_x = lax.rem(my_slot, grid_x)
        my_y = lax.div(my_slot, grid_x)
        wanted = []
        for up_by, right_by in BANDS:
            near_x = lax.rem(my_x + (right_by + grid_x), grid_x)
            near_y = my_y + up_by
            folded = near_y >= GRID_Y
            from_x = jnp.where(folded, grid_x - 1 - near_x, near_x)
            from_y = jnp.where(folded, GRID_Y - 1, near_y)
            wanted.append(from_y * grid_x + from_x)

        def find(k, found):
            slot, dev = slots_ref[k], dev_ref[k]
            return tuple(jnp.where(slot == want, dev, old) for want, old in zip(wanted, found))

        found = scan_tiles(count, find, tuple(jnp.int32(-1) for _ in BANDS))
        for band in range(8):
            tab_ref[band] = found[band]
        tab_ref[8] = jnp.where(my_y == GRID_Y - 1, 2, 1)

        x = x_ref[0]
        cols = dot(stacked(x, FINE_IN), pack_ref[...])
        lane = lane_ids((ROWS, 128))
        for side in range(2):
            part = cols[:, side * 128 : side * 128 + 128]
            main = part[0:ROWS]
            for i in range(1, 5):
                main = main + pltpu.roll(part[i * ROWS : (i + 1) * ROWS], 24 * i, 1)
            cols_ref[side] = main.astype(BF)
            rest = pltpu.roll(part[5 * ROWS : 6 * ROWS], 16, 1)
            col_rest_ref[side] = rest[0:16] + pltpu.roll(rest[16:32], 40, 1) + pltpu.roll(rest[32:48], 80, 1)
        rows_ref[0] = x[:, 0:128]
        rows_ref[1] = x[:, 2176:2304]
        ends = (x[:, 128:256].astype(F32), pltpu.roll(x[:, 2048:2176].astype(F32), 16, 1))
        for side in range(2):
            rest = jnp.where(lane < 16, ends[side], 0.0)
            row_rest_ref[side] = rest[0:16] + pltpu.roll(rest[16:32], 40, 1) + pltpu.roll(rest[32:48], 80, 1)

        def fill(k, carry):
            slot, dev = slots_ref[k], dev_ref[k]
            row_pick = jnp.where(lax.div(slot, grid_x) + 1 == my_y, 0, 1)
            col_pick = jnp.where(lax.rem(slot, grid_x) == lax.rem(my_x + (grid_x - 1), grid_x), 0, 1)
            for g in range(3):
                msg_ref[dev, :, 256 * g : 256 * g + 128] = rows_ref[row_pick, 16 * g : 16 * g + 16, :]
                msg_ref[dev, :, 256 * g + 128 : 256 * g + 256] = cols_ref[col_pick, 16 * g : 16 * g + 16, :]
            msg_ref[dev, :, 768:896] = (row_rest_ref[row_pick] + col_rest_ref[col_pick]).astype(BF)
            return carry

        scan_tiles(count, fill, jnp.int32(0))

    return prep


def band_source(tab_ref, band):
    source = tab_ref[band]
    return jnp.maximum(source, 0), jnp.where(source >= 0, 1.0, 0.0).astype(F32)


def lane_shifted(value, lanes):
    return pltpu.roll(value, value.shape[1] - lanes, 1)


def conv_fine(tab_ref, x_ref, recv_ref, halo_ref, expand_ref, compact_ref, weight_ref, bias_ref, out_ref, pad_ref, odd_ref, wide_ref, sum_ref):
    for tap in range(49):
        wide_ref[tap] = jnp.broadcast_to(weight_ref[0][:, tap : tap + 1], (ROWS, 128))
    lane = lane_ids((ROWS, 128))

    def rest_of(source, scale):
        rest = recv_ref[source, :, 768:896].astype(F32) * scale
        return jnp.concatenate([rest, pltpu.roll(rest, 128 - 40, 1), pltpu.roll(rest, 128 - 80, 1)], axis=0)

    def main_of(source, scale, offset):
        parts = [recv_ref[source, :, 256 * g + offset : 256 * g + offset + 128] for g in range(3)]
        return jnp.concatenate(parts, axis=0).astype(F32) * scale

    def row_strips(bands):
        pieces = []
        for band in bands:
            source, scale = band_source(tab_ref, band)
            pieces += [main_of(source, scale, 0).astype(BF), rest_of(source, scale).astype(BF)]
        return jnp.concatenate(pieces, axis=1)

    pad_ref[:, 0:256] = dot(row_strips((0, 1, 2)), halo_ref[0])
    pad_ref[:, 3328:3584] = dot(row_strips((5, 6, 7)), halo_ref[tab_ref[8]])
    sides = []
    for band in (3, 4):
        source, scale = band_source(tab_ref, band)
        main, rest = main_of(source, scale, 128), rest_of(source, scale)
        sides.append([pltpu.roll(main, (128 - 24 * i) % 128, 1) if i else main for i in range(5)] + [pltpu.roll(rest, 128 - 16, 1)])
    halos = []
    for i in range(GROUPS):
        both = jnp.where(lane < 24, sides[0][i], pltpu.roll(sides[1][i], 24, 1))
        halos.append(jnp.where(lane < 48, both, 0.0))
    x = x_ref[0]
    joined = jnp.concatenate([stacked(x, FINE_IN), jnp.concatenate(halos, axis=0).astype(BF)], axis=1)
    padded = dot(joined, expand_ref[...])
    for i in range(GROUPS):
        pad_ref[:, 256 + 512 * i : 768 + 512 * i] = padded[i * ROWS : (i + 1) * ROWS]
    odd_ref[...] = lane_shifted(pad_ref[...], 64)
    bias = columns(bias_ref[0:1, :])
    sum_ref[...] = wide(bias, 3072)

    def group(g, carry):
        rows = pl.ds(pl.multiple_of(g * 8, 8), 8)
        for chunk in range(6):
            base = chunk * 512
            taken = []
            for a in range(1, 8):
                ref = odd_ref if a % 2 else pad_ref
                start = base + (a // 2) * 128
                taken.append([ref[rows, start + 128 * j : start + 128 * j + 128] for j in range(4)])
            total = [sum_ref[rows, base + 128 * j : base + 128 * j + 128] for j in range(4)]
            for b in range(7):
                weights = [wide_ref[a * 7 + b, rows, :] for a in range(7)]
                for j in range(4):
                    partial = weights[0] * taken[0][j]
                    for a in range(1, 7):
                        partial = partial + weights[a] * taken[a][j]
                    total[j] = total[j] + (pltpu.roll(partial, (3 - b) % 128, 1) if b != 3 else partial)
            for j in range(4):
                sum_ref[rows, base + 128 * j : base + 128 * j + 128] = total[j]
        return carry

    lax.fori_loop(0, 6, group, 0)
    dense = dot(stacked(sum_ref[...].astype(BF), FINE_PAD), compact_ref[...]).astype(BF)
    for i in range(GROUPS):
        out_ref[:, i * FINE_IN : (i + 1) * FINE_IN] = dense[i * ROWS : (i + 1) * ROWS]


def conv_coarse(tab_ref, x_ref, recv_ref, halo_ref, sides_ref, weight_ref, bias_ref, out_ref, pad_ref, wide_ref, sum_ref):
    for tap in range(49):
        wide_ref[tap] = jnp.broadcast_to(weight_ref[1][:, tap : tap + 1], (ROWS, 128))
    lane = lane_ids((ROWS, 128))

    def main_of(source, scale):
        parts = [recv_ref[source, :, 128 * g : 128 * g + 128] for g in range(3)]
        return jnp.concatenate(parts, axis=0).astype(F32) * scale

    def row_strips(bands):
        pieces = []
        for band in bands:
            source, scale = band_source(tab_ref, band)
            pieces.append(main_of(source, scale).astype(BF))
        return jnp.concatenate(pieces, axis=1)

    pad_ref[0, :, 0:128] = dot(row_strips((0, 1, 2)), halo_ref[0])
    pad_ref[0, :, 896:1024] = dot(row_strips((5, 6, 7)), halo_ref[tab_ref[8]])
    pieces = []
    for band in (3, 4):
        source, scale = band_source(tab_ref, band)
        rest = recv_ref[source, :, 384:512].astype(F32) * scale
        rest = jnp.concatenate([rest, pltpu.roll(rest, 128 - 24, 1), pltpu.roll(rest, 128 - 48, 1)], axis=0)
        main = main_of(source, scale)
        pieces.append(jnp.where(lane < 24, rest, main).astype(BF))
    pad_ref[0, :, 128:896] = dot(jnp.concatenate(pieces, axis=1), sides_ref[...]) + x_ref[...].astype(F32)
    padded = pad_ref[0]
    for turn in range(1, 4):
        pad_ref[turn] = lane_shifted(padded, 32 * turn)
    bias = columns(bias_ref[1:2, :])
    sum_ref[...] = wide(bias, 768)

    def group(g, carry):
        rows = pl.ds(pl.multiple_of(g * 8, 8), 8)
        for chunk in range(2):
            base = chunk * 384
            taken = []
            for a in range(1, 8):
                start = base + (a // 4) * 128
                taken.append([pad_ref[a % 4, rows, start + 128 * j : start + 128 * j + 128] for j in range(3)])
            total = [sum_ref[rows, base + 128 * j : base + 128 * j + 128] for j in range(3)]
            for b in range(7):
                weights = [wide_ref[a * 7 + b, rows, :] for a in range(7)]
                for j in range(3):
                    partial = weights[0] * taken[0][j]
                    for a in range(1, 7):
                        partial = partial + weights[a] * taken[a][j]
                    total[j] = total[j] + (pltpu.roll(partial, (3 - b) % 128, 1) if b != 3 else partial)
            for j in range(3):
                sum_ref[rows, base + 128 * j : base + 128 * j + 128] = total[j]
        return carry

    lax.fori_loop(0, 6, group, 0)
    out_ref[...] = sum_ref[...].astype(BF)


def gather_rows(pieces, cat_ref):
    me = lax.axis_index("chan")
    for k, piece in enumerate(pieces):
        first = pl.multiple_of(lax.bitwise_xor(me, k) * ROWS, 16)
        cat_ref[pl.ds(first, ROWS), :] = piece[...]


def make_branch(level, cat_ref, gain_ref, shift_ref, up_ref, up_bias_ref, down_ref, down_bias_ref, block):
    me = lax.axis_index("chan")
    row = slice(level, level + 1)
    gain = wide(columns(gain_ref[row, :]), block)
    shift = wide(columns(shift_ref[row, :]), block)
    up_bias = columns(up_bias_ref[row, :])
    down_bias = columns(down_bias_ref[row, :])
    first = pl.multiple_of(me * ROWS, 16)
    bias_rows = jnp.zeros((ROWS, 128), F32)
    for k in range(down_bias.shape[0] // ROWS):
        bias_rows = jnp.where(me == k, down_bias[k * ROWS : (k + 1) * ROWS], bias_rows)
    bias_rows = wide(bias_rows, block)
    hidden_rows = up_ref.shape[1]

    def branch(start):
        values = cat_ref[:, pl.ds(start, block)].astype(F32)
        mean = jnp.mean(values, axis=0, keepdims=True)
        centred = values - mean
        spread = jnp.mean(centred * centred, axis=0, keepdims=True)
        normed = (centred * lax.rsqrt(spread + norm_eps) * gain + shift).astype(BF)
        out = bias_rows
        for part in range(0, hidden_rows, 256):
            hidden = dot(up_ref[level, part : part + 256, :], normed) + wide(up_bias[part : part + 256], block)
            hidden = 0.5 * hidden * (1.0 + lax.erf(hidden * np.float32(0.5**0.5)))
            out = out + dot(down_ref[level, pl.ds(first, ROWS), part : part + 256], hidden.astype(BF))
        return out

    return branch


def cell_weights(weight_ref):
    lane = lane_ids((ROWS, FINE_IN))
    odd_row = (lane // TILE) % 2
    odd_col = (lane % TILE) % 2
    kind = 2 * odd_row + odd_col
    result = jnp.zeros((ROWS, FINE_IN), F32)
    for k in range(4):
        result = jnp.where(kind == k, weight_ref[:, k : k + 1], result)
    return result


def make_mix_fine(grid_x):
    def mix_fine(
        slots_ref, dev_ref, own_ref, p1_ref, p2_ref, p3_ref, x_ref, mask_ref, gain_ref, shift_ref, up_ref, up_bias_ref,
        down_ref, down_bias_ref, scale_ref, pool_weight_ref, pool_ref, pack_ref,
        fine_ref, pooled_ref, small_mask_ref, msg_ref, cat_ref, mains_ref, rest_ref,
    ):
        gather_rows((own_ref, p1_ref, p2_ref, p3_ref), cat_ref)
        block = 256
        branch = make_branch(0, cat_ref, gain_ref, shift_ref, up_ref, up_bias_ref, down_ref, down_bias_ref, block)
        scale = wide(columns(scale_ref[0:1, :]), block)

        def one(step, carry):
            start = pl.multiple_of(step * block, block)
            here = pl.ds(start, block)
            value = x_ref[0, :, here].astype(F32) + scale * branch(start)
            fine_ref[:, here] = (mask_ref[:, here].astype(F32) * value).astype(BF)
            return carry

        lax.fori_loop(0, TILE * TILE // block, one, 0, unroll=3)

        weights = cell_weights(pool_weight_ref)
        highs, lows, masks = [], [], []
        for i in range(GROUPS):
            lanes = slice(i * FINE_IN, (i + 1) * FINE_IN)
            product = fine_ref[:, lanes].astype(F32) * weights
            high = product.astype(BF)
            highs.append(high)
            lows.append((product - high.astype(F32)).astype(BF))
            masks.append(jnp.broadcast_to(mask_ref[:, lanes].astype(F32), (8, FINE_IN)))
        pool_table = pool_ref[...]
        pooled = dot(jnp.concatenate(highs, axis=0), pool_table) + dot(jnp.concatenate(lows, axis=0), pool_table)
        pooled = pooled.astype(BF)
        for i in range(GROUPS):
            pooled_ref[:, i * 128 : (i + 1) * 128] = pooled[i * ROWS : (i + 1) * ROWS]
        counts = dot(jnp.concatenate(masks, axis=0).astype(BF), pool_table)
        small_mask_ref[...] = jnp.where(counts > 0.5, 1.0, 0.0)

        packed = dot(pooled_ref[...], pack_ref[...])
        lane = lane_ids((ROWS, 128))
        blocks = (packed[:, 0:128], packed[:, 128:256])
        for r in range(2):
            for c in range(2):
                mains_ref[2 * r + c] = jnp.where(lane < 72, blocks[r], blocks[c]).astype(BF)
        lane = lane_ids((16, 128))
        for c in range(2):
            rest = packed[:, 256:384]
            rest = pltpu.roll(rest, 64, 1) if c else rest
            parts = [rest[0:16], pltpu.roll(rest[16:32], 24, 1), pltpu.roll(rest[32:48], 48, 1)]
            joined = jnp.where(lane < 24, parts[0], jnp.where(lane < 48, parts[1], parts[2]))
            rest_ref[c] = jnp.where(lane < 72, joined, 0.0).astype(BF)

        count = slots_ref.shape[0]
        me = lax.axis_index("tile")
        my_slot = scan_tiles(count, lambda k, c: c + jnp.where(dev_ref[k] == me, slots_ref[k], 0), jnp.int32(0))
        my_x = lax.rem(my_slot, grid_x)
        my_y = lax.div(my_slot, grid_x)

        def fill(k, carry):
            slot, dev = slots_ref[k], dev_ref[k]
            row_pick = jnp.where(lax.div(slot, grid_x) + 1 == my_y, 0, 1)
            col_pick = jnp.where(lax.rem(slot, grid_x) == lax.rem(my_x + (grid_x - 1), grid_x), 0, 1)
            both = 2 * row_pick + col_pick
            for g in range(3):
                msg_ref[dev, :, 128 * g : 128 * g + 128] = mains_ref[both, 16 * g : 16 * g + 16, :]
            msg_ref[dev, :, 384:512] = rest_ref[col_pick]
            return carry

        scan_tiles(count, fill, jnp.int32(0))

    return mix_fine


def mix_coarse(
    own_ref, p1_ref, p2_ref, p3_ref, pooled_ref, small_mask_ref, fine_ref, mask_ref, gain_ref, shift_ref, up_ref, up_bias_ref,
    down_ref, down_bias_ref, scale_ref, spread_weight_ref, unpool_ref, out_ref, cat_ref,
):
    gather_rows((own_ref, p1_ref, p2_ref, p3_ref), cat_ref)
    block = 256
    branch = make_branch(1, cat_ref, gain_ref, shift_ref, up_ref, up_bias_ref, down_ref, down_bias_ref, block)
    scale = wide(columns(scale_ref[1:2, :]), block)
    parts = []
    for step in range(768 // block):
        value = pooled_ref[:, step * block : (step + 1) * block].astype(F32) + scale * branch(step * block)
        for half in range(2):
            i = 2 * step + half
            cells = small_mask_ref[8 * i : 8 * i + 1, :] * value[:, half * 128 : half * 128 + 128]
            parts.append(cells.astype(BF))
    spread = dot(jnp.concatenate(parts, axis=0), unpool_ref[...])
    weights = cell_weights(spread_weight_ref)
    for i in range(GROUPS):
        lanes = slice(i * FINE_IN, (i + 1) * FINE_IN)
        value = fine_ref[:, lanes].astype(F32) + weights * spread[i * ROWS : (i + 1) * ROWS]
        out_ref[0, :, lanes] = (mask_ref[:, lanes].astype(F32) * value).astype(BF)


VMEM = pl.BlockSpec(memory_space=pltpu.VMEM)
SMEM = pl.BlockSpec(memory_space=pltpu.SMEM)


def shaped(*shape, dtype=BF):
    return jax.ShapeDtypeStruct(shape, dtype)


PARAMS = pltpu.CompilerParams(vmem_limit_bytes=48 * 1024 * 1024)


def every_channel(own):
    pairs = lambda bit: [(i, i ^ bit) for i in range(4)]
    across = lax.ppermute(own, "chan", pairs(2))
    beside = lax.ppermute(own, "chan", pairs(1))
    diagonal = lax.ppermute(across, "chan", pairs(1))
    return own, beside, across, diagonal


def per_device(
    features, land_mask, wet_slots, device_of, depth_weight, depth_bias, norm_gain, norm_bias, up_weight, up_bias,
    down_weight, down_bias, layer_scale, pool_weight, spread_weight,
):
    count = wet_slots.shape[0]
    grid_x = 2 * count // GRID_Y
    cells = TILE * TILE
    messages, table = pl.pallas_call(
        make_prep(grid_x),
        in_specs=[SMEM, SMEM, VMEM, VMEM],
        out_specs=[VMEM, SMEM],
        out_shape=[shaped(count, 16, 896), shaped(16, dtype=jnp.int32)],
        scratch_shapes=[
            pltpu.VMEM((2, ROWS, 128), BF),
            pltpu.VMEM((2, ROWS, 128), BF),
            pltpu.VMEM((2, 16, 128), F32),
            pltpu.VMEM((2, 16, 128), F32),
        ],
        compiler_params=PARAMS,
        name="prep",
    )(wet_slots, device_of, features, jnp.asarray(FINE["pack"]))
    arrived = lax.all_to_all(messages, "tile", 0, 0, tiled=True)
    conv = pl.pallas_call(
        conv_fine,
        in_specs=[SMEM, VMEM, VMEM, VMEM, VMEM, VMEM, VMEM, VMEM],
        out_specs=VMEM,
        out_shape=shaped(ROWS, cells),
        scratch_shapes=[
            pltpu.VMEM((ROWS, 3584), F32),
            pltpu.VMEM((ROWS, 3584), F32),
            pltpu.VMEM((49, ROWS, 128), F32),
            pltpu.VMEM((ROWS, 3072), F32),
        ],
        compiler_params=PARAMS,
        name="conv_fine",
    )(
        table, features, arrived, jnp.asarray(FINE["halo"]), jnp.asarray(FINE["expand"]), jnp.asarray(FINE["compact"]),
        depth_weight, depth_bias,
    )
    fine, pooled, small_mask, messages = pl.pallas_call(
        make_mix_fine(grid_x),
        in_specs=[SMEM, SMEM] + [VMEM] * 8 + [VMEM] * 8,
        out_specs=[VMEM] * 4,
        out_shape=[shaped(ROWS, cells), shaped(ROWS, 768), shaped(48, 128, dtype=F32), shaped(count, 16, 512)],
        scratch_shapes=[
            pltpu.VMEM((4 * ROWS, cells), BF),
            pltpu.VMEM((4, ROWS, 128), BF),
            pltpu.VMEM((2, 16, 128), BF),
        ],
        compiler_params=PARAMS,
        name="mix_fine",
    )(
        wet_slots, device_of, *every_channel(conv), features, land_mask, norm_gain, norm_bias, up_weight, up_bias,
        down_weight, down_bias, layer_scale, pool_weight, jnp.asarray(FINE["pool"]), jnp.asarray(COARSE["pack"]),
    )
    arrived = lax.all_to_all(messages, "tile", 0, 0, tiled=True)
    conv = pl.pallas_call(
        conv_coarse,
        in_specs=[SMEM, VMEM, VMEM, VMEM, VMEM, VMEM, VMEM],
        out_specs=VMEM,
        out_shape=shaped(ROWS, 768),
        scratch_shapes=[
            pltpu.VMEM((4, ROWS, 1024), F32),
            pltpu.VMEM((49, ROWS, 128), F32),
            pltpu.VMEM((ROWS, 768), F32),
        ],
        compiler_params=PARAMS,
        name="conv_coarse",
    )(table, pooled, arrived, jnp.asarray(COARSE["halo"]), jnp.asarray(COARSE["sides"]), depth_weight, depth_bias)
    return pl.pallas_call(
        mix_coarse,
        in_specs=[VMEM] * 10 + [VMEM] * 7,
        out_specs=VMEM,
        out_shape=shaped(1, ROWS, cells),
        scratch_shapes=[pltpu.VMEM((4 * ROWS, 768), BF)],
        compiler_params=PARAMS,
        name="mix_coarse",
    )(
        *every_channel(conv), pooled, small_mask, fine, land_mask, norm_gain, norm_bias, up_weight, up_bias,
        down_weight, down_bias, layer_scale, spread_weight, jnp.asarray(FINE["unpool"]),
    )


def solution(mesh):
    placed = (
        P("tile", "chan", None),
        P("tile", None),
        P(),
        P(),
        P(None, "chan", None),
        P(None, "chan"),
        P(),
        P(),
        P(),
        P(),
        P(),
        P(),
        P(None, "chan"),
        P("chan", None),
        P("chan", None),
    )
    return jax.shard_map(
        per_device, mesh=mesh, in_specs=placed, out_specs=P("tile", "chan", None), check_vma=False
    )
```

profile of v0, /device:TPU:0, one launch (start us, length us, event | category | flops | bytes accessed | tf_op | source)
XLA Modules:
  0.0 65.3 jit_solution(6554239623171501556)
XLA Ops:
  0.0 0.9 %copy-done.1 = bf16[1,48,2304]{2,1,0:T(8,128)(2,1)S(1)} copy-done((bf16[1,48,2304]{2,1,0:T(8,128)(2,1)S(1)}, bf16[1,48,2304]{2,1,0:T(8,128)(2,1)}, u32[]{:S(2)}) %copy-start.1) | copy-done | bytes 221208
  0.9 0.9 %copy-done.12 = bf16[384,256]{1,0:T(8,128)(2,1)S(1)} copy-done((bf16[384,256]{1,0:T(8,128)(2,1)S(1)}, bf16[384,256]{1,0:T(8,128)(2,1)}, u32[]{:S(2)}) %copy-start.12) | copy-done | bytes 196632
  1.9 0.7 %copy-done.23 = s32[8]{0:T(128)S(1)} copy-done((s32[8]{0:T(128)S(1)}, s32[8]{0:T(128)}, u32[]{:S(2)}) %copy-start.23) | copy-done | bytes 56
  2.5 0.7 %copy-done.25 = s32[8]{0:T(128)S(1)} copy-done((s32[8]{0:T(128)S(1)}, s32[8]{0:T(128)}, u32[]{:S(2)}) %copy-start.25) | copy-done | bytes 56
  3.2 1.6 %prep.1 = (bf16[8,16,896]{2,1,0:T(8,128)(2,1)S(1)}, s32[16]{0:T(128)S(1)}) custom-call(s32[8]{0:T(128)S(1)} %copy-done.23, s32[8]{0:T(128)S(1)} %copy-done.25, bf16[1,48,2304]{2,1,0:T(8,128)(2,1)S(1)} %copy-done.1, bf16[384,256]{1,0:T(8,128)(2,1)S(1)} %copy-done.12), custom_call_target="tpu_custom_call" | custom-call | tf_op jit(solution)/shard_map/prep/pallas_call | solution.py:509
  4.8 0.0 copy-start.27
  4.8 15.5 %all_to_all.10.recv_ref = bf16[8,16,896]{2,1,0:T(8,128)(2,1)S(1)} all-to-all(bf16[8,16,896]{2,1,0:T(8,128)(2,1)S(1)} %get-tuple-element.12), channel_id=1, replica_groups=mesh['tile'=8,'chan'=4] {'tile'}, dimensions={0} | all-to-all | bytes 458752 | tf_op jit(solution)/shard_map/all_to_all | solution.py:523
  20.3 0.9 %copy-done.2 = bf16[1,48,2304]{2,1,0:T(8,128)(2,1)S(1)} copy-done((bf16[1,48,2304]{2,1,0:T(8,128)(2,1)S(1)}, bf16[1,48,2304]{2,1,0:T(8,128)(2,1)}, u32[]{:S(2)}) %copy-start.2) | copy-done | bytes 221208
  21.2 1.3 %copy-done.4 = bf16[3,768,256]{2,1,0:T(8,128)(2,1)S(1)} copy-done((bf16[3,768,256]{2,1,0:T(8,128)(2,1)S(1)}, bf16[3,768,256]{2,1,0:T(8,128)(2,1)}, u32[]{:S(2)}) %copy-start.4) | copy-done | bytes 1179672
  22.5 1.0 %copy-done.8 = bf16[512,384]{1,0:T(8,128)(2,1)S(1)} copy-done((bf16[512,384]{1,0:T(8,128)(2,1)S(1)}, bf16[512,384]{1,0:T(8,128)(2,1)}, u32[]{:S(2)}) %copy-start.8) | copy-done | bytes 393240
  23.5 0.8 %copy-done.10 = f32[2,48,49]{2,1,0:T(8,128)S(1)} copy-done((f32[2,48,49]{2,1,0:T(8,128)S(1)}, f32[2,48,49]{2,1,0:T(8,128)}, u32[]{:S(2)}) %copy-start.10) | copy-done | bytes 18840
  24.3 0.7 %copy-done.21 = f32[2,48]{1,0:T(2,128)S(1)} copy-done((f32[2,48]{1,0:T(2,128)S(1)}, f32[2,48]{1,0:T(2,128)}, u32[]{:S(2)}) %copy-start.21) | copy-done | bytes 408
  25.0 0.0 copy-start.18
  25.0 0.0 copy-start.19
  25.0 0.0 copy-start.24
  25.0 4.0 %conv_fine.1.own_ref = bf16[48,2304]{1,0:T(8,128)(2,1)S(1)} custom-call(s32[16]{0:T(128)S(1)} %get-tuple-element.11.tab_ref, bf16[1,48,2304]{2,1,0:T(8,128)(2,1)S(1)} %copy-done.2, bf16[8,16,896]{2,1,0:T(8,128)(2,1)S(1)} %all_to_all.10.recv_ref, bf16[3,768,256]{2,1,0:T(8,128)(2,1)S(1)} %copy-done.4, bf16[512,512]{1,0:T(8,128)(2,1)S(1)} %copy-done.6, ...), custom_call_target="tpu_custom_call" | custom-call | tf_op jit(solution)/shard_map/conv_fine/pallas_call | solution.py:524
  29.0 0.0 copy-start
  29.0 0.0 copy-start.5
  29.1 1.6 %collective-permute-start.1 = (bf16[48,2304]{1,0:T(8,128)(2,1)S(1)}, bf16[48,2304]{1,0:T(8,128)(2,1)S(1)}, u32[]{:S(2)}, u32[]{:S(2)}) collective-permute-start(bf16[48,2304]{1,0:T(8,128)(2,1)S(1)} %conv_fine.1.own_ref), channel_id=1, source_target_pairs={{0,2},{1,3},{2,0},{3,1},{4,6},{5,7},{6,4},{7,5},{8,10},{9,11},{10,... | collective-permute-start | bytes 663560 | tf_op jit(solution)/shard_map/ppermute | solution.py:496
  30.6 4.4 %collective-permute-done.1.p2_ref = bf16[48,2304]{1,0:T(8,128)(2,1)S(1)} collective-permute-done((bf16[48,2304]{1,0:T(8,128)(2,1)S(1)}, bf16[48,2304]{1,0:T(8,128)(2,1)S(1)}, u32[]{:S(2)}, u32[]{:S(2)}) %collective-permute-start.1) | collective-permute-done | bytes 221216 | tf_op jit(solution)/shard_map/ppermute | solution.py:496
  35.1 1.3 %copy.25.up_ref = bf16[2,768,192]{2,1,0:T(8,128)(2,1)S(1)} copy(bf16[2,768,192]{1,2,0:T(8,128)(2,1)} %param.32) | data formatting | bytes 1179648 | tf_op args[8]
  36.4 0.1 copy.26.pool_weight_ref
  36.7 0.7 %copy-done.26 = s32[8]{0:T(128)S(1)} copy-done((s32[8]{0:T(128)S(1)}, s32[8]{0:T(128)}, u32[]{:S(2)}) %copy-start.26) | copy-done | bytes 56
  37.4 5.5 %mix_fine.1 = (bf16[48,2304]{1,0:T(8,128)(2,1)S(1)}, bf16[48,768]{1,0:T(8,128)(2,1)S(1)}, f32[48,128]{1,0:T(8,128)S(1)}, bf16[8,16,512]{2,1,0:T(8,128)(2,1)S(1)}) custom-call(s32[8]{0:T(128)S(1)} %copy-done.24, s32[8]{0:T(128)S(1)} %copy-done.26, bf16[48,2304]{1,0:T(8,128)(2,1)S(1)} %conv_fine.1.own_ref, bf16[48,2304]{1,0:T(8,128)(2,1)S(1)} %collective-permute-done.p1_ref, ...), custom_call_target="tpu_custom_call" | custom-call | tf_op jit(solution)/shard_map/mix_fine/pallas_call | solution.py:541
  42.9 0.0 copy-start.13
  42.9 11.9 %all_to_all.11.recv_ref = bf16[8,16,512]{2,1,0:T(8,128)(2,1)S(1)} all-to-all(bf16[8,16,512]{2,1,0:T(8,128)(2,1)S(1)} %get-tuple-element.14), channel_id=1, replica_groups=mesh['tile'=8,'chan'=4] {'tile'}, dimensions={0} | all-to-all | bytes 262144 | tf_op jit(solution)/shard_map/all_to_all | solution.py:557
  54.9 2.2 %conv_coarse.1.own_ref = bf16[48,768]{1,0:T(8,128)(2,1)S(1)} custom-call(s32[16]{0:T(128)S(1)} %copy-done.28, bf16[48,768]{1,0:T(8,128)(2,1)S(1)} %get-tuple-element.13.x_ref.pooled_ref, bf16[8,16,512]{2,1,0:T(8,128)(2,1)S(1)} %all_to_all.11.recv_ref, bf16[3,384,128]{2,1,0:T(8,128)(2,1)S(1)} %copy-done.9, bf16[256,768]{1,0:T(8,128)(2,1)S(1)} %copy-done.7, ...), custom_call_target="tpu_custom_call" | custom-call | tf_op jit(solution)/shard_map/conv_coarse/pallas_call | solution.py:558
  57.0 1.5 %collective-permute-start.4 = (bf16[48,768]{1,0:T(8,128)(2,1)S(1)}, bf16[48,768]{1,0:T(8,128)(2,1)S(1)}, u32[]{:S(2)}, u32[]{:S(2)}) collective-permute-start(bf16[48,768]{1,0:T(8,128)(2,1)S(1)} %conv_coarse.1.own_ref), channel_id=1, source_target_pairs={{0,2},{1,3},{2,0},{3,1},{4,6},{5,7},{6,4},{7,5},{8,10},{9,11},{10,... | collective-permute-start | bytes 221192 | tf_op jit(solution)/shard_map/ppermute | solution.py:496
  58.6 2.9 %collective-permute-done.4.p2_ref = bf16[48,768]{1,0:T(8,128)(2,1)S(1)} collective-permute-done((bf16[48,768]{1,0:T(8,128)(2,1)S(1)}, bf16[48,768]{1,0:T(8,128)(2,1)S(1)}, u32[]{:S(2)}, u32[]{:S(2)}) %collective-permute-start.4) | collective-permute-done | bytes 73760 | tf_op jit(solution)/shard_map/ppermute | solution.py:496
  61.4 0.1 copy.28.spread_weight_ref
  61.5 1.2 %collective-permute-done.5.p3_ref = bf16[48,768]{1,0:T(8,128)(2,1)S(1)} collective-permute-done((bf16[48,768]{1,0:T(8,128)(2,1)S(1)}, bf16[48,768]{1,0:T(8,128)(2,1)S(1)}, u32[]{:S(2)}, u32[]{:S(2)}) %collective-permute-start.5) | collective-permute-done | bytes 73760 | tf_op jit(solution)/shard_map/ppermute | solution.py:498
  62.7 2.6 %mix_coarse.1 = bf16[1,48,2304]{2,1,0:T(8,128)(2,1)} custom-call(bf16[48,768]{1,0:T(8,128)(2,1)S(1)} %conv_coarse.1.own_ref, bf16[48,768]{1,0:T(8,128)(2,1)S(1)} %collective-permute-done.3.p1_ref, bf16[48,768]{1,0:T(8,128)(2,1)S(1)} %collective-permute-done.4.p2_ref, bf16[48,768]{1,0:T(8,128)(2,1)S(1)} %collective-permute-done.5.p3_ref, ...), custom_call_target="tpu_custom_call" | custom-call | tf_op jit(solution)/shard_map/mix_coarse/pallas_call | solution.py:571
  (52 shorter events, 0.1 us)
Async XLA Ops:
  0.0 0.9 %copy-start.1 = (bf16[1,48,2304]{2,1,0:T(8,128)(2,1)S(1)}, bf16[1,48,2304]{2,1,0:T(8,128)(2,1)}, u32[]{:S(2)}) copy-start(bf16[1,48,2304]{2,1,0:T(8,128)(2,1)} %x_ref.5) | copy-start | bytes 663556
  0.9 0.9 %copy-start.12 = (bf16[384,256]{1,0:T(8,128)(2,1)S(1)}, bf16[384,256]{1,0:T(8,128)(2,1)}, u32[]{:S(2)}) copy-start(bf16[384,256]{1,0:T(8,128)(2,1)} %constant.18.clone.pack_ref) | copy-start | bytes 589828
  3.2 17.1 %copy-start.6 = (bf16[512,512]{1,0:T(8,128)(2,1)S(1)}, bf16[512,512]{1,0:T(8,128)(2,1)}, u32[]{:S(2)}) copy-start(bf16[512,512]{1,0:T(8,128)(2,1)} %constant.20.clone.expand_ref) | copy-start | bytes 1572868
  4.8 24.3 %copy-start.27 = (s32[16]{0:T(128)}, s32[16]{0:T(128)S(1)}, u32[]{:S(2)}) copy-start(s32[16]{0:T(128)S(1)} %get-tuple-element.11.tab_ref) | copy-start | bytes 196
  20.3 0.9 %copy-start.2 = (bf16[1,48,2304]{2,1,0:T(8,128)(2,1)S(1)}, bf16[1,48,2304]{2,1,0:T(8,128)(2,1)}, u32[]{:S(2)}) copy-start(bf16[1,48,2304]{2,1,0:T(8,128)(2,1)} %x_ref.5) | copy-start | bytes 663556
  21.2 1.3 %copy-start.4 = (bf16[3,768,256]{2,1,0:T(8,128)(2,1)S(1)}, bf16[3,768,256]{2,1,0:T(8,128)(2,1)}, u32[]{:S(2)}) copy-start(bf16[3,768,256]{2,1,0:T(8,128)(2,1)} %constant.19.clone.halo_ref) | copy-start | bytes 3538948
  22.5 1.0 %copy-start.8 = (bf16[512,384]{1,0:T(8,128)(2,1)S(1)}, bf16[512,384]{1,0:T(8,128)(2,1)}, u32[]{:S(2)}) copy-start(bf16[512,384]{1,0:T(8,128)(2,1)} %constant.21.clone.compact_ref) | copy-start | bytes 1179652
  25.0 11.4 %copy-start.29 = (f32[48,4]{0,1:T(4,128)S(1)}, f32[48,4]{0,1:T(4,128)}, u32[]{:S(2)}) copy-start(f32[48,4]{0,1:T(4,128)} %param.37) | copy-start | bytes 2308
  25.0 11.6 %copy-start.14 = (bf16[384,128]{1,0:T(8,128)(2,1)S(1)}, bf16[384,128]{1,0:T(8,128)(2,1)}, u32[]{:S(2)}) copy-start(bf16[384,128]{1,0:T(8,128)(2,1)} %constant.22.clone.pool_ref) | copy-start | bytes 294916
  25.0 11.6 %copy-start.15 = (s32[1,2304]{1,0:T(1,128)S(1)}, s32[1,2304]{1,0:T(1,128)}, u32[]{:S(2)}) copy-start(s32[1,2304]{1,0:T(1,128)} %mask_ref.3) | copy-start | bytes 27652
  25.0 11.6 %copy-start.16 = (f32[2,768]{1,0:T(2,128)S(1)}, f32[2,768]{1,0:T(2,128)}, u32[]{:S(2)}) copy-start(f32[2,768]{1,0:T(2,128)} %up_bias_ref.3) | copy-start | bytes 18436
  25.0 11.6 %copy-start.18 = (f32[2,192]{1,0:T(2,128)S(1)}, f32[2,192]{1,0:T(2,128)}, u32[]{:S(2)}) copy-start(f32[2,192]{1,0:T(2,128)} %shift_ref.3) | copy-start | bytes 4612
  25.0 11.6 %copy-start.19 = (f32[2,192]{1,0:T(2,128)S(1)}, f32[2,192]{1,0:T(2,128)}, u32[]{:S(2)}) copy-start(f32[2,192]{1,0:T(2,128)} %down_bias_ref.3) | copy-start | bytes 4612
  25.0 11.6 %copy-start.20 = (f32[2,48]{1,0:T(2,128)S(1)}, f32[2,48]{1,0:T(2,128)}, u32[]{:S(2)}) copy-start(f32[2,48]{1,0:T(2,128)} %scale_ref.3) | copy-start | bytes 1156
  25.0 11.6 %copy-start.24 = (s32[8]{0:T(128)S(1)}, s32[8]{0:T(128)}, u32[]{:S(2)}) copy-start(s32[8]{0:T(128)} %slots_ref.3) | copy-start | bytes 100
  29.0 7.6 %copy-start = (bf16[2,192,768]{2,1,0:T(8,128)(2,1)S(1)}, bf16[2,192,768]{2,1,0:T(8,128)(2,1)}, u32[]{:S(2)}) copy-start(bf16[2,192,768]{2,1,0:T(8,128)(2,1)} %down_ref.3) | copy-start | bytes 1769476
  29.0 7.6 %copy-start.3 = (bf16[1,48,2304]{2,1,0:T(8,128)(2,1)S(1)}, bf16[1,48,2304]{2,1,0:T(8,128)(2,1)}, u32[]{:S(2)}) copy-start(bf16[1,48,2304]{2,1,0:T(8,128)(2,1)} %x_ref.5) | copy-start | bytes 663556
  29.0 7.6 %copy-start.5 = (bf16[768,384]{1,0:T(8,128)(2,1)S(1)}, bf16[768,384]{1,0:T(8,128)(2,1)}, u32[]{:S(2)}) copy-start(bf16[768,384]{1,0:T(8,128)(2,1)} %constant.23.clone.pack_ref) | copy-start | bytes 1769476
  29.1 7.6 %copy-start.17 = (f32[2,192]{1,0:T(2,128)S(1)}, f32[2,192]{1,0:T(2,128)}, u32[]{:S(2)}) copy-start(f32[2,192]{1,0:T(2,128)} %gain_ref.3) | copy-start | bytes 4612
  29.1 6.0 %collective-permute-start.1 = (bf16[48,2304]{1,0:T(8,128)(2,1)S(1)}, bf16[48,2304]{1,0:T(8,128)(2,1)S(1)}, u32[]{:S(2)}, u32[]{:S(2)}) collective-permute-start(bf16[48,2304]{1,0:T(8,128)(2,1)S(1)} %conv_fine.1.own_ref), channel_id=1, source_target_pairs={{0,2},{1,3},{2,0},{3,1},{4,6},{5,7},{6,4},{7,5},{8,10},{9,11},{10,... | collective-permute-start | bytes 663560 | tf_op jit(solution)/shard_map/ppermute | solution.py:496
  30.6 5.9 %collective-permute-start = (bf16[48,2304]{1,0:T(8,128)(2,1)S(1)}, bf16[48,2304]{1,0:T(8,128)(2,1)S(1)}, u32[]{:S(2)}, u32[]{:S(2)}) collective-permute-start(bf16[48,2304]{1,0:T(8,128)(2,1)S(1)} %conv_fine.1.own_ref), channel_id=1, source_target_pairs={{0,1},{1,0},{2,3},{3,2},{4,5},{5,4},{6,7},{7,6},{8,9},{9,8},{10,11... | collective-permute-start | bytes 663560 | tf_op jit(solution)/shard_map/ppermute | solution.py:497
  35.1 1.5 %collective-permute-start.2 = (bf16[48,2304]{1,0:T(8,128)(2,1)S(1)}, bf16[48,2304]{1,0:T(8,128)(2,1)S(1)}, u32[]{:S(2)}, u32[]{:S(2)}) collective-permute-start(bf16[48,2304]{1,0:T(8,128)(2,1)S(1)} %collective-permute-done.1.p2_ref), channel_id=1, source_target_pairs={{0,1},{1,0},{2,3},{3,2},{4,5},{5,4},{6,7},{7,6},{8,9},{9,8},{10,11... | collective-permute-start | bytes 663560 | tf_op jit(solution)/shard_map/ppermute | solution.py:498
  36.5 18.3 %copy-start.7 = (bf16[256,768]{1,0:T(8,128)(2,1)S(1)}, bf16[256,768]{1,0:T(8,128)(2,1)}, u32[]{:S(2)}) copy-start(bf16[256,768]{1,0:T(8,128)(2,1)} %constant.25.clone.sides_ref) | copy-start | bytes 1179652
  36.5 18.3 %copy-start.9 = (bf16[3,384,128]{2,1,0:T(8,128)(2,1)S(1)}, bf16[3,384,128]{2,1,0:T(8,128)(2,1)}, u32[]{:S(2)}) copy-start(bf16[3,384,128]{2,1,0:T(8,128)(2,1)} %constant.24.clone.halo_ref) | copy-start | bytes 884740
  36.5 18.3 %copy-start.11 = (f32[2,48,49]{2,1,0:T(8,128)S(1)}, f32[2,48,49]{2,1,0:T(8,128)}, u32[]{:S(2)}) copy-start(f32[2,48,49]{2,1,0:T(8,128)} %weight_ref.3) | copy-start | bytes 56452
  36.5 18.3 %copy-start.22 = (f32[2,48]{1,0:T(2,128)S(1)}, f32[2,48]{1,0:T(2,128)}, u32[]{:S(2)}) copy-start(f32[2,48]{1,0:T(2,128)} %bias_ref.3) | copy-start | bytes 1156
  37.4 17.4 %copy-start.28 = (s32[16]{0:T(128)S(1)}, s32[16]{0:T(128)}, u32[]{:S(2)}) copy-start(s32[16]{0:T(128)} %copy-done.27) | copy-start | bytes 196
  42.9 18.5 %copy-start.30 = (f32[48,4]{0,1:T(4,128)S(1)}, f32[48,4]{0,1:T(4,128)}, u32[]{:S(2)}) copy-start(f32[48,4]{0,1:T(4,128)} %param.38) | copy-start | bytes 2308
  42.9 19.8 %copy-start.13 = (bf16[128,384]{1,0:T(8,128)(2,1)S(1)}, bf16[128,384]{1,0:T(8,128)(2,1)}, u32[]{:S(2)}) copy-start(bf16[128,384]{1,0:T(8,128)(2,1)} %constant.26.clone.unpool_ref) | copy-start | bytes 294916
  57.0 4.4 %collective-permute-start.4 = (bf16[48,768]{1,0:T(8,128)(2,1)S(1)}, bf16[48,768]{1,0:T(8,128)(2,1)S(1)}, u32[]{:S(2)}, u32[]{:S(2)}) collective-permute-start(bf16[48,768]{1,0:T(8,128)(2,1)S(1)} %conv_coarse.1.own_ref), channel_id=1, source_target_pairs={{0,2},{1,3},{2,0},{3,1},{4,6},{5,7},{6,4},{7,5},{8,10},{9,11},{10,... | collective-permute-start | bytes 221192 | tf_op jit(solution)/shard_map/ppermute | solution.py:496
  58.6 3.0 %collective-permute-start.3 = (bf16[48,768]{1,0:T(8,128)(2,1)S(1)}, bf16[48,768]{1,0:T(8,128)(2,1)S(1)}, u32[]{:S(2)}, u32[]{:S(2)}) collective-permute-start(bf16[48,768]{1,0:T(8,128)(2,1)S(1)} %conv_coarse.1.own_ref), channel_id=1, source_target_pairs={{0,1},{1,0},{2,3},{3,2},{4,5},{5,4},{6,7},{7,6},{8,9},{9,8},{10,11... | collective-permute-start | bytes 221192 | tf_op jit(solution)/shard_map/ppermute | solution.py:497
  61.4 1.3 %collective-permute-start.5 = (bf16[48,768]{1,0:T(8,128)(2,1)S(1)}, bf16[48,768]{1,0:T(8,128)(2,1)S(1)}, u32[]{:S(2)}, u32[]{:S(2)}) collective-permute-start(bf16[48,768]{1,0:T(8,128)(2,1)S(1)} %collective-permute-done.4.p2_ref), channel_id=1, source_target_pairs={{0,1},{1,0},{2,3},{3,2},{4,5},{5,4},{6,7},{7,6},{8,9},{9,8},{10,11... | collective-permute-start | bytes 221192 | tf_op jit(solution)/shard_map/ppermute | solution.py:498
  (5 other events, 3.5 us)
where the time goes:
time: 65.8 us; the launch traced here: 65.3 us
  blocking collectives  27.4 us (42%)
  Pallas kernels  15.8 us (24%)
  local copies, waits for them, and re-layouts  10.2 us (16%)
  waiting for transfers between devices  8.47 us (13%)
  starting transfers between devices  3.12 us (5%)
    all_to_all x2, blocking collectives, per_device(): arrived = lax.all_to_all(messages, 'tile', 0, 0, tiled=True)  27.4 us
    unnamed x65, local copies, waits for them, and re-layouts  10.2 us
    ppermute x2, waiting for transfers between devices, every_channel(): across = lax.ppermute(own, 'chan', pairs(2))  7.3 us
    pallas_call x1, Pallas kernels, per_device(): pl.pallas_call(make_mix_fine(grid_x), in_specs=[SMEM, SMEM] + [VMEM] * 8...  5.49 us
    pallas_call x1, Pallas kernels, per_device(): pl.pallas_call(conv_fine, in_specs=[SMEM, VMEM, VMEM, VMEM, VMEM, VMEM, V...  3.98 us
    ppermute x2, starting transfers between devices, every_channel(): across = lax.ppermute(own, 'chan', pairs(2))  3.11 us
    pallas_call x1, Pallas kernels, per_device(): pl.pallas_call(mix_coarse, in_specs=[VMEM] * 10 + [VMEM] * 7, out_specs=V...  2.59 us
    pallas_call x1, Pallas kernels, per_device(): pl.pallas_call(conv_coarse, in_specs=[SMEM, VMEM, VMEM, VMEM, VMEM, VMEM,...  2.15 us
  transfers between devices with their start and end apart: 6, of which 3 were waited for; matrix products, arithmetic and copies ran while one was open for 2% of the time, Pallas kernels for 0%

commit v1 on v0

--- a/solution.py
+++ b/solution.py
@@ -147,8 +147,21 @@
     return lax.fori_loop(0, count, step, carry)
 
 
+LOADED = ("x", "mask", "weight", "bias", "halo", "expand", "compact", "small_halo", "sides", "pool", "unpool", "small_pack")
+
+
 def make_prep(grid_x):
-    def prep(slots_ref, dev_ref, x_ref, pack_ref, msg_ref, tab_ref, rows_ref, cols_ref, row_rest_ref, col_rest_ref):
+    def prep(slots_hbm, dev_hbm, pack_hbm, *refs):
+        size = len(LOADED)
+        sources, (msg_ref, tab_ref), targets = refs[:size], refs[size : size + 2], refs[size + 2 : 2 * size + 2]
+        slots_ref, dev_ref, pack_ref, rows_ref, cols_ref, row_rest_ref, col_rest_ref, sems = refs[2 * size + 2 :]
+        pairs = [(slots_hbm, slots_ref), (dev_hbm, dev_ref), (sources[0], targets[0]), (pack_hbm, pack_ref)]
+        pairs += list(zip(sources[1:], targets[1:]))
+        loads = [pltpu.make_async_copy(source, target, sems.at[i]) for i, (source, target) in enumerate(pairs)]
+        for load in loads:
+            load.start()
+        loads[0].wait()
+        loads[1].wait()
         count = slots_ref.shape[0]
         me = lax.axis_index("tile")
         my_slot = scan_tiles(count, lambda k, c: c + jnp.where(dev_ref[k] == me, slots_ref[k], 0), jnp.int32(0))
@@ -165,14 +178,21 @@
 
         def find(k, found):
             slot, dev = slots_ref[k], dev_ref[k]
+            row_pick = jnp.where(lax.div(slot, grid_x) + 1 == my_y, 0, 1)
+            col_pick = jnp.where(lax.rem(slot, grid_x) == lax.rem(my_x + (grid_x - 1), grid_x), 0, 1)
+            tab_ref[16 + dev] = 2 * row_pick + col_pick
             return tuple(jnp.where(slot == want, dev, old) for want, old in zip(wanted, found))
 
         found = scan_tiles(count, find, tuple(jnp.int32(-1) for _ in BANDS))
         for band in range(8):
             tab_ref[band] = found[band]
         tab_ref[8] = jnp.where(my_y == GRID_Y - 1, 2, 1)
-
-        x = x_ref[0]
+        for spare in range(9, 16):
+            tab_ref[spare] = 0
+
+        loads[2].wait()
+        loads[3].wait()
+        x = targets[0][0]
         cols = dot(stacked(x, FINE_IN), pack_ref[...])
         lane = lane_ids((ROWS, 128))
         for side in range(2):
@@ -190,10 +210,9 @@
             rest = jnp.where(lane < 16, ends[side], 0.0)
             row_rest_ref[side] = rest[0:16] + pltpu.roll(rest[16:32], 40, 1) + pltpu.roll(rest[32:48], 80, 1)
 
-        def fill(k, carry):
-            slot, dev = slots_ref[k], dev_ref[k]
-            row_pick = jnp.where(lax.div(slot, grid_x) + 1 == my_y, 0, 1)
-            col_pick = jnp.where(lax.rem(slot, grid_x) == lax.rem(my_x + (grid_x - 1), grid_x), 0, 1)
+        def fill(dev, carry):
+            row_pick = lax.div(tab_ref[16 + dev], 2)
+            col_pick = lax.rem(tab_ref[16 + dev], 2)
             for g in range(3):
                 msg_ref[dev, :, 256 * g : 256 * g + 128] = rows_ref[row_pick, 16 * g : 16 * g + 16, :]
                 msg_ref[dev, :, 256 * g + 128 : 256 * g + 256] = cols_ref[col_pick, 16 * g : 16 * g + 16, :]
@@ -201,6 +220,8 @@
             return carry
 
         scan_tiles(count, fill, jnp.int32(0))
+        for load in loads[4:]:
+            load.wait()
 
     return prep
 
@@ -385,9 +406,9 @@
     return result
 
 
-def make_mix_fine(grid_x):
+def make_mix_fine(count):
     def mix_fine(
-        slots_ref, dev_ref, own_ref, p1_ref, p2_ref, p3_ref, x_ref, mask_ref, gain_ref, shift_ref, up_ref, up_bias_ref,
+        tab_ref, own_ref, p1_ref, p2_ref, p3_ref, x_ref, mask_ref, gain_ref, shift_ref, up_ref, up_bias_ref,
         down_ref, down_bias_ref, scale_ref, pool_weight_ref, pool_ref, pack_ref,
         fine_ref, pooled_ref, small_mask_ref, msg_ref, cat_ref, mains_ref, rest_ref,
     ):
@@ -436,17 +457,9 @@
             joined = jnp.where(lane < 24, parts[0], jnp.where(lane < 48, parts[1], parts[2]))
             rest_ref[c] = jnp.where(lane < 72, joined, 0.0).astype(BF)
 
-        count = slots_ref.shape[0]
-        me = lax.axis_index("tile")
-        my_slot = scan_tiles(count, lambda k, c: c + jnp.where(dev_ref[k] == me, slots_ref[k], 0), jnp.int32(0))
-        my_x = lax.rem(my_slot, grid_x)
-        my_y = lax.div(my_slot, grid_x)
-
-        def fill(k, carry):
-            slot, dev = slots_ref[k], dev_ref[k]
-            row_pick = jnp.where(lax.div(slot, grid_x) + 1 == my_y, 0, 1)
-            col_pick = jnp.where(lax.rem(slot, grid_x) == lax.rem(my_x + (grid_x - 1), grid_x), 0, 1)
-            both = 2 * row_pick + col_pick
+        def fill(dev, carry):
+            both = tab_ref[16 + dev]
+            col_pick = lax.rem(both, 2)
             for g in range(3):
                 msg_ref[dev, :, 128 * g : 128 * g + 128] = mains_ref[both, 16 * g : 16 * g + 16, :]
             msg_ref[dev, :, 384:512] = rest_ref[col_pick]
@@ -482,13 +495,14 @@
 
 VMEM = pl.BlockSpec(memory_space=pltpu.VMEM)
 SMEM = pl.BlockSpec(memory_space=pltpu.SMEM)
+ANY = pl.BlockSpec(memory_space=pl.ANY)
 
 
 def shaped(*shape, dtype=BF):
     return jax.ShapeDtypeStruct(shape, dtype)
 
 
-PARAMS = pltpu.CompilerParams(vmem_limit_bytes=48 * 1024 * 1024)
+PARAMS = pltpu.CompilerParams(vmem_limit_bytes=24 * 1024 * 1024)
 
 
 def every_channel(own):
@@ -506,24 +520,47 @@
     count = wet_slots.shape[0]
     grid_x = 2 * count // GRID_Y
     cells = TILE * TILE
-    messages, table = pl.pallas_call(
+    given = {
+        "x": features,
+        "mask": land_mask,
+        "weight": depth_weight,
+        "bias": depth_bias,
+        "halo": jnp.asarray(FINE["halo"]),
+        "expand": jnp.asarray(FINE["expand"]),
+        "compact": jnp.asarray(FINE["compact"]),
+        "small_halo": jnp.asarray(COARSE["halo"]),
+        "sides": jnp.asarray(COARSE["sides"]),
+        "pool": jnp.asarray(FINE["pool"]),
+        "unpool": jnp.asarray(FINE["unpool"]),
+        "small_pack": jnp.asarray(COARSE["pack"]),
+    }
+    given = [given[name] for name in LOADED]
+    pack = jnp.asarray(FINE["pack"])
+    results = pl.pallas_call(
         make_prep(grid_x),
-        in_specs=[SMEM, SMEM, VMEM, VMEM],
-        out_specs=[VMEM, SMEM],
-        out_shape=[shaped(count, 16, 896), shaped(16, dtype=jnp.int32)],
+        in_specs=[ANY] * (3 + len(given)),
+        out_specs=[VMEM, SMEM] + [VMEM] * len(given),
+        out_shape=[shaped(count, 16, 896), shaped(16 + count, dtype=jnp.int32)]
+        + [shaped(*array.shape, dtype=array.dtype) for array in given],
         scratch_shapes=[
+            pltpu.SMEM((count,), jnp.int32),
+            pltpu.SMEM((count,), jnp.int32),
+            pltpu.VMEM(pack.shape, BF),
             pltpu.VMEM((2, ROWS, 128), BF),
             pltpu.VMEM((2, ROWS, 128), BF),
             pltpu.VMEM((2, 16, 128), F32),
             pltpu.VMEM((2, 16, 128), F32),
+            pltpu.SemaphoreType.DMA((3 + len(given),)),
         ],
         compiler_params=PARAMS,
         name="prep",
-    )(wet_slots, device_of, features, jnp.asarray(FINE["pack"]))
+    )(wet_slots, device_of, pack, *given)
+    messages, table = results[:2]
+    held = dict(zip(LOADED, results[2:]))
     arrived = lax.all_to_all(messages, "tile", 0, 0, tiled=True)
     conv = pl.pallas_call(
         conv_fine,
-        in_specs=[SMEM, VMEM, VMEM, VMEM, VMEM, VMEM, VMEM, VMEM],
+        in_specs=[SMEM] + [VMEM] * 7,
         out_specs=VMEM,
         out_shape=shaped(ROWS, cells),
         scratch_shapes=[
@@ -534,13 +571,10 @@
         ],
         compiler_params=PARAMS,
         name="conv_fine",
-    )(
-        table, features, arrived, jnp.asarray(FINE["halo"]), jnp.asarray(FINE["expand"]), jnp.asarray(FINE["compact"]),
-        depth_weight, depth_bias,
-    )
+    )(table, held["x"], arrived, held["halo"], held["expand"], held["compact"], held["weight"], held["bias"])
     fine, pooled, small_mask, messages = pl.pallas_call(
-        make_mix_fine(grid_x),
-        in_specs=[SMEM, SMEM] + [VMEM] * 8 + [VMEM] * 8,
+        make_mix_fine(count),
+        in_specs=[SMEM] + [VMEM] * 16,
         out_specs=[VMEM] * 4,
         out_shape=[shaped(ROWS, cells), shaped(ROWS, 768), shaped(48, 128, dtype=F32), shaped(count, 16, 512)],
         scratch_shapes=[
@@ -551,13 +585,13 @@
         compiler_params=PARAMS,
         name="mix_fine",
     )(
-        wet_slots, device_of, *every_channel(conv), features, land_mask, norm_gain, norm_bias, up_weight, up_bias,
-        down_weight, down_bias, layer_scale, pool_weight, jnp.asarray(FINE["pool"]), jnp.asarray(COARSE["pack"]),
+        table, *every_channel(conv), held["x"], held["mask"], norm_gain, norm_bias, up_weight, up_bias,
+        down_weight, down_bias, layer_scale, pool_weight, held["pool"], held["small_pack"],
     )
     arrived = lax.all_to_all(messages, "tile", 0, 0, tiled=True)
     conv = pl.pallas_call(
         conv_coarse,
-        in_specs=[SMEM, VMEM, VMEM, VMEM, VMEM, VMEM, VMEM],
+        in_specs=[SMEM] + [VMEM] * 6,
         out_specs=VMEM,
         out_shape=shaped(ROWS, 768),
         scratch_shapes=[
@@ -567,18 +601,18 @@
         ],
         compiler_params=PARAMS,
         name="conv_coarse",
-    )(table, pooled, arrived, jnp.asarray(COARSE["halo"]), jnp.asarray(COARSE["sides"]), depth_weight, depth_bias)
+    )(table, pooled, arrived, held["small_halo"], held["sides"], held["weight"], held["bias"])
     return pl.pallas_call(
         mix_coarse,
-        in_specs=[VMEM] * 10 + [VMEM] * 7,
+        in_specs=[VMEM] * 17,
         out_specs=VMEM,
         out_shape=shaped(1, ROWS, cells),
         scratch_shapes=[pltpu.VMEM((4 * ROWS, 768), BF)],
         compiler_params=PARAMS,
         name="mix_coarse",
     )(
-        *every_channel(conv), pooled, small_mask, fine, land_mask, norm_gain, norm_bias, up_weight, up_bias,
-        down_weight, down_bias, layer_scale, spread_weight, jnp.asarray(FINE["unpool"]),
+        *every_channel(conv), pooled, small_mask, fine, held["mask"], norm_gain, norm_bias, up_weight, up_bias,
+        down_weight, down_bias, layer_scale, spread_weight, held["unpool"],
     )
 
 

time: 65.8 us -> 73.9 us (1.12)
  local copies, waits for them, and re-layouts: 10.2 us -> 15.9 us
  Pallas kernels: 15.8 us -> 18 us
    unnamed x65 -> x61, local copies, waits for them, and re-layouts: 10.2 us -> 15.9 us
    pallas_call x5, Pallas kernels: 15.8 us -> 18 us  [the longest x1 6.01 us: per_device(): pl.pallas_call(make_mix_fine(count), in_specs=[SMEM] + [VMEM] * 16, out_s...]
  transfers between devices with their start and end apart: 6 -> 6, of which waited for: 3 -> 4; matrix products, arithmetic and copies ran while one was open for 2% -> 2% of each run, Pallas kernels for 0% -> 0%
where the time goes in v1:
time: 73.9 us; the launch traced here: 73.1 us
  blocking collectives  27.2 us (37%)
  Pallas kernels  18 us (24%)
  local copies, waits for them, and re-layouts  15.9 us (22%)
  waiting for transfers between devices  8.63 us (12%)
  starting transfers between devices  3.13 us (4%)
    all_to_all x2, blocking collectives, per_device(): arrived = lax.all_to_all(messages, 'tile', 0, 0, tiled=True)  27.2 us
    unnamed x61, local copies, waits for them, and re-layouts  15.9 us
    ppermute x2, waiting for transfers between devices, every_channel(): across = lax.ppermute(own, 'chan', pairs(2))  7.29 us
    pallas_call x1, Pallas kernels, per_device(): pl.pallas_call(make_mix_fine(count), in_specs=[SMEM] + [VMEM] * 16, out_s...  6.01 us
    pallas_call x1, Pallas kernels, per_device(): pl.pallas_call(conv_fine, in_specs=[SMEM] + [VMEM] * 7, out_specs=VMEM, o...  4 us
    pallas_call x1, Pallas kernels, per_device(): pl.pallas_call(make_prep(grid_x), in_specs=[ANY] * (3 + len(given)), out_...  3.24 us
    ppermute x2, starting transfers between devices, every_channel(): across = lax.ppermute(own, 'chan', pairs(2))  3.12 us
    pallas_call x1, Pallas kernels, per_device(): pl.pallas_call(mix_coarse, in_specs=[VMEM] * 17, out_specs=VMEM, out_shap...  2.59 us
  transfers between devices with their start and end apart: 6, of which 4 were waited for; matrix products, arithmetic and copies ran while one was open for 2% of the time, Pallas kernels for 0%

profile of v1, /device:TPU:0, one launch (start us, length us, event | category | flops | bytes accessed | tf_op | source)
XLA Modules:
  0.0 73.1 jit_solution(300270465048979400)
XLA Ops:
  0.0 1.3 %copy-done.1 = bf16[3,768,256]{2,1,0:T(8,128)(2,1)S(1)} copy-done((bf16[3,768,256]{2,1,0:T(8,128)(2,1)S(1)}, bf16[3,768,256]{2,1,0:T(8,128)(2,1)}, u32[]{:S(2)}) %copy-start.1) | copy-done | bytes 1179672
  1.3 1.1 %copy-done.2 = bf16[768,384]{1,0:T(8,128)(2,1)S(1)} copy-done((bf16[768,384]{1,0:T(8,128)(2,1)S(1)}, bf16[768,384]{1,0:T(8,128)(2,1)}, u32[]{:S(2)}) %copy-start.2) | copy-done | bytes 589848
  2.3 1.0 %copy-done.3 = bf16[512,512]{1,0:T(8,128)(2,1)S(1)} copy-done((bf16[512,512]{1,0:T(8,128)(2,1)S(1)}, bf16[512,512]{1,0:T(8,128)(2,1)}, u32[]{:S(2)}) %copy-start.3) | copy-done | bytes 524312
  3.4 1.0 %copy-done.4 = bf16[512,384]{1,0:T(8,128)(2,1)S(1)} copy-done((bf16[512,384]{1,0:T(8,128)(2,1)S(1)}, bf16[512,384]{1,0:T(8,128)(2,1)}, u32[]{:S(2)}) %copy-start.4) | copy-done | bytes 393240
  4.4 1.0 %copy-done.5 = bf16[256,768]{1,0:T(8,128)(2,1)S(1)} copy-done((bf16[256,768]{1,0:T(8,128)(2,1)S(1)}, bf16[256,768]{1,0:T(8,128)(2,1)}, u32[]{:S(2)}) %copy-start.5) | copy-done | bytes 393240
  5.4 1.0 %copy-done.6 = bf16[3,384,128]{2,1,0:T(8,128)(2,1)S(1)} copy-done((bf16[3,384,128]{2,1,0:T(8,128)(2,1)S(1)}, bf16[3,384,128]{2,1,0:T(8,128)(2,1)}, u32[]{:S(2)}) %copy-start.6) | copy-done | bytes 294936
  6.3 0.9 %copy-done.7 = bf16[1,48,2304]{2,1,0:T(8,128)(2,1)S(1)} copy-done((bf16[1,48,2304]{2,1,0:T(8,128)(2,1)S(1)}, bf16[1,48,2304]{2,1,0:T(8,128)(2,1)}, u32[]{:S(2)}) %copy-start.7) | copy-done | bytes 221208
  7.3 0.9 %copy-done.10 = bf16[384,256]{1,0:T(8,128)(2,1)S(1)} copy-done((bf16[384,256]{1,0:T(8,128)(2,1)S(1)}, bf16[384,256]{1,0:T(8,128)(2,1)}, u32[]{:S(2)}) %copy-start.10) | copy-done | bytes 196632
  8.2 0.9 %copy-done.15 = bf16[384,128]{1,0:T(8,128)(2,1)S(1)} copy-done((bf16[384,128]{1,0:T(8,128)(2,1)S(1)}, bf16[384,128]{1,0:T(8,128)(2,1)}, u32[]{:S(2)}) %copy-start.15) | copy-done | bytes 98328
  9.1 0.9 %copy-done.16 = bf16[128,384]{1,0:T(8,128)(2,1)S(1)} copy-done((bf16[128,384]{1,0:T(8,128)(2,1)S(1)}, bf16[128,384]{1,0:T(8,128)(2,1)}, u32[]{:S(2)}) %copy-start.16) | copy-done | bytes 98328
  10.0 0.8 %copy-done.17 = f32[2,48,49]{2,1,0:T(8,128)S(1)} copy-done((f32[2,48,49]{2,1,0:T(8,128)S(1)}, f32[2,48,49]{2,1,0:T(8,128)}, u32[]{:S(2)}) %copy-start.17) | copy-done | bytes 18840
  10.8 0.7 copy-done.19
  11.5 0.7 copy-done.24
  12.2 0.7 copy-done.25
  12.8 0.7 copy-done.26
  13.5 3.2 %prep.1 = (bf16[8,16,896]{2,1,0:T(8,128)(2,1)S(1)}, s32[24]{0:T(128)S(1)}, bf16[1,48,2304]{2,1,0:T(8,128)(2,1)S(1)}, s32[1,2304]{1,0:T(1,128)S(1)}, f32[2,48,49]...) custom-call(s32[8]{0:T(128)S(1)} %copy-done.25, ...), custom_call_target="tpu_custom_call" | custom-call | tf_op jit(solution)/shard_map/prep/pallas_call | solution.py:539
  16.7 15.5 %all_to_all.10.recv_ref = bf16[8,16,896]{2,1,0:T(8,128)(2,1)S(1)} all-to-all(bf16[8,16,896]{2,1,0:T(8,128)(2,1)S(1)} %get-tuple-element.25), channel_id=1, replica_groups=mesh['tile'=8,'chan'=4] {'tile'}, dimensions={0} | all-to-all | bytes 458752 | tf_op jit(solution)/shard_map/all_to_all | solution.py:560
  32.3 4.0 %conv_fine.1.own_ref = bf16[48,2304]{1,0:T(8,128)(2,1)S(1)} custom-call(s32[24]{0:T(128)S(1)} %get-tuple-element.23.tab_ref, bf16[1,48,2304]{2,1,0:T(8,128)(2,1)S(1)} %get-tuple-element.24.x_ref, bf16[8,16,896]{2,1,0:T(8,128)(2,1)S(1)} %all_to_all.10.recv_ref, bf16[3,768,256]{2,1,0:T(8,128)(2,1)S(1)} %get-tuple-element.26.halo_ref, ...), custom_call_target="tpu_custom_call" | custom-call | tf_op jit(solution)/shard_map/conv_fine/pallas_call | solution.py:561
  36.4 1.6 %collective-permute-start.1 = (bf16[48,2304]{1,0:T(8,128)(2,1)S(1)}, bf16[48,2304]{1,0:T(8,128)(2,1)S(1)}, u32[]{:S(2)}, u32[]{:S(2)}) collective-permute-start(bf16[48,2304]{1,0:T(8,128)(2,1)S(1)} %conv_fine.1.own_ref), channel_id=1, source_target_pairs={{0,2},{1,3},{2,0},{3,1},{4,6},{5,7},{6,4},{7,5},{8,10},{9,11},{10,... | collective-permute-start | bytes 663560 | tf_op jit(solution)/shard_map/ppermute | solution.py:510
  37.9 4.4 %collective-permute-done.1.p2_ref = bf16[48,2304]{1,0:T(8,128)(2,1)S(1)} collective-permute-done((bf16[48,2304]{1,0:T(8,128)(2,1)S(1)}, bf16[48,2304]{1,0:T(8,128)(2,1)S(1)}, u32[]{:S(2)}, u32[]{:S(2)}) %collective-permute-start.1) | collective-permute-done | bytes 221216 | tf_op jit(solution)/shard_map/ppermute | solution.py:510
  42.4 1.3 %copy.25.up_ref = bf16[2,768,192]{2,1,0:T(8,128)(2,1)S(1)} copy(bf16[2,768,192]{1,2,0:T(8,128)(2,1)} %param.32) | data formatting | bytes 1179648 | tf_op args[8]
  43.7 0.1 copy.26.pool_weight_ref
  43.8 0.2 collective-permute-done.2.p3_ref
  44.0 0.9 %copy-done.12 = bf16[384,128]{1,0:T(8,128)(2,1)S(1)} copy-done((bf16[384,128]{1,0:T(8,128)(2,1)S(1)}, bf16[384,128]{1,0:T(8,128)(2,1)}, u32[]{:S(2)}) %copy-start.12) | copy-done | bytes 98328
  44.9 6.0 %mix_fine.1 = (bf16[48,2304]{1,0:T(8,128)(2,1)S(1)}, bf16[48,768]{1,0:T(8,128)(2,1)S(1)}, f32[48,128]{1,0:T(8,128)S(1)}, bf16[8,16,512]{2,1,0:T(8,128)(2,1)S(1)}) custom-call(s32[24]{0:T(128)S(1)} %get-tuple-element.23.tab_ref, bf16[48,2304]{1,0:T(8,128)(2,1)S(1)} %conv_fine.1.own_ref, bf16[48,2304]{1,0:T(8,128)(2,1)} %collective-permute-done.p1_ref, ...), custom_call_target="tpu_custom_call" | custom-call | tf_op jit(solution)/shard_map/mix_fine/pallas_call | solution.py:575
  51.0 11.7 %all_to_all.11.recv_ref = bf16[8,16,512]{2,1,0:T(8,128)(2,1)S(1)} all-to-all(bf16[8,16,512]{2,1,0:T(8,128)(2,1)S(1)} %get-tuple-element.35), channel_id=1, replica_groups=mesh['tile'=8,'chan'=4] {'tile'}, dimensions={0} | all-to-all | bytes 262144 | tf_op jit(solution)/shard_map/all_to_all | solution.py:591
  62.7 2.2 %conv_coarse.1.own_ref = bf16[48,768]{1,0:T(8,128)(2,1)S(1)} custom-call(s32[24]{0:T(128)S(1)} %get-tuple-element.23.tab_ref, bf16[48,768]{1,0:T(8,128)(2,1)S(1)} %get-tuple-element.34.x_ref.pooled_ref, bf16[8,16,512]{2,1,0:T(8,128)(2,1)S(1)} %all_to_all.11.recv_ref, bf16[3,384,128]{2,1,0:T(8,128)(2,1)S(1)} %get-tuple-element.36.halo_ref, ...), custom_call_target="tpu_custom_call" | custom-call | tf_op jit(solution)/shard_map/conv_coarse/pallas_call | solution.py:592
  64.9 1.6 %collective-permute-start.4 = (bf16[48,768]{1,0:T(8,128)(2,1)S(1)}, bf16[48,768]{1,0:T(8,128)(2,1)S(1)}, u32[]{:S(2)}, u32[]{:S(2)}) collective-permute-start(bf16[48,768]{1,0:T(8,128)(2,1)S(1)} %conv_coarse.1.own_ref), channel_id=1, source_target_pairs={{0,2},{1,3},{2,0},{3,1},{4,6},{5,7},{6,4},{7,5},{8,10},{9,11},{10,... | collective-permute-start | bytes 221192 | tf_op jit(solution)/shard_map/ppermute | solution.py:510
  66.4 2.9 %collective-permute-done.4.p2_ref = bf16[48,768]{1,0:T(8,128)(2,1)S(1)} collective-permute-done((bf16[48,768]{1,0:T(8,128)(2,1)S(1)}, bf16[48,768]{1,0:T(8,128)(2,1)S(1)}, u32[]{:S(2)}, u32[]{:S(2)}) %collective-permute-start.4) | collective-permute-done | bytes 73760 | tf_op jit(solution)/shard_map/ppermute | solution.py:510
  69.3 0.1 copy.28.spread_weight_ref
  69.4 1.2 %collective-permute-done.5.p3_ref = bf16[48,768]{1,0:T(8,128)(2,1)S(1)} collective-permute-done((bf16[48,768]{1,0:T(8,128)(2,1)S(1)}, bf16[48,768]{1,0:T(8,128)(2,1)S(1)}, u32[]{:S(2)}, u32[]{:S(2)}) %collective-permute-start.5) | collective-permute-done | bytes 73760 | tf_op jit(solution)/shard_map/ppermute | solution.py:512
  70.5 2.6 %mix_coarse.1 = bf16[1,48,2304]{2,1,0:T(8,128)(2,1)} custom-call(bf16[48,768]{1,0:T(8,128)(2,1)S(1)} %conv_coarse.1.own_ref, bf16[48,768]{1,0:T(8,128)(2,1)S(1)} %collective-permute-done.3.p1_ref, bf16[48,768]{1,0:T(8,128)(2,1)S(1)} %collective-permute-done.4.p2_ref, bf16[48,768]{1,0:T(8,128)(2,1)S(1)} %collective-permute-done.5.p3_ref, ...), custom_call_target="tpu_custom_call" | custom-call | tf_op jit(solution)/shard_map/mix_coarse/pallas_call | solution.py:605
  (48 shorter events, 0.1 us)
Async XLA Ops:
  0.0 1.3 %copy-start.1 = (bf16[3,768,256]{2,1,0:T(8,128)(2,1)S(1)}, bf16[3,768,256]{2,1,0:T(8,128)(2,1)}, u32[]{:S(2)}) copy-start(bf16[3,768,256]{2,1,0:T(8,128)(2,1)} %constant.18.clone.refs_4_) | copy-start | bytes 3538948
  1.3 1.1 %copy-start.2 = (bf16[768,384]{1,0:T(8,128)(2,1)S(1)}, bf16[768,384]{1,0:T(8,128)(2,1)}, u32[]{:S(2)}) copy-start(bf16[768,384]{1,0:T(8,128)(2,1)} %constant.25.clone.refs_11_) | copy-start | bytes 1769476
  2.3 1.0 %copy-start.3 = (bf16[512,512]{1,0:T(8,128)(2,1)S(1)}, bf16[512,512]{1,0:T(8,128)(2,1)}, u32[]{:S(2)}) copy-start(bf16[512,512]{1,0:T(8,128)(2,1)} %constant.19.clone.refs_5_) | copy-start | bytes 1572868
  3.4 1.0 %copy-start.4 = (bf16[512,384]{1,0:T(8,128)(2,1)S(1)}, bf16[512,384]{1,0:T(8,128)(2,1)}, u32[]{:S(2)}) copy-start(bf16[512,384]{1,0:T(8,128)(2,1)} %constant.20.clone.refs_6_) | copy-start | bytes 1179652
  4.4 1.0 %copy-start.5 = (bf16[256,768]{1,0:T(8,128)(2,1)S(1)}, bf16[256,768]{1,0:T(8,128)(2,1)}, u32[]{:S(2)}) copy-start(bf16[256,768]{1,0:T(8,128)(2,1)} %constant.22.clone.refs_8_) | copy-start | bytes 1179652
  5.4 1.0 %copy-start.6 = (bf16[3,384,128]{2,1,0:T(8,128)(2,1)S(1)}, bf16[3,384,128]{2,1,0:T(8,128)(2,1)}, u32[]{:S(2)}) copy-start(bf16[3,384,128]{2,1,0:T(8,128)(2,1)} %constant.21.clone.refs_7_) | copy-start | bytes 884740
  6.3 0.9 %copy-start.7 = (bf16[1,48,2304]{2,1,0:T(8,128)(2,1)S(1)}, bf16[1,48,2304]{2,1,0:T(8,128)(2,1)}, u32[]{:S(2)}) copy-start(bf16[1,48,2304]{2,1,0:T(8,128)(2,1)} %refs_0_.1) | copy-start | bytes 663556
  7.3 0.9 %copy-start.10 = (bf16[384,256]{1,0:T(8,128)(2,1)S(1)}, bf16[384,256]{1,0:T(8,128)(2,1)}, u32[]{:S(2)}) copy-start(bf16[384,256]{1,0:T(8,128)(2,1)} %constant.26.clone.pack_hbm) | copy-start | bytes 589828
  8.2 0.9 %copy-start.15 = (bf16[384,128]{1,0:T(8,128)(2,1)S(1)}, bf16[384,128]{1,0:T(8,128)(2,1)}, u32[]{:S(2)}) copy-start(bf16[384,128]{1,0:T(8,128)(2,1)} %constant.23.clone.refs_9_) | copy-start | bytes 294916
  9.1 0.9 %copy-start.16 = (bf16[128,384]{1,0:T(8,128)(2,1)S(1)}, bf16[128,384]{1,0:T(8,128)(2,1)}, u32[]{:S(2)}) copy-start(bf16[128,384]{1,0:T(8,128)(2,1)} %constant.24.clone.refs_10_) | copy-start | bytes 294916
  10.0 0.8 %copy-start.17 = (f32[2,48,49]{2,1,0:T(8,128)S(1)}, f32[2,48,49]{2,1,0:T(8,128)}, u32[]{:S(2)}) copy-start(f32[2,48,49]{2,1,0:T(8,128)} %refs_2_.1) | copy-start | bytes 56452
  10.8 0.7 copy-start.19
  16.7 19.5 %copy-start.11 = (bf16[384,128]{1,0:T(8,128)(2,1)}, bf16[384,128]{1,0:T(8,128)(2,1)S(1)}, u32[]{:S(2)}) copy-start(bf16[384,128]{1,0:T(8,128)(2,1)S(1)} %get-tuple-element.32.pool_ref) | copy-start | bytes 294916
  16.7 19.5 %copy-start.13 = (bf16[128,384]{1,0:T(8,128)(2,1)}, bf16[128,384]{1,0:T(8,128)(2,1)S(1)}, u32[]{:S(2)}) copy-start(bf16[128,384]{1,0:T(8,128)(2,1)S(1)} %get-tuple-element.40.unpool_ref) | copy-start | bytes 294916
  36.3 7.4 %copy-start.27 = (f32[48,4]{0,1:T(4,128)S(1)}, f32[48,4]{0,1:T(4,128)}, u32[]{:S(2)}) copy-start(f32[48,4]{0,1:T(4,128)} %param.37) | copy-start | bytes 2308
  36.3 7.7 %copy-start = (bf16[2,192,768]{2,1,0:T(8,128)(2,1)S(1)}, bf16[2,192,768]{2,1,0:T(8,128)(2,1)}, u32[]{:S(2)}) copy-start(bf16[2,192,768]{2,1,0:T(8,128)(2,1)} %down_ref.3) | copy-start | bytes 1769476
  36.3 7.7 %copy-start.18 = (f32[2,768]{1,0:T(2,128)S(1)}, f32[2,768]{1,0:T(2,128)}, u32[]{:S(2)}) copy-start(f32[2,768]{1,0:T(2,128)} %up_bias_ref.3) | copy-start | bytes 18436
  36.3 7.7 %copy-start.20 = (f32[2,192]{1,0:T(2,128)S(1)}, f32[2,192]{1,0:T(2,128)}, u32[]{:S(2)}) copy-start(f32[2,192]{1,0:T(2,128)} %gain_ref.3) | copy-start | bytes 4612
  36.3 7.7 %copy-start.21 = (f32[2,192]{1,0:T(2,128)S(1)}, f32[2,192]{1,0:T(2,128)}, u32[]{:S(2)}) copy-start(f32[2,192]{1,0:T(2,128)} %shift_ref.3) | copy-start | bytes 4612
  36.3 7.7 %copy-start.22 = (f32[2,192]{1,0:T(2,128)S(1)}, f32[2,192]{1,0:T(2,128)}, u32[]{:S(2)}) copy-start(f32[2,192]{1,0:T(2,128)} %down_bias_ref.3) | copy-start | bytes 4612
  36.4 7.7 %copy-start.23 = (f32[2,48]{1,0:T(2,128)S(1)}, f32[2,48]{1,0:T(2,128)}, u32[]{:S(2)}) copy-start(f32[2,48]{1,0:T(2,128)} %scale_ref.3) | copy-start | bytes 1156
  36.4 6.0 %collective-permute-start.1 = (bf16[48,2304]{1,0:T(8,128)(2,1)S(1)}, bf16[48,2304]{1,0:T(8,128)(2,1)S(1)}, u32[]{:S(2)}, u32[]{:S(2)}) collective-permute-start(bf16[48,2304]{1,0:T(8,128)(2,1)S(1)} %conv_fine.1.own_ref), channel_id=1, source_target_pairs={{0,2},{1,3},{2,0},{3,1},{4,6},{5,7},{6,4},{7,5},{8,10},{9,11},{10,... | collective-permute-start | bytes 663560 | tf_op jit(solution)/shard_map/ppermute | solution.py:510
  37.9 5.9 %collective-permute-start = (bf16[48,2304]{1,0:T(8,128)(2,1)S(1)}, bf16[48,2304]{1,0:T(8,128)(2,1)}, u32[]{:S(2)}, u32[]{:S(2)}) collective-permute-start(bf16[48,2304]{1,0:T(8,128)(2,1)S(1)} %conv_fine.1.own_ref), channel_id=1, source_target_pairs={{0,1},{1,0},{2,3},{3,2},{4,5},{5,4},{6,7},{7,6},{8,9},{9,8},{10,11... | collective-permute-start | bytes 663560 | tf_op jit(solution)/shard_map/ppermute | solution.py:511
  42.4 1.6 %collective-permute-start.2 = (bf16[48,2304]{1,0:T(8,128)(2,1)S(1)}, bf16[48,2304]{1,0:T(8,128)(2,1)}, u32[]{:S(2)}, u32[]{:S(2)}) collective-permute-start(bf16[48,2304]{1,0:T(8,128)(2,1)S(1)} %collective-permute-done.1.p2_ref), channel_id=1, source_target_pairs={{0,1},{1,0},{2,3},{3,2},{4,5},{5,4},{6,7},{7,6},{8,9},{9,8},{10,11... | collective-permute-start | bytes 663560 | tf_op jit(solution)/shard_map/ppermute | solution.py:512
  44.0 0.9 %copy-start.12 = (bf16[384,128]{1,0:T(8,128)(2,1)S(1)}, bf16[384,128]{1,0:T(8,128)(2,1)}, u32[]{:S(2)}) copy-start(bf16[384,128]{1,0:T(8,128)(2,1)} %copy-done.11) | copy-start | bytes 294916
  50.9 11.8 %copy-start.8 = (bf16[48,2304]{1,0:T(8,128)(2,1)}, bf16[48,2304]{1,0:T(8,128)(2,1)S(1)}, u32[]{:S(2)}) copy-start(bf16[48,2304]{1,0:T(8,128)(2,1)S(1)} %get-tuple-element.39.fine_ref) | copy-start | bytes 663556
  50.9 18.3 %copy-start.28 = (f32[48,4]{0,1:T(4,128)S(1)}, f32[48,4]{0,1:T(4,128)}, u32[]{:S(2)}) copy-start(f32[48,4]{0,1:T(4,128)} %param.38) | copy-start | bytes 2308
  51.0 19.6 %copy-start.14 = (bf16[128,384]{1,0:T(8,128)(2,1)S(1)}, bf16[128,384]{1,0:T(8,128)(2,1)}, u32[]{:S(2)}) copy-start(bf16[128,384]{1,0:T(8,128)(2,1)} %copy-done.13) | copy-start | bytes 294916
  62.7 7.9 %copy-start.9 = (bf16[48,2304]{1,0:T(8,128)(2,1)S(1)}, bf16[48,2304]{1,0:T(8,128)(2,1)}, u32[]{:S(2)}) copy-start(bf16[48,2304]{1,0:T(8,128)(2,1)} %copy-done.8) | copy-start | bytes 663556
  64.9 4.4 %collective-permute-start.4 = (bf16[48,768]{1,0:T(8,128)(2,1)S(1)}, bf16[48,768]{1,0:T(8,128)(2,1)S(1)}, u32[]{:S(2)}, u32[]{:S(2)}) collective-permute-start(bf16[48,768]{1,0:T(8,128)(2,1)S(1)} %conv_coarse.1.own_ref), channel_id=1, source_target_pairs={{0,2},{1,3},{2,0},{3,1},{4,6},{5,7},{6,4},{7,5},{8,10},{9,11},{10,... | collective-permute-start | bytes 221192 | tf_op jit(solution)/shard_map/ppermute | solution.py:510
  66.4 3.0 %collective-permute-start.3 = (bf16[48,768]{1,0:T(8,128)(2,1)S(1)}, bf16[48,768]{1,0:T(8,128)(2,1)S(1)}, u32[]{:S(2)}, u32[]{:S(2)}) collective-permute-start(bf16[48,768]{1,0:T(8,128)(2,1)S(1)} %conv_coarse.1.own_ref), channel_id=1, source_target_pairs={{0,1},{1,0},{2,3},{3,2},{4,5},{5,4},{6,7},{7,6},{8,9},{9,8},{10,11... | collective-permute-start | bytes 221192 | tf_op jit(solution)/shard_map/ppermute | solution.py:511
  69.3 1.3 %collective-permute-start.5 = (bf16[48,768]{1,0:T(8,128)(2,1)S(1)}, bf16[48,768]{1,0:T(8,128)(2,1)S(1)}, u32[]{:S(2)}, u32[]{:S(2)}) collective-permute-start(bf16[48,768]{1,0:T(8,128)(2,1)S(1)} %collective-permute-done.4.p2_ref), channel_id=1, source_target_pairs={{0,1},{1,0},{2,3},{3,2},{4,5},{5,4},{6,7},{7,6},{8,9},{9,8},{10,11... | collective-permute-start | bytes 221192 | tf_op jit(solution)/shard_map/ppermute | solution.py:512
  (3 other events, 2.0 us)

commit v2 on v1

--- a/solution.py
+++ b/solution.py
@@ -147,21 +147,17 @@
     return lax.fori_loop(0, count, step, carry)
 
 
-LOADED = ("x", "mask", "weight", "bias", "halo", "expand", "compact", "small_halo", "sides", "pool", "unpool", "small_pack")
+def strip_table(pack_ref):
+    shape = (FINE_IN, 256)
+    source = lax.broadcasted_iota(jnp.int32, shape, 0)
+    lane = lane_ids(shape)
+    within = lane % 128
+    wanted = (within // 3) * TILE + within % 3 + jnp.where(lane >= 128, TILE - 3, 0)
+    pack_ref[...] = jnp.where((within < 24) & (source == wanted), 1.0, 0.0).astype(BF)
 
 
 def make_prep(grid_x):
-    def prep(slots_hbm, dev_hbm, pack_hbm, *refs):
-        size = len(LOADED)
-        sources, (msg_ref, tab_ref), targets = refs[:size], refs[size : size + 2], refs[size + 2 : 2 * size + 2]
-        slots_ref, dev_ref, pack_ref, rows_ref, cols_ref, row_rest_ref, col_rest_ref, sems = refs[2 * size + 2 :]
-        pairs = [(slots_hbm, slots_ref), (dev_hbm, dev_ref), (sources[0], targets[0]), (pack_hbm, pack_ref)]
-        pairs += list(zip(sources[1:], targets[1:]))
-        loads = [pltpu.make_async_copy(source, target, sems.at[i]) for i, (source, target) in enumerate(pairs)]
-        for load in loads:
-            load.start()
-        loads[0].wait()
-        loads[1].wait()
+    def prep(slots_ref, dev_ref, x_ref, pack_ref, msg_ref, tab_ref, rows_ref, cols_ref, row_rest_ref, col_rest_ref):
         count = slots_ref.shape[0]
         me = lax.axis_index("tile")
         my_slot = scan_tiles(count, lambda k, c: c + jnp.where(dev_ref[k] == me, slots_ref[k], 0), jnp.int32(0))
@@ -190,9 +186,7 @@
         for spare in range(9, 16):
             tab_ref[spare] = 0
 
-        loads[2].wait()
-        loads[3].wait()
-        x = targets[0][0]
+        x = x_ref[0]
         cols = dot(stacked(x, FINE_IN), pack_ref[...])
         lane = lane_ids((ROWS, 128))
         for side in range(2):
@@ -220,8 +214,6 @@
             return carry
 
         scan_tiles(count, fill, jnp.int32(0))
-        for load in loads[4:]:
-            load.wait()
 
     return prep
 
@@ -495,7 +487,9 @@
 
 VMEM = pl.BlockSpec(memory_space=pltpu.VMEM)
 SMEM = pl.BlockSpec(memory_space=pltpu.SMEM)
-ANY = pl.BlockSpec(memory_space=pl.ANY)
+
+def takes(microseconds):
+    return pl.CostEstimate(flops=microseconds * 1_000_000_000, bytes_accessed=0, transcendentals=0)
 
 
 def shaped(*shape, dtype=BF):
@@ -520,7 +514,25 @@
     count = wet_slots.shape[0]
     grid_x = 2 * count // GRID_Y
     cells = TILE * TILE
-    given = {
+    pack = pl.pallas_call(
+        strip_table, out_specs=VMEM, out_shape=shaped(FINE_IN, 256), compiler_params=PARAMS, cost_estimate=takes(2), name="strip_table"
+    )()
+    messages, table = pl.pallas_call(
+        make_prep(grid_x),
+        in_specs=[SMEM, SMEM, VMEM, VMEM],
+        out_specs=[VMEM, SMEM],
+        out_shape=[shaped(count, 16, 896), shaped(16 + count, dtype=jnp.int32)],
+        scratch_shapes=[
+            pltpu.VMEM((2, ROWS, 128), BF),
+            pltpu.VMEM((2, ROWS, 128), BF),
+            pltpu.VMEM((2, 16, 128), F32),
+            pltpu.VMEM((2, 16, 128), F32),
+        ],
+        compiler_params=PARAMS,
+        cost_estimate=takes(10),
+        name="prep",
+    )(wet_slots, device_of, features, pack)
+    held = {
         "x": features,
         "mask": land_mask,
         "weight": depth_weight,
@@ -534,29 +546,6 @@
         "unpool": jnp.asarray(FINE["unpool"]),
         "small_pack": jnp.asarray(COARSE["pack"]),
     }
-    given = [given[name] for name in LOADED]
-    pack = jnp.asarray(FINE["pack"])
-    results = pl.pallas_call(
-        make_prep(grid_x),
-        in_specs=[ANY] * (3 + len(given)),
-        out_specs=[VMEM, SMEM] + [VMEM] * len(given),
-        out_shape=[shaped(count, 16, 896), shaped(16 + count, dtype=jnp.int32)]
-        + [shaped(*array.shape, dtype=array.dtype) for array in given],
-        scratch_shapes=[
-            pltpu.SMEM((count,), jnp.int32),
-            pltpu.SMEM((count,), jnp.int32),
-            pltpu.VMEM(pack.shape, BF),
-            pltpu.VMEM((2, ROWS, 128), BF),
-            pltpu.VMEM((2, ROWS, 128), BF),
-            pltpu.VMEM((2, 16, 128), F32),
-            pltpu.VMEM((2, 16, 128), F32),
-            pltpu.SemaphoreType.DMA((3 + len(given),)),
-        ],
-        compiler_params=PARAMS,
-        name="prep",
-    )(wet_slots, device_of, pack, *given)
-    messages, table = results[:2]
-    held = dict(zip(LOADED, results[2:]))
     arrived = lax.all_to_all(messages, "tile", 0, 0, tiled=True)
     conv = pl.pallas_call(
         conv_fine,
@@ -570,6 +559,7 @@
             pltpu.VMEM((ROWS, 3072), F32),
         ],
         compiler_params=PARAMS,
+        cost_estimate=takes(4),
         name="conv_fine",
     )(table, held["x"], arrived, held["halo"], held["expand"], held["compact"], held["weight"], held["bias"])
     fine, pooled, small_mask, messages = pl.pallas_call(
@@ -583,6 +573,7 @@
             pltpu.VMEM((2, 16, 128), BF),
         ],
         compiler_params=PARAMS,
+        cost_estimate=takes(6),
         name="mix_fine",
     )(
         table, *every_channel(conv), held["x"], held["mask"], norm_gain, norm_bias, up_weight, up_bias,
@@ -600,6 +591,7 @@
             pltpu.VMEM((ROWS, 768), F32),
         ],
         compiler_params=PARAMS,
+        cost_estimate=takes(2),
         name="conv_coarse",
     )(table, pooled, arrived, held["small_halo"], held["sides"], held["weight"], held["bias"])
     return pl.pallas_call(
@@ -609,6 +601,7 @@
         out_shape=shaped(1, ROWS, cells),
         scratch_shapes=[pltpu.VMEM((4 * ROWS, 768), BF)],
         compiler_params=PARAMS,
+        cost_estimate=takes(3),
         name="mix_coarse",
     )(
         *every_channel(conv), pooled, small_mask, fine, held["mask"], norm_gain, norm_bias, up_weight, up_bias,

time: 73.9 us -> 58.6 us (0.79)
  local copies, waits for them, and re-layouts: 15.9 us -> 3.39 us
  Pallas kernels: 18 us -> 15.8 us
    unnamed x61 -> x51, local copies, waits for them, and re-layouts: 15.9 us -> 3.39 us
    pallas_call x1 -> x2, Pallas kernels: 3.24 us -> 1.59 us  [the longest x1 1.53 us: per_device(): pl.pallas_call(make_prep(grid_x), in_specs=[SMEM, SMEM, VMEM, VMEM], out_...]
  transfers between devices with their start and end apart: 6 -> 6, of which waited for: 4 -> 3; matrix products, arithmetic and copies ran while one was open for 2% -> 3% of each run, Pallas kernels for 0% -> 0%
where the time goes in v2:
time: 58.6 us; the launch traced here: 58.3 us
  blocking collectives  27.2 us (46%)
  Pallas kernels  15.8 us (27%)
  waiting for transfers between devices  8.49 us (14%)
  local copies, waits for them, and re-layouts  3.39 us (6%)
  starting transfers between devices  3.13 us (5%)
    all_to_all x2, blocking collectives, per_device(): arrived = lax.all_to_all(messages, 'tile', 0, 0, tiled=True)  27.2 us
    ppermute x2, waiting for transfers between devices, every_channel(): across = lax.ppermute(own, 'chan', pairs(2))  7.29 us
    pallas_call x1, Pallas kernels, per_device(): pl.pallas_call(make_mix_fine(count), in_specs=[SMEM] + [VMEM] * 16, out_s...  5.48 us
    pallas_call x1, Pallas kernels, per_device(): pl.pallas_call(conv_fine, in_specs=[SMEM] + [VMEM] * 7, out_specs=VMEM, o...  4 us
    unnamed x51, local copies, waits for them, and re-layouts  3.39 us
    ppermute x2, starting transfers between devices, every_channel(): across = lax.ppermute(own, 'chan', pairs(2))  3.11 us
    pallas_call x1, Pallas kernels, per_device(): pl.pallas_call(mix_coarse, in_specs=[VMEM] * 17, out_specs=VMEM, out_shap...  2.59 us
    pallas_call x1, Pallas kernels, per_device(): pl.pallas_call(conv_coarse, in_specs=[SMEM] + [VMEM] * 6, out_specs=VMEM,...  2.16 us
  transfers between devices with their start and end apart: 6, of which 3 were waited for; matrix products, arithmetic and copies ran while one was open for 3% of the time, Pallas kernels for 0%

profile of v2, /device:TPU:0, one launch (start us, length us, event | category | flops | bytes accessed | tf_op | source)
XLA Modules:
  0.0 58.3 jit_solution(9830546246153452576)
XLA Ops:
  0.0 0.1 strip_table.1.pack_ref
  0.1 0.9 %copy-done.1 = bf16[1,48,2304]{2,1,0:T(8,128)(2,1)S(1)} copy-done((bf16[1,48,2304]{2,1,0:T(8,128)(2,1)S(1)}, bf16[1,48,2304]{2,1,0:T(8,128)(2,1)}, u32[]{:S(2)}) %copy-start.1) | copy-done | bytes 221208
  1.0 0.0 copy-start.12
  1.0 0.0 copy-start.14
  1.0 0.0 copy-start.16
  1.0 1.5 %prep.1 = (bf16[8,16,896]{2,1,0:T(8,128)(2,1)S(1)}, s32[24]{0:T(128)S(1)}) custom-call(s32[8]{0:T(128)S(1)} %copy-done.10, s32[8]{0:T(128)S(1)} %copy-done.11, bf16[1,48,2304]{2,1,0:T(8,128)(2,1)S(1)} %copy-done.1, bf16[384,256]{1,0:T(8,128)(2,1)S(1)} %strip_table.1.pack_ref), custom_call_target="tpu_custom_call" | custom-call | flops 10000000000 | tf_op jit(solution)/shard_map/prep/pallas_call | solution.py:520
  2.5 15.5 %all_to_all.10.recv_ref = bf16[8,16,896]{2,1,0:T(8,128)(2,1)S(1)} all-to-all(bf16[8,16,896]{2,1,0:T(8,128)(2,1)S(1)} %get-tuple-element.12), channel_id=1, replica_groups=mesh['tile'=8,'chan'=4] {'tile'}, dimensions={0} | all-to-all | bytes 458752 | tf_op jit(solution)/shard_map/all_to_all | solution.py:549
  18.1 4.0 %conv_fine.1.own_ref = bf16[48,2304]{1,0:T(8,128)(2,1)S(1)} custom-call(s32[24]{0:T(128)S(1)} %get-tuple-element.11.tab_ref, bf16[1,48,2304]{2,1,0:T(8,128)(2,1)S(1)} %copy-done.1, bf16[8,16,896]{2,1,0:T(8,128)(2,1)S(1)} %all_to_all.10.recv_ref, bf16[3,768,256]{2,1,0:T(8,128)(2,1)S(1)} %copy-done.12, bf16[512,512]{1,0:T(8,128)(2,1)S(1)} %copy-done.14, ...), custom_call_target="tpu_custom_call" | custom-call | flops 4000000000 | tf_op jit(solution)/shard_map/conv_fine/pallas_call | solution.py:550
  22.1 0.0 copy-start.22
  22.1 0.0 copy-start
  22.1 0.0 copy-start.3
  22.1 0.0 copy-start.4
  22.1 0.0 copy-start.5
  22.1 0.0 copy-start.6
  22.2 0.0 copy-start.7
  22.2 0.0 copy-start.9
  22.2 0.0 copy-start.13
  22.2 0.0 copy-start.19
  22.2 1.6 %collective-permute-start.1 = (bf16[48,2304]{1,0:T(8,128)(2,1)S(1)}, bf16[48,2304]{1,0:T(8,128)(2,1)S(1)}, u32[]{:S(2)}, u32[]{:S(2)}) collective-permute-start(bf16[48,2304]{1,0:T(8,128)(2,1)S(1)} %conv_fine.1.own_ref), channel_id=1, source_target_pairs={{0,2},{1,3},{2,0},{3,1},{4,6},{5,7},{6,4},{7,5},{8,10},{9,11},{10,... | collective-permute-start | bytes 663560 | tf_op jit(solution)/shard_map/ppermute | solution.py:504
  23.8 4.4 %collective-permute-done.1.p2_ref = bf16[48,2304]{1,0:T(8,128)(2,1)S(1)} collective-permute-done((bf16[48,2304]{1,0:T(8,128)(2,1)S(1)}, bf16[48,2304]{1,0:T(8,128)(2,1)S(1)}, u32[]{:S(2)}, u32[]{:S(2)}) %collective-permute-start.1) | collective-permute-done | bytes 221216 | tf_op jit(solution)/shard_map/ppermute | solution.py:504
  28.2 1.3 %copy.24.up_ref = bf16[2,768,192]{2,1,0:T(8,128)(2,1)S(1)} copy(bf16[2,768,192]{1,2,0:T(8,128)(2,1)} %param.31) | data formatting | bytes 1179648 | tf_op args[8]
  29.6 0.1 copy.25.pool_weight_ref
  29.7 0.0 collective-permute-done.2.p3_ref
  29.8 5.5 %mix_fine.1 = (bf16[48,2304]{1,0:T(8,128)(2,1)S(1)}, bf16[48,768]{1,0:T(8,128)(2,1)S(1)}, f32[48,128]{1,0:T(8,128)S(1)}, bf16[8,16,512]{2,1,0:T(8,128)(2,1)S(1)}) custom-call(s32[24]{0:T(128)S(1)} %get-tuple-element.11.tab_ref, bf16[48,2304]{1,0:T(8,128)(2,1)S(1)} %conv_fine.1.own_ref, bf16[48,2304]{1,0:T(8,128)(2,1)S(1)} %collective-permute-done.p1_ref, ...), custom_call_target="tpu_custom_call" | custom-call | flops 6000000000 | tf_op jit(solution)/shard_map/mix_fine/pallas_call | solution.py:565
  35.3 11.7 %all_to_all.11.recv_ref = bf16[8,16,512]{2,1,0:T(8,128)(2,1)S(1)} all-to-all(bf16[8,16,512]{2,1,0:T(8,128)(2,1)S(1)} %get-tuple-element.14), channel_id=1, replica_groups=mesh['tile'=8,'chan'=4] {'tile'}, dimensions={0} | all-to-all | bytes 262144 | tf_op jit(solution)/shard_map/all_to_all | solution.py:582
  47.0 2.2 %conv_coarse.1.own_ref = bf16[48,768]{1,0:T(8,128)(2,1)S(1)} custom-call(s32[24]{0:T(128)S(1)} %get-tuple-element.11.tab_ref, bf16[48,768]{1,0:T(8,128)(2,1)S(1)} %get-tuple-element.13.x_ref.pooled_ref, bf16[8,16,512]{2,1,0:T(8,128)(2,1)S(1)} %all_to_all.11.recv_ref, bf16[3,384,128]{2,1,0:T(8,128)(2,1)S(1)} %copy-done.17, bf16[256,768]{1,0:T(8,128)(2,1)S(1)} %copy-done.15, ...), custom_call_target="tpu_custom_call" | custom-call | flops 2000000000 | tf_op jit(solution)/shard_map/conv_coarse/pallas_call | solution.py:583
  49.2 1.6 %collective-permute-start.4 = (bf16[48,768]{1,0:T(8,128)(2,1)S(1)}, bf16[48,768]{1,0:T(8,128)(2,1)S(1)}, u32[]{:S(2)}, u32[]{:S(2)}) collective-permute-start(bf16[48,768]{1,0:T(8,128)(2,1)S(1)} %conv_coarse.1.own_ref), channel_id=1, source_target_pairs={{0,2},{1,3},{2,0},{3,1},{4,6},{5,7},{6,4},{7,5},{8,10},{9,11},{10,... | collective-permute-start | bytes 221192 | tf_op jit(solution)/shard_map/ppermute | solution.py:504
  50.7 2.9 %collective-permute-done.4.p2_ref = bf16[48,768]{1,0:T(8,128)(2,1)S(1)} collective-permute-done((bf16[48,768]{1,0:T(8,128)(2,1)S(1)}, bf16[48,768]{1,0:T(8,128)(2,1)S(1)}, u32[]{:S(2)}, u32[]{:S(2)}) %collective-permute-start.4) | collective-permute-done | bytes 73760 | tf_op jit(solution)/shard_map/ppermute | solution.py:504
  53.6 0.1 copy.27.spread_weight_ref
  53.7 1.2 %collective-permute-done.5.p3_ref = bf16[48,768]{1,0:T(8,128)(2,1)S(1)} collective-permute-done((bf16[48,768]{1,0:T(8,128)(2,1)S(1)}, bf16[48,768]{1,0:T(8,128)(2,1)S(1)}, u32[]{:S(2)}, u32[]{:S(2)}) %collective-permute-start.5) | collective-permute-done | bytes 73760 | tf_op jit(solution)/shard_map/ppermute | solution.py:506
  54.9 0.9 %copy-done.21 = bf16[48,768]{1,0:T(8,128)(2,1)S(1)} copy-done((bf16[48,768]{1,0:T(8,128)(2,1)S(1)}, bf16[48,768]{1,0:T(8,128)(2,1)}, u32[]{:S(2)}) %copy-start.21) | copy-done | bytes 73752
  55.7 2.6 %mix_coarse.1 = bf16[1,48,2304]{2,1,0:T(8,128)(2,1)} custom-call(bf16[48,768]{1,0:T(8,128)(2,1)S(1)} %conv_coarse.1.own_ref, bf16[48,768]{1,0:T(8,128)(2,1)S(1)} %collective-permute-done.3.p1_ref, bf16[48,768]{1,0:T(8,128)(2,1)S(1)} %collective-permute-done.4.p2_ref, bf16[48,768]{1,0:T(8,128)(2,1)S(1)} %collective-permute-done.5.p3_ref, ...), custom_call_target="tpu_custom_call" | custom-call | flops 3000000000 | tf_op jit(solution)/shard_map/mix_coarse/pallas_call | solution.py:597
  (39 shorter events, 0.1 us)
Async XLA Ops:
  0.0 0.9 %copy-start.1 = (bf16[1,48,2304]{2,1,0:T(8,128)(2,1)S(1)}, bf16[1,48,2304]{2,1,0:T(8,128)(2,1)}, u32[]{:S(2)}) copy-start(bf16[1,48,2304]{2,1,0:T(8,128)(2,1)} %x_ref.5) | copy-start | bytes 663556
  0.0 0.9 %copy-start.10 = (s32[8]{0:T(128)S(1)}, s32[8]{0:T(128)}, u32[]{:S(2)}) copy-start(s32[8]{0:T(128)} %slots_ref.1) | copy-start | bytes 100
  0.0 0.9 %copy-start.11 = (s32[8]{0:T(128)S(1)}, s32[8]{0:T(128)}, u32[]{:S(2)}) copy-start(s32[8]{0:T(128)} %dev_ref.1) | copy-start | bytes 100
  0.9 17.1 %copy-start.2 = (f32[2,48,49]{2,1,0:T(8,128)S(1)}, f32[2,48,49]{2,1,0:T(8,128)}, u32[]{:S(2)}) copy-start(f32[2,48,49]{2,1,0:T(8,128)} %weight_ref.3) | copy-start | bytes 56452
  0.9 17.1 %copy-start.8 = (f32[2,48]{1,0:T(2,128)S(1)}, f32[2,48]{1,0:T(2,128)}, u32[]{:S(2)}) copy-start(f32[2,48]{1,0:T(2,128)} %bias_ref.3) | copy-start | bytes 1156
  1.0 17.1 %copy-start.12 = (bf16[3,768,256]{2,1,0:T(8,128)(2,1)S(1)}, bf16[3,768,256]{2,1,0:T(8,128)(2,1)}, u32[]{:S(2)}) copy-start(bf16[3,768,256]{2,1,0:T(8,128)(2,1)} %constant.16.clone.halo_ref) | copy-start | bytes 3538948
  1.0 17.1 %copy-start.14 = (bf16[512,512]{1,0:T(8,128)(2,1)S(1)}, bf16[512,512]{1,0:T(8,128)(2,1)}, u32[]{:S(2)}) copy-start(bf16[512,512]{1,0:T(8,128)(2,1)} %constant.17.clone.expand_ref) | copy-start | bytes 1572868
  1.0 17.1 %copy-start.16 = (bf16[512,384]{1,0:T(8,128)(2,1)S(1)}, bf16[512,384]{1,0:T(8,128)(2,1)}, u32[]{:S(2)}) copy-start(bf16[512,384]{1,0:T(8,128)(2,1)} %constant.18.clone.compact_ref) | copy-start | bytes 1179652
  22.1 7.5 %copy-start.22 = (f32[48,4]{0,1:T(4,128)S(1)}, f32[48,4]{0,1:T(4,128)}, u32[]{:S(2)}) copy-start(f32[48,4]{0,1:T(4,128)} %param.36) | copy-start | bytes 2308
  22.1 7.6 %copy-start = (bf16[2,192,768]{2,1,0:T(8,128)(2,1)S(1)}, bf16[2,192,768]{2,1,0:T(8,128)(2,1)}, u32[]{:S(2)}) copy-start(bf16[2,192,768]{2,1,0:T(8,128)(2,1)} %down_ref.3) | copy-start | bytes 1769476
  22.1 7.6 %copy-start.3 = (s32[1,2304]{1,0:T(1,128)S(1)}, s32[1,2304]{1,0:T(1,128)}, u32[]{:S(2)}) copy-start(s32[1,2304]{1,0:T(1,128)} %mask_ref.3) | copy-start | bytes 27652
  22.1 7.6 %copy-start.4 = (f32[2,768]{1,0:T(2,128)S(1)}, f32[2,768]{1,0:T(2,128)}, u32[]{:S(2)}) copy-start(f32[2,768]{1,0:T(2,128)} %up_bias_ref.3) | copy-start | bytes 18436
  22.1 7.6 %copy-start.5 = (f32[2,192]{1,0:T(2,128)S(1)}, f32[2,192]{1,0:T(2,128)}, u32[]{:S(2)}) copy-start(f32[2,192]{1,0:T(2,128)} %gain_ref.3) | copy-start | bytes 4612
  22.1 7.6 %copy-start.6 = (f32[2,192]{1,0:T(2,128)S(1)}, f32[2,192]{1,0:T(2,128)}, u32[]{:S(2)}) copy-start(f32[2,192]{1,0:T(2,128)} %shift_ref.3) | copy-start | bytes 4612
  22.2 7.6 %copy-start.7 = (f32[2,192]{1,0:T(2,128)S(1)}, f32[2,192]{1,0:T(2,128)}, u32[]{:S(2)}) copy-start(f32[2,192]{1,0:T(2,128)} %down_bias_ref.3) | copy-start | bytes 4612
  22.2 7.6 %copy-start.9 = (f32[2,48]{1,0:T(2,128)S(1)}, f32[2,48]{1,0:T(2,128)}, u32[]{:S(2)}) copy-start(f32[2,48]{1,0:T(2,128)} %scale_ref.3) | copy-start | bytes 1156
  22.2 7.6 %copy-start.13 = (bf16[768,384]{1,0:T(8,128)(2,1)S(1)}, bf16[768,384]{1,0:T(8,128)(2,1)}, u32[]{:S(2)}) copy-start(bf16[768,384]{1,0:T(8,128)(2,1)} %constant.23.clone.pack_ref) | copy-start | bytes 1769476
  22.2 7.6 %copy-start.19 = (bf16[384,128]{1,0:T(8,128)(2,1)S(1)}, bf16[384,128]{1,0:T(8,128)(2,1)}, u32[]{:S(2)}) copy-start(bf16[384,128]{1,0:T(8,128)(2,1)} %constant.21.clone.pool_ref) | copy-start | bytes 294916
  22.2 6.0 %collective-permute-start.1 = (bf16[48,2304]{1,0:T(8,128)(2,1)S(1)}, bf16[48,2304]{1,0:T(8,128)(2,1)S(1)}, u32[]{:S(2)}, u32[]{:S(2)}) collective-permute-start(bf16[48,2304]{1,0:T(8,128)(2,1)S(1)} %conv_fine.1.own_ref), channel_id=1, source_target_pairs={{0,2},{1,3},{2,0},{3,1},{4,6},{5,7},{6,4},{7,5},{8,10},{9,11},{10,... | collective-permute-start | bytes 663560 | tf_op jit(solution)/shard_map/ppermute | solution.py:504
  23.8 5.9 %collective-permute-start = (bf16[48,2304]{1,0:T(8,128)(2,1)S(1)}, bf16[48,2304]{1,0:T(8,128)(2,1)S(1)}, u32[]{:S(2)}, u32[]{:S(2)}) collective-permute-start(bf16[48,2304]{1,0:T(8,128)(2,1)S(1)} %conv_fine.1.own_ref), channel_id=1, source_target_pairs={{0,1},{1,0},{2,3},{3,2},{4,5},{5,4},{6,7},{7,6},{8,9},{9,8},{10,11... | collective-permute-start | bytes 663560 | tf_op jit(solution)/shard_map/ppermute | solution.py:505
  28.2 1.5 %collective-permute-start.2 = (bf16[48,2304]{1,0:T(8,128)(2,1)S(1)}, bf16[48,2304]{1,0:T(8,128)(2,1)S(1)}, u32[]{:S(2)}, u32[]{:S(2)}) collective-permute-start(bf16[48,2304]{1,0:T(8,128)(2,1)S(1)} %collective-permute-done.1.p2_ref), channel_id=1, source_target_pairs={{0,1},{1,0},{2,3},{3,2},{4,5},{5,4},{6,7},{7,6},{8,9},{9,8},{10,11... | collective-permute-start | bytes 663560 | tf_op jit(solution)/shard_map/ppermute | solution.py:506
  29.6 17.3 %copy-start.15 = (bf16[256,768]{1,0:T(8,128)(2,1)S(1)}, bf16[256,768]{1,0:T(8,128)(2,1)}, u32[]{:S(2)}) copy-start(bf16[256,768]{1,0:T(8,128)(2,1)} %constant.20.clone.sides_ref) | copy-start | bytes 1179652
  29.6 17.3 %copy-start.17 = (bf16[3,384,128]{2,1,0:T(8,128)(2,1)S(1)}, bf16[3,384,128]{2,1,0:T(8,128)(2,1)}, u32[]{:S(2)}) copy-start(bf16[3,384,128]{2,1,0:T(8,128)(2,1)} %constant.19.clone.halo_ref) | copy-start | bytes 884740
  35.2 13.9 %copy-start.20 = (bf16[48,768]{1,0:T(8,128)(2,1)}, bf16[48,768]{1,0:T(8,128)(2,1)S(1)}, u32[]{:S(2)}) copy-start(bf16[48,768]{1,0:T(8,128)(2,1)S(1)} %get-tuple-element.13.x_ref.pooled_ref) | copy-start | bytes 221188
  47.0 6.6 %copy-start.23 = (f32[48,4]{0,1:T(4,128)S(1)}, f32[48,4]{0,1:T(4,128)}, u32[]{:S(2)}) copy-start(f32[48,4]{0,1:T(4,128)} %param.37) | copy-start | bytes 2308
  47.0 7.9 %copy-start.18 = (bf16[128,384]{1,0:T(8,128)(2,1)S(1)}, bf16[128,384]{1,0:T(8,128)(2,1)}, u32[]{:S(2)}) copy-start(bf16[128,384]{1,0:T(8,128)(2,1)} %constant.22.clone.unpool_ref) | copy-start | bytes 294916
  49.2 4.4 %collective-permute-start.4 = (bf16[48,768]{1,0:T(8,128)(2,1)S(1)}, bf16[48,768]{1,0:T(8,128)(2,1)S(1)}, u32[]{:S(2)}, u32[]{:S(2)}) collective-permute-start(bf16[48,768]{1,0:T(8,128)(2,1)S(1)} %conv_coarse.1.own_ref), channel_id=1, source_target_pairs={{0,2},{1,3},{2,0},{3,1},{4,6},{5,7},{6,4},{7,5},{8,10},{9,11},{10,... | collective-permute-start | bytes 221192 | tf_op jit(solution)/shard_map/ppermute | solution.py:504
  50.7 3.0 %collective-permute-start.3 = (bf16[48,768]{1,0:T(8,128)(2,1)S(1)}, bf16[48,768]{1,0:T(8,128)(2,1)S(1)}, u32[]{:S(2)}, u32[]{:S(2)}) collective-permute-start(bf16[48,768]{1,0:T(8,128)(2,1)S(1)} %conv_coarse.1.own_ref), channel_id=1, source_target_pairs={{0,1},{1,0},{2,3},{3,2},{4,5},{5,4},{6,7},{7,6},{8,9},{9,8},{10,11... | collective-permute-start | bytes 221192 | tf_op jit(solution)/shard_map/ppermute | solution.py:505
  53.6 1.3 %collective-permute-start.5 = (bf16[48,768]{1,0:T(8,128)(2,1)S(1)}, bf16[48,768]{1,0:T(8,128)(2,1)S(1)}, u32[]{:S(2)}, u32[]{:S(2)}) collective-permute-start(bf16[48,768]{1,0:T(8,128)(2,1)S(1)} %collective-permute-done.4.p2_ref), channel_id=1, source_target_pairs={{0,1},{1,0},{2,3},{3,2},{4,5},{5,4},{6,7},{7,6},{8,9},{9,8},{10,11... | collective-permute-start | bytes 221192 | tf_op jit(solution)/shard_map/ppermute | solution.py:506
  54.9 0.9 %copy-start.21 = (bf16[48,768]{1,0:T(8,128)(2,1)S(1)}, bf16[48,768]{1,0:T(8,128)(2,1)}, u32[]{:S(2)}) copy-start(bf16[48,768]{1,0:T(8,128)(2,1)} %copy-done.20) | copy-start | bytes 221188

commit v3 on v2

--- a/solution.py
+++ b/solution.py
@@ -59,11 +59,9 @@
             one_hot((768, 256), halo_pairs(last, TILE, 64, 0, True)),
         ]
     )
-    pack, expand, compact, pool = [], [], [], []
+    expand, compact, pool = [], [], []
     for row in range(8):
         for j in range(3):
-            pack.append((row * 48 + j, row * 3 + j))
-            pack.append((row * 48 + 45 + j, 128 + row * 3 + j))
             expand.append((384 + row * 3 + j, row * 64 + j))
             expand.append((384 + 24 + row * 3 + j, row * 64 + 51 + j))
         for col in range(48):
@@ -72,11 +70,9 @@
             pool.append((row * 48 + col, (row // 2) * 32 + 3 + col // 2))
     return {
         "halo": halo,
-        "pack": one_hot((384, 256), pack),
         "expand": one_hot((512, 512), expand),
         "compact": one_hot((512, 384), compact),
         "pool": one_hot((384, 128), pool),
-        "unpool": np.ascontiguousarray(one_hot((384, 128), pool).T),
     }
 
 
@@ -227,76 +223,101 @@
     return pltpu.roll(value, value.shape[1] - lanes, 1)
 
 
-def conv_fine(tab_ref, x_ref, recv_ref, halo_ref, expand_ref, compact_ref, weight_ref, bias_ref, out_ref, pad_ref, odd_ref, wide_ref, sum_ref):
+def make_conv_fine(first, rows):
+    def conv_fine(tab_ref, x_ref, recv_ref, halo_ref, expand_ref, compact_ref, weight_ref, bias_ref, out_ref, pad_ref, odd_ref, wide_ref, sum_ref):
+        for tap in range(49):
+            wide_ref[tap] = jnp.broadcast_to(weight_ref[0, first : first + rows, tap : tap + 1], (rows, 128))
+        lane = lane_ids((rows, 128))
+        parts = range(first // 16, (first + rows) // 16)
+
+        def rest_of(source, scale):
+            rest = recv_ref[source, :, 768:896].astype(F32) * scale
+            return jnp.concatenate([pltpu.roll(rest, 128 - 40 * g, 1) if g else rest for g in parts], axis=0)
+
+        def main_of(source, scale, offset):
+            pieces = [recv_ref[source, :, 256 * g + offset : 256 * g + offset + 128] for g in parts]
+            return jnp.concatenate(pieces, axis=0).astype(F32) * scale
+
+        def row_strips(bands):
+            pieces = []
+            for band in bands:
+                source, scale = band_source(tab_ref, band)
+                pieces += [main_of(source, scale, 0).astype(BF), rest_of(source, scale).astype(BF)]
+            return jnp.concatenate(pieces, axis=1)
+
+        pad_ref[:, 0:256] = dot(row_strips((0, 1, 2)), halo_ref[0])
+        pad_ref[:, 3328:3584] = dot(row_strips((5, 6, 7)), halo_ref[tab_ref[8]])
+        sides = []
+        for band in (3, 4):
+            source, scale = band_source(tab_ref, band)
+            main, rest = main_of(source, scale, 128), rest_of(source, scale)
+            turned = [pltpu.roll(main, 128 - 24 * i, 1) if i else main for i in range(5)]
+            sides.append(turned + [pltpu.roll(rest, 128 - 16, 1)])
+        halos = []
+        for i in range(GROUPS):
+            both = jnp.where(lane < 24, sides[0][i], pltpu.roll(sides[1][i], 24, 1))
+            halos.append(jnp.where(lane < 48, both, 0.0))
+        x = x_ref[0, first : first + rows, :]
+        joined = jnp.concatenate([stacked(x, FINE_IN), jnp.concatenate(halos, axis=0).astype(BF)], axis=1)
+        padded = dot(joined, expand_ref[...])
+        for i in range(GROUPS):
+            pad_ref[:, 256 + 512 * i : 768 + 512 * i] = padded[i * rows : (i + 1) * rows]
+        odd_ref[...] = lane_shifted(pad_ref[...], 64)
+        sum_ref[...] = wide(columns(bias_ref[0:1, :])[first : first + rows], 3072)
+
+        def group(g, carry):
+            here = pl.ds(pl.multiple_of(g * 8, 8), 8)
+            for chunk in range(6):
+                base = chunk * 512
+                taken = []
+                for a in range(1, 8):
+                    ref = odd_ref if a % 2 else pad_ref
+                    start = base + (a // 2) * 128
+                    taken.append([ref[here, start + 128 * j : start + 128 * j + 128] for j in range(4)])
+                total = [sum_ref[here, base + 128 * j : base + 128 * j + 128] for j in range(4)]
+                for b in range(7):
+                    weights = [wide_ref[a * 7 + b, here, :] for a in range(7)]
+                    for j in range(4):
+                        partial = weights[0] * taken[0][j]
+                        for a in range(1, 7):
+                            partial = partial + weights[a] * taken[a][j]
+                        total[j] = total[j] + (pltpu.roll(partial, (3 - b) % 128, 1) if b != 3 else partial)
+                for j in range(4):
+                    sum_ref[here, base + 128 * j : base + 128 * j + 128] = total[j]
+            return carry
+
+        lax.fori_loop(0, rows // 8, group, 0)
+        dense = dot(stacked(sum_ref[...].astype(BF), FINE_PAD), compact_ref[...]).astype(BF)
+        for i in range(GROUPS):
+            out_ref[:, i * FINE_IN : (i + 1) * FINE_IN] = dense[i * rows : (i + 1) * rows]
+
+    return conv_fine
+
+
+def params(
+    after_ref, weight_ref, bias_ref, gain_ref, shift_ref, up_bias_ref, down_bias_ref, scale_ref, pool_weight_ref, spread_weight_ref,
+    taps_ref, conv_bias_ref, gains_ref, shifts_ref, up_biases_ref, down_biases_ref, scales_ref, pool_cells_ref, spread_cells_ref,
+):
     for tap in range(49):
-        wide_ref[tap] = jnp.broadcast_to(weight_ref[0][:, tap : tap + 1], (ROWS, 128))
-    lane = lane_ids((ROWS, 128))
-
-    def rest_of(source, scale):
-        rest = recv_ref[source, :, 768:896].astype(F32) * scale
-        return jnp.concatenate([rest, pltpu.roll(rest, 128 - 40, 1), pltpu.roll(rest, 128 - 80, 1)], axis=0)
-
-    def main_of(source, scale, offset):
-        parts = [recv_ref[source, :, 256 * g + offset : 256 * g + offset + 128] for g in range(3)]
-        return jnp.concatenate(parts, axis=0).astype(F32) * scale
-
-    def row_strips(bands):
-        pieces = []
-        for band in bands:
-            source, scale = band_source(tab_ref, band)
-            pieces += [main_of(source, scale, 0).astype(BF), rest_of(source, scale).astype(BF)]
-        return jnp.concatenate(pieces, axis=1)
-
-    pad_ref[:, 0:256] = dot(row_strips((0, 1, 2)), halo_ref[0])
-    pad_ref[:, 3328:3584] = dot(row_strips((5, 6, 7)), halo_ref[tab_ref[8]])
-    sides = []
-    for band in (3, 4):
-        source, scale = band_source(tab_ref, band)
-        main, rest = main_of(source, scale, 128), rest_of(source, scale)
-        sides.append([pltpu.roll(main, (128 - 24 * i) % 128, 1) if i else main for i in range(5)] + [pltpu.roll(rest, 128 - 16, 1)])
-    halos = []
-    for i in range(GROUPS):
-        both = jnp.where(lane < 24, sides[0][i], pltpu.roll(sides[1][i], 24, 1))
-        halos.append(jnp.where(lane < 48, both, 0.0))
-    x = x_ref[0]
-    joined = jnp.concatenate([stacked(x, FINE_IN), jnp.concatenate(halos, axis=0).astype(BF)], axis=1)
-    padded = dot(joined, expand_ref[...])
-    for i in range(GROUPS):
-        pad_ref[:, 256 + 512 * i : 768 + 512 * i] = padded[i * ROWS : (i + 1) * ROWS]
-    odd_ref[...] = lane_shifted(pad_ref[...], 64)
-    bias = columns(bias_ref[0:1, :])
-    sum_ref[...] = wide(bias, 3072)
-
-    def group(g, carry):
-        rows = pl.ds(pl.multiple_of(g * 8, 8), 8)
-        for chunk in range(6):
-            base = chunk * 512
-            taken = []
-            for a in range(1, 8):
-                ref = odd_ref if a % 2 else pad_ref
-                start = base + (a // 2) * 128
-                taken.append([ref[rows, start + 128 * j : start + 128 * j + 128] for j in range(4)])
-            total = [sum_ref[rows, base + 128 * j : base + 128 * j + 128] for j in range(4)]
-            for b in range(7):
-                weights = [wide_ref[a * 7 + b, rows, :] for a in range(7)]
-                for j in range(4):
-                    partial = weights[0] * taken[0][j]
-                    for a in range(1, 7):
-                        partial = partial + weights[a] * taken[a][j]
-                    total[j] = total[j] + (pltpu.roll(partial, (3 - b) % 128, 1) if b != 3 else partial)
-            for j in range(4):
-                sum_ref[rows, base + 128 * j : base + 128 * j + 128] = total[j]
-        return carry
-
-    lax.fori_loop(0, 6, group, 0)
-    dense = dot(stacked(sum_ref[...].astype(BF), FINE_PAD), compact_ref[...]).astype(BF)
-    for i in range(GROUPS):
-        out_ref[:, i * FINE_IN : (i + 1) * FINE_IN] = dense[i * ROWS : (i + 1) * ROWS]
-
-
-def conv_coarse(tab_ref, x_ref, recv_ref, halo_ref, sides_ref, weight_ref, bias_ref, out_ref, pad_ref, wide_ref, sum_ref):
-    for tap in range(49):
-        wide_ref[tap] = jnp.broadcast_to(weight_ref[1][:, tap : tap + 1], (ROWS, 128))
+        taps_ref[tap] = jnp.broadcast_to(weight_ref[1, :, tap : tap + 1], (ROWS, 128))
+    conv_bias_ref[...] = columns(bias_ref[1:2, :])
+    me = lax.axis_index("chan")
+    for level in range(2):
+        row = slice(level, level + 1)
+        gains_ref[level] = columns(gain_ref[row, :])
+        shifts_ref[level] = columns(shift_ref[row, :])
+        up_biases_ref[level] = columns(up_bias_ref[row, :])
+        scales_ref[level] = columns(scale_ref[row, :])
+        down_bias = columns(down_bias_ref[row, :])
+        own = down_bias[0:ROWS]
+        for k in range(1, down_bias.shape[0] // ROWS):
+            own = jnp.where(me == k, down_bias[k * ROWS : (k + 1) * ROWS], own)
+        down_biases_ref[level] = own
+    pool_cells_ref[...] = cell_weights(pool_weight_ref)
+    spread_cells_ref[...] = cell_weights(spread_weight_ref)
+
+
+def conv_coarse(tab_ref, x_ref, recv_ref, halo_ref, sides_ref, wide_ref, bias_ref, out_ref, pad_ref, sum_ref):
     lane = lane_ids((ROWS, 128))
 
     def main_of(source, scale):
@@ -323,8 +344,7 @@
     padded = pad_ref[0]
     for turn in range(1, 4):
         pad_ref[turn] = lane_shifted(padded, 32 * turn)
-    bias = columns(bias_ref[1:2, :])
-    sum_ref[...] = wide(bias, 768)
+    sum_ref[...] = wide(bias_ref[...], 768)
 
     def group(g, carry):
         rows = pl.ds(pl.multiple_of(g * 8, 8), 8)
@@ -352,24 +372,17 @@
 
 def gather_rows(pieces, cat_ref):
     me = lax.axis_index("chan")
-    for k, piece in enumerate(pieces):
+    for k, parts in enumerate(pieces):
         first = pl.multiple_of(lax.bitwise_xor(me, k) * ROWS, 16)
-        cat_ref[pl.ds(first, ROWS), :] = piece[...]
+        for part in parts:
+            rows = part.shape[0]
+            cat_ref[pl.ds(first, rows), :] = part[...]
+            first = pl.multiple_of(first + rows, 16)
 
 
 def make_branch(level, cat_ref, gain_ref, shift_ref, up_ref, up_bias_ref, down_ref, down_bias_ref, block):
-    me = lax.axis_index("chan")
-    row = slice(level, level + 1)
-    gain = wide(columns(gain_ref[row, :]), block)
-    shift = wide(columns(shift_ref[row, :]), block)
-    up_bias = columns(up_bias_ref[row, :])
-    down_bias = columns(down_bias_ref[row, :])
-    first = pl.multiple_of(me * ROWS, 16)
-    bias_rows = jnp.zeros((ROWS, 128), F32)
-    for k in range(down_bias.shape[0] // ROWS):
-        bias_rows = jnp.where(me == k, down_bias[k * ROWS : (k + 1) * ROWS], bias_rows)
-    bias_rows = wide(bias_rows, block)
-    hidden_rows = up_ref.shape[1]
+    first = pl.multiple_of(lax.axis_index("chan") * ROWS, 16)
+    gain, shift = wide(gain_ref[level], block), wide(shift_ref[level], block)
 
     def branch(start):
         values = cat_ref[:, pl.ds(start, block)].astype(F32)
@@ -377,12 +390,9 @@
         centred = values - mean
         spread = jnp.mean(centred * centred, axis=0, keepdims=True)
         normed = (centred * lax.rsqrt(spread + norm_eps) * gain + shift).astype(BF)
-        out = bias_rows
-        for part in range(0, hidden_rows, 256):
-            hidden = dot(up_ref[level, part : part + 256, :], normed) + wide(up_bias[part : part + 256], block)
-            hidden = 0.5 * hidden * (1.0 + lax.erf(hidden * np.float32(0.5**0.5)))
-            out = out + dot(down_ref[level, pl.ds(first, ROWS), part : part + 256], hidden.astype(BF))
-        return out
+        hidden = dot(up_ref[level], normed) + wide(up_bias_ref[level], block)
+        hidden = 0.5 * hidden * (1.0 + lax.erf(hidden * np.float32(0.5**0.5)))
+        return dot(down_ref[level, pl.ds(first, ROWS), :], hidden.astype(BF)) + wide(down_bias_ref[level], block)
 
     return branch
 
@@ -400,25 +410,21 @@
 
 def make_mix_fine(count):
     def mix_fine(
-        tab_ref, own_ref, p1_ref, p2_ref, p3_ref, x_ref, mask_ref, gain_ref, shift_ref, up_ref, up_bias_ref,
-        down_ref, down_bias_ref, scale_ref, pool_weight_ref, pool_ref, pack_ref,
+        tab_ref, own_a_ref, own_b_ref, p1_a_ref, p1_b_ref, p2_a_ref, p2_b_ref, p3_a_ref, p3_b_ref, x_ref, mask_ref,
+        gain_ref, shift_ref, up_ref, up_bias_ref, down_ref, down_bias_ref, scale_ref, pool_cells_ref, pool_ref, pack_ref,
         fine_ref, pooled_ref, small_mask_ref, msg_ref, cat_ref, mains_ref, rest_ref,
     ):
-        gather_rows((own_ref, p1_ref, p2_ref, p3_ref), cat_ref)
-        block = 256
+        gather_rows(((own_a_ref, own_b_ref), (p1_a_ref, p1_b_ref), (p2_a_ref, p2_b_ref), (p3_a_ref, p3_b_ref)), cat_ref)
+        block = 768
         branch = make_branch(0, cat_ref, gain_ref, shift_ref, up_ref, up_bias_ref, down_ref, down_bias_ref, block)
-        scale = wide(columns(scale_ref[0:1, :]), block)
-
-        def one(step, carry):
-            start = pl.multiple_of(step * block, block)
-            here = pl.ds(start, block)
+        scale = wide(scale_ref[0], block)
+
+        for start in range(0, TILE * TILE, block):
+            here = slice(start, start + block)
             value = x_ref[0, :, here].astype(F32) + scale * branch(start)
             fine_ref[:, here] = (mask_ref[:, here].astype(F32) * value).astype(BF)
-            return carry
-
-        lax.fori_loop(0, TILE * TILE // block, one, 0, unroll=3)
-
-        weights = cell_weights(pool_weight_ref)
+
+        weights = pool_cells_ref[...]
         highs, lows, masks = [], [], []
         for i in range(GROUPS):
             lanes = slice(i * FINE_IN, (i + 1) * FINE_IN)
@@ -464,25 +470,23 @@
 
 def mix_coarse(
     own_ref, p1_ref, p2_ref, p3_ref, pooled_ref, small_mask_ref, fine_ref, mask_ref, gain_ref, shift_ref, up_ref, up_bias_ref,
-    down_ref, down_bias_ref, scale_ref, spread_weight_ref, unpool_ref, out_ref, cat_ref,
+    down_ref, down_bias_ref, scale_ref, spread_cells_ref, pool_ref, out_ref, cat_ref,
 ):
-    gather_rows((own_ref, p1_ref, p2_ref, p3_ref), cat_ref)
-    block = 256
-    branch = make_branch(1, cat_ref, gain_ref, shift_ref, up_ref, up_bias_ref, down_ref, down_bias_ref, block)
-    scale = wide(columns(scale_ref[1:2, :]), block)
+    gather_rows(((own_ref,), (p1_ref,), (p2_ref,), (p3_ref,)), cat_ref)
+    cells = cat_ref.shape[1]
+    branch = make_branch(1, cat_ref, gain_ref, shift_ref, up_ref, up_bias_ref, down_ref, down_bias_ref, cells)
+    value = pooled_ref[...].astype(F32) + wide(scale_ref[1], cells) * branch(0)
     parts = []
-    for step in range(768 // block):
-        value = pooled_ref[:, step * block : (step + 1) * block].astype(F32) + scale * branch(step * block)
-        for half in range(2):
-            i = 2 * step + half
-            cells = small_mask_ref[8 * i : 8 * i + 1, :] * value[:, half * 128 : half * 128 + 128]
-            parts.append(cells.astype(BF))
-    spread = dot(jnp.concatenate(parts, axis=0), unpool_ref[...])
-    weights = cell_weights(spread_weight_ref)
+    for i in range(GROUPS):
+        parts.append((small_mask_ref[8 * i : 8 * i + 1, :] * value[:, 128 * i : 128 * i + 128]).astype(BF))
+    spread = lax.dot_general(
+        jnp.concatenate(parts, axis=0), pool_ref[...], (((1,), (1,)), ((), ())), preferred_element_type=F32
+    )
+    weights = spread_cells_ref[...]
     for i in range(GROUPS):
         lanes = slice(i * FINE_IN, (i + 1) * FINE_IN)
-        value = fine_ref[:, lanes].astype(F32) + weights * spread[i * ROWS : (i + 1) * ROWS]
-        out_ref[0, :, lanes] = (mask_ref[:, lanes].astype(F32) * value).astype(BF)
+        merged = fine_ref[:, lanes].astype(F32) + weights * spread[i * ROWS : (i + 1) * ROWS]
+        out_ref[0, :, lanes] = (mask_ref[:, lanes].astype(F32) * merged).astype(BF)
 
 
 VMEM = pl.BlockSpec(memory_space=pltpu.VMEM)
@@ -543,28 +547,47 @@
         "small_halo": jnp.asarray(COARSE["halo"]),
         "sides": jnp.asarray(COARSE["sides"]),
         "pool": jnp.asarray(FINE["pool"]),
-        "unpool": jnp.asarray(FINE["unpool"]),
         "small_pack": jnp.asarray(COARSE["pack"]),
     }
     arrived = lax.all_to_all(messages, "tile", 0, 0, tiled=True)
-    conv = pl.pallas_call(
-        conv_fine,
-        in_specs=[SMEM] + [VMEM] * 7,
-        out_specs=VMEM,
-        out_shape=shaped(ROWS, cells),
-        scratch_shapes=[
-            pltpu.VMEM((ROWS, 3584), F32),
-            pltpu.VMEM((ROWS, 3584), F32),
-            pltpu.VMEM((49, ROWS, 128), F32),
-            pltpu.VMEM((ROWS, 3072), F32),
+    convs = []
+    for first, rows in ((0, 32), (32, 16)):
+        own = pl.pallas_call(
+            make_conv_fine(first, rows),
+            in_specs=[SMEM] + [VMEM] * 7,
+            out_specs=VMEM,
+            out_shape=shaped(rows, cells),
+            scratch_shapes=[
+                pltpu.VMEM((rows, 3584), F32),
+                pltpu.VMEM((rows, 3584), F32),
+                pltpu.VMEM((49, rows, 128), F32),
+                pltpu.VMEM((rows, 3072), F32),
+            ],
+            compiler_params=PARAMS,
+            cost_estimate=takes(2),
+            name=f"conv_fine_{first}",
+        )(table, held["x"], arrived, held["halo"], held["expand"], held["compact"], held["weight"], held["bias"])
+        convs.append(every_channel(own))
+    taps, conv_bias, gains, shifts, up_biases, down_biases, scales, pool_cells, spread_cells = pl.pallas_call(
+        params,
+        in_specs=[VMEM] * 10,
+        out_specs=[VMEM] * 9,
+        out_shape=[
+            shaped(*shape, dtype=F32)
+            for shape in (
+                (49, ROWS, 128), (ROWS, 128), (2, 192, 128), (2, 192, 128), (2, 768, 128), (2, ROWS, 128), (2, ROWS, 128),
+                (ROWS, FINE_IN), (ROWS, FINE_IN),
+            )
         ],
         compiler_params=PARAMS,
-        cost_estimate=takes(4),
-        name="conv_fine",
-    )(table, held["x"], arrived, held["halo"], held["expand"], held["compact"], held["weight"], held["bias"])
+        cost_estimate=takes(2),
+        name="params",
+    )(
+        convs[0][0], depth_weight, depth_bias, norm_gain, norm_bias, up_bias, down_bias, layer_scale, pool_weight, spread_weight
+    )
     fine, pooled, small_mask, messages = pl.pallas_call(
         make_mix_fine(count),
-        in_specs=[SMEM] + [VMEM] * 16,
+        in_specs=[SMEM] + [VMEM] * 20,
         out_specs=[VMEM] * 4,
         out_shape=[shaped(ROWS, cells), shaped(ROWS, 768), shaped(48, 128, dtype=F32), shaped(count, 16, 512)],
         scratch_shapes=[
@@ -573,11 +596,11 @@
             pltpu.VMEM((2, 16, 128), BF),
         ],
         compiler_params=PARAMS,
-        cost_estimate=takes(6),
+        cost_estimate=takes(4),
         name="mix_fine",
     )(
-        table, *every_channel(conv), held["x"], held["mask"], norm_gain, norm_bias, up_weight, up_bias,
-        down_weight, down_bias, layer_scale, pool_weight, held["pool"], held["small_pack"],
+        table, *(part for pair in zip(*convs) for part in pair), held["x"], held["mask"], gains, shifts, up_weight, up_biases,
+        down_weight, down_biases, scales, pool_cells, held["pool"], held["small_pack"],
     )
     arrived = lax.all_to_all(messages, "tile", 0, 0, tiled=True)
     conv = pl.pallas_call(
@@ -585,15 +608,11 @@
         in_specs=[SMEM] + [VMEM] * 6,
         out_specs=VMEM,
         out_shape=shaped(ROWS, 768),
-        scratch_shapes=[
-            pltpu.VMEM((4, ROWS, 1024), F32),
-            pltpu.VMEM((49, ROWS, 128), F32),
-            pltpu.VMEM((ROWS, 768), F32),
-        ],
+        scratch_shapes=[pltpu.VMEM((4, ROWS, 1024), F32), pltpu.VMEM((ROWS, 768), F32)],
         compiler_params=PARAMS,
         cost_estimate=takes(2),
         name="conv_coarse",
-    )(table, pooled, arrived, held["small_halo"], held["sides"], held["weight"], held["bias"])
+    )(table, pooled, arrived, held["small_halo"], held["sides"], taps, conv_bias)
     return pl.pallas_call(
         mix_coarse,
         in_specs=[VMEM] * 17,
@@ -601,11 +620,11 @@
         out_shape=shaped(1, ROWS, cells),
         scratch_shapes=[pltpu.VMEM((4 * ROWS, 768), BF)],
         compiler_params=PARAMS,
-        cost_estimate=takes(3),
+        cost_estimate=takes(2),
         name="mix_coarse",
     )(
-        *every_channel(conv), pooled, small_mask, fine, held["mask"], norm_gain, norm_bias, up_weight, up_bias,
-        down_weight, down_bias, layer_scale, spread_weight, held["unpool"],
+        *every_channel(conv), pooled, small_mask, fine, held["mask"], gains, shifts, up_weight, up_biases, down_weight, down_biases,
+        scales, spread_cells, held["pool"],
     )
 
 

time: 58.6 us -> 54.7 us (0.933)
  local copies, waits for them, and re-layouts: 3.39 us -> 1.45 us
  Pallas kernels: 15.8 us -> 14.8 us
  blocking collectives: 27.2 us -> 26.2 us
  starting transfers between devices: 3.13 us -> 3.86 us
    unnamed x51 -> x47, local copies, waits for them, and re-layouts: 3.39 us -> 1.45 us
    all_to_all x2, blocking collectives: 27.2 us -> 26.2 us  [per_device(): arrived = lax.all_to_all(messages, 'tile', 0, 0, tiled=True)]
    ppermute x2 -> x3, waiting for transfers between devices: 7.29 us -> 6.53 us  [every_channel(): across = lax.ppermute(own, 'chan', pairs(2))]
    pallas_call x1, Pallas kernels: 2.59 us -> 1.86 us  [per_device(): pl.pallas_call(mix_coarse, in_specs=[VMEM] * 17, out_specs=VMEM, out_shap...]
    ppermute x2 -> x3, starting transfers between devices: 3.11 us -> 2.78 us  [every_channel(): across = lax.ppermute(own, 'chan', pairs(2))]
    ppermute x2 -> x3, waiting for transfers between devices: 1.19 us -> 1.45 us  [every_channel(): diagonal = lax.ppermute(across, 'chan', pairs(1))]
    pallas_call x2 -> x4, Pallas kernels: 9.48 us -> 9.6 us  [the longest x2 4.89 us: per_device(): pl.pallas_call(make_conv_fine(first, rows), in_specs=[SMEM] + [VMEM] * 7,...]
  transfers between devices with their start and end apart: 6 -> 9, of which waited for: 3 -> 4; matrix products, arithmetic and copies ran while one was open for 3% -> 1% of each run, Pallas kernels for 0% -> 5%
where the time goes in v3:
time: 54.7 us; the launch traced here: 54.5 us
  blocking collectives  26.2 us (48%)
  Pallas kernels  14.8 us (27%)
  waiting for transfers between devices  7.99 us (15%)
  starting transfers between devices  3.86 us (7%)
  local copies, waits for them, and re-layouts  1.45 us (3%)
    all_to_all x2, blocking collectives, per_device(): arrived = lax.all_to_all(messages, 'tile', 0, 0, tiled=True)  26.2 us
    ppermute x3, waiting for transfers between devices, every_channel(): across = lax.ppermute(own, 'chan', pairs(2))  6.53 us
    pallas_call x2, Pallas kernels, per_device(): pl.pallas_call(make_conv_fine(first, rows), in_specs=[SMEM] + [VMEM] * 7,...  4.89 us
    pallas_call x1, Pallas kernels, per_device(): pl.pallas_call(make_mix_fine(count), in_specs=[SMEM] + [VMEM] * 20, out_s...  3.95 us
    ppermute x3, starting transfers between devices, every_channel(): across = lax.ppermute(own, 'chan', pairs(2))  2.78 us
    pallas_call x1, Pallas kernels, per_device(): pl.pallas_call(mix_coarse, in_specs=[VMEM] * 17, out_specs=VMEM, out_shap...  1.86 us
    pallas_call x1, Pallas kernels, per_device(): pl.pallas_call(conv_coarse, in_specs=[SMEM] + [VMEM] * 6, out_specs=VMEM,...  1.75 us
    pallas_call x1, Pallas kernels, per_device(): pl.pallas_call(make_prep(grid_x), in_specs=[SMEM, SMEM, VMEM, VMEM], out_...  1.53 us
  transfers between devices with their start and end apart: 9, of which 4 were waited for; matrix products, arithmetic and copies ran while one was open for 1% of the time, Pallas kernels for 5%

profile of v3, /device:TPU:0, one launch (start us, length us, event | category | flops | bytes accessed | tf_op | source)
XLA Modules:
  0.0 54.5 jit_solution(14958998501529609477)
XLA Ops:
  0.0 0.1 strip_table.1.pack_ref
  0.1 0.9 %copy-done.1 = bf16[1,48,2304]{2,1,0:T(8,128)(2,1)S(1)} copy-done((bf16[1,48,2304]{2,1,0:T(8,128)(2,1)S(1)}, bf16[1,48,2304]{2,1,0:T(8,128)(2,1)}, u32[]{:S(2)}) %copy-start.1) | copy-done | bytes 221208
  1.0 0.0 copy-start.12
  1.0 0.0 copy-start.14
  1.0 0.0 copy-start.16
  1.0 1.5 %prep.1 = (bf16[8,16,896]{2,1,0:T(8,128)(2,1)S(1)}, s32[24]{0:T(128)S(1)}) custom-call(s32[8]{0:T(128)S(1)} %copy-done.10, s32[8]{0:T(128)S(1)} %copy-done.11, bf16[1,48,2304]{2,1,0:T(8,128)(2,1)S(1)} %copy-done.1, bf16[384,256]{1,0:T(8,128)(2,1)S(1)} %strip_table.1.pack_ref), custom_call_target="tpu_custom_call" | custom-call | flops 10000000000 | tf_op jit(solution)/shard_map/prep/pallas_call | solution.py:524
  2.5 15.5 %all_to_all.10.recv_ref = bf16[8,16,896]{2,1,0:T(8,128)(2,1)S(1)} all-to-all(bf16[8,16,896]{2,1,0:T(8,128)(2,1)S(1)} %get-tuple-element.21), channel_id=1, replica_groups=mesh['tile'=8,'chan'=4] {'tile'}, dimensions={0} | all-to-all | bytes 458752 | tf_op jit(solution)/shard_map/all_to_all | solution.py:552
  18.1 2.9 %conv_fine_0.1.after_ref.own_a_ref = bf16[32,2304]{1,0:T(8,128)(2,1)S(1)} custom-call(s32[24]{0:T(128)S(1)} %get-tuple-element.20.tab_ref, bf16[1,48,2304]{2,1,0:T(8,128)(2,1)S(1)} %copy-done.1, bf16[8,16,896]{2,1,0:T(8,128)(2,1)S(1)} %all_to_all.10.recv_ref, bf16[3,768,256]{2,1,0:T(8,128)(2,1)S(1)} %copy-done.12, bf16[512,512]{1,0:T(8,128)(2,1)S(1)} %copy-done.14, ...), custom_call_target="tpu_custom_call" | custom-call | flops 2000000000 | tf_op jit(solution)/shard_map/conv_fine_0/pallas_call | solution.py:555
  21.0 0.0 copy-start.20
  21.1 1.6 %collective-permute-start.2 = (bf16[32,2304]{1,0:T(8,128)(2,1)S(1)}, bf16[32,2304]{1,0:T(8,128)(2,1)S(1)}, u32[]{:S(2)}, u32[]{:S(2)}) collective-permute-start(bf16[32,2304]{1,0:T(8,128)(2,1)S(1)} %conv_fine_0.1.after_ref.own_a_ref), channel_id=1, source_target_pairs={{0,2},{1,3},{2,0},{3,1},{4,6},{5,7},{6,4},{7,5},{8,10},{9,11},{10,... | collective-permute-start | bytes 442376 | tf_op jit(solution)/shard_map/ppermute | solution.py:508
  22.6 1.9 %conv_fine_32.1.own_b_ref = bf16[16,2304]{1,0:T(8,128)(2,1)S(1)} custom-call(s32[24]{0:T(128)S(1)} %get-tuple-element.20.tab_ref, bf16[1,48,2304]{2,1,0:T(8,128)(2,1)S(1)} %copy-done.1, bf16[8,16,896]{2,1,0:T(8,128)(2,1)S(1)} %all_to_all.10.recv_ref, bf16[3,768,256]{2,1,0:T(8,128)(2,1)S(1)} %copy-done.12, bf16[512,512]{1,0:T(8,128)(2,1)S(1)} %copy-done.14, ...), custom_call_target="tpu_custom_call" | custom-call | flops 2000000000 | tf_op jit(solution)/shard_map/conv_fine_32/pallas_call | solution.py:555
  24.6 0.6 %collective-permute-start.3 = (bf16[16,2304]{1,0:T(8,128)(2,1)S(1)}, bf16[16,2304]{1,0:T(8,128)(2,1)S(1)}, u32[]{:S(2)}, u32[]{:S(2)}) collective-permute-start(bf16[16,2304]{1,0:T(8,128)(2,1)S(1)} %conv_fine_32.1.own_b_ref), channel_id=1, source_target_pairs={{0,2},{1,3},{2,0},{3,1},{4,6},{5,7},{6,4},{7,5},{8,10},{9,11},{10,... | collective-permute-start | bytes 221192 | tf_op jit(solution)/shard_map/ppermute | solution.py:508
  25.2 0.1 copy.23.pool_weight_ref
  25.3 0.1 copy.24.spread_weight_ref
  25.4 0.3 copy.25.up_ref
  25.7 0.0 copy-start.13
  25.7 0.0 copy-start.18
  25.7 0.1 collective-permute-start.1
  25.8 0.5 collective-permute-start
  26.3 2.7 %collective-permute-done.3.p2_b_ref = bf16[16,2304]{1,0:T(8,128)(2,1)S(1)} collective-permute-done((bf16[16,2304]{1,0:T(8,128)(2,1)S(1)}, bf16[16,2304]{1,0:T(8,128)(2,1)S(1)}, u32[]{:S(2)}, u32[]{:S(2)}) %collective-permute-start.3) | collective-permute-done | bytes 73760 | tf_op jit(solution)/shard_map/ppermute | solution.py:508
  29.1 0.5 collective-permute-start.4
  29.6 0.8 %params.1 = (f32[49,48,128]{2,1,0:T(8,128)S(1)}, f32[48,128]{1,0:T(8,128)S(1)}, f32[2,192,128]{2,1,0:T(8,128)S(1)}, f32[2,192,128]{2,1,0:T(8,128)S(1)}, f32[2,76...) custom-call(bf16[32,2304]{1,0:T(8,128)(2,1)S(1)} %conv_fine_0.1.afte, ...), custom_call_target="tpu_custom_call" | custom-call | flops 2000000000 | tf_op jit(solution)/shard_map/params/pallas_call | solution.py:571
  30.4 0.2 collective-permute-done.4.p3_a_ref
  30.6 0.0 copy-start.15
  30.6 0.0 copy-start.17
  30.6 3.9 %mix_fine.1 = (bf16[48,2304]{1,0:T(8,128)(2,1)S(1)}, bf16[48,768]{1,0:T(8,128)(2,1)S(1)}, f32[48,128]{1,0:T(8,128)S(1)}, bf16[8,16,512]{2,1,0:T(8,128)(2,1)S(1)}) custom-call(s32[24]{0:T(128)S(1)} %get-tuple-element.20.tab_ref, bf16[32,2304]{1,0:T(8,128)(2,1)S(1)} %conv_fine_0.1.after_ref.own_a_ref, bf16[16,2304]{1,0:T(8,128)(2,1)S(1)} %conv_fine_32.1.own_b_ref, ...), custom_call_target="tpu_custom_call" | custom-call | flops 4000000000 | tf_op jit(solution)/shard_map/mix_fine/pallas_call | solution.py:588
  34.6 10.6 %all_to_all.11.recv_ref = bf16[8,16,512]{2,1,0:T(8,128)(2,1)S(1)} all-to-all(bf16[8,16,512]{2,1,0:T(8,128)(2,1)S(1)} %get-tuple-element.29), channel_id=1, replica_groups=mesh['tile'=8,'chan'=4] {'tile'}, dimensions={0} | all-to-all | bytes 262144 | tf_op jit(solution)/shard_map/all_to_all | solution.py:605
  45.2 1.8 %conv_coarse.1.own_ref = bf16[48,768]{1,0:T(8,128)(2,1)S(1)} custom-call(s32[24]{0:T(128)S(1)} %get-tuple-element.20.tab_ref, bf16[48,768]{1,0:T(8,128)(2,1)S(1)} %get-tuple-element.28.x_ref.pooled_ref, bf16[8,16,512]{2,1,0:T(8,128)(2,1)S(1)} %all_to_all.11.recv_ref, bf16[3,384,128]{2,1,0:T(8,128)(2,1)S(1)} %copy-done.17, bf16[256,768]{1,0:T(8,128)(2,1)S(1)} %copy-done.15, ...), custom_call_target="tpu_custom_call" | custom-call | flops 2000000000 | tf_op jit(solution)/shard_map/conv_coarse/pallas_call | solution.py:606
  47.0 0.6 %collective-permute-start.7 = (bf16[48,768]{1,0:T(8,128)(2,1)S(1)}, bf16[48,768]{1,0:T(8,128)(2,1)S(1)}, u32[]{:S(2)}, u32[]{:S(2)}) collective-permute-start(bf16[48,768]{1,0:T(8,128)(2,1)S(1)} %conv_coarse.1.own_ref), channel_id=1, source_target_pairs={{0,2},{1,3},{2,0},{3,1},{4,6},{5,7},{6,4},{7,5},{8,10},{9,11},{10,... | collective-permute-start | bytes 221192 | tf_op jit(solution)/shard_map/ppermute | solution.py:508
  47.6 3.8 %collective-permute-done.7.p2_ref = bf16[48,768]{1,0:T(8,128)(2,1)S(1)} collective-permute-done((bf16[48,768]{1,0:T(8,128)(2,1)S(1)}, bf16[48,768]{1,0:T(8,128)(2,1)S(1)}, u32[]{:S(2)}, u32[]{:S(2)}) %collective-permute-start.7) | collective-permute-done | bytes 73760 | tf_op jit(solution)/shard_map/ppermute | solution.py:508
  51.4 1.3 %collective-permute-done.8.p3_ref = bf16[48,768]{1,0:T(8,128)(2,1)S(1)} collective-permute-done((bf16[48,768]{1,0:T(8,128)(2,1)S(1)}, bf16[48,768]{1,0:T(8,128)(2,1)S(1)}, u32[]{:S(2)}, u32[]{:S(2)}) %collective-permute-start.8) | collective-permute-done | bytes 73760 | tf_op jit(solution)/shard_map/ppermute | solution.py:510
  52.7 1.9 %mix_coarse.1 = bf16[1,48,2304]{2,1,0:T(8,128)(2,1)} custom-call(bf16[48,768]{1,0:T(8,128)(2,1)S(1)} %conv_coarse.1.own_ref, bf16[48,768]{1,0:T(8,128)(2,1)S(1)} %collective-permute-done.6.p1_ref, bf16[48,768]{1,0:T(8,128)(2,1)S(1)} %collective-permute-done.7.p2_ref, bf16[48,768]{1,0:T(8,128)(2,1)S(1)} %collective-permute-done.8.p3_ref, ...), custom_call_target="tpu_custom_call" | custom-call | flops 2000000000 | tf_op jit(solution)/shard_map/mix_coarse/pallas_call | solution.py:616
  (43 shorter events, 0.1 us)
Async XLA Ops:
  0.0 0.9 %copy-start.1 = (bf16[1,48,2304]{2,1,0:T(8,128)(2,1)S(1)}, bf16[1,48,2304]{2,1,0:T(8,128)(2,1)}, u32[]{:S(2)}) copy-start(bf16[1,48,2304]{2,1,0:T(8,128)(2,1)} %x_ref.7) | copy-start | bytes 663556
  0.0 0.9 %copy-start.11 = (s32[8]{0:T(128)S(1)}, s32[8]{0:T(128)}, u32[]{:S(2)}) copy-start(s32[8]{0:T(128)} %dev_ref.1) | copy-start | bytes 100
  0.0 0.9 %copy-start.10 = (s32[8]{0:T(128)S(1)}, s32[8]{0:T(128)}, u32[]{:S(2)}) copy-start(s32[8]{0:T(128)} %slots_ref.1) | copy-start | bytes 100
  0.9 17.1 %copy-start.2 = (f32[2,48,49]{2,1,0:T(8,128)S(1)}, f32[2,48,49]{2,1,0:T(8,128)}, u32[]{:S(2)}) copy-start(f32[2,48,49]{2,1,0:T(8,128)} %weight_ref.5) | copy-start | bytes 56452
  0.9 17.1 %copy-start.8 = (f32[2,48]{1,0:T(2,128)S(1)}, f32[2,48]{1,0:T(2,128)}, u32[]{:S(2)}) copy-start(f32[2,48]{1,0:T(2,128)} %bias_ref.5) | copy-start | bytes 1156
  1.0 17.1 %copy-start.12 = (bf16[3,768,256]{2,1,0:T(8,128)(2,1)S(1)}, bf16[3,768,256]{2,1,0:T(8,128)(2,1)}, u32[]{:S(2)}) copy-start(bf16[3,768,256]{2,1,0:T(8,128)(2,1)} %constant.14.clone.halo_ref) | copy-start | bytes 3538948
  1.0 17.1 %copy-start.14 = (bf16[512,512]{1,0:T(8,128)(2,1)S(1)}, bf16[512,512]{1,0:T(8,128)(2,1)}, u32[]{:S(2)}) copy-start(bf16[512,512]{1,0:T(8,128)(2,1)} %constant.15.clone.expand_ref) | copy-start | bytes 1572868
  1.0 17.1 %copy-start.16 = (bf16[512,384]{1,0:T(8,128)(2,1)S(1)}, bf16[512,384]{1,0:T(8,128)(2,1)}, u32[]{:S(2)}) copy-start(bf16[512,384]{1,0:T(8,128)(2,1)} %constant.16.clone.compact_ref) | copy-start | bytes 1179652
  21.0 4.2 %copy-start.20 = (f32[48,4]{0,1:T(4,128)S(1)}, f32[48,4]{0,1:T(4,128)}, u32[]{:S(2)}) copy-start(f32[48,4]{0,1:T(4,128)} %param.35) | copy-start | bytes 2308
  21.0 4.3 %copy-start.21 = (f32[48,4]{0,1:T(4,128)S(1)}, f32[48,4]{0,1:T(4,128)}, u32[]{:S(2)}) copy-start(f32[48,4]{0,1:T(4,128)} %param.36) | copy-start | bytes 2308
  21.1 4.4 %copy-start.19 = (bf16[2,768,192]{1,2,0:T(8,128)(2,1)S(1)}, bf16[2,768,192]{1,2,0:T(8,128)(2,1)}, u32[]{:S(2)}) copy-start(bf16[2,768,192]{1,2,0:T(8,128)(2,1)} %param.30) | copy-start | bytes 1769476
  21.1 8.0 %collective-permute-start.2 = (bf16[32,2304]{1,0:T(8,128)(2,1)S(1)}, bf16[32,2304]{1,0:T(8,128)(2,1)S(1)}, u32[]{:S(2)}, u32[]{:S(2)}) collective-permute-start(bf16[32,2304]{1,0:T(8,128)(2,1)S(1)} %conv_fine_0.1.after_ref.own_a_ref), channel_id=1, source_target_pairs={{0,2},{1,3},{2,0},{3,1},{4,6},{5,7},{6,4},{7,5},{8,10},{9,11},{10,... | collective-permute-start | bytes 442376 | tf_op jit(solution)/shard_map/ppermute | solution.py:508
  24.6 5.0 %copy-start.4 = (f32[2,768]{1,0:T(2,128)S(1)}, f32[2,768]{1,0:T(2,128)}, u32[]{:S(2)}) copy-start(f32[2,768]{1,0:T(2,128)} %up_bias_ref.1) | copy-start | bytes 18436
  24.6 5.0 %copy-start.5 = (f32[2,192]{1,0:T(2,128)S(1)}, f32[2,192]{1,0:T(2,128)}, u32[]{:S(2)}) copy-start(f32[2,192]{1,0:T(2,128)} %gain_ref.1) | copy-start | bytes 4612
  24.6 5.0 %copy-start.6 = (f32[2,192]{1,0:T(2,128)S(1)}, f32[2,192]{1,0:T(2,128)}, u32[]{:S(2)}) copy-start(f32[2,192]{1,0:T(2,128)} %shift_ref.1) | copy-start | bytes 4612
  24.6 5.0 %copy-start.7 = (f32[2,192]{1,0:T(2,128)S(1)}, f32[2,192]{1,0:T(2,128)}, u32[]{:S(2)}) copy-start(f32[2,192]{1,0:T(2,128)} %down_bias_ref.1) | copy-start | bytes 4612
  24.6 5.0 %copy-start.9 = (f32[2,48]{1,0:T(2,128)S(1)}, f32[2,48]{1,0:T(2,128)}, u32[]{:S(2)}) copy-start(f32[2,48]{1,0:T(2,128)} %scale_ref.1) | copy-start | bytes 1156
  24.6 4.4 %collective-permute-start.3 = (bf16[16,2304]{1,0:T(8,128)(2,1)S(1)}, bf16[16,2304]{1,0:T(8,128)(2,1)S(1)}, u32[]{:S(2)}, u32[]{:S(2)}) collective-permute-start(bf16[16,2304]{1,0:T(8,128)(2,1)S(1)} %conv_fine_32.1.own_b_ref), channel_id=1, source_target_pairs={{0,2},{1,3},{2,0},{3,1},{4,6},{5,7},{6,4},{7,5},{8,10},{9,11},{10,... | collective-permute-start | bytes 221192 | tf_op jit(solution)/shard_map/ppermute | solution.py:508
  25.7 4.9 %copy-start = (bf16[2,192,768]{2,1,0:T(8,128)(2,1)S(1)}, bf16[2,192,768]{2,1,0:T(8,128)(2,1)}, u32[]{:S(2)}) copy-start(bf16[2,192,768]{2,1,0:T(8,128)(2,1)} %down_ref.3) | copy-start | bytes 1769476
  25.7 4.9 %copy-start.3 = (s32[1,2304]{1,0:T(1,128)S(1)}, s32[1,2304]{1,0:T(1,128)}, u32[]{:S(2)}) copy-start(s32[1,2304]{1,0:T(1,128)} %mask_ref.3) | copy-start | bytes 27652
  25.7 4.9 %copy-start.13 = (bf16[768,384]{1,0:T(8,128)(2,1)S(1)}, bf16[768,384]{1,0:T(8,128)(2,1)}, u32[]{:S(2)}) copy-start(bf16[768,384]{1,0:T(8,128)(2,1)} %constant.20.clone.pack_ref) | copy-start | bytes 1769476
  25.7 4.9 %copy-start.18 = (bf16[384,128]{1,0:T(8,128)(2,1)S(1)}, bf16[384,128]{1,0:T(8,128)(2,1)}, u32[]{:S(2)}) copy-start(bf16[384,128]{1,0:T(8,128)(2,1)} %constant.19.clone.pool_ref) | copy-start | bytes 294916
  25.7 4.6 %collective-permute-start.1 = (bf16[16,2304]{1,0:T(8,128)(2,1)S(1)}, bf16[16,2304]{1,0:T(8,128)(2,1)S(1)}, u32[]{:S(2)}, u32[]{:S(2)}) collective-permute-start(bf16[16,2304]{1,0:T(8,128)(2,1)S(1)} %conv_fine_32.1.own_b_ref), channel_id=1, source_target_pairs={{0,1},{1,0},{2,3},{3,2},{4,5},{5,4},{6,7},{7,6},{8,9},{9,8},{10,11... | collective-permute-start | bytes 221192 | tf_op jit(solution)/shard_map/ppermute | solution.py:509
  25.8 4.6 %collective-permute-start = (bf16[32,2304]{1,0:T(8,128)(2,1)S(1)}, bf16[32,2304]{1,0:T(8,128)(2,1)S(1)}, u32[]{:S(2)}, u32[]{:S(2)}) collective-permute-start(bf16[32,2304]{1,0:T(8,128)(2,1)S(1)} %conv_fine_0.1.after_ref.own_a_ref), channel_id=1, source_target_pairs={{0,1},{1,0},{2,3},{3,2},{4,5},{5,4},{6,7},{7,6},{8,9},{9,8},{10,11... | collective-permute-start | bytes 442376 | tf_op jit(solution)/shard_map/ppermute | solution.py:509
  29.1 1.3 %collective-permute-start.5 = (bf16[16,2304]{1,0:T(8,128)(2,1)S(1)}, bf16[16,2304]{1,0:T(8,128)(2,1)S(1)}, u32[]{:S(2)}, u32[]{:S(2)}) collective-permute-start(bf16[16,2304]{1,0:T(8,128)(2,1)S(1)} %collective-permute-done.3.p2_b_ref), channel_id=1, source_target_pairs={{0,1},{1,0},{2,3},{3,2},{4,5},{5,4},{6,7},{7,6},{8,9},{9,8},{10,11... | collective-permute-start | bytes 221192 | tf_op jit(solution)/shard_map/ppermute | solution.py:510
  29.1 1.5 %collective-permute-start.4 = (bf16[32,2304]{1,0:T(8,128)(2,1)S(1)}, bf16[32,2304]{1,0:T(8,128)(2,1)S(1)}, u32[]{:S(2)}, u32[]{:S(2)}) collective-permute-start(bf16[32,2304]{1,0:T(8,128)(2,1)S(1)} %collective-permute-done.2.p2_a_ref), channel_id=1, source_target_pairs={{0,1},{1,0},{2,3},{3,2},{4,5},{5,4},{6,7},{7,6},{8,9},{9,8},{10,11... | collective-permute-start | bytes 442376 | tf_op jit(solution)/shard_map/ppermute | solution.py:510
  30.6 14.6 %copy-start.15 = (bf16[256,768]{1,0:T(8,128)(2,1)S(1)}, bf16[256,768]{1,0:T(8,128)(2,1)}, u32[]{:S(2)}) copy-start(bf16[256,768]{1,0:T(8,128)(2,1)} %constant.18.clone.sides_ref) | copy-start | bytes 1179652
  30.6 14.6 %copy-start.17 = (bf16[3,384,128]{2,1,0:T(8,128)(2,1)S(1)}, bf16[3,384,128]{2,1,0:T(8,128)(2,1)}, u32[]{:S(2)}) copy-start(bf16[3,384,128]{2,1,0:T(8,128)(2,1)} %constant.17.clone.halo_ref) | copy-start | bytes 884740
  47.0 4.4 %collective-permute-start.7 = (bf16[48,768]{1,0:T(8,128)(2,1)S(1)}, bf16[48,768]{1,0:T(8,128)(2,1)S(1)}, u32[]{:S(2)}, u32[]{:S(2)}) collective-permute-start(bf16[48,768]{1,0:T(8,128)(2,1)S(1)} %conv_coarse.1.own_ref), channel_id=1, source_target_pairs={{0,2},{1,3},{2,0},{3,1},{4,6},{5,7},{6,4},{7,5},{8,10},{9,11},{10,... | collective-permute-start | bytes 221192 | tf_op jit(solution)/shard_map/ppermute | solution.py:508
  47.6 3.8 %collective-permute-start.6 = (bf16[48,768]{1,0:T(8,128)(2,1)S(1)}, bf16[48,768]{1,0:T(8,128)(2,1)S(1)}, u32[]{:S(2)}, u32[]{:S(2)}) collective-permute-start(bf16[48,768]{1,0:T(8,128)(2,1)S(1)} %conv_coarse.1.own_ref), channel_id=1, source_target_pairs={{0,1},{1,0},{2,3},{3,2},{4,5},{5,4},{6,7},{7,6},{8,9},{9,8},{10,11... | collective-permute-start | bytes 221192 | tf_op jit(solution)/shard_map/ppermute | solution.py:509
  51.4 1.3 %collective-permute-start.8 = (bf16[48,768]{1,0:T(8,128)(2,1)S(1)}, bf16[48,768]{1,0:T(8,128)(2,1)S(1)}, u32[]{:S(2)}, u32[]{:S(2)}) collective-permute-start(bf16[48,768]{1,0:T(8,128)(2,1)S(1)} %collective-permute-done.7.p2_ref), channel_id=1, source_target_pairs={{0,1},{1,0},{2,3},{3,2},{4,5},{5,4},{6,7},{7,6},{8,9},{9,8},{10,11... | collective-permute-start | bytes 221192 | tf_op jit(solution)/shard_map/ppermute | solution.py:510

commit v4 on v3

--- a/solution.py
+++ b/solution.py
@@ -59,20 +59,27 @@
             one_hot((768, 256), halo_pairs(last, TILE, 64, 0, True)),
         ]
     )
-    expand, compact, pool = [], [], []
+    expand, compact, pool, spread, sides = [], [], [], [], []
     for row in range(8):
-        for j in range(3):
-            expand.append((384 + row * 3 + j, row * 64 + j))
-            expand.append((384 + 24 + row * 3 + j, row * 64 + 51 + j))
         for col in range(48):
             expand.append((row * 48 + col, row * 64 + 3 + col))
             compact.append((row * 64 + 3 + col, row * 48 + col))
             pool.append((row * 48 + col, (row // 2) * 32 + 3 + col // 2))
+        for q in range(3):
+            spread.append((8 * q + row, row * 64 + 3 + q))
+            spread.append((64 + 8 * q + row, row * 64 + 3 + 47 - q))
+    for row in range(TILE):
+        for j in range(3):
+            lane = 3 * row + j if row < 40 else 128 + 16 + 3 * (row - 40) + j
+            sides.append((lane, 128 * j + row))
+            sides.append((256 + lane, 128 * (2 - j) + 64 + row))
     return {
         "halo": halo,
-        "expand": one_hot((512, 512), expand),
+        "expand": one_hot((384, 512), expand),
         "compact": one_hot((512, 384), compact),
         "pool": one_hot((384, 128), pool),
+        "spread": one_hot((128, 512), spread),
+        "sides": one_hot((512, 384), sides),
     }
 
 
@@ -152,16 +159,28 @@
     pack_ref[...] = jnp.where((within < 24) & (source == wanted), 1.0, 0.0).astype(BF)
 
 
+def quotient(value, divisor):
+    if divisor & (divisor - 1) == 0:
+        return lax.shift_right_logical(value, jnp.int32(divisor.bit_length() - 1))
+    return lax.div(value, divisor)
+
+
+def remainder(value, divisor):
+    if divisor & (divisor - 1) == 0:
+        return lax.bitwise_and(value, jnp.int32(divisor - 1))
+    return lax.rem(value, divisor)
+
+
 def make_prep(grid_x):
     def prep(slots_ref, dev_ref, x_ref, pack_ref, msg_ref, tab_ref, rows_ref, cols_ref, row_rest_ref, col_rest_ref):
         count = slots_ref.shape[0]
         me = lax.axis_index("tile")
         my_slot = scan_tiles(count, lambda k, c: c + jnp.where(dev_ref[k] == me, slots_ref[k], 0), jnp.int32(0))
-        my_x = lax.rem(my_slot, grid_x)
-        my_y = lax.div(my_slot, grid_x)
+        my_x = remainder(my_slot, grid_x)
+        my_y = quotient(my_slot, grid_x)
         wanted = []
         for up_by, right_by in BANDS:
-            near_x = lax.rem(my_x + (right_by + grid_x), grid_x)
+            near_x = remainder(my_x + (right_by + grid_x), grid_x)
             near_y = my_y + up_by
             folded = near_y >= GRID_Y
             from_x = jnp.where(folded, grid_x - 1 - near_x, near_x)
@@ -170,8 +189,8 @@
 
         def find(k, found):
             slot, dev = slots_ref[k], dev_ref[k]
-            row_pick = jnp.where(lax.div(slot, grid_x) + 1 == my_y, 0, 1)
-            col_pick = jnp.where(lax.rem(slot, grid_x) == lax.rem(my_x + (grid_x - 1), grid_x), 0, 1)
+            row_pick = jnp.where(quotient(slot, grid_x) + 1 == my_y, 0, 1)
+            col_pick = jnp.where(remainder(slot, grid_x) == remainder(my_x + (grid_x - 1), grid_x), 0, 1)
             tab_ref[16 + dev] = 2 * row_pick + col_pick
             return tuple(jnp.where(slot == want, dev, old) for want, old in zip(wanted, found))
 
@@ -201,8 +220,8 @@
             row_rest_ref[side] = rest[0:16] + pltpu.roll(rest[16:32], 40, 1) + pltpu.roll(rest[32:48], 80, 1)
 
         def fill(dev, carry):
-            row_pick = lax.div(tab_ref[16 + dev], 2)
-            col_pick = lax.rem(tab_ref[16 + dev], 2)
+            row_pick = quotient(tab_ref[16 + dev], 2)
+            col_pick = remainder(tab_ref[16 + dev], 2)
             for g in range(3):
                 msg_ref[dev, :, 256 * g : 256 * g + 128] = rows_ref[row_pick, 16 * g : 16 * g + 16, :]
                 msg_ref[dev, :, 256 * g + 128 : 256 * g + 256] = cols_ref[col_pick, 16 * g : 16 * g + 16, :]
@@ -223,79 +242,115 @@
     return pltpu.roll(value, value.shape[1] - lanes, 1)
 
 
-def make_conv_fine(first, rows):
-    def conv_fine(tab_ref, x_ref, recv_ref, halo_ref, expand_ref, compact_ref, weight_ref, bias_ref, out_ref, pad_ref, odd_ref, wide_ref, sum_ref):
-        for tap in range(49):
-            wide_ref[tap] = jnp.broadcast_to(weight_ref[0, first : first + rows, tap : tap + 1], (rows, 128))
-        lane = lane_ids((rows, 128))
-        parts = range(first // 16, (first + rows) // 16)
-
-        def rest_of(source, scale):
-            rest = recv_ref[source, :, 768:896].astype(F32) * scale
-            return jnp.concatenate([pltpu.roll(rest, 128 - 40 * g, 1) if g else rest for g in parts], axis=0)
-
-        def main_of(source, scale, offset):
-            pieces = [recv_ref[source, :, 256 * g + offset : 256 * g + offset + 128] for g in parts]
-            return jnp.concatenate(pieces, axis=0).astype(F32) * scale
-
-        def row_strips(bands):
-            pieces = []
-            for band in bands:
-                source, scale = band_source(tab_ref, band)
-                pieces += [main_of(source, scale, 0).astype(BF), rest_of(source, scale).astype(BF)]
-            return jnp.concatenate(pieces, axis=1)
-
-        pad_ref[:, 0:256] = dot(row_strips((0, 1, 2)), halo_ref[0])
-        pad_ref[:, 3328:3584] = dot(row_strips((5, 6, 7)), halo_ref[tab_ref[8]])
-        sides = []
-        for band in (3, 4):
+def conv_inner(x_ref, expand_ref, weight_ref, bias_ref, sum_ref, wide_ref, pad_ref, odd_ref):
+    for tap in range(49):
+        wide_ref[tap] = jnp.broadcast_to(weight_ref[0, :, tap : tap + 1], (ROWS, 128))
+    pad_ref[:, 0:256] = jnp.zeros((ROWS, 256), F32)
+    pad_ref[:, 3328:3584] = jnp.zeros((ROWS, 256), F32)
+    padded = dot(stacked(x_ref[0], FINE_IN), expand_ref[...])
+    for i in range(GROUPS):
+        pad_ref[:, 256 + 512 * i : 768 + 512 * i] = padded[i * ROWS : (i + 1) * ROWS]
+    odd_ref[...] = lane_shifted(pad_ref[...], 64)
+    sum_ref[...] = wide(columns(bias_ref[0:1, :]), 3072)
+
+    def group(g, carry):
+        here = pl.ds(pl.multiple_of(g * 8, 8), 8)
+        for chunk in range(6):
+            base = chunk * 512
+            taken = []
+            for a in range(1, 8):
+                ref = odd_ref if a % 2 else pad_ref
+                start = base + (a // 2) * 128
+                taken.append([ref[here, start + 128 * j : start + 128 * j + 128] for j in range(4)])
+            total = [sum_ref[here, base + 128 * j : base + 128 * j + 128] for j in range(4)]
+            for b in range(7):
+                weights = [wide_ref[a * 7 + b, here, :] for a in range(7)]
+                for j in range(4):
+                    partial = weights[0] * taken[0][j]
+                    for a in range(1, 7):
+                        partial = partial + weights[a] * taken[a][j]
+                    total[j] = total[j] + (pltpu.roll(partial, (3 - b) % 128, 1) if b != 3 else partial)
+            for j in range(4):
+                sum_ref[here, base + 128 * j : base + 128 * j + 128] = total[j]
+        return carry
+
+    lax.fori_loop(0, ROWS // 8, group, 0)
+
+
+def conv_border(tab_ref, recv_ref, sum_ref, wide_ref, halo_ref, sides_ref, spread_ref, compact_ref, out_ref):
+    lane = lane_ids((ROWS, 128))
+    low_half = lane < 64
+
+    def rest_of(source, scale):
+        rest = recv_ref[source, :, 768:896].astype(F32) * scale
+        return jnp.concatenate([rest, pltpu.roll(rest, 128 - 40, 1), pltpu.roll(rest, 128 - 80, 1)], axis=0)
+
+    def strips(bands, offset):
+        pieces = []
+        for band in bands:
             source, scale = band_source(tab_ref, band)
-            main, rest = main_of(source, scale, 128), rest_of(source, scale)
-            turned = [pltpu.roll(main, 128 - 24 * i, 1) if i else main for i in range(5)]
-            sides.append(turned + [pltpu.roll(rest, 128 - 16, 1)])
-        halos = []
-        for i in range(GROUPS):
-            both = jnp.where(lane < 24, sides[0][i], pltpu.roll(sides[1][i], 24, 1))
-            halos.append(jnp.where(lane < 48, both, 0.0))
-        x = x_ref[0, first : first + rows, :]
-        joined = jnp.concatenate([stacked(x, FINE_IN), jnp.concatenate(halos, axis=0).astype(BF)], axis=1)
-        padded = dot(joined, expand_ref[...])
-        for i in range(GROUPS):
-            pad_ref[:, 256 + 512 * i : 768 + 512 * i] = padded[i * rows : (i + 1) * rows]
-        odd_ref[...] = lane_shifted(pad_ref[...], 64)
-        sum_ref[...] = wide(columns(bias_ref[0:1, :])[first : first + rows], 3072)
-
-        def group(g, carry):
-            here = pl.ds(pl.multiple_of(g * 8, 8), 8)
-            for chunk in range(6):
-                base = chunk * 512
-                taken = []
-                for a in range(1, 8):
-                    ref = odd_ref if a % 2 else pad_ref
-                    start = base + (a // 2) * 128
-                    taken.append([ref[here, start + 128 * j : start + 128 * j + 128] for j in range(4)])
-                total = [sum_ref[here, base + 128 * j : base + 128 * j + 128] for j in range(4)]
-                for b in range(7):
-                    weights = [wide_ref[a * 7 + b, here, :] for a in range(7)]
-                    for j in range(4):
-                        partial = weights[0] * taken[0][j]
-                        for a in range(1, 7):
-                            partial = partial + weights[a] * taken[a][j]
-                        total[j] = total[j] + (pltpu.roll(partial, (3 - b) % 128, 1) if b != 3 else partial)
-                for j in range(4):
-                    sum_ref[here, base + 128 * j : base + 128 * j + 128] = total[j]
-            return carry
-
-        lax.fori_loop(0, rows // 8, group, 0)
-        dense = dot(stacked(sum_ref[...].astype(BF), FINE_PAD), compact_ref[...]).astype(BF)
-        for i in range(GROUPS):
-            out_ref[:, i * FINE_IN : (i + 1) * FINE_IN] = dense[i * rows : (i + 1) * rows]
-
-    return conv_fine
+            main = jnp.concatenate([recv_ref[source, :, 256 * g + offset : 256 * g + offset + 128] for g in range(3)], axis=0)
+            pieces += [(main.astype(F32) * scale).astype(BF), rest_of(source, scale).astype(BF)]
+        return jnp.concatenate(pieces, axis=1)
+
+    def tap(a, b):
+        return wide_ref[a * 7 + b]
+
+    def row_fix(uses):
+        total = [jnp.zeros((ROWS, 128), F32)] * 2
+        for b in range(7):
+            partial = [None, None]
+            for place, a, cells in uses:
+                term = tap(a, b) * cells
+                partial[place] = term if partial[place] is None else partial[place] + term
+            for place in range(2):
+                total[place] = total[place] + (pltpu.roll(partial[place], (3 - b) % 128, 1) if b != 3 else partial[place])
+        return total
+
+    below = dot(strips((0, 1, 2), 0), halo_ref[0])
+    above = dot(strips((5, 6, 7), 0), halo_ref[tab_ref[8]])
+    turned = [pltpu.roll(below[:, 128 * k : 128 * k + 128], 64, 1) for k in range(2)]
+    last = jnp.where(low_half, turned[1], 0.0)
+    first_fix = row_fix(((0, 0, jnp.where(low_half, turned[0], turned[1])), (0, 1, below[:, 128:256]), (0, 2, last), (1, 0, last)))
+    turned = [pltpu.roll(above[:, 128 * k : 128 * k + 128], 64, 1) for k in range(2)]
+    first = jnp.where(low_half, 0.0, turned[0])
+    last_fix = row_fix(((0, 6, first), (1, 4, first), (1, 5, above[:, 0:128]), (1, 6, jnp.where(low_half, turned[0], turned[1]))))
+
+    beside = dot(strips((3, 4), 128), sides_ref[...])
+    beside = [beside[:, 128 * j : 128 * j + 128] for j in range(3)]
+    column_fix = [jnp.zeros((ROWS, 128), F32)] * 3
+    for a in range(7):
+        weights = [jnp.where(low_half, tap(a, b), tap(a, 6 - b)) for b in range(3)]
+        for q in range(3):
+            partial = weights[0] * beside[q]
+            for j in range(q + 1, 3):
+                partial = partial + weights[j - q] * beside[j]
+            column_fix[q] = column_fix[q] + (pltpu.roll(partial, (3 - a) % 128, 1) if a != 3 else partial)
+    within = lane % 64
+    highs, lows = [], []
+    for i in range(GROUPS):
+        parts = [pltpu.roll(column_fix[q], (8 * q - 8 * i) % 128, 1) if q != i else column_fix[q] for q in range(3)]
+        value = jnp.where(within < 8, parts[0], jnp.where(within < 16, parts[1], jnp.where(within < 24, parts[2], 0.0)))
+        high = value.astype(BF)
+        highs.append(high)
+        lows.append((value - high.astype(F32)).astype(BF))
+    table = spread_ref[...]
+    fixes = dot(jnp.concatenate(highs, axis=0), table) + dot(jnp.concatenate(lows, axis=0), table)
+    sums = []
+    for i in range(GROUPS):
+        value = sum_ref[:, 512 * i : 512 * i + 512] + fixes[i * ROWS : (i + 1) * ROWS]
+        if i == 0:
+            value = jnp.concatenate([value[:, 0:128] + first_fix[0], value[:, 128:256] + first_fix[1], value[:, 256:512]], axis=1)
+        if i == GROUPS - 1:
+            value = jnp.concatenate([value[:, 0:256], value[:, 256:384] + last_fix[0], value[:, 384:512] + last_fix[1]], axis=1)
+        sums.append(value.astype(BF))
+    dense = dot(jnp.concatenate(sums, axis=0), compact_ref[...]).astype(BF)
+    for i in range(GROUPS):
+        out_ref[:, i * FINE_IN : (i + 1) * FINE_IN] = dense[i * ROWS : (i + 1) * ROWS]
 
 
 def params(
-    after_ref, weight_ref, bias_ref, gain_ref, shift_ref, up_bias_ref, down_bias_ref, scale_ref, pool_weight_ref, spread_weight_ref,
+    tab_ref, weight_ref, bias_ref, gain_ref, shift_ref, up_bias_ref, down_bias_ref, scale_ref, pool_weight_ref, spread_weight_ref,
     taps_ref, conv_bias_ref, gains_ref, shifts_ref, up_biases_ref, down_biases_ref, scales_ref, pool_cells_ref, spread_cells_ref,
 ):
     for tap in range(49):
@@ -372,12 +427,9 @@
 
 def gather_rows(pieces, cat_ref):
     me = lax.axis_index("chan")
-    for k, parts in enumerate(pieces):
+    for k, piece in enumerate(pieces):
         first = pl.multiple_of(lax.bitwise_xor(me, k) * ROWS, 16)
-        for part in parts:
-            rows = part.shape[0]
-            cat_ref[pl.ds(first, rows), :] = part[...]
-            first = pl.multiple_of(first + rows, 16)
+        cat_ref[pl.ds(first, ROWS), :] = piece[...]
 
 
 def make_branch(level, cat_ref, gain_ref, shift_ref, up_ref, up_bias_ref, down_ref, down_bias_ref, block):
@@ -410,11 +462,11 @@
 
 def make_mix_fine(count):
     def mix_fine(
-        tab_ref, own_a_ref, own_b_ref, p1_a_ref, p1_b_ref, p2_a_ref, p2_b_ref, p3_a_ref, p3_b_ref, x_ref, mask_ref,
+        tab_ref, own_ref, p1_ref, p2_ref, p3_ref, x_ref, mask_ref,
         gain_ref, shift_ref, up_ref, up_bias_ref, down_ref, down_bias_ref, scale_ref, pool_cells_ref, pool_ref, pack_ref,
         fine_ref, pooled_ref, small_mask_ref, msg_ref, cat_ref, mains_ref, rest_ref,
     ):
-        gather_rows(((own_a_ref, own_b_ref), (p1_a_ref, p1_b_ref), (p2_a_ref, p2_b_ref), (p3_a_ref, p3_b_ref)), cat_ref)
+        gather_rows((own_ref, p1_ref, p2_ref, p3_ref), cat_ref)
         block = 768
         branch = make_branch(0, cat_ref, gain_ref, shift_ref, up_ref, up_bias_ref, down_ref, down_bias_ref, block)
         scale = wide(scale_ref[0], block)
@@ -472,7 +524,7 @@
     own_ref, p1_ref, p2_ref, p3_ref, pooled_ref, small_mask_ref, fine_ref, mask_ref, gain_ref, shift_ref, up_ref, up_bias_ref,
     down_ref, down_bias_ref, scale_ref, spread_cells_ref, pool_ref, out_ref, cat_ref,
 ):
-    gather_rows(((own_ref,), (p1_ref,), (p2_ref,), (p3_ref,)), cat_ref)
+    gather_rows((own_ref, p1_ref, p2_ref, p3_ref), cat_ref)
     cells = cat_ref.shape[1]
     branch = make_branch(1, cat_ref, gain_ref, shift_ref, up_ref, up_bias_ref, down_ref, down_bias_ref, cells)
     value = pooled_ref[...].astype(F32) + wide(scale_ref[1], cells) * branch(0)
@@ -544,33 +596,17 @@
         "halo": jnp.asarray(FINE["halo"]),
         "expand": jnp.asarray(FINE["expand"]),
         "compact": jnp.asarray(FINE["compact"]),
+        "spread": jnp.asarray(FINE["spread"]),
+        "fine_sides": jnp.asarray(FINE["sides"]),
         "small_halo": jnp.asarray(COARSE["halo"]),
         "sides": jnp.asarray(COARSE["sides"]),
         "pool": jnp.asarray(FINE["pool"]),
         "small_pack": jnp.asarray(COARSE["pack"]),
     }
     arrived = lax.all_to_all(messages, "tile", 0, 0, tiled=True)
-    convs = []
-    for first, rows in ((0, 32), (32, 16)):
-        own = pl.pallas_call(
-            make_conv_fine(first, rows),
-            in_specs=[SMEM] + [VMEM] * 7,
-            out_specs=VMEM,
-            out_shape=shaped(rows, cells),
-            scratch_shapes=[
-                pltpu.VMEM((rows, 3584), F32),
-                pltpu.VMEM((rows, 3584), F32),
-                pltpu.VMEM((49, rows, 128), F32),
-                pltpu.VMEM((rows, 3072), F32),
-            ],
-            compiler_params=PARAMS,
-            cost_estimate=takes(2),
-            name=f"conv_fine_{first}",
-        )(table, held["x"], arrived, held["halo"], held["expand"], held["compact"], held["weight"], held["bias"])
-        convs.append(every_channel(own))
     taps, conv_bias, gains, shifts, up_biases, down_biases, scales, pool_cells, spread_cells = pl.pallas_call(
         params,
-        in_specs=[VMEM] * 10,
+        in_specs=[SMEM] + [VMEM] * 9,
         out_specs=[VMEM] * 9,
         out_shape=[
             shaped(*shape, dtype=F32)
@@ -580,14 +616,31 @@
             )
         ],
         compiler_params=PARAMS,
+        cost_estimate=takes(1),
+        name="params",
+    )(table, depth_weight, depth_bias, norm_gain, norm_bias, up_bias, down_bias, layer_scale, pool_weight, spread_weight)
+    inner, fine_taps = pl.pallas_call(
+        lambda tab_ref, *refs: conv_inner(*refs),
+        in_specs=[SMEM] + [VMEM] * 4,
+        out_specs=[VMEM] * 2,
+        out_shape=[shaped(ROWS, 3072, dtype=F32), shaped(49, ROWS, 128, dtype=F32)],
+        scratch_shapes=[pltpu.VMEM((ROWS, 3584), F32), pltpu.VMEM((ROWS, 3584), F32)],
+        compiler_params=PARAMS,
+        cost_estimate=takes(4),
+        name="conv_inner",
+    )(table, held["x"], held["expand"], held["weight"], held["bias"])
+    conv = pl.pallas_call(
+        conv_border,
+        in_specs=[SMEM] + [VMEM] * 7,
+        out_specs=VMEM,
+        out_shape=shaped(ROWS, cells),
+        compiler_params=PARAMS,
         cost_estimate=takes(2),
-        name="params",
-    )(
-        convs[0][0], depth_weight, depth_bias, norm_gain, norm_bias, up_bias, down_bias, layer_scale, pool_weight, spread_weight
-    )
+        name="conv_border",
+    )(table, arrived, inner, fine_taps, held["halo"], held["fine_sides"], held["spread"], held["compact"])
     fine, pooled, small_mask, messages = pl.pallas_call(
         make_mix_fine(count),
-        in_specs=[SMEM] + [VMEM] * 20,
+        in_specs=[SMEM] + [VMEM] * 16,
         out_specs=[VMEM] * 4,
         out_shape=[shaped(ROWS, cells), shaped(ROWS, 768), shaped(48, 128, dtype=F32), shaped(count, 16, 512)],
         scratch_shapes=[
@@ -599,7 +652,7 @@
         cost_estimate=takes(4),
         name="mix_fine",
     )(
-        table, *(part for pair in zip(*convs) for part in pair), held["x"], held["mask"], gains, shifts, up_weight, up_biases,
+        table, *every_channel(conv), held["x"], held["mask"], gains, shifts, up_weight, up_biases,
         down_weight, down_biases, scales, pool_cells, held["pool"], held["small_pack"],
     )
     arrived = lax.all_to_all(messages, "tile", 0, 0, tiled=True)

time: 54.7 us -> 57.7 us (1.055)
  blocking collectives: 26.2 us -> 11.7 us
  starting transfers between devices: 3.86 us -> 10.4 us
  local copies, waits for them, and re-layouts: 1.45 us -> 7.73 us
  waiting for transfers between devices: 7.99 us -> 11.7 us
  Pallas kernels: 14.8 us -> 15.5 us
    all_to_all x2 -> x1, blocking collectives: 26.2 us -> 11.7 us  [per_device(): arrived = lax.all_to_all(messages, 'tile', 0, 0, tiled=True)]
    all_to_all x0 -> x1, starting transfers between devices: none -> 7.29 us  [per_device(): arrived = lax.all_to_all(messages, 'tile', 0, 0, tiled=True)]
    unnamed x47 -> x57, local copies, waits for them, and re-layouts: 1.45 us -> 7.73 us
    all_to_all x0 -> x1, waiting for transfers between devices: none -> 3.09 us  [per_device(): arrived = lax.all_to_all(messages, 'tile', 0, 0, tiled=True)]
    ppermute x3 -> x2, waiting for transfers between devices: 6.53 us -> 7.32 us  [every_channel(): across = lax.ppermute(own, 'chan', pairs(2))]
    pallas_call x4, Pallas kernels: 9.6 us -> 10.2 us  [the longest x1 3.83 us: per_device(): pl.pallas_call(make_mix_fine(count), in_specs=[SMEM] + [VMEM] * 16, out_s...]
    ppermute x3 -> x2, starting transfers between devices: 2.78 us -> 3.09 us  [every_channel(): across = lax.ppermute(own, 'chan', pairs(2))]
    ppermute x3 -> x2, waiting for transfers between devices: 1.45 us -> 1.26 us  [every_channel(): diagonal = lax.ppermute(across, 'chan', pairs(1))]
  transfers between devices with their start and end apart: 9 -> 7, of which waited for: 4 -> 4; matrix products, arithmetic and copies ran while one was open for 1% -> 3% of each run, Pallas kernels for 5% -> 8%
where the time goes in v4:
time: 57.7 us; the launch traced here: 57.3 us
  Pallas kernels  15.5 us (27%)
  waiting for transfers between devices  11.7 us (20%)
  blocking collectives  11.7 us (20%)
  starting transfers between devices  10.4 us (18%)
  local copies, waits for them, and re-layouts  7.73 us (13%)
    all_to_all x1, blocking collectives, per_device(): arrived = lax.all_to_all(messages, 'tile', 0, 0, tiled=True)  11.7 us
    unnamed x57, local copies, waits for them, and re-layouts  7.73 us
    ppermute x2, waiting for transfers between devices, every_channel(): across = lax.ppermute(own, 'chan', pairs(2))  7.32 us
    all_to_all x1, starting transfers between devices, per_device(): arrived = lax.all_to_all(messages, 'tile', 0, 0, tiled=True)  7.29 us
    pallas_call x1, Pallas kernels, per_device(): pl.pallas_call(make_mix_fine(count), in_specs=[SMEM] + [VMEM] * 16, out_s...  3.83 us
    pallas_call x1, Pallas kernels, per_device(): pl.pallas_call(lambda tab_ref, *refs: conv_inner(*refs), in_specs=[SMEM]...  3.38 us
    ppermute x2, starting transfers between devices, every_channel(): across = lax.ppermute(own, 'chan', pairs(2))  3.09 us
    all_to_all x1, waiting for transfers between devices, per_device(): arrived = lax.all_to_all(messages, 'tile', 0, 0, tiled=True)  3.09 us
  transfers between devices with their start and end apart: 7, of which 4 were waited for; matrix products, arithmetic and copies ran while one was open for 3% of the time, Pallas kernels for 8%

profile of v4, /device:TPU:0, one launch (start us, length us, event | category | flops | bytes accessed | tf_op | source)
XLA Modules:
  0.0 57.3 jit_solution(17768907373227288948)
XLA Ops:
  0.0 0.1 strip_table.1.pack_ref
  0.1 0.9 %copy-done.1 = bf16[1,48,2304]{2,1,0:T(8,128)(2,1)S(1)} copy-done((bf16[1,48,2304]{2,1,0:T(8,128)(2,1)S(1)}, bf16[1,48,2304]{2,1,0:T(8,128)(2,1)}, u32[]{:S(2)}) %copy-start.1) | copy-done | bytes 221208
  1.0 0.0 copy-start.15
  1.0 1.7 %prep.1 = (bf16[8,16,896]{2,1,0:T(8,128)(2,1)}, s32[24]{0:T(128)S(1)}) custom-call(s32[8]{0:T(128)S(1)} %copy-done.10, s32[8]{0:T(128)S(1)} %copy-done.11, bf16[1,48,2304]{2,1,0:T(8,128)(2,1)S(1)} %copy-done.1, bf16[384,256]{1,0:T(8,128)(2,1)S(1)} %strip_table.1.pack_ref), custom_call_target="tpu_custom_call" | custom-call | flops 10000000000 | tf_op jit(solution)/shard_map/prep/pallas_call | solution.py:576
  2.6 7.3 %all-to-all-start = ((bf16[8,16,896]{2,1,0:T(8,128)(2,1)}), bf16[8,16,896]{2,1,0:T(8,128)(2,1)S(1)}, u32[]{:S(2)}, u32[]{:S(2)}) async-start(bf16[8,16,896]{2,1,0:T(8,128)(2,1)} %get-tuple-element.23), calls=%async_computation | async-start | bytes 458752 | tf_op jit(solution)/shard_map/all_to_all | solution.py:606
  9.9 0.0 copy-start.12
  10.0 0.0 copy-start.19
  10.0 3.4 %conv_inner.1 = (f32[48,3072]{1,0:T(8,128)S(1)}, f32[49,48,128]{2,1,0:T(8,128)S(1)}) custom-call(s32[24]{0:T(128)S(1)} %get-tuple-element.22.tab_ref, bf16[1,48,2304]{2,1,0:T(8,128)(2,1)S(1)} %copy-done.1, bf16[384,512]{1,0:T(8,128)(2,1)S(1)} %copy-done.15, f32[2,48,49]{2,1,0:T(8,128)S(1)} %copy-done.2, f32[2,48]{1,0:T(2,128)S(1)} %copy-done.8), custom_call_target="tpu_custom_call" | custom-call | flops 4000000000 | tf_op jit(solution)/shard_map/conv_inner/pallas_call | solution.py:622
  13.4 1.0 %copy-done.21 = f32[49,48,128]{2,1,0:T(8,128)} copy-done((f32[49,48,128]{2,1,0:T(8,128)}, f32[49,48,128]{2,1,0:T(8,128)S(1)}, u32[]{:S(2)}) %copy-start.21) | copy-done | bytes 1204248
  14.4 0.8 %copy-done.23 = f32[48,3072]{1,0:T(8,128)} copy-done((f32[48,3072]{1,0:T(8,128)}, f32[48,3072]{1,0:T(8,128)S(1)}, u32[]{:S(2)}) %copy-start.23) | copy-done | bytes 589848
  15.3 3.1 %all-to-all-done.recv_ref = bf16[8,16,896]{2,1,0:T(8,128)(2,1)S(1)} async-done(((bf16[8,16,896]{2,1,0:T(8,128)(2,1)}), bf16[8,16,896]{2,1,0:T(8,128)(2,1)S(1)}, u32[]{:S(2)}, u32[]{:S(2)}) %all-to-all-start) | async-done | bytes 229408 | tf_op jit(solution)/shard_map/all_to_all | solution.py:606
  18.4 0.0 copy-start.17
  18.4 1.0 %copy-done.17 = bf16[512,384]{1,0:T(8,128)(2,1)S(1)} copy-done((bf16[512,384]{1,0:T(8,128)(2,1)S(1)}, bf16[512,384]{1,0:T(8,128)(2,1)}, u32[]{:S(2)}) %copy-start.17) | copy-done | bytes 393240
  19.4 1.3 %copy-done.22 = f32[49,48,128]{2,1,0:T(8,128)S(1)} copy-done((f32[49,48,128]{2,1,0:T(8,128)S(1)}, f32[49,48,128]{2,1,0:T(8,128)}, u32[]{:S(2)}) %copy-start.22) | copy-done | bytes 1204248
  20.6 1.1 %copy-done.24 = f32[48,3072]{1,0:T(8,128)S(1)} copy-done((f32[48,3072]{1,0:T(8,128)S(1)}, f32[48,3072]{1,0:T(8,128)}, u32[]{:S(2)}) %copy-start.24) | copy-done | bytes 589848
  21.7 1.7 %conv_border.1.own_ref = bf16[48,2304]{1,0:T(8,128)(2,1)S(1)} custom-call(s32[24]{0:T(128)S(1)} %get-tuple-element.22.tab_ref, bf16[8,16,896]{2,1,0:T(8,128)(2,1)S(1)} %all-to-all-done.recv_ref, f32[48,3072]{1,0:T(8,128)S(1)} %copy-done.24, f32[49,48,128]{2,1,0:T(8,128)S(1)} %copy-done.22, bf16[3,768,256]{2,1,0:T(8,128)(2,1)S(1)} %copy-done.12, ...), custom_call_target="tpu_custom_call" | custom-call | flops 2000000000 | tf_op jit(solution)/shard_map/conv_border/pallas_call | solution.py:632
  23.5 1.5 %collective-permute-start.1 = (bf16[48,2304]{1,0:T(8,128)(2,1)S(1)}, bf16[48,2304]{1,0:T(8,128)(2,1)S(1)}, u32[]{:S(2)}, u32[]{:S(2)}) collective-permute-start(bf16[48,2304]{1,0:T(8,128)(2,1)S(1)} %conv_border.1.own_ref), channel_id=1, source_target_pairs={{0,2},{1,3},{2,0},{3,1},{4,6},{5,7},{6,4},{7,5},{8,10},{9,11},{10,... | collective-permute-start | bytes 663560 | tf_op jit(solution)/shard_map/ppermute | solution.py:560
  25.0 4.5 %collective-permute-done.1.p2_ref = bf16[48,2304]{1,0:T(8,128)(2,1)S(1)} collective-permute-done((bf16[48,2304]{1,0:T(8,128)(2,1)S(1)}, bf16[48,2304]{1,0:T(8,128)(2,1)S(1)}, u32[]{:S(2)}, u32[]{:S(2)}) %collective-permute-start.1) | collective-permute-done | bytes 221216 | tf_op jit(solution)/shard_map/ppermute | solution.py:560
  29.5 0.1 copy.25.pool_weight_ref
  29.6 0.1 copy.26.spread_weight_ref
  29.7 1.3 %copy.27.up_ref = bf16[2,768,192]{2,1,0:T(8,128)(2,1)S(1)} copy(bf16[2,768,192]{1,2,0:T(8,128)(2,1)} %param.32) | data formatting | bytes 1179648 | tf_op args[8]
  31.1 0.0 copy-start.13
  31.1 0.0 copy-start.20
  31.1 1.3 %params.1 = (f32[49,48,128]{2,1,0:T(8,128)S(1)}, f32[48,128]{1,0:T(8,128)S(1)}, f32[2,192,128]{2,1,0:T(8,128)S(1)}, f32[2,192,128]{2,1,0:T(8,128)S(1)}, f32[2,76...) custom-call(s32[24]{0:T(128)S(1)} %get-tuple-element.22.tab_ref, ...), custom_call_target="tpu_custom_call" | custom-call | flops 1000000000 | tf_op jit(solution)/shard_map/params/pallas_call | solution.py:607
  32.5 0.0 copy-start.14
  32.5 3.8 %mix_fine.1 = (bf16[48,2304]{1,0:T(8,128)(2,1)S(1)}, bf16[48,768]{1,0:T(8,128)(2,1)S(1)}, f32[48,128]{1,0:T(8,128)S(1)}, bf16[8,16,512]{2,1,0:T(8,128)(2,1)S(1)}) custom-call(s32[24]{0:T(128)S(1)} %get-tuple-element.22.tab_ref, bf16[48,2304]{1,0:T(8,128)(2,1)S(1)} %conv_border.1.own_ref, bf16[48,2304]{1,0:T(8,128)(2,1)S(1)} %collective-permute-done.p1_ref, ...), custom_call_target="tpu_custom_call" | custom-call | flops 4000000000 | tf_op jit(solution)/shard_map/mix_fine/pallas_call | solution.py:641
  36.3 11.7 %all_to_all.10.recv_ref = bf16[8,16,512]{2,1,0:T(8,128)(2,1)S(1)} all-to-all(bf16[8,16,512]{2,1,0:T(8,128)(2,1)S(1)} %get-tuple-element.33), channel_id=1, replica_groups=mesh['tile'=8,'chan'=4] {'tile'}, dimensions={0} | all-to-all | bytes 262144 | tf_op jit(solution)/shard_map/all_to_all | solution.py:658
  48.0 1.8 %conv_coarse.1.own_ref = bf16[48,768]{1,0:T(8,128)(2,1)S(1)} custom-call(s32[24]{0:T(128)S(1)} %get-tuple-element.22.tab_ref, bf16[48,768]{1,0:T(8,128)(2,1)S(1)} %get-tuple-element.32.x_ref.pooled_ref, bf16[8,16,512]{2,1,0:T(8,128)(2,1)S(1)} %all_to_all.10.recv_ref, bf16[3,384,128]{2,1,0:T(8,128)(2,1)S(1)} %copy-done.18, bf16[256,768]{1,0:T(8,128)(2,1)S(1)} %copy-done.14, ...), custom_call_target="tpu_custom_call" | custom-call | flops 2000000000 | tf_op jit(solution)/shard_map/conv_coarse/pallas_call | solution.py:659
  49.8 1.6 %collective-permute-start.4 = (bf16[48,768]{1,0:T(8,128)(2,1)S(1)}, bf16[48,768]{1,0:T(8,128)(2,1)S(1)}, u32[]{:S(2)}, u32[]{:S(2)}) collective-permute-start(bf16[48,768]{1,0:T(8,128)(2,1)S(1)} %conv_coarse.1.own_ref), channel_id=1, source_target_pairs={{0,2},{1,3},{2,0},{3,1},{4,6},{5,7},{6,4},{7,5},{8,10},{9,11},{10,... | collective-permute-start | bytes 221192 | tf_op jit(solution)/shard_map/ppermute | solution.py:560
  51.4 2.9 %collective-permute-done.4.p2_ref = bf16[48,768]{1,0:T(8,128)(2,1)S(1)} collective-permute-done((bf16[48,768]{1,0:T(8,128)(2,1)S(1)}, bf16[48,768]{1,0:T(8,128)(2,1)S(1)}, u32[]{:S(2)}, u32[]{:S(2)}) %collective-permute-start.4) | collective-permute-done | bytes 73760 | tf_op jit(solution)/shard_map/ppermute | solution.py:560
  54.2 1.3 %collective-permute-done.5.p3_ref = bf16[48,768]{1,0:T(8,128)(2,1)S(1)} collective-permute-done((bf16[48,768]{1,0:T(8,128)(2,1)S(1)}, bf16[48,768]{1,0:T(8,128)(2,1)S(1)}, u32[]{:S(2)}, u32[]{:S(2)}) %collective-permute-start.5) | collective-permute-done | bytes 73760 | tf_op jit(solution)/shard_map/ppermute | solution.py:562
  55.5 1.8 %mix_coarse.1 = bf16[1,48,2304]{2,1,0:T(8,128)(2,1)} custom-call(bf16[48,768]{1,0:T(8,128)(2,1)S(1)} %conv_coarse.1.own_ref, bf16[48,768]{1,0:T(8,128)(2,1)S(1)} %collective-permute-done.3.p1_ref, bf16[48,768]{1,0:T(8,128)(2,1)S(1)} %collective-permute-done.4.p2_ref, bf16[48,768]{1,0:T(8,128)(2,1)S(1)} %collective-permute-done.5.p3_ref, ...), custom_call_target="tpu_custom_call" | custom-call | flops 2000000000 | tf_op jit(solution)/shard_map/mix_coarse/pallas_call | solution.py:669
  (48 shorter events, 0.1 us)
Async XLA Ops:
  0.0 0.9 %copy-start.11 = (s32[8]{0:T(128)S(1)}, s32[8]{0:T(128)}, u32[]{:S(2)}) copy-start(s32[8]{0:T(128)} %dev_ref.1) | copy-start | bytes 100
  0.0 0.9 %copy-start.10 = (s32[8]{0:T(128)S(1)}, s32[8]{0:T(128)}, u32[]{:S(2)}) copy-start(s32[8]{0:T(128)} %slots_ref.1) | copy-start | bytes 100
  0.9 9.0 %copy-start.2 = (f32[2,48,49]{2,1,0:T(8,128)S(1)}, f32[2,48,49]{2,1,0:T(8,128)}, u32[]{:S(2)}) copy-start(f32[2,48,49]{2,1,0:T(8,128)} %weight_ref.1) | copy-start | bytes 56452
  0.9 9.0 %copy-start.8 = (f32[2,48]{1,0:T(2,128)S(1)}, f32[2,48]{1,0:T(2,128)}, u32[]{:S(2)}) copy-start(f32[2,48]{1,0:T(2,128)} %bias_ref.1) | copy-start | bytes 1156
  1.0 9.0 %copy-start.15 = (bf16[384,512]{1,0:T(8,128)(2,1)S(1)}, bf16[384,512]{1,0:T(8,128)(2,1)}, u32[]{:S(2)}) copy-start(bf16[384,512]{1,0:T(8,128)(2,1)} %constant.19.clone.refs_1_) | copy-start | bytes 1179652
  2.6 15.7 %all-to-all-start = ((bf16[8,16,896]{2,1,0:T(8,128)(2,1)}), bf16[8,16,896]{2,1,0:T(8,128)(2,1)S(1)}, u32[]{:S(2)}, u32[]{:S(2)}) async-start(bf16[8,16,896]{2,1,0:T(8,128)(2,1)} %get-tuple-element.23), calls=%async_computation | async-start | bytes 458752 | tf_op jit(solution)/shard_map/all_to_all | solution.py:606
  9.9 8.4 %copy-start.12 = (bf16[3,768,256]{2,1,0:T(8,128)(2,1)S(1)}, bf16[3,768,256]{2,1,0:T(8,128)(2,1)}, u32[]{:S(2)}) copy-start(bf16[3,768,256]{2,1,0:T(8,128)(2,1)} %constant.18.clone.halo_ref) | copy-start | bytes 3538948
  10.0 8.4 %copy-start.16 = (bf16[512,384]{1,0:T(8,128)(2,1)S(1)}, bf16[512,384]{1,0:T(8,128)(2,1)}, u32[]{:S(2)}) copy-start(bf16[512,384]{1,0:T(8,128)(2,1)} %constant.22.clone.sides_ref) | copy-start | bytes 1179652
  10.0 8.4 %copy-start.19 = (bf16[128,512]{1,0:T(8,128)(2,1)S(1)}, bf16[128,512]{1,0:T(8,128)(2,1)}, u32[]{:S(2)}) copy-start(bf16[128,512]{1,0:T(8,128)(2,1)} %constant.21.clone.spread_ref) | copy-start | bytes 393220
  13.4 1.1 %copy-start.21 = (f32[49,48,128]{2,1,0:T(8,128)}, f32[49,48,128]{2,1,0:T(8,128)S(1)}, u32[]{:S(2)}) copy-start(f32[49,48,128]{2,1,0:T(8,128)S(1)} %get-tuple-element.25.wide_ref) | copy-start | bytes 3612676
  18.4 1.0 %copy-start.17 = (bf16[512,384]{1,0:T(8,128)(2,1)S(1)}, bf16[512,384]{1,0:T(8,128)(2,1)}, u32[]{:S(2)}) copy-start(bf16[512,384]{1,0:T(8,128)(2,1)} %constant.20.clone.compact_ref) | copy-start | bytes 1179652
  19.4 1.3 %copy-start.22 = (f32[49,48,128]{2,1,0:T(8,128)S(1)}, f32[49,48,128]{2,1,0:T(8,128)}, u32[]{:S(2)}) copy-start(f32[49,48,128]{2,1,0:T(8,128)} %copy-done.21) | copy-start | bytes 3612676
  20.6 1.1 %copy-start.24 = (f32[48,3072]{1,0:T(8,128)S(1)}, f32[48,3072]{1,0:T(8,128)}, u32[]{:S(2)}) copy-start(f32[48,3072]{1,0:T(8,128)} %copy-done.23) | copy-start | bytes 1769476
  21.7 7.8 %copy-start.25 = (f32[48,4]{0,1:T(4,128)S(1)}, f32[48,4]{0,1:T(4,128)}, u32[]{:S(2)}) copy-start(f32[48,4]{0,1:T(4,128)} %param.37) | copy-start | bytes 2308
  21.7 7.8 %copy-start.26 = (f32[48,4]{0,1:T(4,128)S(1)}, f32[48,4]{0,1:T(4,128)}, u32[]{:S(2)}) copy-start(f32[48,4]{0,1:T(4,128)} %param.38) | copy-start | bytes 2308
  23.4 7.6 %copy-start.4 = (f32[2,768]{1,0:T(2,128)S(1)}, f32[2,768]{1,0:T(2,128)}, u32[]{:S(2)}) copy-start(f32[2,768]{1,0:T(2,128)} %up_bias_ref.1) | copy-start | bytes 18436
  23.4 7.6 %copy-start.5 = (f32[2,192]{1,0:T(2,128)S(1)}, f32[2,192]{1,0:T(2,128)}, u32[]{:S(2)}) copy-start(f32[2,192]{1,0:T(2,128)} %gain_ref.1) | copy-start | bytes 4612
  23.4 7.6 %copy-start.6 = (f32[2,192]{1,0:T(2,128)S(1)}, f32[2,192]{1,0:T(2,128)}, u32[]{:S(2)}) copy-start(f32[2,192]{1,0:T(2,128)} %shift_ref.1) | copy-start | bytes 4612
  23.4 7.6 %copy-start.7 = (f32[2,192]{1,0:T(2,128)S(1)}, f32[2,192]{1,0:T(2,128)}, u32[]{:S(2)}) copy-start(f32[2,192]{1,0:T(2,128)} %down_bias_ref.1) | copy-start | bytes 4612
  23.5 7.6 %copy-start.9 = (f32[2,48]{1,0:T(2,128)S(1)}, f32[2,48]{1,0:T(2,128)}, u32[]{:S(2)}) copy-start(f32[2,48]{1,0:T(2,128)} %scale_ref.1) | copy-start | bytes 1156
  23.5 6.0 %collective-permute-start.1 = (bf16[48,2304]{1,0:T(8,128)(2,1)S(1)}, bf16[48,2304]{1,0:T(8,128)(2,1)S(1)}, u32[]{:S(2)}, u32[]{:S(2)}) collective-permute-start(bf16[48,2304]{1,0:T(8,128)(2,1)S(1)} %conv_border.1.own_ref), channel_id=1, source_target_pairs={{0,2},{1,3},{2,0},{3,1},{4,6},{5,7},{6,4},{7,5},{8,10},{9,11},{10,... | collective-permute-start | bytes 663560 | tf_op jit(solution)/shard_map/ppermute | solution.py:560
  25.0 7.4 %collective-permute-start = (bf16[48,2304]{1,0:T(8,128)(2,1)S(1)}, bf16[48,2304]{1,0:T(8,128)(2,1)S(1)}, u32[]{:S(2)}, u32[]{:S(2)}) collective-permute-start(bf16[48,2304]{1,0:T(8,128)(2,1)S(1)} %conv_border.1.own_ref), channel_id=1, source_target_pairs={{0,1},{1,0},{2,3},{3,2},{4,5},{5,4},{6,7},{7,6},{8,9},{9,8},{10,11... | collective-permute-start | bytes 663560 | tf_op jit(solution)/shard_map/ppermute | solution.py:561
  29.5 3.0 %collective-permute-start.2 = (bf16[48,2304]{1,0:T(8,128)(2,1)S(1)}, bf16[48,2304]{1,0:T(8,128)(2,1)S(1)}, u32[]{:S(2)}, u32[]{:S(2)}) collective-permute-start(bf16[48,2304]{1,0:T(8,128)(2,1)S(1)} %collective-permute-done.1.p2_ref), channel_id=1, source_target_pairs={{0,1},{1,0},{2,3},{3,2},{4,5},{5,4},{6,7},{7,6},{8,9},{9,8},{10,11... | collective-permute-start | bytes 663560 | tf_op jit(solution)/shard_map/ppermute | solution.py:562
  31.0 1.4 %copy-start = (bf16[2,192,768]{2,1,0:T(8,128)(2,1)S(1)}, bf16[2,192,768]{2,1,0:T(8,128)(2,1)}, u32[]{:S(2)}) copy-start(bf16[2,192,768]{2,1,0:T(8,128)(2,1)} %down_ref.3) | copy-start | bytes 1769476
  31.1 1.4 %copy-start.3 = (s32[1,2304]{1,0:T(1,128)S(1)}, s32[1,2304]{1,0:T(1,128)}, u32[]{:S(2)}) copy-start(s32[1,2304]{1,0:T(1,128)} %mask_ref.3) | copy-start | bytes 27652
  31.1 1.4 %copy-start.13 = (bf16[768,384]{1,0:T(8,128)(2,1)S(1)}, bf16[768,384]{1,0:T(8,128)(2,1)}, u32[]{:S(2)}) copy-start(bf16[768,384]{1,0:T(8,128)(2,1)} %constant.26.clone.pack_ref) | copy-start | bytes 1769476
  31.1 1.4 %copy-start.20 = (bf16[384,128]{1,0:T(8,128)(2,1)S(1)}, bf16[384,128]{1,0:T(8,128)(2,1)}, u32[]{:S(2)}) copy-start(bf16[384,128]{1,0:T(8,128)(2,1)} %constant.25.clone.pool_ref) | copy-start | bytes 294916
  32.5 15.6 %copy-start.14 = (bf16[256,768]{1,0:T(8,128)(2,1)S(1)}, bf16[256,768]{1,0:T(8,128)(2,1)}, u32[]{:S(2)}) copy-start(bf16[256,768]{1,0:T(8,128)(2,1)} %constant.24.clone.sides_ref) | copy-start | bytes 1179652
  32.5 15.6 %copy-start.18 = (bf16[3,384,128]{2,1,0:T(8,128)(2,1)S(1)}, bf16[3,384,128]{2,1,0:T(8,128)(2,1)}, u32[]{:S(2)}) copy-start(bf16[3,384,128]{2,1,0:T(8,128)(2,1)} %constant.23.clone.halo_ref) | copy-start | bytes 884740
  49.8 4.4 %collective-permute-start.4 = (bf16[48,768]{1,0:T(8,128)(2,1)S(1)}, bf16[48,768]{1,0:T(8,128)(2,1)S(1)}, u32[]{:S(2)}, u32[]{:S(2)}) collective-permute-start(bf16[48,768]{1,0:T(8,128)(2,1)S(1)} %conv_coarse.1.own_ref), channel_id=1, source_target_pairs={{0,2},{1,3},{2,0},{3,1},{4,6},{5,7},{6,4},{7,5},{8,10},{9,11},{10,... | collective-permute-start | bytes 221192 | tf_op jit(solution)/shard_map/ppermute | solution.py:560
  51.4 2.9 %collective-permute-start.3 = (bf16[48,768]{1,0:T(8,128)(2,1)S(1)}, bf16[48,768]{1,0:T(8,128)(2,1)S(1)}, u32[]{:S(2)}, u32[]{:S(2)}) collective-permute-start(bf16[48,768]{1,0:T(8,128)(2,1)S(1)} %conv_coarse.1.own_ref), channel_id=1, source_target_pairs={{0,1},{1,0},{2,3},{3,2},{4,5},{5,4},{6,7},{7,6},{8,9},{9,8},{10,11... | collective-permute-start | bytes 221192 | tf_op jit(solution)/shard_map/ppermute | solution.py:561
  54.2 1.3 %collective-permute-start.5 = (bf16[48,768]{1,0:T(8,128)(2,1)S(1)}, bf16[48,768]{1,0:T(8,128)(2,1)S(1)}, u32[]{:S(2)}, u32[]{:S(2)}) collective-permute-start(bf16[48,768]{1,0:T(8,128)(2,1)S(1)} %collective-permute-done.4.p2_ref), channel_id=1, source_target_pairs={{0,1},{1,0},{2,3},{3,2},{4,5},{5,4},{6,7},{7,6},{8,9},{9,8},{10,11... | collective-permute-start | bytes 221192 | tf_op jit(solution)/shard_map/ppermute | solution.py:562
  (2 other events, 1.8 us)

commit v5 on v4

--- a/solution.py
+++ b/solution.py
@@ -49,38 +49,9 @@
     return pairs
 
 
-def fine_tables():
-    first = [(t, t) for t in range(128)] + [(128 + t, 128 + t) for t in range(16)]
-    last = [(t, 16 + t) for t in range(128)] + [(128 + t, t) for t in range(16)]
-    halo = np.stack(
-        [
-            one_hot((768, 256), halo_pairs(last, TILE, 64, 1, False)),
-            one_hot((768, 256), halo_pairs(first, TILE, 64, 0, False)),
-            one_hot((768, 256), halo_pairs(last, TILE, 64, 0, True)),
-        ]
-    )
-    expand, compact, pool, spread, sides = [], [], [], [], []
-    for row in range(8):
-        for col in range(48):
-            expand.append((row * 48 + col, row * 64 + 3 + col))
-            compact.append((row * 64 + 3 + col, row * 48 + col))
-            pool.append((row * 48 + col, (row // 2) * 32 + 3 + col // 2))
-        for q in range(3):
-            spread.append((8 * q + row, row * 64 + 3 + q))
-            spread.append((64 + 8 * q + row, row * 64 + 3 + 47 - q))
-    for row in range(TILE):
-        for j in range(3):
-            lane = 3 * row + j if row < 40 else 128 + 16 + 3 * (row - 40) + j
-            sides.append((lane, 128 * j + row))
-            sides.append((256 + lane, 128 * (2 - j) + 64 + row))
-    return {
-        "halo": halo,
-        "expand": one_hot((384, 512), expand),
-        "compact": one_hot((512, 384), compact),
-        "pool": one_hot((384, 128), pool),
-        "spread": one_hot((128, 512), spread),
-        "sides": one_hot((512, 384), sides),
-    }
+def pool_table():
+    pairs = [(row * 48 + col, (row // 2) * 32 + 3 + col // 2) for row in range(8) for col in range(48)]
+    return one_hot((384, 128), pairs)
 
 
 def coarse_tables():
@@ -112,7 +83,7 @@
     }
 
 
-FINE = fine_tables()
+POOL = pool_table()
 COARSE = coarse_tables()
 
 
@@ -242,16 +213,36 @@
     return pltpu.roll(value, value.shape[1] - lanes, 1)
 
 
-def conv_inner(x_ref, expand_ref, weight_ref, bias_ref, sum_ref, wide_ref, pad_ref, odd_ref):
+def tall(row_block):
+    return jnp.concatenate([row_block] * (ROWS // 8), axis=0)
+
+
+def lanes_from(value, index):
+    return jnp.take_along_axis(value, index, axis=1)
+
+
+def conv_inner(x_ref, weight_ref, bias_ref, sum_ref, pad_ref, odd_ref, wide_ref, total_ref):
     for tap in range(49):
         wide_ref[tap] = jnp.broadcast_to(weight_ref[0, :, tap : tap + 1], (ROWS, 128))
     pad_ref[:, 0:256] = jnp.zeros((ROWS, 256), F32)
     pad_ref[:, 3328:3584] = jnp.zeros((ROWS, 256), F32)
-    padded = dot(stacked(x_ref[0], FINE_IN), expand_ref[...])
+    lane = lane_ids((8, 128))
+    half, within = lane // 64, lane % 64
+    valid = tall((within >= 3) & (within < 51))
+    col = jnp.clip(within - 3, 0, 47)
+    cells = [96 * k + 48 * half + col for k in range(4)]
+    indices = [tall(cell % 128) for cell in cells]
     for i in range(GROUPS):
-        pad_ref[:, 256 + 512 * i : 768 + 512 * i] = padded[i * ROWS : (i + 1) * ROWS]
+        tiles = [x_ref[0, :, 384 * i + 128 * m : 384 * i + 128 * m + 128].astype(F32) for m in range(3)]
+        for k in range(4):
+            first, final = (96 * k) // 128, (96 * k + 95) // 128
+            value = lanes_from(tiles[first], indices[k])
+            if final != first:
+                value = jnp.where(tall(cells[k] < 128 * final), value, lanes_from(tiles[final], indices[k]))
+            start = 256 + 512 * i + 128 * k
+            pad_ref[:, start : start + 128] = jnp.where(valid, value, 0.0)
     odd_ref[...] = lane_shifted(pad_ref[...], 64)
-    sum_ref[...] = wide(columns(bias_ref[0:1, :]), 3072)
+    total_ref[...] = wide(columns(bias_ref[0:1, :]), 3072)
 
     def group(g, carry):
         here = pl.ds(pl.multiple_of(g * 8, 8), 8)
@@ -262,7 +253,7 @@
                 ref = odd_ref if a % 2 else pad_ref
                 start = base + (a // 2) * 128
                 taken.append([ref[here, start + 128 * j : start + 128 * j + 128] for j in range(4)])
-            total = [sum_ref[here, base + 128 * j : base + 128 * j + 128] for j in range(4)]
+            total = [total_ref[here, base + 128 * j : base + 128 * j + 128] for j in range(4)]
             for b in range(7):
                 weights = [wide_ref[a * 7 + b, here, :] for a in range(7)]
                 for j in range(4):
@@ -271,87 +262,116 @@
                         partial = partial + weights[a] * taken[a][j]
                     total[j] = total[j] + (pltpu.roll(partial, (3 - b) % 128, 1) if b != 3 else partial)
             for j in range(4):
-                sum_ref[here, base + 128 * j : base + 128 * j + 128] = total[j]
+                total_ref[here, base + 128 * j : base + 128 * j + 128] = total[j]
         return carry
 
     lax.fori_loop(0, ROWS // 8, group, 0)
-
-
-def conv_border(tab_ref, recv_ref, sum_ref, wide_ref, halo_ref, sides_ref, spread_ref, compact_ref, out_ref):
-    lane = lane_ids((ROWS, 128))
-    low_half = lane < 64
-
-    def rest_of(source, scale):
+    cells = [128 * m + lane for m in range(3)]
+    indices = [tall((cell // 48) % 2 * 64 + 3 + cell % 48) for cell in cells]
+    for i in range(GROUPS):
+        tiles = [total_ref[:, 512 * i + 128 * k : 512 * i + 128 * k + 128] for k in range(4)]
+        for m in range(3):
+            value = jnp.where(
+                tall(cells[m] < 96 * (m + 1)), lanes_from(tiles[m], indices[m]), lanes_from(tiles[m + 1], indices[m])
+            )
+            sum_ref[:, 384 * i + 128 * m : 384 * i + 128 * m + 128] = value
+
+
+def conv_border(tab_ref, recv_ref, sum_ref, weight_ref, out_ref, taps_ref):
+    lane = lane_ids((8, 128))
+    half, within = lane // 64, lane % 64
+    low_half = tall(lane < 64)
+    taps_ref[...] = jnp.zeros((ROWS, 128), F32)
+    taps_ref[:, 0:49] = weight_ref[0]
+    taps = taps_ref[...]
+
+    def band_cells(band, offset):
+        source, scale = band_source(tab_ref, band)
+        main = jnp.concatenate([recv_ref[source, :, 256 * g + offset : 256 * g + offset + 128] for g in range(3)], axis=0)
         rest = recv_ref[source, :, 768:896].astype(F32) * scale
-        return jnp.concatenate([rest, pltpu.roll(rest, 128 - 40, 1), pltpu.roll(rest, 128 - 80, 1)], axis=0)
-
-    def strips(bands, offset):
-        pieces = []
-        for band in bands:
-            source, scale = band_source(tab_ref, band)
-            main = jnp.concatenate([recv_ref[source, :, 256 * g + offset : 256 * g + offset + 128] for g in range(3)], axis=0)
-            pieces += [(main.astype(F32) * scale).astype(BF), rest_of(source, scale).astype(BF)]
-        return jnp.concatenate(pieces, axis=1)
-
-    def tap(a, b):
-        return wide_ref[a * 7 + b]
+        rest = jnp.concatenate([rest, pltpu.roll(rest, 128 - 40, 1), pltpu.roll(rest, 128 - 80, 1)], axis=0)
+        return main.astype(F32) * scale, rest
+
+    def halo_rows(bands, folded, last):
+        left, middle, right = [band_cells(band, 0) for band in bands]
+        tiles = []
+        for first_row in (0, 2):
+            row = first_row + half
+            col = jnp.where(within < 3, 45 + within, jnp.where(within < 51, within - 3, within - 51))
+            index = row * 48 + col
+            index = jnp.where(folded, 143 - index, index)
+            in_main = index - jnp.where(last, 16, 0)
+            rest = (in_main < 0) | (in_main > 127)
+            in_rest = jnp.where(in_main < 0, in_main + 16, in_main - 128)
+            main_index, rest_index = tall(in_main & 127), tall(in_rest & 127)
+            picked = [jnp.where(tall(rest), lanes_from(r, rest_index), lanes_from(m, main_index)) for m, r in (left, middle, right)]
+            value = jnp.where(tall(within < 3), picked[0], jnp.where(tall(within < 51), picked[1], picked[2]))
+            tiles.append(jnp.where(tall((within < 54) & (row < 3)), value, 0.0))
+        return tiles
 
     def row_fix(uses):
         total = [jnp.zeros((ROWS, 128), F32)] * 2
         for b in range(7):
             partial = [None, None]
+            weights = {}
             for place, a, cells in uses:
-                term = tap(a, b) * cells
+                if a not in weights:
+                    weights[a] = jnp.broadcast_to(taps[:, a * 7 + b : a * 7 + b + 1], (ROWS, 128))
+                term = weights[a] * cells
                 partial[place] = term if partial[place] is None else partial[place] + term
             for place in range(2):
                 total[place] = total[place] + (pltpu.roll(partial[place], (3 - b) % 128, 1) if b != 3 else partial[place])
         return total
 
-    below = dot(strips((0, 1, 2), 0), halo_ref[0])
-    above = dot(strips((5, 6, 7), 0), halo_ref[tab_ref[8]])
-    turned = [pltpu.roll(below[:, 128 * k : 128 * k + 128], 64, 1) for k in range(2)]
-    last = jnp.where(low_half, turned[1], 0.0)
-    first_fix = row_fix(((0, 0, jnp.where(low_half, turned[0], turned[1])), (0, 1, below[:, 128:256]), (0, 2, last), (1, 0, last)))
-    turned = [pltpu.roll(above[:, 128 * k : 128 * k + 128], 64, 1) for k in range(2)]
-    first = jnp.where(low_half, 0.0, turned[0])
-    last_fix = row_fix(((0, 6, first), (1, 4, first), (1, 5, above[:, 0:128]), (1, 6, jnp.where(low_half, turned[0], turned[1]))))
-
-    beside = dot(strips((3, 4), 128), sides_ref[...])
-    beside = [beside[:, 128 * j : 128 * j + 128] for j in range(3)]
-    column_fix = [jnp.zeros((ROWS, 128), F32)] * 3
+    def joined(first, second):
+        return jnp.where(low_half, pltpu.roll(first, 64, 1), pltpu.roll(second, 64, 1))
+
+    zeros = jnp.zeros((ROWS, 128), F32)
+    below = halo_rows((0, 1, 2), False, True)
+    first_fix = row_fix(((0, 0, below[0]), (0, 1, joined(below[0], below[1])), (0, 2, below[1]), (1, 0, below[1])))
+    folded = tab_ref[8] == 2
+    above = halo_rows((5, 6, 7), folded, folded)
+    edge = joined(zeros, above[0])
+    last_fix = row_fix(((0, 6, edge), (1, 4, edge), (1, 5, above[0]), (1, 6, joined(above[0], above[1]))))
+
+    left, right = band_cells(3, 128), band_cells(4, 128)
+    beside = []
+    for j in range(3):
+        which = jnp.where(half == 0, j, 2 - j)
+        in_main = jnp.minimum(3 * within + which, 127)
+        main_index, rest_index = tall(in_main), tall(jnp.clip(3 * (within - 40) + 16 + which, 0, 127))
+        picked = [
+            jnp.where(tall(within < 40), lanes_from(main, main_index), lanes_from(rest, rest_index)) for main, rest in (left, right)
+        ]
+        beside.append(jnp.where(tall(within < 48), jnp.where(low_half, picked[0], picked[1]), 0.0))
+    column_fix = [zeros] * 3
     for a in range(7):
-        weights = [jnp.where(low_half, tap(a, b), tap(a, 6 - b)) for b in range(3)]
+        weights = [lanes_from(taps, tall(jnp.where(half == 0, a * 7 + b, a * 7 + 6 - b))) for b in range(3)]
         for q in range(3):
             partial = weights[0] * beside[q]
             for j in range(q + 1, 3):
                 partial = partial + weights[j - q] * beside[j]
             column_fix[q] = column_fix[q] + (pltpu.roll(partial, (3 - a) % 128, 1) if a != 3 else partial)
-    within = lane % 64
-    highs, lows = [], []
-    for i in range(GROUPS):
-        parts = [pltpu.roll(column_fix[q], (8 * q - 8 * i) % 128, 1) if q != i else column_fix[q] for q in range(3)]
-        value = jnp.where(within < 8, parts[0], jnp.where(within < 16, parts[1], jnp.where(within < 24, parts[2], 0.0)))
-        high = value.astype(BF)
-        highs.append(high)
-        lows.append((value - high.astype(F32)).astype(BF))
-    table = spread_ref[...]
-    fixes = dot(jnp.concatenate(highs, axis=0), table) + dot(jnp.concatenate(lows, axis=0), table)
-    sums = []
-    for i in range(GROUPS):
-        value = sum_ref[:, 512 * i : 512 * i + 512] + fixes[i * ROWS : (i + 1) * ROWS]
-        if i == 0:
-            value = jnp.concatenate([value[:, 0:128] + first_fix[0], value[:, 128:256] + first_fix[1], value[:, 256:512]], axis=1)
-        if i == GROUPS - 1:
-            value = jnp.concatenate([value[:, 0:256], value[:, 256:384] + last_fix[0], value[:, 384:512] + last_fix[1]], axis=1)
-        sums.append(value.astype(BF))
-    dense = dot(jnp.concatenate(sums, axis=0), compact_ref[...]).astype(BF)
-    for i in range(GROUPS):
-        out_ref[:, i * FINE_IN : (i + 1) * FINE_IN] = dense[i * ROWS : (i + 1) * ROWS]
+
+    for m in range(TILE * TILE // 128):
+        cell = 128 * m + lane
+        row, col = cell // 48, cell % 48
+        index = tall(jnp.where(col < 24, row, 64 + row))
+        value = sum_ref[:, 128 * m : 128 * m + 128]
+        fix = zeros
+        for q in range(3):
+            fix = jnp.where(tall((col == q) | (col == 47 - q)), lanes_from(column_fix[q], index), fix)
+        value = value + fix
+        row_index = tall(row % 2 * 64 + 3 + col)
+        for pair, tile in ((0, first_fix[0]), (1, first_fix[1]), (22, last_fix[0]), (23, last_fix[1])):
+            if 96 * pair < 128 * m + 128 and 96 * pair + 96 > 128 * m:
+                value = value + jnp.where(tall(row // 2 == pair), lanes_from(tile, row_index), 0.0)
+        out_ref[:, 128 * m : 128 * m + 128] = value.astype(BF)
 
 
 def params(
-    tab_ref, weight_ref, bias_ref, gain_ref, shift_ref, up_bias_ref, down_bias_ref, scale_ref, pool_weight_ref, spread_weight_ref,
-    taps_ref, conv_bias_ref, gains_ref, shifts_ref, up_biases_ref, down_biases_ref, scales_ref, pool_cells_ref, spread_cells_ref,
+    after_ref, weight_ref, bias_ref, gain_ref, shift_ref, up_ref, up_bias_ref, down_bias_ref, scale_ref, pool_weight_ref, spread_weight_ref,
+    taps_ref, conv_bias_ref, gains_ref, shifts_ref, ups_ref, up_biases_ref, down_biases_ref, scales_ref, pool_cells_ref, spread_cells_ref,
 ):
     for tap in range(49):
         taps_ref[tap] = jnp.broadcast_to(weight_ref[1, :, tap : tap + 1], (ROWS, 128))
@@ -359,6 +379,7 @@
     me = lax.axis_index("chan")
     for level in range(2):
         row = slice(level, level + 1)
+        ups_ref[level] = jnp.transpose(up_ref[level], (1, 0))
         gains_ref[level] = columns(gain_ref[row, :])
         shifts_ref[level] = columns(shift_ref[row, :])
         up_biases_ref[level] = columns(up_bias_ref[row, :])
@@ -555,12 +576,13 @@
 PARAMS = pltpu.CompilerParams(vmem_limit_bytes=24 * 1024 * 1024)
 
 
-def every_channel(own):
+def every_channel(own, beside_work=lambda own: ()):
     pairs = lambda bit: [(i, i ^ bit) for i in range(4)]
     across = lax.ppermute(own, "chan", pairs(2))
     beside = lax.ppermute(own, "chan", pairs(1))
+    across, *results = lax.optimization_barrier((across, *beside_work(own)))
     diagonal = lax.ppermute(across, "chan", pairs(1))
-    return own, beside, across, diagonal
+    return (own, beside, across, diagonal), results
 
 
 def per_device(
@@ -593,51 +615,60 @@
         "mask": land_mask,
         "weight": depth_weight,
         "bias": depth_bias,
-        "halo": jnp.asarray(FINE["halo"]),
-        "expand": jnp.asarray(FINE["expand"]),
-        "compact": jnp.asarray(FINE["compact"]),
-        "spread": jnp.asarray(FINE["spread"]),
-        "fine_sides": jnp.asarray(FINE["sides"]),
         "small_halo": jnp.asarray(COARSE["halo"]),
         "sides": jnp.asarray(COARSE["sides"]),
-        "pool": jnp.asarray(FINE["pool"]),
+        "pool": jnp.asarray(POOL),
         "small_pack": jnp.asarray(COARSE["pack"]),
     }
     arrived = lax.all_to_all(messages, "tile", 0, 0, tiled=True)
-    taps, conv_bias, gains, shifts, up_biases, down_biases, scales, pool_cells, spread_cells = pl.pallas_call(
-        params,
-        in_specs=[SMEM] + [VMEM] * 9,
-        out_specs=[VMEM] * 9,
-        out_shape=[
-            shaped(*shape, dtype=F32)
-            for shape in (
-                (49, ROWS, 128), (ROWS, 128), (2, 192, 128), (2, 192, 128), (2, 768, 128), (2, ROWS, 128), (2, ROWS, 128),
-                (ROWS, FINE_IN), (ROWS, FINE_IN),
-            )
+    inner = pl.pallas_call(
+        lambda tab_ref, *refs: conv_inner(*refs),
+        in_specs=[SMEM] + [VMEM] * 3,
+        out_specs=VMEM,
+        out_shape=shaped(ROWS, cells, dtype=F32),
+        scratch_shapes=[
+            pltpu.VMEM((ROWS, 3584), F32),
+            pltpu.VMEM((ROWS, 3584), F32),
+            pltpu.VMEM((49, ROWS, 128), F32),
+            pltpu.VMEM((ROWS, 3072), F32),
         ],
-        compiler_params=PARAMS,
-        cost_estimate=takes(1),
-        name="params",
-    )(table, depth_weight, depth_bias, norm_gain, norm_bias, up_bias, down_bias, layer_scale, pool_weight, spread_weight)
-    inner, fine_taps = pl.pallas_call(
-        lambda tab_ref, *refs: conv_inner(*refs),
-        in_specs=[SMEM] + [VMEM] * 4,
-        out_specs=[VMEM] * 2,
-        out_shape=[shaped(ROWS, 3072, dtype=F32), shaped(49, ROWS, 128, dtype=F32)],
-        scratch_shapes=[pltpu.VMEM((ROWS, 3584), F32), pltpu.VMEM((ROWS, 3584), F32)],
         compiler_params=PARAMS,
         cost_estimate=takes(4),
         name="conv_inner",
-    )(table, held["x"], held["expand"], held["weight"], held["bias"])
+    )(table, held["x"], held["weight"], held["bias"])
     conv = pl.pallas_call(
         conv_border,
-        in_specs=[SMEM] + [VMEM] * 7,
+        in_specs=[SMEM] + [VMEM] * 3,
         out_specs=VMEM,
         out_shape=shaped(ROWS, cells),
+        scratch_shapes=[pltpu.VMEM((ROWS, 128), F32)],
         compiler_params=PARAMS,
         cost_estimate=takes(2),
         name="conv_border",
-    )(table, arrived, inner, fine_taps, held["halo"], held["fine_sides"], held["spread"], held["compact"])
+    )(table, arrived, inner, held["weight"])
+
+    def spread_params(own):
+        return pl.pallas_call(
+            params,
+            in_specs=[VMEM] * 11,
+            out_specs=[VMEM] * 10,
+            out_shape=[
+                shaped(*shape, dtype=dtype)
+                for shape, dtype in (
+                    ((49, ROWS, 128), F32), ((ROWS, 128), F32), ((2, 192, 128), F32), ((2, 192, 128), F32), (up_weight.shape, BF),
+                    ((2, 768, 128), F32), ((2, ROWS, 128), F32), ((2, ROWS, 128), F32), ((ROWS, FINE_IN), F32), ((ROWS, FINE_IN), F32),
+                )
+            ],
+            compiler_params=PARAMS,
+            cost_estimate=takes(2),
+            name="params",
+        )(
+            own, depth_weight, depth_bias, norm_gain, norm_bias, jnp.swapaxes(up_weight, 1, 2), up_bias, down_bias, layer_scale,
+            pool_weight, spread_weight,
+        )
+
+    pieces, results = every_channel(conv, spread_params)
+    taps, conv_bias, gains, shifts, ups, up_biases, down_biases, scales, pool_cells, spread_cells = results
     fine, pooled, small_mask, messages = pl.pallas_call(
         make_mix_fine(count),
         in_specs=[SMEM] + [VMEM] * 16,
@@ -652,7 +683,7 @@
         cost_estimate=takes(4),
         name="mix_fine",
     )(
-        table, *every_channel(conv), held["x"], held["mask"], gains, shifts, up_weight, up_biases,
+        table, *pieces, held["x"], held["mask"], gains, shifts, ups, up_biases,
         down_weight, down_biases, scales, pool_cells, held["pool"], held["small_pack"],
     )
     arrived = lax.all_to_all(messages, "tile", 0, 0, tiled=True)
@@ -666,6 +697,7 @@
         cost_estimate=takes(2),
         name="conv_coarse",
     )(table, pooled, arrived, held["small_halo"], held["sides"], taps, conv_bias)
+    pieces, _ = every_channel(conv)
     return pl.pallas_call(
         mix_coarse,
         in_specs=[VMEM] * 17,
@@ -676,7 +708,7 @@
         cost_estimate=takes(2),
         name="mix_coarse",
     )(
-        *every_channel(conv), pooled, small_mask, fine, held["mask"], gains, shifts, up_weight, up_biases, down_weight, down_biases,
+        *pieces, pooled, small_mask, fine, held["mask"], gains, shifts, ups, up_biases, down_weight, down_biases,
         scales, spread_cells, held["pool"],
     )
 

time: 57.7 us -> 54.3 us (0.941)
  local copies, waits for them, and re-layouts: 7.73 us -> 1.15 us
  Pallas kernels: 15.5 us -> 17.5 us
  waiting for transfers between devices: 11.7 us -> 13.3 us
    unnamed x57 -> x40, local copies, waits for them, and re-layouts: 7.73 us -> 1.15 us
    pallas_call x2, Pallas kernels: 2.99 us -> 4.54 us  [the longest x1 3.59 us: per_device(): pl.pallas_call(conv_border, in_specs=[SMEM] + [VMEM] * 3, out_specs=VMEM,...]
    ppermute x2, waiting for transfers between devices: 1.26 us -> 2.73 us  [every_channel(): diagonal = lax.ppermute(across, 'chan', pairs(1))]
    all_to_all x1, waiting for transfers between devices: 3.09 us -> 4.49 us  [per_device(): arrived = lax.all_to_all(messages, 'tile', 0, 0, tiled=True)]
    ppermute x2, waiting for transfers between devices: 7.32 us -> 6.05 us  [every_channel(): across = lax.ppermute(own, 'chan', pairs(2))]
  transfers between devices with their start and end apart: 7 -> 7, of which waited for: 4 -> 5; matrix products, arithmetic and copies ran while one was open for 3% -> 0% of each run, Pallas kernels for 8% -> 9%
where the time goes in v5:
time: 54.3 us; the launch traced here: 54 us
  Pallas kernels  17.5 us (32%)
  waiting for transfers between devices  13.3 us (24%)
  blocking collectives  11.4 us (21%)
  starting transfers between devices  10.4 us (19%)
  local copies, waits for them, and re-layouts  1.15 us (2%)
    all_to_all x1, blocking collectives, per_device(): arrived = lax.all_to_all(messages, 'tile', 0, 0, tiled=True)  11.4 us
    all_to_all x1, starting transfers between devices, per_device(): arrived = lax.all_to_all(messages, 'tile', 0, 0, tiled=True)  7.29 us
    ppermute x2, waiting for transfers between devices, every_channel(): across = lax.ppermute(own, 'chan', pairs(2))  6.05 us
    all_to_all x1, waiting for transfers between devices, per_device(): arrived = lax.all_to_all(messages, 'tile', 0, 0, tiled=True)  4.49 us
    pallas_call x1, Pallas kernels, per_device(): pl.pallas_call(make_mix_fine(count), in_specs=[SMEM] + [VMEM] * 16, out_s...  3.85 us
    pallas_call x1, Pallas kernels, per_device(): pl.pallas_call(lambda tab_ref, *refs: conv_inner(*refs), in_specs=[SMEM]...  3.83 us
    pallas_call x1, Pallas kernels, per_device(): pl.pallas_call(conv_border, in_specs=[SMEM] + [VMEM] * 3, out_specs=VMEM,...  3.59 us
    ppermute x2, starting transfers between devices, every_channel(): across = lax.ppermute(own, 'chan', pairs(2))  3.11 us
  transfers between devices with their start and end apart: 7, of which 5 were waited for; matrix products, arithmetic and copies ran while one was open for 0% of the time, Pallas kernels for 9%

profile of v5, /device:TPU:0, one launch (start us, length us, event | category | flops | bytes accessed | tf_op | source)
XLA Modules:
  0.0 54.0 jit_solution(18074828570059812694)
XLA Ops:
  0.0 0.1 strip_table.1.pack_ref
  0.1 0.9 %copy-done.2 = bf16[1,48,2304]{2,1,0:T(8,128)(2,1)S(1)} copy-done((bf16[1,48,2304]{2,1,0:T(8,128)(2,1)S(1)}, bf16[1,48,2304]{2,1,0:T(8,128)(2,1)}, u32[]{:S(2)}) %copy-start.2) | copy-done | bytes 221208
  1.0 1.7 %prep.1 = (bf16[8,16,896]{2,1,0:T(8,128)(2,1)}, s32[24]{0:T(128)S(1)}) custom-call(s32[8]{0:T(128)S(1)} %copy-done.11, s32[8]{0:T(128)S(1)} %copy-done.12, bf16[1,48,2304]{2,1,0:T(8,128)(2,1)S(1)} %copy-done.2, bf16[384,256]{1,0:T(8,128)(2,1)S(1)} %strip_table.1.pack_ref), custom_call_target="tpu_custom_call" | custom-call | flops 10000000000 | tf_op jit(solution)/shard_map/prep/pallas_call | solution.py:598
  2.6 7.3 %all-to-all-start = ((bf16[8,16,896]{2,1,0:T(8,128)(2,1)}), bf16[8,16,896]{2,1,0:T(8,128)(2,1)S(1)}, u32[]{:S(2)}, u32[]{:S(2)}) async-start(bf16[8,16,896]{2,1,0:T(8,128)(2,1)} %get-tuple-element.33), calls=%async_computation | async-start | bytes 458752 | tf_op jit(solution)/shard_map/all_to_all | solution.py:623
  9.9 3.8 %conv_inner.1.sum_ref = f32[48,2304]{1,0:T(8,128)S(1)} custom-call(s32[24]{0:T(128)S(1)} %get-tuple-element.32.tab_ref, bf16[1,48,2304]{2,1,0:T(8,128)(2,1)S(1)} %copy-done.2, f32[2,48,49]{2,1,0:T(8,128)S(1)} %copy-done.3, f32[2,48]{1,0:T(2,128)S(1)} %copy-done.9), custom_call_target="tpu_custom_call" | custom-call | flops 4000000000 | tf_op jit(solution)/shard_map/conv_inner/pallas_call | solution.py:624
  13.8 0.0 copy-start.17
  13.8 0.0 copy-start.18
  13.8 0.0 copy-start
  13.8 0.0 copy-start.5
  13.8 0.0 copy-start.6
  13.8 0.0 copy-start.7
  13.8 0.0 copy-start.8
  13.8 0.0 copy-start.10
  13.9 4.5 %all-to-all-done.recv_ref = bf16[8,16,896]{2,1,0:T(8,128)(2,1)S(1)} async-done(((bf16[8,16,896]{2,1,0:T(8,128)(2,1)}), bf16[8,16,896]{2,1,0:T(8,128)(2,1)S(1)}, u32[]{:S(2)}, u32[]{:S(2)}) %all-to-all-start) | async-done | bytes 229408 | tf_op jit(solution)/shard_map/all_to_all | solution.py:623
  18.3 3.6 %conv_border.1.after_ref.own_ref = bf16[48,2304]{1,0:T(8,128)(2,1)S(1)} custom-call(s32[24]{0:T(128)S(1)} %get-tuple-element.32.tab_ref, bf16[8,16,896]{2,1,0:T(8,128)(2,1)S(1)} %all-to-all-done.recv_ref, f32[48,2304]{1,0:T(8,128)S(1)} %conv_inner.1.sum_ref, f32[2,48,49]{2,1,0:T(8,128)S(1)} %copy-done.3), custom_call_target="tpu_custom_call" | custom-call | flops 2000000000 | tf_op jit(solution)/shard_map/conv_border/pallas_call | solution.py:639
  21.9 1.6 %collective-permute-start.1 = (bf16[48,2304]{1,0:T(8,128)(2,1)S(1)}, bf16[48,2304]{1,0:T(8,128)(2,1)S(1)}, u32[]{:S(2)}, u32[]{:S(2)}) collective-permute-start(bf16[48,2304]{1,0:T(8,128)(2,1)S(1)} %conv_border.1.after_ref.own_ref), channel_id=1, source_target_pairs={{0,2},{1,3},{2,0},{3,1},{4,6},{5,7},{6,4},{7,5},{8,10},{9,11},{10,... | collective-permute-start | bytes 663560 | tf_op jit(solution)/shard_map/ppermute | solution.py:581
  23.5 0.1 copy.20.pool_weight_ref
  23.6 0.1 copy.21.spread_weight_ref
  23.7 0.0 copy-start.1
  23.8 0.0 copy-start.4
  23.8 0.0 copy-start.13
  23.8 0.0 copy-start.16
  23.8 0.9 %params.1 = (f32[49,48,128]{2,1,0:T(8,128)S(1)}, f32[48,128]{1,0:T(8,128)S(1)}, f32[2,192,128]{2,1,0:T(8,128)S(1)}, f32[2,192,128]{2,1,0:T(8,128)S(1)}, bf16[2,7...) custom-call(bf16[48,2304]{1,0:T(8,128)(2,1)S(1)} %conv_border.1.afte, ...), custom_call_target="tpu_custom_call" | custom-call | flops 2000000000 | tf_op jit(solution)/shard_map/params/pallas_call | solution.py:651
  24.8 3.2 %collective-permute-done.1.p2_ref = bf16[48,2304]{1,0:T(8,128)(2,1)S(1)} collective-permute-done((bf16[48,2304]{1,0:T(8,128)(2,1)S(1)}, bf16[48,2304]{1,0:T(8,128)(2,1)S(1)}, u32[]{:S(2)}, u32[]{:S(2)}) %collective-permute-start.1) | collective-permute-done | bytes 221216 | tf_op jit(solution)/shard_map/ppermute | solution.py:581
  28.0 1.5 %collective-permute-done.2.p3_ref = bf16[48,2304]{1,0:T(8,128)(2,1)S(1)} collective-permute-done((bf16[48,2304]{1,0:T(8,128)(2,1)S(1)}, bf16[48,2304]{1,0:T(8,128)(2,1)S(1)}, u32[]{:S(2)}, u32[]{:S(2)}) %collective-permute-start.2) | collective-permute-done | bytes 221216 | tf_op jit(solution)/shard_map/ppermute | solution.py:584
  29.4 3.9 %mix_fine.1 = (bf16[48,2304]{1,0:T(8,128)(2,1)S(1)}, bf16[48,768]{1,0:T(8,128)(2,1)S(1)}, f32[48,128]{1,0:T(8,128)S(1)}, bf16[8,16,512]{2,1,0:T(8,128)(2,1)S(1)}) custom-call(s32[24]{0:T(128)S(1)} %get-tuple-element.32.tab_ref, bf16[48,2304]{1,0:T(8,128)(2,1)S(1)} %conv_border.1.after_ref.own_ref, bf16[48,2304]{1,0:T(8,128)(2,1)S(1)} %collective-permute-done.p1_ref, ...), custom_call_target="tpu_custom_call" | custom-call | flops 4000000000 | tf_op jit(solution)/shard_map/mix_fine/pallas_call | solution.py:672
  33.3 11.4 %all_to_all.10.recv_ref = bf16[8,16,512]{2,1,0:T(8,128)(2,1)S(1)} all-to-all(bf16[8,16,512]{2,1,0:T(8,128)(2,1)S(1)} %get-tuple-element.53), channel_id=1, replica_groups=mesh['tile'=8,'chan'=4] {'tile'}, dimensions={0} | all-to-all | bytes 262144 | tf_op jit(solution)/shard_map/all_to_all | solution.py:689
  44.7 1.8 %conv_coarse.1.own_ref = bf16[48,768]{1,0:T(8,128)(2,1)S(1)} custom-call(s32[24]{0:T(128)S(1)} %get-tuple-element.32.tab_ref, bf16[48,768]{1,0:T(8,128)(2,1)S(1)} %get-tuple-element.52.x_ref.pooled_ref, bf16[8,16,512]{2,1,0:T(8,128)(2,1)S(1)} %all_to_all.10.recv_ref, bf16[3,384,128]{2,1,0:T(8,128)(2,1)S(1)} %copy-done.15, bf16[256,768]{1,0:T(8,128)(2,1)S(1)} %copy-done.14, ...), custom_call_target="tpu_custom_call" | custom-call | flops 2000000000 | tf_op jit(solution)/shard_map/conv_coarse/pallas_call | solution.py:690
  46.5 1.6 %collective-permute-start.4 = (bf16[48,768]{1,0:T(8,128)(2,1)S(1)}, bf16[48,768]{1,0:T(8,128)(2,1)S(1)}, u32[]{:S(2)}, u32[]{:S(2)}) collective-permute-start(bf16[48,768]{1,0:T(8,128)(2,1)S(1)} %conv_coarse.1.own_ref), channel_id=1, source_target_pairs={{0,2},{1,3},{2,0},{3,1},{4,6},{5,7},{6,4},{7,5},{8,10},{9,11},{10,... | collective-permute-start | bytes 221192 | tf_op jit(solution)/shard_map/ppermute | solution.py:581
  48.1 2.9 %collective-permute-done.4.p2_ref = bf16[48,768]{1,0:T(8,128)(2,1)S(1)} collective-permute-done((bf16[48,768]{1,0:T(8,128)(2,1)S(1)}, bf16[48,768]{1,0:T(8,128)(2,1)S(1)}, u32[]{:S(2)}, u32[]{:S(2)}) %collective-permute-start.4) | collective-permute-done | bytes 73760 | tf_op jit(solution)/shard_map/ppermute | solution.py:581
  50.9 1.3 %collective-permute-done.5.p3_ref = bf16[48,768]{1,0:T(8,128)(2,1)S(1)} collective-permute-done((bf16[48,768]{1,0:T(8,128)(2,1)S(1)}, bf16[48,768]{1,0:T(8,128)(2,1)S(1)}, u32[]{:S(2)}, u32[]{:S(2)}) %collective-permute-start.5) | collective-permute-done | bytes 73760 | tf_op jit(solution)/shard_map/ppermute | solution.py:584
  52.2 1.8 %mix_coarse.1 = bf16[1,48,2304]{2,1,0:T(8,128)(2,1)} custom-call(bf16[48,768]{1,0:T(8,128)(2,1)S(1)} %conv_coarse.1.own_ref, bf16[48,768]{1,0:T(8,128)(2,1)S(1)} %collective-permute-done.3.p1_ref, bf16[48,768]{1,0:T(8,128)(2,1)S(1)} %collective-permute-done.4.p2_ref, bf16[48,768]{1,0:T(8,128)(2,1)S(1)} %collective-permute-done.5.p3_ref, ...), custom_call_target="tpu_custom_call" | custom-call | flops 2000000000 | tf_op jit(solution)/shard_map/mix_coarse/pallas_call | solution.py:701
  (31 shorter events, 0.1 us)
Async XLA Ops:
  0.0 0.9 %copy-start.2 = (bf16[1,48,2304]{2,1,0:T(8,128)(2,1)S(1)}, bf16[1,48,2304]{2,1,0:T(8,128)(2,1)}, u32[]{:S(2)}) copy-start(bf16[1,48,2304]{2,1,0:T(8,128)(2,1)} %x_ref.3) | copy-start | bytes 663556
  0.0 0.9 %copy-start.12 = (s32[8]{0:T(128)S(1)}, s32[8]{0:T(128)}, u32[]{:S(2)}) copy-start(s32[8]{0:T(128)} %dev_ref.1) | copy-start | bytes 100
  0.0 0.9 %copy-start.11 = (s32[8]{0:T(128)S(1)}, s32[8]{0:T(128)}, u32[]{:S(2)}) copy-start(s32[8]{0:T(128)} %slots_ref.1) | copy-start | bytes 100
  0.9 9.0 %copy-start.3 = (f32[2,48,49]{2,1,0:T(8,128)S(1)}, f32[2,48,49]{2,1,0:T(8,128)}, u32[]{:S(2)}) copy-start(f32[2,48,49]{2,1,0:T(8,128)} %weight_ref.3) | copy-start | bytes 56452
  0.9 9.0 %copy-start.9 = (f32[2,48]{1,0:T(2,128)S(1)}, f32[2,48]{1,0:T(2,128)}, u32[]{:S(2)}) copy-start(f32[2,48]{1,0:T(2,128)} %bias_ref.1) | copy-start | bytes 1156
  2.6 15.7 %all-to-all-start = ((bf16[8,16,896]{2,1,0:T(8,128)(2,1)}), bf16[8,16,896]{2,1,0:T(8,128)(2,1)S(1)}, u32[]{:S(2)}, u32[]{:S(2)}) async-start(bf16[8,16,896]{2,1,0:T(8,128)(2,1)} %get-tuple-element.33), calls=%async_computation | async-start | bytes 458752 | tf_op jit(solution)/shard_map/all_to_all | solution.py:623
  13.8 9.7 %copy-start.17 = (f32[48,4]{0,1:T(4,128)S(1)}, f32[48,4]{0,1:T(4,128)}, u32[]{:S(2)}) copy-start(f32[48,4]{0,1:T(4,128)} %param.32) | copy-start | bytes 2308
  13.8 9.8 %copy-start.18 = (f32[48,4]{0,1:T(4,128)S(1)}, f32[48,4]{0,1:T(4,128)}, u32[]{:S(2)}) copy-start(f32[48,4]{0,1:T(4,128)} %param.33) | copy-start | bytes 2308
  13.8 9.9 %copy-start = (bf16[2,768,192]{1,2,0:T(8,128)(2,1)S(1)}, bf16[2,768,192]{1,2,0:T(8,128)(2,1)}, u32[]{:S(2)}) copy-start(bf16[2,768,192]{1,2,0:T(8,128)(2,1)} %param.27) | copy-start | bytes 1769476
  13.8 9.9 %copy-start.5 = (f32[2,768]{1,0:T(2,128)S(1)}, f32[2,768]{1,0:T(2,128)}, u32[]{:S(2)}) copy-start(f32[2,768]{1,0:T(2,128)} %up_bias_ref.1) | copy-start | bytes 18436
  13.8 9.9 %copy-start.6 = (f32[2,192]{1,0:T(2,128)S(1)}, f32[2,192]{1,0:T(2,128)}, u32[]{:S(2)}) copy-start(f32[2,192]{1,0:T(2,128)} %gain_ref.1) | copy-start | bytes 4612
  13.8 9.9 %copy-start.7 = (f32[2,192]{1,0:T(2,128)S(1)}, f32[2,192]{1,0:T(2,128)}, u32[]{:S(2)}) copy-start(f32[2,192]{1,0:T(2,128)} %shift_ref.1) | copy-start | bytes 4612
  13.8 9.9 %copy-start.8 = (f32[2,192]{1,0:T(2,128)S(1)}, f32[2,192]{1,0:T(2,128)}, u32[]{:S(2)}) copy-start(f32[2,192]{1,0:T(2,128)} %down_bias_ref.1) | copy-start | bytes 4612
  13.8 9.9 %copy-start.10 = (f32[2,48]{1,0:T(2,128)S(1)}, f32[2,48]{1,0:T(2,128)}, u32[]{:S(2)}) copy-start(f32[2,48]{1,0:T(2,128)} %scale_ref.1) | copy-start | bytes 1156
  21.9 6.0 %collective-permute-start.1 = (bf16[48,2304]{1,0:T(8,128)(2,1)S(1)}, bf16[48,2304]{1,0:T(8,128)(2,1)S(1)}, u32[]{:S(2)}, u32[]{:S(2)}) collective-permute-start(bf16[48,2304]{1,0:T(8,128)(2,1)S(1)} %conv_border.1.after_ref.own_ref), channel_id=1, source_target_pairs={{0,2},{1,3},{2,0},{3,1},{4,6},{5,7},{6,4},{7,5},{8,10},{9,11},{10,... | collective-permute-start | bytes 663560 | tf_op jit(solution)/shard_map/ppermute | solution.py:581
  23.7 4.3 %collective-permute-start = (bf16[48,2304]{1,0:T(8,128)(2,1)S(1)}, bf16[48,2304]{1,0:T(8,128)(2,1)S(1)}, u32[]{:S(2)}, u32[]{:S(2)}) collective-permute-start(bf16[48,2304]{1,0:T(8,128)(2,1)S(1)} %conv_border.1.after_ref.own_ref), channel_id=1, source_target_pairs={{0,1},{1,0},{2,3},{3,2},{4,5},{5,4},{6,7},{7,6},{8,9},{9,8},{10,11... | collective-permute-start | bytes 663560 | tf_op jit(solution)/shard_map/ppermute | solution.py:582
  23.7 5.7 %copy-start.1 = (bf16[2,192,768]{2,1,0:T(8,128)(2,1)S(1)}, bf16[2,192,768]{2,1,0:T(8,128)(2,1)}, u32[]{:S(2)}) copy-start(bf16[2,192,768]{2,1,0:T(8,128)(2,1)} %down_ref.3) | copy-start | bytes 1769476
  23.8 5.7 %copy-start.4 = (s32[1,2304]{1,0:T(1,128)S(1)}, s32[1,2304]{1,0:T(1,128)}, u32[]{:S(2)}) copy-start(s32[1,2304]{1,0:T(1,128)} %mask_ref.3) | copy-start | bytes 27652
  23.8 5.7 %copy-start.13 = (bf16[768,384]{1,0:T(8,128)(2,1)S(1)}, bf16[768,384]{1,0:T(8,128)(2,1)}, u32[]{:S(2)}) copy-start(bf16[768,384]{1,0:T(8,128)(2,1)} %constant.11.clone.pack_ref) | copy-start | bytes 1769476
  23.8 5.6 %copy-start.16 = (bf16[384,128]{1,0:T(8,128)(2,1)S(1)}, bf16[384,128]{1,0:T(8,128)(2,1)}, u32[]{:S(2)}) copy-start(bf16[384,128]{1,0:T(8,128)(2,1)} %constant.10.clone.pool_ref) | copy-start | bytes 294916
  27.9 16.8 %copy-start.14 = (bf16[256,768]{1,0:T(8,128)(2,1)S(1)}, bf16[256,768]{1,0:T(8,128)(2,1)}, u32[]{:S(2)}) copy-start(bf16[256,768]{1,0:T(8,128)(2,1)} %constant.9.clone.sides_ref) | copy-start | bytes 1179652
  27.9 16.8 %copy-start.15 = (bf16[3,384,128]{2,1,0:T(8,128)(2,1)S(1)}, bf16[3,384,128]{2,1,0:T(8,128)(2,1)}, u32[]{:S(2)}) copy-start(bf16[3,384,128]{2,1,0:T(8,128)(2,1)} %constant.8.clone.halo_ref) | copy-start | bytes 884740
  27.9 1.5 %collective-permute-start.2 = (bf16[48,2304]{1,0:T(8,128)(2,1)S(1)}, bf16[48,2304]{1,0:T(8,128)(2,1)S(1)}, u32[]{:S(2)}, u32[]{:S(2)}) collective-permute-start(bf16[48,2304]{1,0:T(8,128)(2,1)S(1)} %collective-permute-done.1.p2_ref), channel_id=1, source_target_pairs={{0,1},{1,0},{2,3},{3,2},{4,5},{5,4},{6,7},{7,6},{8,9},{9,8},{10,11... | collective-permute-start | bytes 663560 | tf_op jit(solution)/shard_map/ppermute | solution.py:584
  46.5 4.4 %collective-permute-start.4 = (bf16[48,768]{1,0:T(8,128)(2,1)S(1)}, bf16[48,768]{1,0:T(8,128)(2,1)S(1)}, u32[]{:S(2)}, u32[]{:S(2)}) collective-permute-start(bf16[48,768]{1,0:T(8,128)(2,1)S(1)} %conv_coarse.1.own_ref), channel_id=1, source_target_pairs={{0,2},{1,3},{2,0},{3,1},{4,6},{5,7},{6,4},{7,5},{8,10},{9,11},{10,... | collective-permute-start | bytes 221192 | tf_op jit(solution)/shard_map/ppermute | solution.py:581
  48.1 2.9 %collective-permute-start.3 = (bf16[48,768]{1,0:T(8,128)(2,1)S(1)}, bf16[48,768]{1,0:T(8,128)(2,1)S(1)}, u32[]{:S(2)}, u32[]{:S(2)}) collective-permute-start(bf16[48,768]{1,0:T(8,128)(2,1)S(1)} %conv_coarse.1.own_ref), channel_id=1, source_target_pairs={{0,1},{1,0},{2,3},{3,2},{4,5},{5,4},{6,7},{7,6},{8,9},{9,8},{10,11... | collective-permute-start | bytes 221192 | tf_op jit(solution)/shard_map/ppermute | solution.py:582
  50.9 1.3 %collective-permute-start.5 = (bf16[48,768]{1,0:T(8,128)(2,1)S(1)}, bf16[48,768]{1,0:T(8,128)(2,1)S(1)}, u32[]{:S(2)}, u32[]{:S(2)}) collective-permute-start(bf16[48,768]{1,0:T(8,128)(2,1)S(1)} %collective-permute-done.4.p2_ref), channel_id=1, source_target_pairs={{0,1},{1,0},{2,3},{3,2},{4,5},{5,4},{6,7},{7,6},{8,9},{9,8},{10,11... | collective-permute-start | bytes 221192 | tf_op jit(solution)/shard_map/ppermute | solution.py:584

commit v6 on v5

--- a/solution.py
+++ b/solution.py
@@ -99,14 +99,18 @@
     return lax.broadcasted_iota(jnp.int32, shape, 1)
 
 
-def columns(row):
+def three_terms(row):
     high = row.astype(BF)
     rest = row - high.astype(F32)
     middle = rest.astype(BF)
     low = (rest - middle.astype(F32)).astype(BF)
-    n = row.shape[1]
-    terms = jnp.concatenate([high, middle, low, jnp.zeros((13, n), BF)], axis=0)
-    return lax.dot_general(terms, jnp.ones((16, 128), BF), (((0,), (0,)), ((), ())), preferred_element_type=F32)
+    return jnp.concatenate([high, middle, low, jnp.zeros((13, row.shape[1]), BF)], axis=0)
+
+
+def columns(row):
+    return lax.dot_general(
+        three_terms(row), jnp.ones((16, 128), BF), (((0,), (0,)), ((), ())), preferred_element_type=F32
+    )
 
 
 def wide(block, lanes):
@@ -221,7 +225,7 @@
     return jnp.take_along_axis(value, index, axis=1)
 
 
-def conv_inner(x_ref, weight_ref, bias_ref, sum_ref, pad_ref, odd_ref, wide_ref, total_ref):
+def conv_inner(x_ref, weight_ref, bias_ref, sum_ref, wide_ref, pad_ref, odd_ref, total_ref):
     for tap in range(49):
         wide_ref[tap] = jnp.broadcast_to(weight_ref[0, :, tap : tap + 1], (ROWS, 128))
     pad_ref[:, 0:256] = jnp.zeros((ROWS, 256), F32)
@@ -277,13 +281,13 @@
             sum_ref[:, 384 * i + 128 * m : 384 * i + 128 * m + 128] = value
 
 
-def conv_border(tab_ref, recv_ref, sum_ref, weight_ref, out_ref, taps_ref):
+def conv_border(tab_ref, recv_ref, sum_ref, wide_ref, out_ref):
     lane = lane_ids((8, 128))
     half, within = lane // 64, lane % 64
     low_half = tall(lane < 64)
-    taps_ref[...] = jnp.zeros((ROWS, 128), F32)
-    taps_ref[:, 0:49] = weight_ref[0]
-    taps = taps_ref[...]
+
+    def tap(a, b):
+        return wide_ref[a * 7 + b]
 
     def band_cells(band, offset):
         source, scale = band_source(tab_ref, band)
@@ -313,11 +317,8 @@
         total = [jnp.zeros((ROWS, 128), F32)] * 2
         for b in range(7):
             partial = [None, None]
-            weights = {}
             for place, a, cells in uses:
-                if a not in weights:
-                    weights[a] = jnp.broadcast_to(taps[:, a * 7 + b : a * 7 + b + 1], (ROWS, 128))
-                term = weights[a] * cells
+                term = tap(a, b) * cells
                 partial[place] = term if partial[place] is None else partial[place] + term
             for place in range(2):
                 total[place] = total[place] + (pltpu.roll(partial[place], (3 - b) % 128, 1) if b != 3 else partial[place])
@@ -346,7 +347,7 @@
         beside.append(jnp.where(tall(within < 48), jnp.where(low_half, picked[0], picked[1]), 0.0))
     column_fix = [zeros] * 3
     for a in range(7):
-        weights = [lanes_from(taps, tall(jnp.where(half == 0, a * 7 + b, a * 7 + 6 - b))) for b in range(3)]
+        weights = [jnp.where(low_half, tap(a, b), tap(a, 6 - b)) for b in range(3)]
         for q in range(3):
             partial = weights[0] * beside[q]
             for j in range(q + 1, 3):
@@ -371,7 +372,7 @@
 
 def params(
     after_ref, weight_ref, bias_ref, gain_ref, shift_ref, up_ref, up_bias_ref, down_bias_ref, scale_ref, pool_weight_ref, spread_weight_ref,
-    taps_ref, conv_bias_ref, gains_ref, shifts_ref, ups_ref, up_biases_ref, down_biases_ref, scales_ref, pool_cells_ref, spread_cells_ref,
+    taps_ref, conv_bias_ref, gains_ref, shifts_ref, ups_ref, down_biases_ref, scales_ref, pool_cells_ref, spread_cells_ref,
 ):
     for tap in range(49):
         taps_ref[tap] = jnp.broadcast_to(weight_ref[1, :, tap : tap + 1], (ROWS, 128))
@@ -379,10 +380,9 @@
     me = lax.axis_index("chan")
     for level in range(2):
         row = slice(level, level + 1)
-        ups_ref[level] = jnp.transpose(up_ref[level], (1, 0))
+        ups_ref[level] = jnp.transpose(jnp.concatenate([up_ref[level], three_terms(up_bias_ref[row, :])], axis=0), (1, 0))
         gains_ref[level] = columns(gain_ref[row, :])
         shifts_ref[level] = columns(shift_ref[row, :])
-        up_biases_ref[level] = columns(up_bias_ref[row, :])
         scales_ref[level] = columns(scale_ref[row, :])
         down_bias = columns(down_bias_ref[row, :])
         own = down_bias[0:ROWS]
@@ -453,7 +453,7 @@
         cat_ref[pl.ds(first, ROWS), :] = piece[...]
 
 
-def make_branch(level, cat_ref, gain_ref, shift_ref, up_ref, up_bias_ref, down_ref, down_bias_ref, block):
+def make_branch(level, cat_ref, gain_ref, shift_ref, up_ref, down_ref, down_bias_ref, block):
     first = pl.multiple_of(lax.axis_index("chan") * ROWS, 16)
     gain, shift = wide(gain_ref[level], block), wide(shift_ref[level], block)
 
@@ -463,7 +463,7 @@
         centred = values - mean
         spread = jnp.mean(centred * centred, axis=0, keepdims=True)
         normed = (centred * lax.rsqrt(spread + norm_eps) * gain + shift).astype(BF)
-        hidden = dot(up_ref[level], normed) + wide(up_bias_ref[level], block)
+        hidden = dot(up_ref[level], jnp.concatenate([normed, jnp.ones((16, block), BF)], axis=0))
         hidden = 0.5 * hidden * (1.0 + lax.erf(hidden * np.float32(0.5**0.5)))
         return dot(down_ref[level, pl.ds(first, ROWS), :], hidden.astype(BF)) + wide(down_bias_ref[level], block)
 
@@ -484,12 +484,12 @@
 def make_mix_fine(count):
     def mix_fine(
         tab_ref, own_ref, p1_ref, p2_ref, p3_ref, x_ref, mask_ref,
-        gain_ref, shift_ref, up_ref, up_bias_ref, down_ref, down_bias_ref, scale_ref, pool_cells_ref, pool_ref, pack_ref,
+        gain_ref, shift_ref, up_ref, down_ref, down_bias_ref, scale_ref, pool_cells_ref, pool_ref, pack_ref,
         fine_ref, pooled_ref, small_mask_ref, msg_ref, cat_ref, mains_ref, rest_ref,
     ):
         gather_rows((own_ref, p1_ref, p2_ref, p3_ref), cat_ref)
         block = 768
-        branch = make_branch(0, cat_ref, gain_ref, shift_ref, up_ref, up_bias_ref, down_ref, down_bias_ref, block)
+        branch = make_branch(0, cat_ref, gain_ref, shift_ref, up_ref, down_ref, down_bias_ref, block)
         scale = wide(scale_ref[0], block)
 
         for start in range(0, TILE * TILE, block):
@@ -542,12 +542,12 @@
 
 
 def mix_coarse(
-    own_ref, p1_ref, p2_ref, p3_ref, pooled_ref, small_mask_ref, fine_ref, mask_ref, gain_ref, shift_ref, up_ref, up_bias_ref,
+    own_ref, p1_ref, p2_ref, p3_ref, pooled_ref, small_mask_ref, fine_ref, mask_ref, gain_ref, shift_ref, up_ref,
     down_ref, down_bias_ref, scale_ref, spread_cells_ref, pool_ref, out_ref, cat_ref,
 ):
     gather_rows((own_ref, p1_ref, p2_ref, p3_ref), cat_ref)
     cells = cat_ref.shape[1]
-    branch = make_branch(1, cat_ref, gain_ref, shift_ref, up_ref, up_bias_ref, down_ref, down_bias_ref, cells)
+    branch = make_branch(1, cat_ref, gain_ref, shift_ref, up_ref, down_ref, down_bias_ref, cells)
     value = pooled_ref[...].astype(F32) + wide(scale_ref[1], cells) * branch(0)
     parts = []
     for i in range(GROUPS):
@@ -621,15 +621,14 @@
         "small_pack": jnp.asarray(COARSE["pack"]),
     }
     arrived = lax.all_to_all(messages, "tile", 0, 0, tiled=True)
-    inner = pl.pallas_call(
+    inner, fine_taps = pl.pallas_call(
         lambda tab_ref, *refs: conv_inner(*refs),
         in_specs=[SMEM] + [VMEM] * 3,
-        out_specs=VMEM,
-        out_shape=shaped(ROWS, cells, dtype=F32),
+        out_specs=[VMEM] * 2,
+        out_shape=[shaped(ROWS, cells, dtype=F32), shaped(49, ROWS, 128, dtype=F32)],
         scratch_shapes=[
             pltpu.VMEM((ROWS, 3584), F32),
             pltpu.VMEM((ROWS, 3584), F32),
-            pltpu.VMEM((49, ROWS, 128), F32),
             pltpu.VMEM((ROWS, 3072), F32),
         ],
         compiler_params=PARAMS,
@@ -641,22 +640,21 @@
         in_specs=[SMEM] + [VMEM] * 3,
         out_specs=VMEM,
         out_shape=shaped(ROWS, cells),
-        scratch_shapes=[pltpu.VMEM((ROWS, 128), F32)],
         compiler_params=PARAMS,
         cost_estimate=takes(2),
         name="conv_border",
-    )(table, arrived, inner, held["weight"])
+    )(table, arrived, inner, fine_taps)
 
     def spread_params(own):
         return pl.pallas_call(
             params,
             in_specs=[VMEM] * 11,
-            out_specs=[VMEM] * 10,
+            out_specs=[VMEM] * 9,
             out_shape=[
                 shaped(*shape, dtype=dtype)
                 for shape, dtype in (
-                    ((49, ROWS, 128), F32), ((ROWS, 128), F32), ((2, 192, 128), F32), ((2, 192, 128), F32), (up_weight.shape, BF),
-                    ((2, 768, 128), F32), ((2, ROWS, 128), F32), ((2, ROWS, 128), F32), ((ROWS, FINE_IN), F32), ((ROWS, FINE_IN), F32),
+                    ((49, ROWS, 128), F32), ((ROWS, 128), F32), ((2, 192, 128), F32), ((2, 192, 128), F32), ((2, up_weight.shape[1], up_weight.shape[2] + 16), BF),
+                    ((2, ROWS, 128), F32), ((2, ROWS, 128), F32), ((ROWS, FINE_IN), F32), ((ROWS, FINE_IN), F32),
                 )
             ],
             compiler_params=PARAMS,
@@ -668,10 +666,10 @@
         )
 
     pieces, results = every_channel(conv, spread_params)
-    taps, conv_bias, gains, shifts, ups, up_biases, down_biases, scales, pool_cells, spread_cells = results
+    taps, conv_bias, gains, shifts, ups, down_biases, scales, pool_cells, spread_cells = results
     fine, pooled, small_mask, messages = pl.pallas_call(
         make_mix_fine(count),
-        in_specs=[SMEM] + [VMEM] * 16,
+        in_specs=[SMEM] + [VMEM] * 15,
         out_specs=[VMEM] * 4,
         out_shape=[shaped(ROWS, cells), shaped(ROWS, 768), shaped(48, 128, dtype=F32), shaped(count, 16, 512)],
         scratch_shapes=[
@@ -683,7 +681,7 @@
         cost_estimate=takes(4),
         name="mix_fine",
     )(
-        table, *pieces, held["x"], held["mask"], gains, shifts, ups, up_biases,
+        table, *pieces, held["x"], held["mask"], gains, shifts, ups,
         down_weight, down_biases, scales, pool_cells, held["pool"], held["small_pack"],
     )
     arrived = lax.all_to_all(messages, "tile", 0, 0, tiled=True)
@@ -700,7 +698,7 @@
     pieces, _ = every_channel(conv)
     return pl.pallas_call(
         mix_coarse,
-        in_specs=[VMEM] * 17,
+        in_specs=[VMEM] * 16,
         out_specs=VMEM,
         out_shape=shaped(1, ROWS, cells),
         scratch_shapes=[pltpu.VMEM((4 * ROWS, 768), BF)],
@@ -708,7 +706,7 @@
         cost_estimate=takes(2),
         name="mix_coarse",
     )(
-        *pieces, pooled, small_mask, fine, held["mask"], gains, shifts, ups, up_biases, down_weight, down_biases,
+        *pieces, pooled, small_mask, fine, held["mask"], gains, shifts, ups, down_weight, down_biases,
         scales, spread_cells, held["pool"],
     )
 

time: 54.3 us -> 52.7 us (0.971)
  Pallas kernels: 17.5 us -> 15.8 us
    pallas_call x1, Pallas kernels: 3.59 us -> 2.18 us  [per_device(): pl.pallas_call(conv_border, in_specs=[SMEM] + [VMEM] * 3, out_specs=VMEM,...]
where the time goes in v6:
time: 52.7 us; the launch traced here: 52.4 us
  Pallas kernels  15.8 us (30%)
  waiting for transfers between devices  13.5 us (26%)
  blocking collectives  11.4 us (22%)
  starting transfers between devices  10.4 us (20%)
  local copies, waits for them, and re-layouts  1.14 us (2%)
    all_to_all x1, blocking collectives, per_device(): arrived = lax.all_to_all(messages, 'tile', 0, 0, tiled=True)  11.4 us
    all_to_all x1, starting transfers between devices, per_device(): arrived = lax.all_to_all(messages, 'tile', 0, 0, tiled=True)  7.29 us
    ppermute x2, waiting for transfers between devices, every_channel(): across = lax.ppermute(own, 'chan', pairs(2))  6.15 us
    all_to_all x1, waiting for transfers between devices, per_device(): arrived = lax.all_to_all(messages, 'tile', 0, 0, tiled=True)  4.58 us
    pallas_call x1, Pallas kernels, per_device(): pl.pallas_call(lambda tab_ref, *refs: conv_inner(*refs), in_specs=[SMEM]...  3.83 us
    pallas_call x1, Pallas kernels, per_device(): pl.pallas_call(make_mix_fine(count), in_specs=[SMEM] + [VMEM] * 15, out_s...  3.67 us
    ppermute x2, starting transfers between devices, every_channel(): across = lax.ppermute(own, 'chan', pairs(2))  3.12 us
    ppermute x2, waiting for transfers between devices, every_channel(): diagonal = lax.ppermute(across, 'chan', pairs(1))  2.73 us
  transfers between devices with their start and end apart: 7, of which 5 were waited for; matrix products, arithmetic and copies ran while one was open for 0% of the time, Pallas kernels for 9%

profile of v6, /device:TPU:0, one launch (start us, length us, event | category | flops | bytes accessed | tf_op | source)
XLA Modules:
  0.0 52.4 jit_solution(17027238002707321030)
XLA Ops:
  0.0 0.1 strip_table.1.pack_ref
  0.1 0.9 %copy-done.2 = bf16[1,48,2304]{2,1,0:T(8,128)(2,1)S(1)} copy-done((bf16[1,48,2304]{2,1,0:T(8,128)(2,1)S(1)}, bf16[1,48,2304]{2,1,0:T(8,128)(2,1)}, u32[]{:S(2)}) %copy-start.2) | copy-done | bytes 221208
  1.0 1.7 %prep.1 = (bf16[8,16,896]{2,1,0:T(8,128)(2,1)}, s32[24]{0:T(128)S(1)}) custom-call(s32[8]{0:T(128)S(1)} %copy-done.11, s32[8]{0:T(128)S(1)} %copy-done.12, bf16[1,48,2304]{2,1,0:T(8,128)(2,1)S(1)} %copy-done.2, bf16[384,256]{1,0:T(8,128)(2,1)S(1)} %strip_table.1.pack_ref), custom_call_target="tpu_custom_call" | custom-call | flops 10000000000 | tf_op jit(solution)/shard_map/prep/pallas_call | solution.py:598
  2.6 7.3 %all-to-all-start = ((bf16[8,16,896]{2,1,0:T(8,128)(2,1)}), bf16[8,16,896]{2,1,0:T(8,128)(2,1)S(1)}, u32[]{:S(2)}, u32[]{:S(2)}) async-start(bf16[8,16,896]{2,1,0:T(8,128)(2,1)} %get-tuple-element.33), calls=%async_computation | async-start | bytes 458752 | tf_op jit(solution)/shard_map/all_to_all | solution.py:623
  9.9 3.8 %conv_inner.1 = (f32[48,2304]{1,0:T(8,128)S(1)}, f32[49,48,128]{2,1,0:T(8,128)S(1)}) custom-call(s32[24]{0:T(128)S(1)} %get-tuple-element.32.tab_ref, bf16[1,48,2304]{2,1,0:T(8,128)(2,1)S(1)} %copy-done.2, f32[2,48,49]{2,1,0:T(8,128)S(1)} %copy-done.3, f32[2,48]{1,0:T(2,128)S(1)} %copy-done.9), custom_call_target="tpu_custom_call" | custom-call | flops 4000000000 | tf_op jit(solution)/shard_map/conv_inner/pallas_call | solution.py:624
  13.8 4.6 %all-to-all-done.recv_ref = bf16[8,16,896]{2,1,0:T(8,128)(2,1)S(1)} async-done(((bf16[8,16,896]{2,1,0:T(8,128)(2,1)}), bf16[8,16,896]{2,1,0:T(8,128)(2,1)S(1)}, u32[]{:S(2)}, u32[]{:S(2)}) %all-to-all-start) | async-done | bytes 229408 | tf_op jit(solution)/shard_map/all_to_all | solution.py:623
  18.4 0.0 copy-start.6
  18.4 0.0 copy-start.7
  18.4 0.0 copy-start.8
  18.4 0.0 copy-start.10
  18.4 2.2 %conv_border.1.after_ref.own_ref = bf16[48,2304]{1,0:T(8,128)(2,1)S(1)} custom-call(s32[24]{0:T(128)S(1)} %get-tuple-element.32.tab_ref, bf16[8,16,896]{2,1,0:T(8,128)(2,1)S(1)} %all-to-all-done.recv_ref, f32[48,2304]{1,0:T(8,128)S(1)} %get-tuple-element.34.sum_ref, f32[49,48,128]{2,1,0:T(8,128)S(1)} %get-tuple-element.35.wide_ref), custom_call_target="tpu_custom_call" | custom-call | flops 2000000000 | tf_op jit(solution)/shard_map/conv_border/pallas_call | solution.py:638
  20.6 1.6 %collective-permute-start.1 = (bf16[48,2304]{1,0:T(8,128)(2,1)S(1)}, bf16[48,2304]{1,0:T(8,128)(2,1)S(1)}, u32[]{:S(2)}, u32[]{:S(2)}) collective-permute-start(bf16[48,2304]{1,0:T(8,128)(2,1)S(1)} %conv_border.1.after_ref.own_ref), channel_id=1, source_target_pairs={{0,2},{1,3},{2,0},{3,1},{4,6},{5,7},{6,4},{7,5},{8,10},{9,11},{10,... | collective-permute-start | bytes 663560 | tf_op jit(solution)/shard_map/ppermute | solution.py:581
  22.1 0.1 copy.20.pool_weight_ref
  22.2 0.1 copy.21.spread_weight_ref
  22.3 0.0 collective-permute-start
  22.4 0.0 copy-start.1
  22.4 0.0 copy-start.4
  22.4 0.0 copy-start.13
  22.4 0.0 copy-start.16
  22.4 0.8 %params.1 = (f32[49,48,128]{2,1,0:T(8,128)S(1)}, f32[48,128]{1,0:T(8,128)S(1)}, f32[2,192,128]{2,1,0:T(8,128)S(1)}, f32[2,192,128]{2,1,0:T(8,128)S(1)}, bf16[2,7...) custom-call(bf16[48,2304]{1,0:T(8,128)(2,1)S(1)} %conv_border.1.afte, ...), custom_call_target="tpu_custom_call" | custom-call | flops 2000000000 | tf_op jit(solution)/shard_map/params/pallas_call | solution.py:649
  23.3 3.3 %collective-permute-done.1.p2_ref = bf16[48,2304]{1,0:T(8,128)(2,1)S(1)} collective-permute-done((bf16[48,2304]{1,0:T(8,128)(2,1)S(1)}, bf16[48,2304]{1,0:T(8,128)(2,1)S(1)}, u32[]{:S(2)}, u32[]{:S(2)}) %collective-permute-start.1) | collective-permute-done | bytes 221216 | tf_op jit(solution)/shard_map/ppermute | solution.py:581
  26.6 0.0 collective-permute-start.2
  26.6 0.0 collective-permute-done.p1_ref
  26.6 1.5 %collective-permute-done.2.p3_ref = bf16[48,2304]{1,0:T(8,128)(2,1)S(1)} collective-permute-done((bf16[48,2304]{1,0:T(8,128)(2,1)S(1)}, bf16[48,2304]{1,0:T(8,128)(2,1)S(1)}, u32[]{:S(2)}, u32[]{:S(2)}) %collective-permute-start.2) | collective-permute-done | bytes 221216 | tf_op jit(solution)/shard_map/ppermute | solution.py:584
  28.1 3.7 %mix_fine.1 = (bf16[48,2304]{1,0:T(8,128)(2,1)S(1)}, bf16[48,768]{1,0:T(8,128)(2,1)S(1)}, f32[48,128]{1,0:T(8,128)S(1)}, bf16[8,16,512]{2,1,0:T(8,128)(2,1)S(1)}) custom-call(s32[24]{0:T(128)S(1)} %get-tuple-element.32.tab_ref, bf16[48,2304]{1,0:T(8,128)(2,1)S(1)} %conv_border.1.after_ref.own_ref, bf16[48,2304]{1,0:T(8,128)(2,1)S(1)} %collective-permute-done.p1_ref, ...), custom_call_target="tpu_custom_call" | custom-call | flops 4000000000 | tf_op jit(solution)/shard_map/mix_fine/pallas_call | solution.py:670
  31.8 11.4 %all_to_all.10.recv_ref = bf16[8,16,512]{2,1,0:T(8,128)(2,1)S(1)} all-to-all(bf16[8,16,512]{2,1,0:T(8,128)(2,1)S(1)} %get-tuple-element.53), channel_id=1, replica_groups=mesh['tile'=8,'chan'=4] {'tile'}, dimensions={0} | all-to-all | bytes 262144 | tf_op jit(solution)/shard_map/all_to_all | solution.py:687
  43.2 1.8 %conv_coarse.1.own_ref = bf16[48,768]{1,0:T(8,128)(2,1)S(1)} custom-call(s32[24]{0:T(128)S(1)} %get-tuple-element.32.tab_ref, bf16[48,768]{1,0:T(8,128)(2,1)S(1)} %get-tuple-element.52.x_ref.pooled_ref, bf16[8,16,512]{2,1,0:T(8,128)(2,1)S(1)} %all_to_all.10.recv_ref, bf16[3,384,128]{2,1,0:T(8,128)(2,1)S(1)} %copy-done.15, bf16[256,768]{1,0:T(8,128)(2,1)S(1)} %copy-done.14, ...), custom_call_target="tpu_custom_call" | custom-call | flops 2000000000 | tf_op jit(solution)/shard_map/conv_coarse/pallas_call | solution.py:688
  45.0 1.6 %collective-permute-start.4 = (bf16[48,768]{1,0:T(8,128)(2,1)S(1)}, bf16[48,768]{1,0:T(8,128)(2,1)S(1)}, u32[]{:S(2)}, u32[]{:S(2)}) collective-permute-start(bf16[48,768]{1,0:T(8,128)(2,1)S(1)} %conv_coarse.1.own_ref), channel_id=1, source_target_pairs={{0,2},{1,3},{2,0},{3,1},{4,6},{5,7},{6,4},{7,5},{8,10},{9,11},{10,... | collective-permute-start | bytes 221192 | tf_op jit(solution)/shard_map/ppermute | solution.py:581
  46.5 2.9 %collective-permute-done.4.p2_ref = bf16[48,768]{1,0:T(8,128)(2,1)S(1)} collective-permute-done((bf16[48,768]{1,0:T(8,128)(2,1)S(1)}, bf16[48,768]{1,0:T(8,128)(2,1)S(1)}, u32[]{:S(2)}, u32[]{:S(2)}) %collective-permute-start.4) | collective-permute-done | bytes 73760 | tf_op jit(solution)/shard_map/ppermute | solution.py:581
  49.4 0.0 collective-permute-start.5
  49.4 1.3 %collective-permute-done.5.p3_ref = bf16[48,768]{1,0:T(8,128)(2,1)S(1)} collective-permute-done((bf16[48,768]{1,0:T(8,128)(2,1)S(1)}, bf16[48,768]{1,0:T(8,128)(2,1)S(1)}, u32[]{:S(2)}, u32[]{:S(2)}) %collective-permute-start.5) | collective-permute-done | bytes 73760 | tf_op jit(solution)/shard_map/ppermute | solution.py:584
  50.7 1.8 %mix_coarse.1 = bf16[1,48,2304]{2,1,0:T(8,128)(2,1)} custom-call(bf16[48,768]{1,0:T(8,128)(2,1)S(1)} %conv_coarse.1.own_ref, bf16[48,768]{1,0:T(8,128)(2,1)S(1)} %collective-permute-done.3.p1_ref, bf16[48,768]{1,0:T(8,128)(2,1)S(1)} %collective-permute-done.4.p2_ref, bf16[48,768]{1,0:T(8,128)(2,1)S(1)} %collective-permute-done.5.p3_ref, ...), custom_call_target="tpu_custom_call" | custom-call | flops 2000000000 | tf_op jit(solution)/shard_map/mix_coarse/pallas_call | solution.py:699
  (31 shorter events, 0.1 us)
Async XLA Ops:
  0.0 0.9 %copy-start.2 = (bf16[1,48,2304]{2,1,0:T(8,128)(2,1)S(1)}, bf16[1,48,2304]{2,1,0:T(8,128)(2,1)}, u32[]{:S(2)}) copy-start(bf16[1,48,2304]{2,1,0:T(8,128)(2,1)} %x_ref.3) | copy-start | bytes 663556
  0.0 0.9 %copy-start.12 = (s32[8]{0:T(128)S(1)}, s32[8]{0:T(128)}, u32[]{:S(2)}) copy-start(s32[8]{0:T(128)} %dev_ref.1) | copy-start | bytes 100
  0.0 0.9 %copy-start.11 = (s32[8]{0:T(128)S(1)}, s32[8]{0:T(128)}, u32[]{:S(2)}) copy-start(s32[8]{0:T(128)} %slots_ref.1) | copy-start | bytes 100
  0.9 9.0 %copy-start.3 = (f32[2,48,49]{2,1,0:T(8,128)S(1)}, f32[2,48,49]{2,1,0:T(8,128)}, u32[]{:S(2)}) copy-start(f32[2,48,49]{2,1,0:T(8,128)} %weight_ref.1) | copy-start | bytes 56452
  0.9 9.0 %copy-start.9 = (f32[2,48]{1,0:T(2,128)S(1)}, f32[2,48]{1,0:T(2,128)}, u32[]{:S(2)}) copy-start(f32[2,48]{1,0:T(2,128)} %bias_ref.1) | copy-start | bytes 1156
  2.6 15.7 %all-to-all-start = ((bf16[8,16,896]{2,1,0:T(8,128)(2,1)}), bf16[8,16,896]{2,1,0:T(8,128)(2,1)S(1)}, u32[]{:S(2)}, u32[]{:S(2)}) async-start(bf16[8,16,896]{2,1,0:T(8,128)(2,1)} %get-tuple-element.33), calls=%async_computation | async-start | bytes 458752 | tf_op jit(solution)/shard_map/all_to_all | solution.py:623
  18.3 3.8 %copy-start.17 = (f32[48,4]{0,1:T(4,128)S(1)}, f32[48,4]{0,1:T(4,128)}, u32[]{:S(2)}) copy-start(f32[48,4]{0,1:T(4,128)} %param.32) | copy-start | bytes 2308
  18.3 3.9 %copy-start.18 = (f32[48,4]{0,1:T(4,128)S(1)}, f32[48,4]{0,1:T(4,128)}, u32[]{:S(2)}) copy-start(f32[48,4]{0,1:T(4,128)} %param.33) | copy-start | bytes 2308
  18.4 4.0 %copy-start = (bf16[2,768,192]{1,2,0:T(8,128)(2,1)S(1)}, bf16[2,768,192]{1,2,0:T(8,128)(2,1)}, u32[]{:S(2)}) copy-start(bf16[2,768,192]{1,2,0:T(8,128)(2,1)} %param.27) | copy-start | bytes 1769476
  18.4 4.0 %copy-start.5 = (f32[2,768]{1,0:T(2,128)S(1)}, f32[2,768]{1,0:T(2,128)}, u32[]{:S(2)}) copy-start(f32[2,768]{1,0:T(2,128)} %up_bias_ref.1) | copy-start | bytes 18436
  18.4 4.0 %copy-start.6 = (f32[2,192]{1,0:T(2,128)S(1)}, f32[2,192]{1,0:T(2,128)}, u32[]{:S(2)}) copy-start(f32[2,192]{1,0:T(2,128)} %gain_ref.1) | copy-start | bytes 4612
  18.4 4.0 %copy-start.7 = (f32[2,192]{1,0:T(2,128)S(1)}, f32[2,192]{1,0:T(2,128)}, u32[]{:S(2)}) copy-start(f32[2,192]{1,0:T(2,128)} %shift_ref.1) | copy-start | bytes 4612
  18.4 4.0 %copy-start.8 = (f32[2,192]{1,0:T(2,128)S(1)}, f32[2,192]{1,0:T(2,128)}, u32[]{:S(2)}) copy-start(f32[2,192]{1,0:T(2,128)} %down_bias_ref.1) | copy-start | bytes 4612
  18.4 4.0 %copy-start.10 = (f32[2,48]{1,0:T(2,128)S(1)}, f32[2,48]{1,0:T(2,128)}, u32[]{:S(2)}) copy-start(f32[2,48]{1,0:T(2,128)} %scale_ref.1) | copy-start | bytes 1156
  20.6 6.0 %collective-permute-start.1 = (bf16[48,2304]{1,0:T(8,128)(2,1)S(1)}, bf16[48,2304]{1,0:T(8,128)(2,1)S(1)}, u32[]{:S(2)}, u32[]{:S(2)}) collective-permute-start(bf16[48,2304]{1,0:T(8,128)(2,1)S(1)} %conv_border.1.after_ref.own_ref), channel_id=1, source_target_pairs={{0,2},{1,3},{2,0},{3,1},{4,6},{5,7},{6,4},{7,5},{8,10},{9,11},{10,... | collective-permute-start | bytes 663560 | tf_op jit(solution)/shard_map/ppermute | solution.py:581
  22.3 4.3 %collective-permute-start = (bf16[48,2304]{1,0:T(8,128)(2,1)S(1)}, bf16[48,2304]{1,0:T(8,128)(2,1)S(1)}, u32[]{:S(2)}, u32[]{:S(2)}) collective-permute-start(bf16[48,2304]{1,0:T(8,128)(2,1)S(1)} %conv_border.1.after_ref.own_ref), channel_id=1, source_target_pairs={{0,1},{1,0},{2,3},{3,2},{4,5},{5,4},{6,7},{7,6},{8,9},{9,8},{10,11... | collective-permute-start | bytes 663560 | tf_op jit(solution)/shard_map/ppermute | solution.py:582
  22.4 5.7 %copy-start.1 = (bf16[2,192,768]{2,1,0:T(8,128)(2,1)S(1)}, bf16[2,192,768]{2,1,0:T(8,128)(2,1)}, u32[]{:S(2)}) copy-start(bf16[2,192,768]{2,1,0:T(8,128)(2,1)} %down_ref.3) | copy-start | bytes 1769476
  22.4 5.7 %copy-start.4 = (s32[1,2304]{1,0:T(1,128)S(1)}, s32[1,2304]{1,0:T(1,128)}, u32[]{:S(2)}) copy-start(s32[1,2304]{1,0:T(1,128)} %mask_ref.3) | copy-start | bytes 27652
  22.4 5.7 %copy-start.13 = (bf16[768,384]{1,0:T(8,128)(2,1)S(1)}, bf16[768,384]{1,0:T(8,128)(2,1)}, u32[]{:S(2)}) copy-start(bf16[768,384]{1,0:T(8,128)(2,1)} %constant.11.clone.pack_ref) | copy-start | bytes 1769476
  22.4 5.6 %copy-start.16 = (bf16[384,128]{1,0:T(8,128)(2,1)S(1)}, bf16[384,128]{1,0:T(8,128)(2,1)}, u32[]{:S(2)}) copy-start(bf16[384,128]{1,0:T(8,128)(2,1)} %constant.10.clone.pool_ref) | copy-start | bytes 294916
  26.6 16.6 %copy-start.14 = (bf16[256,768]{1,0:T(8,128)(2,1)S(1)}, bf16[256,768]{1,0:T(8,128)(2,1)}, u32[]{:S(2)}) copy-start(bf16[256,768]{1,0:T(8,128)(2,1)} %constant.9.clone.sides_ref) | copy-start | bytes 1179652
  26.6 16.6 %copy-start.15 = (bf16[3,384,128]{2,1,0:T(8,128)(2,1)S(1)}, bf16[3,384,128]{2,1,0:T(8,128)(2,1)}, u32[]{:S(2)}) copy-start(bf16[3,384,128]{2,1,0:T(8,128)(2,1)} %constant.8.clone.halo_ref) | copy-start | bytes 884740
  26.6 1.5 %collective-permute-start.2 = (bf16[48,2304]{1,0:T(8,128)(2,1)S(1)}, bf16[48,2304]{1,0:T(8,128)(2,1)S(1)}, u32[]{:S(2)}, u32[]{:S(2)}) collective-permute-start(bf16[48,2304]{1,0:T(8,128)(2,1)S(1)} %collective-permute-done.1.p2_ref), channel_id=1, source_target_pairs={{0,1},{1,0},{2,3},{3,2},{4,5},{5,4},{6,7},{7,6},{8,9},{9,8},{10,11... | collective-permute-start | bytes 663560 | tf_op jit(solution)/shard_map/ppermute | solution.py:584
  45.0 4.4 %collective-permute-start.4 = (bf16[48,768]{1,0:T(8,128)(2,1)S(1)}, bf16[48,768]{1,0:T(8,128)(2,1)S(1)}, u32[]{:S(2)}, u32[]{:S(2)}) collective-permute-start(bf16[48,768]{1,0:T(8,128)(2,1)S(1)} %conv_coarse.1.own_ref), channel_id=1, source_target_pairs={{0,2},{1,3},{2,0},{3,1},{4,6},{5,7},{6,4},{7,5},{8,10},{9,11},{10,... | collective-permute-start | bytes 221192 | tf_op jit(solution)/shard_map/ppermute | solution.py:581
  46.5 2.9 %collective-permute-start.3 = (bf16[48,768]{1,0:T(8,128)(2,1)S(1)}, bf16[48,768]{1,0:T(8,128)(2,1)S(1)}, u32[]{:S(2)}, u32[]{:S(2)}) collective-permute-start(bf16[48,768]{1,0:T(8,128)(2,1)S(1)} %conv_coarse.1.own_ref), channel_id=1, source_target_pairs={{0,1},{1,0},{2,3},{3,2},{4,5},{5,4},{6,7},{7,6},{8,9},{9,8},{10,11... | collective-permute-start | bytes 221192 | tf_op jit(solution)/shard_map/ppermute | solution.py:582
  49.4 1.3 %collective-permute-start.5 = (bf16[48,768]{1,0:T(8,128)(2,1)S(1)}, bf16[48,768]{1,0:T(8,128)(2,1)S(1)}, u32[]{:S(2)}, u32[]{:S(2)}) collective-permute-start(bf16[48,768]{1,0:T(8,128)(2,1)S(1)} %collective-permute-done.4.p2_ref), channel_id=1, source_target_pairs={{0,1},{1,0},{2,3},{3,2},{4,5},{5,4},{6,7},{7,6},{8,9},{9,8},{10,11... | collective-permute-start | bytes 221192 | tf_op jit(solution)/shard_map/ppermute | solution.py:584

commit v7 on v6

--- a/solution.py
+++ b/solution.py
@@ -13,7 +13,8 @@
 GROUPS = 6
 ROWS = 48
 FINE_IN = 8 * TILE
-FINE_PAD = 8 * 64
+RIM = 1280
+MIDDLE = 1024
 BANDS = ((-1, -1), (-1, 0), (-1, 1), (0, -1), (0, 1), (1, -1), (1, 0), (1, 1))
 norm_eps = 1e-06
 BF = jnp.bfloat16
@@ -27,43 +28,21 @@
     return table.astype(ml_dtypes.bfloat16)
 
 
-def side_target(side, row, col, width, stride):
-    if side == 0:
-        return row * stride + 3 + col
-    if side == -1:
-        return row * stride + col - (width - 3) if col >= width - 3 else None
-    return row * stride + 3 + width + col if col < 3 else None
-
-
-def halo_pairs(cells, width, stride, first_row, flipped):
-    block = max(lane for lane, _ in cells) // 128 * 128 + 128
-    pairs = []
-    for place, side in enumerate((-1, 0, 1)):
-        for lane, index in cells:
-            row, col = index // width, index % width
-            if flipped:
-                row, col = 2 - row, width - 1 - col
-            target = side_target(side, row + first_row, col, width, stride)
-            if target is not None:
-                pairs.append((place * block + lane, target))
-    return pairs
-
-
-def pool_table():
-    pairs = [(row * 48 + col, (row // 2) * 32 + 3 + col // 2) for row in range(8) for col in range(48)]
-    return one_hot((384, 128), pairs)
-
-
-def coarse_tables():
-    strip = [(t, t) for t in range(72)]
-    halo = np.stack(
-        [
-            one_hot((384, 128), halo_pairs(strip, HALF, 32, 1, False)),
-            one_hot((384, 128), halo_pairs(strip, HALF, 32, 0, False)),
-            one_hot((384, 128), halo_pairs(strip, HALF, 32, 0, True)),
-        ]
-    )
-    pack, sides = [], []
+def pool_tables():
+    dense, rim, middle = [], [], []
+    for row in range(8):
+        for col in range(48):
+            target = (row // 2) * 32 + 3 + col // 2
+            dense.append((row * 48 + col, target))
+            if 8 <= col < 40:
+                middle.append((row * 32 + col - 8, target))
+            else:
+                rim.append((row * 16 + (col if col < 8 else col - 32), target))
+    return one_hot((384, 128), dense), one_hot((128, 128), rim), one_hot((256, 128), middle)
+
+
+def strip_pairs():
+    pack = []
     for row in range(3):
         for col in range(HALF):
             pack.append((row * 32 + 3 + col, row * 24 + col))
@@ -74,17 +53,11 @@
             lane = 72 + index if row < 16 else index - 48
             pack.append((row * 32 + 3 + j, lane if row < 16 else 256 + lane))
             pack.append((row * 32 + 24 + j, 128 + lane if row < 16 else 256 + 64 + lane))
-            sides.append((lane, row * 32 + j))
-            sides.append((128 + lane, row * 32 + 27 + j))
-    return {
-        "halo": halo,
-        "pack": one_hot((768, 384), pack),
-        "sides": one_hot((256, 768), sides),
-    }
-
-
-POOL = pool_table()
-COARSE = coarse_tables()
+    return pack
+
+
+POOL, RIM_POOL, MIDDLE_POOL = pool_tables()
+SMALL_PACK = one_hot((768, 384), strip_pairs())
 
 
 def dot(left, right):
@@ -270,15 +243,61 @@
         return carry
 
     lax.fori_loop(0, ROWS // 8, group, 0)
-    cells = [128 * m + lane for m in range(3)]
-    indices = [tall((cell // 48) % 2 * 64 + 3 + cell % 48) for cell in cells]
-    for i in range(GROUPS):
-        tiles = [total_ref[:, 512 * i + 128 * k : 512 * i + 128 * k + 128] for k in range(4)]
-        for m in range(3):
-            value = jnp.where(
-                tall(cells[m] < 96 * (m + 1)), lanes_from(tiles[m], indices[m]), lanes_from(tiles[m + 1], indices[m])
-            )
-            sum_ref[:, 384 * i + 128 * m : 384 * i + 128 * m + 128] = value
+    for m in range((RIM + MIDDLE) // 128):
+        row, col = place_of(m)
+        index = tall(row % 2 * 64 + 3 + col)
+        value = None
+        for pair in pairs_of(m):
+            picked = lanes_from(total_ref[:, 128 * pair : 128 * pair + 128], index)
+            value = picked if value is None else jnp.where(tall(row // 2 == pair), picked, value)
+        sum_ref[:, 128 * m : 128 * m + 128] = value
+
+
+def place_of(m):
+    lane = lane_ids((8, 128))
+    if m < 6:
+        cell = 128 * (m % 3) + lane
+        return cell // 48 + (40 if m >= 3 else 0), cell % 48
+    if m < 10:
+        col = lane % 16
+        return 8 * (m - 5) + lane // 16, jnp.where(col < 8, col, col + 32)
+    return 8 + 4 * (m - 10) + lane // 32, 8 + lane % 32
+
+
+def pairs_of(m):
+    if m < 6:
+        first = 128 * (m % 3)
+        start = 20 if m >= 3 else 0
+        return range(start + first // 96, start + (first + 127) // 96 + 1)
+    if m < 10:
+        return range(4 * (m - 5), 4 * (m - 5) + 4)
+    return range(4 + 2 * (m - 10), 6 + 2 * (m - 10))
+
+
+def column_sums(beside, tap):
+    low_half = tall(lane_ids((8, 128)) < 64)
+    total = [jnp.zeros((ROWS, 128), F32)] * 3
+    for a in range(7):
+        weights = [jnp.where(low_half, tap(a, b), tap(a, 6 - b)) for b in range(3)]
+        for q in range(3):
+            partial = weights[0] * beside[q]
+            for j in range(q + 1, 3):
+                partial = partial + weights[j - q] * beside[j]
+            total[q] = total[q] + (pltpu.roll(partial, (3 - a) % 128, 1) if a != 3 else partial)
+    return total
+
+
+def row_sums(uses, tap):
+    places = 1 + max(place for place, _, _ in uses)
+    total = [jnp.zeros((ROWS, 128), F32)] * places
+    for b in range(7):
+        partial = [None] * places
+        for place, a, cells in uses:
+            term = tap(a, b) * cells
+            partial[place] = term if partial[place] is None else partial[place] + term
+        for place in range(places):
+            total[place] = total[place] + (pltpu.roll(partial[place], (3 - b) % 128, 1) if b != 3 else partial[place])
+    return total
 
 
 def conv_border(tab_ref, recv_ref, sum_ref, wide_ref, out_ref):
@@ -313,27 +332,16 @@
             tiles.append(jnp.where(tall((within < 54) & (row < 3)), value, 0.0))
         return tiles
 
-    def row_fix(uses):
-        total = [jnp.zeros((ROWS, 128), F32)] * 2
-        for b in range(7):
-            partial = [None, None]
-            for place, a, cells in uses:
-                term = tap(a, b) * cells
-                partial[place] = term if partial[place] is None else partial[place] + term
-            for place in range(2):
-                total[place] = total[place] + (pltpu.roll(partial[place], (3 - b) % 128, 1) if b != 3 else partial[place])
-        return total
-
     def joined(first, second):
         return jnp.where(low_half, pltpu.roll(first, 64, 1), pltpu.roll(second, 64, 1))
 
     zeros = jnp.zeros((ROWS, 128), F32)
     below = halo_rows((0, 1, 2), False, True)
-    first_fix = row_fix(((0, 0, below[0]), (0, 1, joined(below[0], below[1])), (0, 2, below[1]), (1, 0, below[1])))
+    first_fix = row_sums(((0, 0, below[0]), (0, 1, joined(below[0], below[1])), (0, 2, below[1]), (1, 0, below[1])), tap)
     folded = tab_ref[8] == 2
     above = halo_rows((5, 6, 7), folded, folded)
     edge = joined(zeros, above[0])
-    last_fix = row_fix(((0, 6, edge), (1, 4, edge), (1, 5, above[0]), (1, 6, joined(above[0], above[1]))))
+    last_fix = row_sums(((0, 6, edge), (1, 4, edge), (1, 5, above[0]), (1, 6, joined(above[0], above[1]))), tap)
 
     left, right = band_cells(3, 128), band_cells(4, 128)
     beside = []
@@ -345,38 +353,28 @@
             jnp.where(tall(within < 40), lanes_from(main, main_index), lanes_from(rest, rest_index)) for main, rest in (left, right)
         ]
         beside.append(jnp.where(tall(within < 48), jnp.where(low_half, picked[0], picked[1]), 0.0))
-    column_fix = [zeros] * 3
-    for a in range(7):
-        weights = [jnp.where(low_half, tap(a, b), tap(a, 6 - b)) for b in range(3)]
-        for q in range(3):
-            partial = weights[0] * beside[q]
-            for j in range(q + 1, 3):
-                partial = partial + weights[j - q] * beside[j]
-            column_fix[q] = column_fix[q] + (pltpu.roll(partial, (3 - a) % 128, 1) if a != 3 else partial)
-
-    for m in range(TILE * TILE // 128):
-        cell = 128 * m + lane
-        row, col = cell // 48, cell % 48
-        index = tall(jnp.where(col < 24, row, 64 + row))
+    column_fix = column_sums(beside, tap)
+    fixes = {0: first_fix[0], 1: first_fix[1], 22: last_fix[0], 23: last_fix[1]}
+    for m in range((RIM + MIDDLE) // 128):
         value = sum_ref[:, 128 * m : 128 * m + 128]
-        fix = zeros
-        for q in range(3):
-            fix = jnp.where(tall((col == q) | (col == 47 - q)), lanes_from(column_fix[q], index), fix)
-        value = value + fix
-        row_index = tall(row % 2 * 64 + 3 + col)
-        for pair, tile in ((0, first_fix[0]), (1, first_fix[1]), (22, last_fix[0]), (23, last_fix[1])):
-            if 96 * pair < 128 * m + 128 and 96 * pair + 96 > 128 * m:
-                value = value + jnp.where(tall(row // 2 == pair), lanes_from(tile, row_index), 0.0)
+        if m < RIM // 128:
+            row, col = place_of(m)
+            index = tall(jnp.where(col < 24, row, 64 + row))
+            fix = zeros
+            for q in range(3):
+                fix = jnp.where(tall((col == q) | (col == 47 - q)), lanes_from(column_fix[q], index), fix)
+            value = value + fix
+            row_index = tall(row % 2 * 64 + 3 + col)
+            for pair in pairs_of(m):
+                if pair in fixes:
+                    value = value + jnp.where(tall(row // 2 == pair), lanes_from(fixes[pair], row_index), 0.0)
         out_ref[:, 128 * m : 128 * m + 128] = value.astype(BF)
 
 
 def params(
-    after_ref, weight_ref, bias_ref, gain_ref, shift_ref, up_ref, up_bias_ref, down_bias_ref, scale_ref, pool_weight_ref, spread_weight_ref,
-    taps_ref, conv_bias_ref, gains_ref, shifts_ref, ups_ref, down_biases_ref, scales_ref, pool_cells_ref, spread_cells_ref,
+    after_ref, x_ref, mask_ref, gain_ref, shift_ref, up_ref, up_bias_ref, down_bias_ref, scale_ref, pool_weight_ref, spread_weight_ref, pool_ref,
+    cells_ref, cell_mask_ref, small_mask_ref, gains_ref, shifts_ref, ups_ref, down_biases_ref, scales_ref, pool_cells_ref, spread_cells_ref,
 ):
-    for tap in range(49):
-        taps_ref[tap] = jnp.broadcast_to(weight_ref[1, :, tap : tap + 1], (ROWS, 128))
-    conv_bias_ref[...] = columns(bias_ref[1:2, :])
     me = lax.axis_index("chan")
     for level in range(2):
         row = slice(level, level + 1)
@@ -389,38 +387,68 @@
         for k in range(1, down_bias.shape[0] // ROWS):
             own = jnp.where(me == k, down_bias[k * ROWS : (k + 1) * ROWS], own)
         down_biases_ref[level] = own
-    pool_cells_ref[...] = cell_weights(pool_weight_ref)
-    spread_cells_ref[...] = cell_weights(spread_weight_ref)
-
-
-def conv_coarse(tab_ref, x_ref, recv_ref, halo_ref, sides_ref, wide_ref, bias_ref, out_ref, pad_ref, sum_ref):
+    lane = lane_ids((ROWS, FINE_IN))
+    pool_cells_ref[:, 0:384] = cell_weights(pool_weight_ref, lane // 48, lane % 48)
     lane = lane_ids((ROWS, 128))
-
-    def main_of(source, scale):
-        parts = [recv_ref[source, :, 128 * g : 128 * g + 128] for g in range(3)]
-        return jnp.concatenate(parts, axis=0).astype(F32) * scale
-
-    def row_strips(bands):
-        pieces = []
-        for band in bands:
-            source, scale = band_source(tab_ref, band)
-            pieces.append(main_of(source, scale).astype(BF))
-        return jnp.concatenate(pieces, axis=1)
-
-    pad_ref[0, :, 0:128] = dot(row_strips((0, 1, 2)), halo_ref[0])
-    pad_ref[0, :, 896:1024] = dot(row_strips((5, 6, 7)), halo_ref[tab_ref[8]])
-    pieces = []
-    for band in (3, 4):
-        source, scale = band_source(tab_ref, band)
-        rest = recv_ref[source, :, 384:512].astype(F32) * scale
-        rest = jnp.concatenate([rest, pltpu.roll(rest, 128 - 24, 1), pltpu.roll(rest, 128 - 48, 1)], axis=0)
-        main = main_of(source, scale)
-        pieces.append(jnp.where(lane < 24, rest, main).astype(BF))
-    pad_ref[0, :, 128:896] = dot(jnp.concatenate(pieces, axis=1), sides_ref[...]) + x_ref[...].astype(F32)
+    pool_cells_ref[:, 384:512] = cell_weights(pool_weight_ref, lane // 16, lane)
+    pool_cells_ref[:, 512:640] = cell_weights(pool_weight_ref, lane // 32, lane)
+    lane = lane_ids((ROWS, FINE_IN))
+    spread_cells_ref[...] = cell_weights(spread_weight_ref, lane // 48, lane % 48)
+
+    masks = []
+    for i in range(GROUPS):
+        masks.append(jnp.broadcast_to(mask_ref[:, i * FINE_IN : (i + 1) * FINE_IN].astype(F32), (8, FINE_IN)))
+    counts = dot(jnp.concatenate(masks, axis=0).astype(BF), pool_ref[...])
+    small_mask_ref[...] = jnp.where(counts > 0.5, 1.0, 0.0)
+    for m in range((RIM + MIDDLE) // 128):
+        here = slice(128 * m, 128 * m + 128)
+        if m < 6:
+            source = 128 * (m if m < 3 else m + 12)
+            cells_ref[:, here] = x_ref[0, :, source : source + 128]
+            cell_mask_ref[:, here] = jnp.broadcast_to(mask_ref[:, source : source + 128].astype(F32), (8, 128))
+            continue
+        row, col = place_of(m)
+        cell = row * 48 + col
+        first, final = (8 * (m - 5) * 48, 8 * (m - 4) * 48 - 1) if m < 10 else ((4 * m - 32) * 48 + 8, (4 * m - 29) * 48 + 39)
+        index, value, mask = cell % 128, None, None
+        for tile in range(first // 128, final // 128 + 1):
+            lanes = slice(128 * tile, 128 * tile + 128)
+            part = lanes_from(x_ref[0, :, lanes].astype(F32), tall(index))
+            mask_part = lanes_from(jnp.broadcast_to(mask_ref[:, lanes].astype(F32), (8, 128)), index)
+            value = part if value is None else jnp.where(tall(cell // 128 == tile), part, value)
+            mask = mask_part if mask is None else jnp.where(cell // 128 == tile, mask_part, mask)
+        cells_ref[:, here] = value.astype(BF)
+        cell_mask_ref[:, here] = mask
+
+
+def in_rows(rim_ref, middle_ref, out_ref):
+    out_ref[:, 0:FINE_IN] = rim_ref[:, 0:FINE_IN]
+    out_ref[:, 5 * FINE_IN :] = rim_ref[:, FINE_IN : 2 * FINE_IN]
+    for i in range(1, 5):
+        rim = rim_ref[:, 768 + 128 * (i - 1) : 768 + 128 * i].astype(F32)
+        middle = [middle_ref[:, 256 * (i - 1) + 128 * h : 256 * (i - 1) + 128 * h + 128].astype(F32) for h in range(2)]
+        for m in range(3):
+            cell = 128 * m + lane_ids((8, 128))
+            row, col = cell // 48, cell % 48
+            value = lanes_from(rim, tall((row * 16 + jnp.where(col < 8, col, col - 32)) & 127))
+            in_middle = (col >= 8) & (col < 40)
+            index = tall((row % 4 * 32 + col - 8) & 127)
+            for h in range(2):
+                if 192 * h < 128 * m + 128 and 192 * h + 192 > 128 * m:
+                    value = jnp.where(tall(in_middle & (row // 4 == h)), lanes_from(middle[h], index), value)
+            out_ref[:, i * FINE_IN + 128 * m : i * FINE_IN + 128 * m + 128] = value.astype(BF)
+
+
+def conv_coarse(x_ref, weight_ref, bias_ref, sum_ref, wide_ref, pad_ref):
+    for tap in range(49):
+        wide_ref[tap] = jnp.broadcast_to(weight_ref[1, :, tap : tap + 1], (ROWS, 128))
+    pad_ref[0, :, 0:128] = jnp.zeros((ROWS, 128), F32)
+    pad_ref[0, :, 896:1024] = jnp.zeros((ROWS, 128), F32)
+    pad_ref[0, :, 128:896] = x_ref[...].astype(F32)
     padded = pad_ref[0]
     for turn in range(1, 4):
         pad_ref[turn] = lane_shifted(padded, 32 * turn)
-    sum_ref[...] = wide(bias_ref[...], 768)
+    sum_ref[...] = wide(columns(bias_ref[1:2, :]), 768)
 
     def group(g, carry):
         rows = pl.ds(pl.multiple_of(g * 8, 8), 8)
@@ -443,7 +471,65 @@
         return carry
 
     lax.fori_loop(0, 6, group, 0)
-    out_ref[...] = sum_ref[...].astype(BF)
+
+
+def border_coarse(tab_ref, recv_ref, sum_ref, wide_ref, out_ref):
+    lane = lane_ids((8, 128))
+    half, within, segment, inside = lane // 64, lane % 64, lane // 32, lane % 32
+
+    def tap(a, b):
+        return wide_ref[a * 7 + b]
+
+    def band_main(band):
+        source, scale = band_source(tab_ref, band)
+        return jnp.concatenate([recv_ref[source, :, 128 * g : 128 * g + 128] for g in range(3)], axis=0).astype(F32) * scale
+
+    def band_rest(band):
+        source, scale = band_source(tab_ref, band)
+        rest = recv_ref[source, :, 384:512].astype(F32) * scale
+        return jnp.concatenate([rest, pltpu.roll(rest, 128 - 24, 1), pltpu.roll(rest, 128 - 48, 1)], axis=0)
+
+    def halo_rows(bands, folded):
+        col = jnp.where(inside < 3, 21 + inside, jnp.where(inside < 27, inside - 3, inside - 27))
+        index = segment * 24 + col
+        index = tall(jnp.where(folded, 71 - index, index) & 127)
+        picked = [lanes_from(band_main(band), index) for band in bands]
+        value = jnp.where(tall(inside < 3), picked[0], jnp.where(tall(inside < 27), picked[1], picked[2]))
+        return jnp.where(tall((inside < 30) & (segment < 3)), value, 0.0)
+
+    def turned(cells, lanes, kept):
+        return jnp.where(tall(kept), pltpu.roll(cells, lanes, 1), 0.0)
+
+    below = halo_rows((0, 1, 2), False)
+    first_fix = row_sums(((0, 0, below), (0, 1, turned(below, 96, lane < 64)), (0, 2, turned(below, 64, lane < 32))), tap)[0]
+    above = halo_rows((5, 6, 7), tab_ref[8] == 2)
+    last_fix = row_sums(
+        ((0, 6, turned(above, 32, lane >= 32)), (0, 5, turned(above, 64, lane >= 64)), (0, 4, turned(above, 96, lane >= 96))), tap
+    )[0]
+    sides = [(band_main(band), band_rest(band)) for band in (3, 4)]
+    beside = []
+    for j in range(3):
+        which = jnp.where(half == 0, j, 2 - j)
+        main_index = tall(jnp.minimum(72 + 3 * within + which, 127))
+        rest_index = tall(jnp.clip(3 * (within - 16) + which, 0, 127))
+        picked = [
+            jnp.where(tall(within < 16), lanes_from(main, main_index), lanes_from(rest, rest_index)) for main, rest in sides
+        ]
+        beside.append(jnp.where(tall(within < HALF), jnp.where(tall(half == 0), picked[0], picked[1]), 0.0))
+    column_fix = column_sums(beside, tap)
+    for m in range(GROUPS):
+        row, col = 4 * m + segment, inside - 3
+        index = tall(jnp.where(col < 12, row, 64 + row))
+        value = sum_ref[:, 128 * m : 128 * m + 128]
+        fix = jnp.zeros((ROWS, 128), F32)
+        for q in range(3):
+            fix = jnp.where(tall((col == q) | (col == 23 - q)), lanes_from(column_fix[q], index), fix)
+        value = value + fix
+        if m == 0:
+            value = value + first_fix
+        if m == GROUPS - 1:
+            value = value + last_fix
+        out_ref[:, 128 * m : 128 * m + 128] = value.astype(BF)
 
 
 def gather_rows(pieces, cat_ref):
@@ -470,49 +556,47 @@
     return branch
 
 
-def cell_weights(weight_ref):
-    lane = lane_ids((ROWS, FINE_IN))
-    odd_row = (lane // TILE) % 2
-    odd_col = (lane % TILE) % 2
-    kind = 2 * odd_row + odd_col
-    result = jnp.zeros((ROWS, FINE_IN), F32)
+def cell_weights(weight_ref, row, col):
+    kind = 2 * (row % 2) + col % 2
+    result = jnp.zeros(row.shape, F32)
     for k in range(4):
         result = jnp.where(kind == k, weight_ref[:, k : k + 1], result)
     return result
 
 
-def make_mix_fine(count):
-    def mix_fine(
-        tab_ref, own_ref, p1_ref, p2_ref, p3_ref, x_ref, mask_ref,
-        gain_ref, shift_ref, up_ref, down_ref, down_bias_ref, scale_ref, pool_cells_ref, pool_ref, pack_ref,
-        fine_ref, pooled_ref, small_mask_ref, msg_ref, cat_ref, mains_ref, rest_ref,
+def pooled_cells(products, table):
+    highs = [product.astype(BF) for product in products]
+    lows = [(product - high.astype(F32)).astype(BF) for product, high in zip(products, highs)]
+    return dot(jnp.concatenate(highs, axis=0), table) + dot(jnp.concatenate(lows, axis=0), table)
+
+
+def make_mix_rim(count):
+    def mix_rim(
+        tab_ref, own_ref, p1_ref, p2_ref, p3_ref, x_ref, mask_ref, gain_ref, shift_ref, up_ref, down_ref, down_bias_ref, scale_ref,
+        pool_cells_ref, pool_ref, rim_pool_ref, pack_ref,
+        fine_ref, pooled_ref, msg_ref, middle_ref, cat_ref, mains_ref, rest_ref,
     ):
-        gather_rows((own_ref, p1_ref, p2_ref, p3_ref), cat_ref)
-        block = 768
+        me = lax.axis_index("chan")
+        for k, piece in enumerate((own_ref, p1_ref, p2_ref, p3_ref)):
+            here = pl.ds(pl.multiple_of(lax.bitwise_xor(me, k) * ROWS, 16), ROWS)
+            cat_ref[here, :] = piece[:, 0:RIM]
+            middle_ref[here, :] = piece[:, RIM:]
+        block = RIM // 2
         branch = make_branch(0, cat_ref, gain_ref, shift_ref, up_ref, down_ref, down_bias_ref, block)
         scale = wide(scale_ref[0], block)
-
-        for start in range(0, TILE * TILE, block):
+        for start in range(0, RIM, block):
             here = slice(start, start + block)
-            value = x_ref[0, :, here].astype(F32) + scale * branch(start)
-            fine_ref[:, here] = (mask_ref[:, here].astype(F32) * value).astype(BF)
-
-        weights = pool_cells_ref[...]
-        highs, lows, masks = [], [], []
-        for i in range(GROUPS):
-            lanes = slice(i * FINE_IN, (i + 1) * FINE_IN)
-            product = fine_ref[:, lanes].astype(F32) * weights
-            high = product.astype(BF)
-            highs.append(high)
-            lows.append((product - high.astype(F32)).astype(BF))
-            masks.append(jnp.broadcast_to(mask_ref[:, lanes].astype(F32), (8, FINE_IN)))
-        pool_table = pool_ref[...]
-        pooled = dot(jnp.concatenate(highs, axis=0), pool_table) + dot(jnp.concatenate(lows, axis=0), pool_table)
-        pooled = pooled.astype(BF)
-        for i in range(GROUPS):
-            pooled_ref[:, i * 128 : (i + 1) * 128] = pooled[i * ROWS : (i + 1) * ROWS]
-        counts = dot(jnp.concatenate(masks, axis=0).astype(BF), pool_table)
-        small_mask_ref[...] = jnp.where(counts > 0.5, 1.0, 0.0)
+            value = x_ref[:, here].astype(F32) + scale * branch(start)
+            fine_ref[:, here] = (mask_ref[0:1, here] * value).astype(BF)
+
+        weights = pool_cells_ref[:, 0:384]
+        whole = pooled_cells([fine_ref[:, start : start + 384].astype(F32) * weights for start in (0, 384)], pool_ref[...])
+        weights = pool_cells_ref[:, 384:512]
+        rim = pooled_cells([fine_ref[:, 768 + 128 * i : 896 + 128 * i].astype(F32) * weights for i in range(4)], rim_pool_ref[...])
+        pooled_ref[:, 0:128] = whole[0:ROWS].astype(BF)
+        pooled_ref[:, 640:768] = whole[ROWS : 2 * ROWS].astype(BF)
+        for i in range(4):
+            pooled_ref[:, 128 * i + 128 : 128 * i + 256] = rim[i * ROWS : (i + 1) * ROWS].astype(BF)
 
         packed = dot(pooled_ref[...], pack_ref[...])
         lane = lane_ids((ROWS, 128))
@@ -530,15 +614,33 @@
 
         def fill(dev, carry):
             both = tab_ref[16 + dev]
-            col_pick = lax.rem(both, 2)
             for g in range(3):
                 msg_ref[dev, :, 128 * g : 128 * g + 128] = mains_ref[both, 16 * g : 16 * g + 16, :]
-            msg_ref[dev, :, 384:512] = rest_ref[col_pick]
+            msg_ref[dev, :, 384:512] = rest_ref[lax.bitwise_and(both, 1)]
             return carry
 
         scan_tiles(count, fill, jnp.int32(0))
 
-    return mix_fine
+    return mix_rim
+
+
+def mix_middle(
+    cat_ref, x_ref, mask_ref, gain_ref, shift_ref, up_ref, down_ref, down_bias_ref, scale_ref, pool_cells_ref, middle_pool_ref, rim_ref,
+    fine_ref, pooled_ref,
+):
+    block = MIDDLE // 2
+    branch = make_branch(0, cat_ref, gain_ref, shift_ref, up_ref, down_ref, down_bias_ref, block)
+    scale = wide(scale_ref[0], block)
+    for start in range(0, MIDDLE, block):
+        here, there = slice(start, start + block), slice(RIM + start, RIM + start + block)
+        value = x_ref[:, there].astype(F32) + scale * branch(start)
+        fine_ref[:, here] = (mask_ref[0:1, there] * value).astype(BF)
+    weights = wide(pool_cells_ref[:, 512:640], 256)
+    middle = pooled_cells([fine_ref[:, 256 * i : 256 * i + 256].astype(F32) * weights for i in range(4)], middle_pool_ref[...])
+    pooled_ref[...] = rim_ref[...]
+    for i in range(4):
+        here = slice(128 * i + 128, 128 * i + 256)
+        pooled_ref[:, here] = (rim_ref[:, here].astype(F32) + middle[i * ROWS : (i + 1) * ROWS].astype(BF).astype(F32)).astype(BF)
 
 
 def mix_coarse(
@@ -610,16 +712,7 @@
         cost_estimate=takes(10),
         name="prep",
     )(wet_slots, device_of, features, pack)
-    held = {
-        "x": features,
-        "mask": land_mask,
-        "weight": depth_weight,
-        "bias": depth_bias,
-        "small_halo": jnp.asarray(COARSE["halo"]),
-        "sides": jnp.asarray(COARSE["sides"]),
-        "pool": jnp.asarray(POOL),
-        "small_pack": jnp.asarray(COARSE["pack"]),
-    }
+    pool = jnp.asarray(POOL)
     arrived = lax.all_to_all(messages, "tile", 0, 0, tiled=True)
     inner, fine_taps = pl.pallas_call(
         lambda tab_ref, *refs: conv_inner(*refs),
@@ -634,7 +727,7 @@
         compiler_params=PARAMS,
         cost_estimate=takes(4),
         name="conv_inner",
-    )(table, held["x"], held["weight"], held["bias"])
+    )(table, features, depth_weight, depth_bias)
     conv = pl.pallas_call(
         conv_border,
         in_specs=[SMEM] + [VMEM] * 3,
@@ -648,54 +741,87 @@
     def spread_params(own):
         return pl.pallas_call(
             params,
-            in_specs=[VMEM] * 11,
-            out_specs=[VMEM] * 9,
+            in_specs=[VMEM] * 12,
+            out_specs=[VMEM] * 10,
             out_shape=[
                 shaped(*shape, dtype=dtype)
                 for shape, dtype in (
-                    ((49, ROWS, 128), F32), ((ROWS, 128), F32), ((2, 192, 128), F32), ((2, 192, 128), F32), ((2, up_weight.shape[1], up_weight.shape[2] + 16), BF),
-                    ((2, ROWS, 128), F32), ((2, ROWS, 128), F32), ((ROWS, FINE_IN), F32), ((ROWS, FINE_IN), F32),
+                    ((ROWS, cells), BF), ((8, cells), F32), ((48, 128), F32), ((2, 192, 128), F32), ((2, 192, 128), F32),
+                    ((2, up_weight.shape[1], up_weight.shape[2] + 16), BF), ((2, ROWS, 128), F32), ((2, ROWS, 128), F32),
+                    ((ROWS, 640), F32), ((ROWS, FINE_IN), F32),
                 )
             ],
             compiler_params=PARAMS,
             cost_estimate=takes(2),
             name="params",
         )(
-            own, depth_weight, depth_bias, norm_gain, norm_bias, jnp.swapaxes(up_weight, 1, 2), up_bias, down_bias, layer_scale,
-            pool_weight, spread_weight,
+            own, features, land_mask, norm_gain, norm_bias, jnp.swapaxes(up_weight, 1, 2), up_bias, down_bias, layer_scale,
+            pool_weight, spread_weight, pool,
         )
 
     pieces, results = every_channel(conv, spread_params)
-    taps, conv_bias, gains, shifts, ups, down_biases, scales, pool_cells, spread_cells = results
-    fine, pooled, small_mask, messages = pl.pallas_call(
-        make_mix_fine(count),
-        in_specs=[SMEM] + [VMEM] * 15,
+    own_cells, own_mask, small_mask, gains, shifts, ups, down_biases, scales, pool_cells, spread_cells = results
+    rim, rim_pooled, messages, middle = pl.pallas_call(
+        make_mix_rim(count),
+        in_specs=[SMEM] + [VMEM] * 16,
         out_specs=[VMEM] * 4,
-        out_shape=[shaped(ROWS, cells), shaped(ROWS, 768), shaped(48, 128, dtype=F32), shaped(count, 16, 512)],
+        out_shape=[shaped(ROWS, RIM), shaped(ROWS, 768), shaped(count, 16, 512), shaped(4 * ROWS, MIDDLE)],
         scratch_shapes=[
-            pltpu.VMEM((4 * ROWS, cells), BF),
+            pltpu.VMEM((4 * ROWS, RIM), BF),
             pltpu.VMEM((4, ROWS, 128), BF),
             pltpu.VMEM((2, 16, 128), BF),
         ],
         compiler_params=PARAMS,
-        cost_estimate=takes(4),
-        name="mix_fine",
+        cost_estimate=takes(3),
+        name="mix_rim",
     )(
-        table, *pieces, held["x"], held["mask"], gains, shifts, ups,
-        down_weight, down_biases, scales, pool_cells, held["pool"], held["small_pack"],
+        table, *pieces, own_cells, own_mask, gains, shifts, ups, down_weight, down_biases, scales, pool_cells, pool,
+        jnp.asarray(RIM_POOL), jnp.asarray(SMALL_PACK),
     )
     arrived = lax.all_to_all(messages, "tile", 0, 0, tiled=True)
-    conv = pl.pallas_call(
+    middle, pooled = pl.pallas_call(
+        mix_middle,
+        in_specs=[VMEM] * 12,
+        out_specs=[VMEM] * 2,
+        out_shape=[shaped(ROWS, MIDDLE), shaped(ROWS, 768)],
+        compiler_params=PARAMS,
+        cost_estimate=takes(2),
+        name="mix_middle",
+    )(
+        middle, own_cells, own_mask, gains, shifts, ups, down_weight, down_biases, scales, pool_cells, jnp.asarray(MIDDLE_POOL), rim_pooled
+    )
+    inner, taps = pl.pallas_call(
         conv_coarse,
-        in_specs=[SMEM] + [VMEM] * 6,
-        out_specs=VMEM,
-        out_shape=shaped(ROWS, 768),
-        scratch_shapes=[pltpu.VMEM((4, ROWS, 1024), F32), pltpu.VMEM((ROWS, 768), F32)],
+        in_specs=[VMEM] * 3,
+        out_specs=[VMEM] * 2,
+        out_shape=[shaped(ROWS, 768, dtype=F32), shaped(49, ROWS, 128, dtype=F32)],
+        scratch_shapes=[pltpu.VMEM((4, ROWS, 1024), F32)],
         compiler_params=PARAMS,
         cost_estimate=takes(2),
         name="conv_coarse",
-    )(table, pooled, arrived, held["small_halo"], held["sides"], taps, conv_bias)
-    pieces, _ = every_channel(conv)
+    )(pooled, depth_weight, depth_bias)
+    conv = pl.pallas_call(
+        border_coarse,
+        in_specs=[SMEM] + [VMEM] * 3,
+        out_specs=VMEM,
+        out_shape=shaped(ROWS, 768),
+        compiler_params=PARAMS,
+        cost_estimate=takes(1),
+        name="border_coarse",
+    )(table, arrived, inner, taps)
+
+    def back_in_rows(own):
+        return pl.pallas_call(
+            lambda after_ref, *refs: in_rows(*refs),
+            in_specs=[VMEM] * 3,
+            out_specs=[VMEM],
+            out_shape=[shaped(ROWS, cells)],
+            compiler_params=PARAMS,
+            cost_estimate=takes(1),
+            name="in_rows",
+        )(own, rim, middle)
+
+    pieces, (fine,) = every_channel(conv, back_in_rows)
     return pl.pallas_call(
         mix_coarse,
         in_specs=[VMEM] * 16,
@@ -706,8 +832,7 @@
         cost_estimate=takes(2),
         name="mix_coarse",
     )(
-        *pieces, pooled, small_mask, fine, held["mask"], gains, shifts, ups, down_weight, down_biases,
-        scales, spread_cells, held["pool"],
+        *pieces, pooled, small_mask, fine, land_mask, gains, shifts, ups, down_weight, down_biases, scales, spread_cells, pool
     )
 
 

time: 52.7 us -> 53 us (level)
  blocking collectives: 11.4 us -> 0 us
  local copies, waits for them, and re-layouts: 1.14 us -> 6.97 us
  starting transfers between devices: 10.4 us -> 14.7 us
  Pallas kernels: 15.8 us -> 17.7 us
  waiting for transfers between devices: 13.5 us -> 12.7 us
    all_to_all x1 -> x0, blocking collectives: 11.4 us -> none  [per_device(): arrived = lax.all_to_all(messages, 'tile', 0, 0, tiled=True)]
    unnamed x40 -> x78, local copies, waits for them, and re-layouts: 1.14 us -> 6.97 us
    all_to_all x1 -> x2, starting transfers between devices: 7.29 us -> 11.6 us  [per_device(): arrived = lax.all_to_all(messages, 'tile', 0, 0, tiled=True)]
    pallas_call x3 -> x6, Pallas kernels: 6.27 us -> 8.38 us  [the longest x1 3.29 us: per_device(): pl.pallas_call(make_mix_rim(count), in_specs=[SMEM] + [VMEM] * 16, out_sp...]
    ppermute x2, waiting for transfers between devices: 6.15 us -> 5.39 us  [every_channel(): across = lax.ppermute(own, 'chan', pairs(2))]
    all_to_all x1 -> x2, waiting for transfers between devices: 4.58 us -> 4.54 us  [per_device(): arrived = lax.all_to_all(messages, 'tile', 0, 0, tiled=True)]
  transfers between devices with their start and end apart: 7 -> 8, of which waited for: 5 -> 5; matrix products, arithmetic and copies ran while one was open for 0% -> 0% of each run, Pallas kernels for 9% -> 15%
where the time goes in v7:
time: 53 us; the launch traced here: 52.4 us
  Pallas kernels  17.7 us (33%)
  starting transfers between devices  14.7 us (28%)
  waiting for transfers between devices  12.7 us (24%)
  local copies, waits for them, and re-layouts  6.97 us (13%)
    all_to_all x2, starting transfers between devices, per_device(): arrived = lax.all_to_all(messages, 'tile', 0, 0, tiled=True)  11.6 us
    unnamed x78, local copies, waits for them, and re-layouts  6.97 us
    ppermute x2, waiting for transfers between devices, every_channel(): across = lax.ppermute(own, 'chan', pairs(2))  5.39 us
    all_to_all x2, waiting for transfers between devices, per_device(): arrived = lax.all_to_all(messages, 'tile', 0, 0, tiled=True)  4.54 us
    pallas_call x1, Pallas kernels, per_device(): pl.pallas_call(lambda tab_ref, *refs: conv_inner(*refs), in_specs=[SMEM]...  3.87 us
    pallas_call x1, Pallas kernels, per_device(): pl.pallas_call(make_mix_rim(count), in_specs=[SMEM] + [VMEM] * 16, out_sp...  3.29 us
    ppermute x2, starting transfers between devices, every_channel(): across = lax.ppermute(own, 'chan', pairs(2))  3.11 us
    ppermute x2, waiting for transfers between devices, every_channel(): diagonal = lax.ppermute(across, 'chan', pairs(1))  2.73 us
  transfers between devices with their start and end apart: 8, of which 5 were waited for; matrix products, arithmetic and copies ran while one was open for 0% of the time, Pallas kernels for 15%

profile of v7, /device:TPU:0, one launch (start us, length us, event | category | flops | bytes accessed | tf_op | source)
XLA Modules:
  0.0 52.4 jit_solution(708635574548366880)
XLA Ops:
  0.0 0.1 strip_table.1.pack_ref
  0.1 0.9 %copy-done.2 = bf16[1,48,2304]{2,1,0:T(8,128)(2,1)S(1)} copy-done((bf16[1,48,2304]{2,1,0:T(8,128)(2,1)S(1)}, bf16[1,48,2304]{2,1,0:T(8,128)(2,1)}, u32[]{:S(2)}) %copy-start.2) | copy-done | bytes 221208
  1.0 1.7 %prep.1 = (bf16[8,16,896]{2,1,0:T(8,128)(2,1)}, s32[24]{0:T(128)S(1)}) custom-call(s32[8]{0:T(128)S(1)} %copy-done.11, s32[8]{0:T(128)S(1)} %copy-done.12, bf16[1,48,2304]{2,1,0:T(8,128)(2,1)S(1)} %copy-done.2, bf16[384,256]{1,0:T(8,128)(2,1)S(1)} %strip_table.1.pack_ref), custom_call_target="tpu_custom_call" | custom-call | flops 10000000000 | tf_op jit(solution)/shard_map/prep/pallas_call | solution.py:700
  2.6 7.3 %all-to-all-start = ((bf16[8,16,896]{2,1,0:T(8,128)(2,1)}), bf16[8,16,896]{2,1,0:T(8,128)(2,1)S(1)}, u32[]{:S(2)}, u32[]{:S(2)}) async-start(bf16[8,16,896]{2,1,0:T(8,128)(2,1)} %get-tuple-element.41), calls=%async_computation | async-start | bytes 458752 | tf_op jit(solution)/shard_map/all_to_all | solution.py:716
  9.9 3.9 %conv_inner.1 = (f32[48,2304]{1,0:T(8,128)S(1)}, f32[49,48,128]{2,1,0:T(8,128)S(1)}) custom-call(s32[24]{0:T(128)S(1)} %get-tuple-element.40.tab_ref, bf16[1,48,2304]{2,1,0:T(8,128)(2,1)S(1)} %copy-done.2, f32[2,48,49]{2,1,0:T(8,128)S(1)} %copy-done.3, f32[2,48]{1,0:T(2,128)S(1)} %copy-done.10), custom_call_target="tpu_custom_call" | custom-call | flops 4000000000 | tf_op jit(solution)/shard_map/conv_inner/pallas_call | solution.py:717
  13.8 4.5 %all-to-all-done.recv_ref = bf16[8,16,896]{2,1,0:T(8,128)(2,1)S(1)} async-done(((bf16[8,16,896]{2,1,0:T(8,128)(2,1)}), bf16[8,16,896]{2,1,0:T(8,128)(2,1)S(1)}, u32[]{:S(2)}, u32[]{:S(2)}) %all-to-all-start) | async-done | bytes 229408 | tf_op jit(solution)/shard_map/all_to_all | solution.py:716
  18.4 0.0 copy-start.14
  18.4 2.0 %conv_border.1.after_ref.own_ref = bf16[48,2304]{1,0:T(8,128)(2,1)S(1)} custom-call(s32[24]{0:T(128)S(1)} %get-tuple-element.40.tab_ref, bf16[8,16,896]{2,1,0:T(8,128)(2,1)S(1)} %all-to-all-done.recv_ref, f32[48,2304]{1,0:T(8,128)S(1)} %get-tuple-element.42.sum_ref, f32[49,48,128]{2,1,0:T(8,128)S(1)} %get-tuple-element.43.wide_ref), custom_call_target="tpu_custom_call" | custom-call | flops 2000000000 | tf_op jit(solution)/shard_map/conv_border/pallas_call | solution.py:731
  20.4 1.6 %collective-permute-start.1 = (bf16[48,2304]{1,0:T(8,128)(2,1)S(1)}, bf16[48,2304]{1,0:T(8,128)(2,1)S(1)}, u32[]{:S(2)}, u32[]{:S(2)}) collective-permute-start(bf16[48,2304]{1,0:T(8,128)(2,1)S(1)} %conv_border.1.after_ref.own_ref), channel_id=1, source_target_pairs={{0,2},{1,3},{2,0},{3,1},{4,6},{5,7},{6,4},{7,5},{8,10},{9,11},{10,... | collective-permute-start | bytes 663560 | tf_op jit(solution)/shard_map/ppermute | solution.py:683
  22.0 0.1 copy.20.pool_weight_ref
  22.1 0.1 copy.21.spread_weight_ref
  22.3 0.0 copy-start.13
  22.3 0.7 %params.1 = (bf16[48,2304]{1,0:T(8,128)(2,1)S(1)}, f32[8,2304]{1,0:T(8,128)S(1)}, f32[48,128]{1,0:T(8,128)S(1)}, f32[2,192,128]{2,1,0:T(8,128)S(1)}, f32[2,192,1...) custom-call(bf16[48,2304]{1,0:T(8,128)(2,1)S(1)} %conv_border.1.afte, ...), custom_call_target="tpu_custom_call" | custom-call | flops 2000000000 | tf_op jit(solution)/shard_map/params/pallas_call | solution.py:742
  23.0 0.6 %copy-done.34 = f32[48,128]{1,0:T(8,128)} copy-done((f32[48,128]{1,0:T(8,128)}, f32[48,128]{1,0:T(8,128)S(1)}, u32[]{:S(2)}) %copy-start.34) | copy-done | bytes 24600
  23.6 2.8 %collective-permute-done.1.p2_ref = bf16[48,2304]{1,0:T(8,128)(2,1)S(1)} collective-permute-done((bf16[48,2304]{1,0:T(8,128)(2,1)S(1)}, bf16[48,2304]{1,0:T(8,128)(2,1)S(1)}, u32[]{:S(2)}, u32[]{:S(2)}) %collective-permute-start.1) | collective-permute-done | bytes 221216 | tf_op jit(solution)/shard_map/ppermute | solution.py:683
  26.4 1.5 %collective-permute-done.2.p3_ref = bf16[48,2304]{1,0:T(8,128)(2,1)S(1)} collective-permute-done((bf16[48,2304]{1,0:T(8,128)(2,1)S(1)}, bf16[48,2304]{1,0:T(8,128)(2,1)S(1)}, u32[]{:S(2)}, u32[]{:S(2)}) %collective-permute-start.2) | collective-permute-done | bytes 221216 | tf_op jit(solution)/shard_map/ppermute | solution.py:686
  27.9 3.3 %mix_rim.1 = (bf16[48,1280]{1,0:T(8,128)(2,1)S(1)}, bf16[48,768]{1,0:T(8,128)(2,1)S(1)}, bf16[8,16,512]{2,1,0:T(8,128)(2,1)}, bf16[192,1024]{1,0:T(8,128)(2,1)S(1)}) custom-call(s32[24]{0:T(128)S(1)} %get-tuple-element.40.tab_ref, bf16[48,2304]{1,0:T(8,128)(2,1)S(1)} %conv_border.1.after_ref.own_ref, bf16[48,2304]{1,0:T(8,128)(2,1)S(1)} %collective-permute-done.p1_ref, ...), custom_call_target="tpu_custom_call" | custom-call | flops 3000000000 | tf_op jit(solution)/shard_map/mix_rim/pallas_call | solution.py:764
  31.2 4.3 %all-to-all-start.1 = ((bf16[8,16,512]{2,1,0:T(8,128)(2,1)}), bf16[8,16,512]{2,1,0:T(8,128)(2,1)S(1)}, u32[]{:S(2)}, u32[]{:S(2)}) async-start(bf16[8,16,512]{2,1,0:T(8,128)(2,1)} %get-tuple-element.63), calls=%async_computation.1 | async-start | bytes 262144 | tf_op jit(solution)/shard_map/all_to_all | solution.py:781
  35.6 0.9 %copy-done.22 = f32[2,192,128]{2,1,0:T(8,128)S(1)} copy-done((f32[2,192,128]{2,1,0:T(8,128)S(1)}, f32[2,192,128]{2,1,0:T(8,128)}, u32[]{:S(2)}) %copy-start.22) | copy-done | bytes 196632
  36.5 0.9 %copy-done.25 = f32[48,640]{1,0:T(8,128)S(1)} copy-done((f32[48,640]{1,0:T(8,128)S(1)}, f32[48,640]{1,0:T(8,128)}, u32[]{:S(2)}) %copy-start.25) | copy-done | bytes 122904
  37.4 0.9 %copy-done.27 = f32[8,2304]{1,0:T(8,128)S(1)} copy-done((f32[8,2304]{1,0:T(8,128)S(1)}, f32[8,2304]{1,0:T(8,128)}, u32[]{:S(2)}) %copy-start.27) | copy-done | bytes 73752
  38.3 0.9 %copy-done.29 = bf16[48,768]{1,0:T(8,128)(2,1)S(1)} copy-done((bf16[48,768]{1,0:T(8,128)(2,1)S(1)}, bf16[48,768]{1,0:T(8,128)(2,1)}, u32[]{:S(2)}) %copy-start.29) | copy-done | bytes 73752
  39.2 0.8 %copy-done.31 = f32[2,48,128]{2,1,0:T(8,128)S(1)} copy-done((f32[2,48,128]{2,1,0:T(8,128)S(1)}, f32[2,48,128]{2,1,0:T(8,128)}, u32[]{:S(2)}) %copy-start.31) | copy-done | bytes 49176
  40.0 0.8 %copy-done.33 = f32[2,48,128]{2,1,0:T(8,128)S(1)} copy-done((f32[2,48,128]{2,1,0:T(8,128)S(1)}, f32[2,48,128]{2,1,0:T(8,128)}, u32[]{:S(2)}) %copy-start.33) | copy-done | bytes 49176
  40.8 1.5 %mix_middle.1 = (bf16[48,1024]{1,0:T(8,128)(2,1)S(1)}, bf16[48,768]{1,0:T(8,128)(2,1)S(1)}) custom-call(bf16[192,1024]{1,0:T(8,128)(2,1)S(1)} %get-tuple-element.64.cat_ref, bf16[48,2304]{1,0:T(8,128)(2,1)S(1)} %get-tuple-element.55.x_ref, f32[8,2304]{1,0:T(8,128)S(1)} %copy-done.27, f32[2,192,128]{2,1,0:T(8,128)S(1)} %get-tuple-element.57.gain_ref, ...), custom_call_target="tpu_custom_call" | custom-call | flops 2000000000 | tf_op jit(solution)/shard_map/mix_middle/pallas_call | solution.py:782
  42.2 1.4 %conv_coarse.1 = (f32[48,768]{1,0:T(8,128)S(1)}, f32[49,48,128]{2,1,0:T(8,128)S(1)}) custom-call(bf16[48,768]{1,0:T(8,128)(2,1)S(1)} %get-tuple-element.66.x_ref.pooled_ref, f32[2,48,49]{2,1,0:T(8,128)S(1)} %copy-done.3, f32[2,48]{1,0:T(2,128)S(1)} %copy-done.10), custom_call_target="tpu_custom_call" | custom-call | flops 2000000000 | tf_op jit(solution)/shard_map/conv_coarse/pallas_call | solution.py:793
  43.6 1.3 %border_coarse.1.after_ref.own_ref = bf16[48,768]{1,0:T(8,128)(2,1)S(1)} custom-call(s32[24]{0:T(128)S(1)} %get-tuple-element.40.tab_ref, bf16[8,16,512]{2,1,0:T(8,128)(2,1)S(1)} %all-to-all-done.1.recv_ref, f32[48,768]{1,0:T(8,128)S(1)} %get-tuple-element.67.sum_ref, f32[49,48,128]{2,1,0:T(8,128)S(1)} %get-tuple-element.68.wide_ref), custom_call_target="tpu_custom_call" | custom-call | flops 1000000000 | tf_op jit(solution)/shard_map/border_coarse/pallas_call | solution.py:803
  45.0 1.6 %collective-permute-start.4 = (bf16[48,768]{1,0:T(8,128)(2,1)S(1)}, bf16[48,768]{1,0:T(8,128)(2,1)S(1)}, u32[]{:S(2)}, u32[]{:S(2)}) collective-permute-start(bf16[48,768]{1,0:T(8,128)(2,1)S(1)} %border_coarse.1.after_ref.own_ref), channel_id=1, source_target_pairs={{0,2},{1,3},{2,0},{3,1},{4,6},{5,7},{6,4},{7,5},{8,10},{9,11},{10,... | collective-permute-start | bytes 221192 | tf_op jit(solution)/shard_map/ppermute | solution.py:683
  46.5 0.2 in_rows.1.fine_ref
  46.8 2.6 %collective-permute-done.4.p2_ref = bf16[48,768]{1,0:T(8,128)(2,1)S(1)} collective-permute-done((bf16[48,768]{1,0:T(8,128)(2,1)S(1)}, bf16[48,768]{1,0:T(8,128)(2,1)S(1)}, u32[]{:S(2)}, u32[]{:S(2)}) %collective-permute-start.4) | collective-permute-done | bytes 73760 | tf_op jit(solution)/shard_map/ppermute | solution.py:683
  49.4 1.3 %collective-permute-done.5.p3_ref = bf16[48,768]{1,0:T(8,128)(2,1)S(1)} collective-permute-done((bf16[48,768]{1,0:T(8,128)(2,1)S(1)}, bf16[48,768]{1,0:T(8,128)(2,1)S(1)}, u32[]{:S(2)}, u32[]{:S(2)}) %collective-permute-start.5) | collective-permute-done | bytes 73760 | tf_op jit(solution)/shard_map/ppermute | solution.py:686
  50.7 1.8 %mix_coarse.1 = bf16[1,48,2304]{2,1,0:T(8,128)(2,1)} custom-call(bf16[48,768]{1,0:T(8,128)(2,1)S(1)} %border_coarse.1.after_ref.own_ref, bf16[48,768]{1,0:T(8,128)(2,1)S(1)} %collective-permute-done.3.p1_ref, bf16[48,768]{1,0:T(8,128)(2,1)S(1)} %collective-permute-done.4.p2_ref, bf16[48,768]{1,0:T(8,128)(2,1)S(1)} %collective-permute-done.5.p3_ref, ...), custom_call_target="tpu_custom_call" | custom-call | flops 2000000000 | tf_op jit(solution)/shard_map/mix_coarse/pallas_call | solution.py:825
  (73 shorter events, 0.2 us)
Async XLA Ops:
  0.9 9.0 %copy-start.3 = (f32[2,48,49]{2,1,0:T(8,128)S(1)}, f32[2,48,49]{2,1,0:T(8,128)}, u32[]{:S(2)}) copy-start(f32[2,48,49]{2,1,0:T(8,128)} %weight_ref.1) | copy-start | bytes 56452
  0.9 9.0 %copy-start.10 = (f32[2,48]{1,0:T(2,128)S(1)}, f32[2,48]{1,0:T(2,128)}, u32[]{:S(2)}) copy-start(f32[2,48]{1,0:T(2,128)} %bias_ref.1) | copy-start | bytes 1156
  2.6 15.7 %all-to-all-start = ((bf16[8,16,896]{2,1,0:T(8,128)(2,1)}), bf16[8,16,896]{2,1,0:T(8,128)(2,1)S(1)}, u32[]{:S(2)}, u32[]{:S(2)}) async-start(bf16[8,16,896]{2,1,0:T(8,128)(2,1)} %get-tuple-element.41), calls=%async_computation | async-start | bytes 458752 | tf_op jit(solution)/shard_map/all_to_all | solution.py:716
  18.3 3.8 %copy-start.4 = (s32[1,2304]{1,0:T(1,128)S(1)}, s32[1,2304]{1,0:T(1,128)}, u32[]{:S(2)}) copy-start(s32[1,2304]{1,0:T(1,128)} %mask_ref.3) | copy-start | bytes 27652
  18.4 3.8 %copy-start.5 = (f32[2,768]{1,0:T(2,128)S(1)}, f32[2,768]{1,0:T(2,128)}, u32[]{:S(2)}) copy-start(f32[2,768]{1,0:T(2,128)} %up_bias_ref.1) | copy-start | bytes 18436
  18.4 3.8 %copy-start.6 = (f32[2,192]{1,0:T(2,128)S(1)}, f32[2,192]{1,0:T(2,128)}, u32[]{:S(2)}) copy-start(f32[2,192]{1,0:T(2,128)} %gain_ref.1) | copy-start | bytes 4612
  18.4 3.8 %copy-start.7 = (f32[2,192]{1,0:T(2,128)S(1)}, f32[2,192]{1,0:T(2,128)}, u32[]{:S(2)}) copy-start(f32[2,192]{1,0:T(2,128)} %shift_ref.1) | copy-start | bytes 4612
  18.4 3.8 %copy-start.8 = (f32[2,192]{1,0:T(2,128)S(1)}, f32[2,192]{1,0:T(2,128)}, u32[]{:S(2)}) copy-start(f32[2,192]{1,0:T(2,128)} %down_bias_ref.1) | copy-start | bytes 4612
  18.4 3.8 %copy-start.9 = (f32[2,48]{1,0:T(2,128)S(1)}, f32[2,48]{1,0:T(2,128)}, u32[]{:S(2)}) copy-start(f32[2,48]{1,0:T(2,128)} %scale_ref.1) | copy-start | bytes 1156
  20.4 6.0 %collective-permute-start.1 = (bf16[48,2304]{1,0:T(8,128)(2,1)S(1)}, bf16[48,2304]{1,0:T(8,128)(2,1)S(1)}, u32[]{:S(2)}, u32[]{:S(2)}) collective-permute-start(bf16[48,2304]{1,0:T(8,128)(2,1)S(1)} %conv_border.1.after_ref.own_ref), channel_id=1, source_target_pairs={{0,2},{1,3},{2,0},{3,1},{4,6},{5,7},{6,4},{7,5},{8,10},{9,11},{10,... | collective-permute-start | bytes 663560 | tf_op jit(solution)/shard_map/ppermute | solution.py:683
  22.2 4.3 %collective-permute-start = (bf16[48,2304]{1,0:T(8,128)(2,1)S(1)}, bf16[48,2304]{1,0:T(8,128)(2,1)S(1)}, u32[]{:S(2)}, u32[]{:S(2)}) collective-permute-start(bf16[48,2304]{1,0:T(8,128)(2,1)S(1)} %conv_border.1.after_ref.own_ref), channel_id=1, source_target_pairs={{0,1},{1,0},{2,3},{3,2},{4,5},{5,4},{6,7},{7,6},{8,9},{9,8},{10,11... | collective-permute-start | bytes 663560 | tf_op jit(solution)/shard_map/ppermute | solution.py:684
  22.2 5.7 %copy-start.1 = (bf16[2,192,768]{2,1,0:T(8,128)(2,1)S(1)}, bf16[2,192,768]{2,1,0:T(8,128)(2,1)}, u32[]{:S(2)}) copy-start(bf16[2,192,768]{2,1,0:T(8,128)(2,1)} %down_ref.5) | copy-start | bytes 1769476
  22.3 5.6 %copy-start.13 = (bf16[768,384]{1,0:T(8,128)(2,1)S(1)}, bf16[768,384]{1,0:T(8,128)(2,1)}, u32[]{:S(2)}) copy-start(bf16[768,384]{1,0:T(8,128)(2,1)} %constant.10.clone.pack_ref) | copy-start | bytes 1769476
  22.3 5.6 %copy-start.16 = (bf16[128,128]{1,0:T(8,128)(2,1)S(1)}, bf16[128,128]{1,0:T(8,128)(2,1)}, u32[]{:S(2)}) copy-start(bf16[128,128]{1,0:T(8,128)(2,1)} %constant.9.clone.rim_pool_ref) | copy-start | bytes 98308
  23.6 7.6 %copy-start.21 = (f32[2,192,128]{2,1,0:T(8,128)}, f32[2,192,128]{2,1,0:T(8,128)S(1)}, u32[]{:S(2)}) copy-start(f32[2,192,128]{2,1,0:T(8,128)S(1)} %get-tuple-element.58.shift_ref) | copy-start | bytes 589828
  23.6 7.6 %copy-start.24 = (f32[48,640]{1,0:T(8,128)}, f32[48,640]{1,0:T(8,128)S(1)}, u32[]{:S(2)}) copy-start(f32[48,640]{1,0:T(8,128)S(1)} %get-tuple-element.62.pool_cells_ref) | copy-start | bytes 368644
  23.6 7.6 %copy-start.26 = (f32[8,2304]{1,0:T(8,128)}, f32[8,2304]{1,0:T(8,128)S(1)}, u32[]{:S(2)}) copy-start(f32[8,2304]{1,0:T(8,128)S(1)} %get-tuple-element.56.mask_ref) | copy-start | bytes 221188
  23.6 7.6 %copy-start.30 = (f32[2,48,128]{2,1,0:T(8,128)}, f32[2,48,128]{2,1,0:T(8,128)S(1)}, u32[]{:S(2)}) copy-start(f32[2,48,128]{2,1,0:T(8,128)S(1)} %get-tuple-element.60.down_bias_ref) | copy-start | bytes 147460
  23.6 7.6 %copy-start.32 = (f32[2,48,128]{2,1,0:T(8,128)}, f32[2,48,128]{2,1,0:T(8,128)S(1)}, u32[]{:S(2)}) copy-start(f32[2,48,128]{2,1,0:T(8,128)S(1)} %get-tuple-element.61.scale_ref) | copy-start | bytes 147460
  23.6 11.9 %copy-start.17 = (bf16[2,768,208]{2,1,0:T(8,128)(2,1)}, bf16[2,768,208]{2,1,0:T(8,128)(2,1)S(1)}, u32[]{:S(2)}) copy-start(bf16[2,768,208]{2,1,0:T(8,128)(2,1)S(1)} %get-tuple-element.59.up_ref) | copy-start | bytes 1916932
  23.6 11.9 %copy-start.19 = (f32[2,192,128]{2,1,0:T(8,128)}, f32[2,192,128]{2,1,0:T(8,128)S(1)}, u32[]{:S(2)}) copy-start(f32[2,192,128]{2,1,0:T(8,128)S(1)} %get-tuple-element.57.gain_ref) | copy-start | bytes 589828
  26.4 9.2 %copy-start.15 = (bf16[256,128]{1,0:T(8,128)(2,1)S(1)}, bf16[256,128]{1,0:T(8,128)(2,1)}, u32[]{:S(2)}) copy-start(bf16[256,128]{1,0:T(8,128)(2,1)} %constant.11.clone.middle_pool_ref) | copy-start | bytes 196612
  26.4 1.5 %collective-permute-start.2 = (bf16[48,2304]{1,0:T(8,128)(2,1)S(1)}, bf16[48,2304]{1,0:T(8,128)(2,1)S(1)}, u32[]{:S(2)}, u32[]{:S(2)}) collective-permute-start(bf16[48,2304]{1,0:T(8,128)(2,1)S(1)} %collective-permute-done.1.p2_ref), channel_id=1, source_target_pairs={{0,1},{1,0},{2,3},{3,2},{4,5},{5,4},{6,7},{7,6},{8,9},{9,8},{10,11... | collective-permute-start | bytes 663560 | tf_op jit(solution)/shard_map/ppermute | solution.py:686
  31.2 4.3 %copy-start.28 = (bf16[48,768]{1,0:T(8,128)(2,1)}, bf16[48,768]{1,0:T(8,128)(2,1)S(1)}, u32[]{:S(2)}) copy-start(bf16[48,768]{1,0:T(8,128)(2,1)S(1)} %get-tuple-element.65.rim_ref) | copy-start | bytes 221188
  31.2 12.4 %all-to-all-start.1 = ((bf16[8,16,512]{2,1,0:T(8,128)(2,1)}), bf16[8,16,512]{2,1,0:T(8,128)(2,1)S(1)}, u32[]{:S(2)}, u32[]{:S(2)}) async-start(bf16[8,16,512]{2,1,0:T(8,128)(2,1)} %get-tuple-element.63), calls=%async_computation.1 | async-start | bytes 262144 | tf_op jit(solution)/shard_map/all_to_all | solution.py:781
  45.0 4.4 %collective-permute-start.4 = (bf16[48,768]{1,0:T(8,128)(2,1)S(1)}, bf16[48,768]{1,0:T(8,128)(2,1)S(1)}, u32[]{:S(2)}, u32[]{:S(2)}) collective-permute-start(bf16[48,768]{1,0:T(8,128)(2,1)S(1)} %border_coarse.1.after_ref.own_ref), channel_id=1, source_target_pairs={{0,2},{1,3},{2,0},{3,1},{4,6},{5,7},{6,4},{7,5},{8,10},{9,11},{10,... | collective-permute-start | bytes 221192 | tf_op jit(solution)/shard_map/ppermute | solution.py:683
  46.5 2.9 %collective-permute-start.3 = (bf16[48,768]{1,0:T(8,128)(2,1)S(1)}, bf16[48,768]{1,0:T(8,128)(2,1)S(1)}, u32[]{:S(2)}, u32[]{:S(2)}) collective-permute-start(bf16[48,768]{1,0:T(8,128)(2,1)S(1)} %border_coarse.1.after_ref.own_ref), channel_id=1, source_target_pairs={{0,1},{1,0},{2,3},{3,2},{4,5},{5,4},{6,7},{7,6},{8,9},{9,8},{10,11... | collective-permute-start | bytes 221192 | tf_op jit(solution)/shard_map/ppermute | solution.py:684
  46.5 4.1 %copy-start.18 = (bf16[2,768,208]{2,1,0:T(8,128)(2,1)S(1)}, bf16[2,768,208]{2,1,0:T(8,128)(2,1)}, u32[]{:S(2)}) copy-start(bf16[2,768,208]{2,1,0:T(8,128)(2,1)} %copy-done.17) | copy-start | bytes 1916932
  46.5 4.1 %copy-start.20 = (f32[2,192,128]{2,1,0:T(8,128)S(1)}, f32[2,192,128]{2,1,0:T(8,128)}, u32[]{:S(2)}) copy-start(f32[2,192,128]{2,1,0:T(8,128)} %copy-done.19) | copy-start | bytes 589828
  46.5 4.1 %copy-start.23 = (f32[2,192,128]{2,1,0:T(8,128)S(1)}, f32[2,192,128]{2,1,0:T(8,128)}, u32[]{:S(2)}) copy-start(f32[2,192,128]{2,1,0:T(8,128)} %copy-done.21) | copy-start | bytes 589828
  46.5 4.1 %copy-start.35 = (f32[48,128]{1,0:T(8,128)S(1)}, f32[48,128]{1,0:T(8,128)}, u32[]{:S(2)}) copy-start(f32[48,128]{1,0:T(8,128)} %copy-done.34) | copy-start | bytes 73732
  49.4 1.3 %collective-permute-start.5 = (bf16[48,768]{1,0:T(8,128)(2,1)S(1)}, bf16[48,768]{1,0:T(8,128)(2,1)S(1)}, u32[]{:S(2)}, u32[]{:S(2)}) collective-permute-start(bf16[48,768]{1,0:T(8,128)(2,1)S(1)} %collective-permute-done.4.p2_ref), channel_id=1, source_target_pairs={{0,1},{1,0},{2,3},{3,2},{4,5},{5,4},{6,7},{7,6},{8,9},{9,8},{10,11... | collective-permute-start | bytes 221192 | tf_op jit(solution)/shard_map/ppermute | solution.py:686
  (14 other events, 23.6 us)

commit v8 on v7

--- a/solution.py
+++ b/solution.py
@@ -198,9 +198,10 @@
     return jnp.take_along_axis(value, index, axis=1)
 
 
-def conv_inner(x_ref, weight_ref, bias_ref, sum_ref, wide_ref, pad_ref, odd_ref, total_ref):
+def conv_inner(x_ref, weight_ref, bias_ref, sum_ref, middle_ref, mirror_ref, wide_ref, pad_ref, odd_ref, total_ref):
     for tap in range(49):
         wide_ref[tap] = jnp.broadcast_to(weight_ref[0, :, tap : tap + 1], (ROWS, 128))
+    mirrored_taps(wide_ref, mirror_ref)
     pad_ref[:, 0:256] = jnp.zeros((ROWS, 256), F32)
     pad_ref[:, 3328:3584] = jnp.zeros((ROWS, 256), F32)
     lane = lane_ids((8, 128))
@@ -250,7 +251,10 @@
         for pair in pairs_of(m):
             picked = lanes_from(total_ref[:, 128 * pair : 128 * pair + 128], index)
             value = picked if value is None else jnp.where(tall(row // 2 == pair), picked, value)
-        sum_ref[:, 128 * m : 128 * m + 128] = value
+        if m < RIM // 128:
+            sum_ref[:, 128 * m : 128 * m + 128] = value
+        else:
+            middle_ref[:, 128 * m - RIM : 128 * m - RIM + 128] = value.astype(BF)
 
 
 def place_of(m):
@@ -274,11 +278,14 @@
     return range(4 + 2 * (m - 10), 6 + 2 * (m - 10))
 
 
-def column_sums(beside, tap):
-    low_half = tall(lane_ids((8, 128)) < 64)
+def column_sums(beside, mirror_ref):
     total = [jnp.zeros((ROWS, 128), F32)] * 3
     for a in range(7):
-        weights = [jnp.where(low_half, tap(a, b), tap(a, 6 - b)) for b in range(3)]
+        if mirror_ref.shape[0] == 49:
+            low_half = tall(lane_ids((8, 128)) < 64)
+            weights = [jnp.where(low_half, mirror_ref[7 * a + b], mirror_ref[7 * a + 6 - b]) for b in range(3)]
+        else:
+            weights = [mirror_ref[4 * a + b] for b in range(3)]
         for q in range(3):
             partial = weights[0] * beside[q]
             for j in range(q + 1, 3):
@@ -287,26 +294,42 @@
     return total
 
 
-def row_sums(uses, tap):
+def row_sums(uses, mirror_ref):
     places = 1 + max(place for place, _, _ in uses)
+    taps = {a: whole_row(mirror_ref, a) for _, a, _ in uses}
     total = [jnp.zeros((ROWS, 128), F32)] * places
     for b in range(7):
         partial = [None] * places
         for place, a, cells in uses:
-            term = tap(a, b) * cells
+            term = taps[a][b] * cells
             partial[place] = term if partial[place] is None else partial[place] + term
         for place in range(places):
             total[place] = total[place] + (pltpu.roll(partial[place], (3 - b) % 128, 1) if b != 3 else partial[place])
     return total
 
 
-def conv_border(tab_ref, recv_ref, sum_ref, wide_ref, out_ref):
+def mirrored_taps(wide_ref, mirror_ref):
+    low_half = tall(lane_ids((8, 128)) < 64)
+    for a in range(7):
+        for b in range(3):
+            mirror_ref[4 * a + b] = jnp.where(low_half, wide_ref[a * 7 + b], wide_ref[a * 7 + 6 - b])
+        mirror_ref[4 * a + 3] = wide_ref[a * 7 + 3]
+
+
+def whole_row(mirror_ref, a):
+    if mirror_ref.shape[0] == 49:
+        return [mirror_ref[7 * a + b] for b in range(7)]
+    low_half = tall(lane_ids((8, 128)) < 64)
+    ends = [(mirror_ref[4 * a + b], pltpu.roll(mirror_ref[4 * a + b], 64, 1)) for b in range(3)]
+    first = [jnp.where(low_half, plain, turned) for plain, turned in ends]
+    last = [jnp.where(low_half, turned, plain) for plain, turned in ends]
+    return first + [mirror_ref[4 * a + 3]] + last[::-1]
+
+
+def conv_border(tab_ref, recv_ref, sum_ref, mirror_ref, out_ref):
     lane = lane_ids((8, 128))
     half, within = lane // 64, lane % 64
     low_half = tall(lane < 64)
-
-    def tap(a, b):
-        return wide_ref[a * 7 + b]
 
     def band_cells(band, offset):
         source, scale = band_source(tab_ref, band)
@@ -337,11 +360,11 @@
 
     zeros = jnp.zeros((ROWS, 128), F32)
     below = halo_rows((0, 1, 2), False, True)
-    first_fix = row_sums(((0, 0, below[0]), (0, 1, joined(below[0], below[1])), (0, 2, below[1]), (1, 0, below[1])), tap)
+    first_fix = row_sums(((0, 0, below[0]), (0, 1, joined(below[0], below[1])), (0, 2, below[1]), (1, 0, below[1])), mirror_ref)
     folded = tab_ref[8] == 2
     above = halo_rows((5, 6, 7), folded, folded)
     edge = joined(zeros, above[0])
-    last_fix = row_sums(((0, 6, edge), (1, 4, edge), (1, 5, above[0]), (1, 6, joined(above[0], above[1]))), tap)
+    last_fix = row_sums(((0, 6, edge), (1, 4, edge), (1, 5, above[0]), (1, 6, joined(above[0], above[1]))), mirror_ref)
 
     left, right = band_cells(3, 128), band_cells(4, 128)
     beside = []
@@ -353,59 +376,67 @@
             jnp.where(tall(within < 40), lanes_from(main, main_index), lanes_from(rest, rest_index)) for main, rest in (left, right)
         ]
         beside.append(jnp.where(tall(within < 48), jnp.where(low_half, picked[0], picked[1]), 0.0))
-    column_fix = column_sums(beside, tap)
+    column_fix = column_sums(beside, mirror_ref)
     fixes = {0: first_fix[0], 1: first_fix[1], 22: last_fix[0], 23: last_fix[1]}
-    for m in range((RIM + MIDDLE) // 128):
+    for m in range(RIM // 128):
+        row, col = place_of(m)
+        index = tall(jnp.where(col < 24, row, 64 + row))
         value = sum_ref[:, 128 * m : 128 * m + 128]
-        if m < RIM // 128:
-            row, col = place_of(m)
-            index = tall(jnp.where(col < 24, row, 64 + row))
-            fix = zeros
-            for q in range(3):
-                fix = jnp.where(tall((col == q) | (col == 47 - q)), lanes_from(column_fix[q], index), fix)
-            value = value + fix
-            row_index = tall(row % 2 * 64 + 3 + col)
-            for pair in pairs_of(m):
-                if pair in fixes:
-                    value = value + jnp.where(tall(row // 2 == pair), lanes_from(fixes[pair], row_index), 0.0)
+        fix = zeros
+        for q in range(3):
+            fix = jnp.where(tall((col == q) | (col == 47 - q)), lanes_from(column_fix[q], index), fix)
+        value = value + fix
+        row_index = tall(row % 2 * 64 + 3 + col)
+        for pair in pairs_of(m):
+            if pair in fixes:
+                value = value + jnp.where(tall(row // 2 == pair), lanes_from(fixes[pair], row_index), 0.0)
         out_ref[:, 128 * m : 128 * m + 128] = value.astype(BF)
 
 
 def params(
-    after_ref, x_ref, mask_ref, gain_ref, shift_ref, up_ref, up_bias_ref, down_bias_ref, scale_ref, pool_weight_ref, spread_weight_ref, pool_ref,
-    cells_ref, cell_mask_ref, small_mask_ref, gains_ref, shifts_ref, ups_ref, down_biases_ref, scales_ref, pool_cells_ref, spread_cells_ref,
+    after_ref, x_ref, mask_ref, gain_ref, shift_ref, up_ref, up_bias_ref, down_ref, down_bias_ref, scale_ref, pool_weight_ref, spread_weight_ref,
+    pool_ref, rim_cells_ref, middle_cells_ref, rim_mask_ref, rim_weights_ref, *level_refs,
 ):
     me = lax.axis_index("chan")
+    lane = lane_ids((192, 128))
     for level in range(2):
+        weights_ref, values_ref = level_refs[2 * level : 2 * level + 2]
         row = slice(level, level + 1)
-        ups_ref[level] = jnp.transpose(jnp.concatenate([up_ref[level], three_terms(up_bias_ref[row, :])], axis=0), (1, 0))
-        gains_ref[level] = columns(gain_ref[row, :])
-        shifts_ref[level] = columns(shift_ref[row, :])
-        scales_ref[level] = columns(scale_ref[row, :])
+        spare = jnp.zeros((48, up_ref.shape[2]), BF)
+        turned = jnp.concatenate([up_ref[level], three_terms(up_bias_ref[row, :]), spare], axis=0)
+        weights_ref[0:768, :] = jnp.transpose(turned, (1, 0))
+        own = down_ref[level, pl.ds(pl.multiple_of(me * ROWS, 16), ROWS), :]
+        for j in range(3):
+            weights_ref[768 + ROWS * j : 768 + ROWS * (j + 1), :] = own[:, 256 * j : 256 * j + 256]
         down_bias = columns(down_bias_ref[row, :])
         own = down_bias[0:ROWS]
         for k in range(1, down_bias.shape[0] // ROWS):
             own = jnp.where(me == k, down_bias[k * ROWS : (k + 1) * ROWS], own)
-        down_biases_ref[level] = own
+        rest = jnp.zeros((192 - ROWS, 128), F32)
+        own, scale = [jnp.concatenate([value, rest], axis=0) for value in (own, columns(scale_ref[row, :]))]
+        norm = jnp.where(lane == 0, columns(gain_ref[row, :]), columns(shift_ref[row, :]))
+        values_ref[0:192, :] = jnp.where(lane < 2, norm, jnp.where(lane == 2, own, scale))
+    fine_values_ref, coarse_values_ref = level_refs[1], level_refs[3]
     lane = lane_ids((ROWS, FINE_IN))
-    pool_cells_ref[:, 0:384] = cell_weights(pool_weight_ref, lane // 48, lane % 48)
+    rim_weights_ref[:, 0:384] = cell_weights(pool_weight_ref, lane // 48, lane % 48)
+    spread = cell_weights(spread_weight_ref, lane // 48, lane % 48)
+    for j in range(3):
+        coarse_values_ref[240 + ROWS * j : 240 + ROWS * (j + 1), :] = spread[:, 128 * j : 128 * j + 128]
     lane = lane_ids((ROWS, 128))
-    pool_cells_ref[:, 384:512] = cell_weights(pool_weight_ref, lane // 16, lane)
-    pool_cells_ref[:, 512:640] = cell_weights(pool_weight_ref, lane // 32, lane)
-    lane = lane_ids((ROWS, FINE_IN))
-    spread_cells_ref[...] = cell_weights(spread_weight_ref, lane // 48, lane % 48)
+    rim_weights_ref[:, 384:512] = cell_weights(pool_weight_ref, lane // 16, lane)
+    fine_values_ref[192:240, :] = cell_weights(pool_weight_ref, lane // 32, lane)
 
     masks = []
     for i in range(GROUPS):
         masks.append(jnp.broadcast_to(mask_ref[:, i * FINE_IN : (i + 1) * FINE_IN].astype(F32), (8, FINE_IN)))
     counts = dot(jnp.concatenate(masks, axis=0).astype(BF), pool_ref[...])
-    small_mask_ref[...] = jnp.where(counts > 0.5, 1.0, 0.0)
+    coarse_values_ref[192:240, :] = jnp.where(counts > 0.5, 1.0, 0.0)
     for m in range((RIM + MIDDLE) // 128):
-        here = slice(128 * m, 128 * m + 128)
         if m < 6:
+            here = slice(128 * m, 128 * m + 128)
             source = 128 * (m if m < 3 else m + 12)
-            cells_ref[:, here] = x_ref[0, :, source : source + 128]
-            cell_mask_ref[:, here] = jnp.broadcast_to(mask_ref[:, source : source + 128].astype(F32), (8, 128))
+            rim_cells_ref[:, here] = x_ref[0, :, source : source + 128]
+            rim_mask_ref[:, here] = jnp.broadcast_to(mask_ref[:, source : source + 128].astype(F32), (8, 128))
             continue
         row, col = place_of(m)
         cell = row * 48 + col
@@ -417,8 +448,12 @@
             mask_part = lanes_from(jnp.broadcast_to(mask_ref[:, lanes].astype(F32), (8, 128)), index)
             value = part if value is None else jnp.where(tall(cell // 128 == tile), part, value)
             mask = mask_part if mask is None else jnp.where(cell // 128 == tile, mask_part, mask)
-        cells_ref[:, here] = value.astype(BF)
-        cell_mask_ref[:, here] = mask
+        if m < 10:
+            rim_cells_ref[:, 128 * m : 128 * m + 128] = value.astype(BF)
+            rim_mask_ref[:, 128 * m : 128 * m + 128] = mask
+        else:
+            middle_cells_ref[:, 128 * m - RIM : 128 * m - RIM + 128] = value.astype(BF)
+            fine_values_ref[240 + 8 * (m - 10) : 248 + 8 * (m - 10), :] = mask
 
 
 def in_rows(rim_ref, middle_ref, out_ref):
@@ -473,12 +508,9 @@
     lax.fori_loop(0, 6, group, 0)
 
 
-def border_coarse(tab_ref, recv_ref, sum_ref, wide_ref, out_ref):
+def border_coarse(tab_ref, recv_ref, sum_ref, mirror_ref, out_ref):
     lane = lane_ids((8, 128))
     half, within, segment, inside = lane // 64, lane % 64, lane // 32, lane % 32
-
-    def tap(a, b):
-        return wide_ref[a * 7 + b]
 
     def band_main(band):
         source, scale = band_source(tab_ref, band)
@@ -501,10 +533,10 @@
         return jnp.where(tall(kept), pltpu.roll(cells, lanes, 1), 0.0)
 
     below = halo_rows((0, 1, 2), False)
-    first_fix = row_sums(((0, 0, below), (0, 1, turned(below, 96, lane < 64)), (0, 2, turned(below, 64, lane < 32))), tap)[0]
+    first_fix = row_sums(((0, 0, below), (0, 1, turned(below, 96, lane < 64)), (0, 2, turned(below, 64, lane < 32))), mirror_ref)[0]
     above = halo_rows((5, 6, 7), tab_ref[8] == 2)
     last_fix = row_sums(
-        ((0, 6, turned(above, 32, lane >= 32)), (0, 5, turned(above, 64, lane >= 64)), (0, 4, turned(above, 96, lane >= 96))), tap
+        ((0, 6, turned(above, 32, lane >= 32)), (0, 5, turned(above, 64, lane >= 64)), (0, 4, turned(above, 96, lane >= 96))), mirror_ref
     )[0]
     sides = [(band_main(band), band_rest(band)) for band in (3, 4)]
     beside = []
@@ -516,7 +548,7 @@
             jnp.where(tall(within < 16), lanes_from(main, main_index), lanes_from(rest, rest_index)) for main, rest in sides
         ]
         beside.append(jnp.where(tall(within < HALF), jnp.where(tall(half == 0), picked[0], picked[1]), 0.0))
-    column_fix = column_sums(beside, tap)
+    column_fix = column_sums(beside, mirror_ref)
     for m in range(GROUPS):
         row, col = 4 * m + segment, inside - 3
         index = tall(jnp.where(col < 12, row, 64 + row))
@@ -539,19 +571,23 @@
         cat_ref[pl.ds(first, ROWS), :] = piece[...]
 
 
-def make_branch(level, cat_ref, gain_ref, shift_ref, up_ref, down_ref, down_bias_ref, block):
-    first = pl.multiple_of(lax.axis_index("chan") * ROWS, 16)
-    gain, shift = wide(gain_ref[level], block), wide(shift_ref[level], block)
+def make_branch(cat_ref, weights_ref, values_ref, block):
+    def spread_lane(rows, lane):
+        return wide(jnp.broadcast_to(values_ref[0:rows, lane : lane + 1], (rows, 128)), block)
+
+    gain, shift, down_bias, scale = spread_lane(192, 0), spread_lane(192, 1), spread_lane(ROWS, 2), spread_lane(ROWS, 3)
+    down = jnp.concatenate([weights_ref[768 + ROWS * j : 768 + ROWS * (j + 1), :] for j in range(3)], axis=1)
+    inputs = 4 * ROWS
 
     def branch(start):
-        values = cat_ref[:, pl.ds(start, block)].astype(F32)
+        values = cat_ref[0:inputs, start : start + block].astype(F32)
         mean = jnp.mean(values, axis=0, keepdims=True)
         centred = values - mean
         spread = jnp.mean(centred * centred, axis=0, keepdims=True)
         normed = (centred * lax.rsqrt(spread + norm_eps) * gain + shift).astype(BF)
-        hidden = dot(up_ref[level], jnp.concatenate([normed, jnp.ones((16, block), BF)], axis=0))
+        hidden = dot(weights_ref[0:768, 0 : inputs + 16], jnp.concatenate([normed, jnp.ones((16, block), BF)], axis=0))
         hidden = 0.5 * hidden * (1.0 + lax.erf(hidden * np.float32(0.5**0.5)))
-        return dot(down_ref[level, pl.ds(first, ROWS), :], hidden.astype(BF)) + wide(down_bias_ref[level], block)
+        return scale * (dot(down, hidden.astype(BF)) + down_bias)
 
     return branch
 
@@ -572,21 +608,15 @@
 
 def make_mix_rim(count):
     def mix_rim(
-        tab_ref, own_ref, p1_ref, p2_ref, p3_ref, x_ref, mask_ref, gain_ref, shift_ref, up_ref, down_ref, down_bias_ref, scale_ref,
-        pool_cells_ref, pool_ref, rim_pool_ref, pack_ref,
-        fine_ref, pooled_ref, msg_ref, middle_ref, cat_ref, mains_ref, rest_ref,
+        tab_ref, own_ref, p1_ref, p2_ref, p3_ref, x_ref, mask_ref, pool_cells_ref, weights_ref, values_ref, pool_ref, rim_pool_ref,
+        pack_ref, middle_pooled_ref, fine_ref, msg_ref, all_pooled_ref, cat_ref, pooled_ref, mains_ref, rest_ref,
     ):
-        me = lax.axis_index("chan")
-        for k, piece in enumerate((own_ref, p1_ref, p2_ref, p3_ref)):
-            here = pl.ds(pl.multiple_of(lax.bitwise_xor(me, k) * ROWS, 16), ROWS)
-            cat_ref[here, :] = piece[:, 0:RIM]
-            middle_ref[here, :] = piece[:, RIM:]
+        gather_rows((own_ref, p1_ref, p2_ref, p3_ref), cat_ref)
         block = RIM // 2
-        branch = make_branch(0, cat_ref, gain_ref, shift_ref, up_ref, down_ref, down_bias_ref, block)
-        scale = wide(scale_ref[0], block)
+        branch = make_branch(cat_ref, weights_ref, values_ref, block)
         for start in range(0, RIM, block):
             here = slice(start, start + block)
-            value = x_ref[:, here].astype(F32) + scale * branch(start)
+            value = x_ref[:, here].astype(F32) + branch(start)
             fine_ref[:, here] = (mask_ref[0:1, here] * value).astype(BF)
 
         weights = pool_cells_ref[:, 0:384]
@@ -620,44 +650,45 @@
             return carry
 
         scan_tiles(count, fill, jnp.int32(0))
+        all_pooled_ref[...] = pooled_ref[...]
+        for i in range(4):
+            here = slice(128 * i + 128, 128 * i + 256)
+            all_pooled_ref[:, here] = (pooled_ref[:, here].astype(F32) + middle_pooled_ref[:, 128 * i : 128 * i + 128].astype(F32)).astype(BF)
 
     return mix_rim
 
 
 def mix_middle(
-    cat_ref, x_ref, mask_ref, gain_ref, shift_ref, up_ref, down_ref, down_bias_ref, scale_ref, pool_cells_ref, middle_pool_ref, rim_ref,
-    fine_ref, pooled_ref,
+    own_ref, p1_ref, p2_ref, p3_ref, x_ref, weights_ref, values_ref, middle_pool_ref, fine_ref, pooled_ref, cat_ref
 ):
+    gather_rows((own_ref, p1_ref, p2_ref, p3_ref), cat_ref)
     block = MIDDLE // 2
-    branch = make_branch(0, cat_ref, gain_ref, shift_ref, up_ref, down_ref, down_bias_ref, block)
-    scale = wide(scale_ref[0], block)
+    branch = make_branch(cat_ref, weights_ref, values_ref, block)
     for start in range(0, MIDDLE, block):
-        here, there = slice(start, start + block), slice(RIM + start, RIM + start + block)
-        value = x_ref[:, there].astype(F32) + scale * branch(start)
-        fine_ref[:, here] = (mask_ref[0:1, there] * value).astype(BF)
-    weights = wide(pool_cells_ref[:, 512:640], 256)
+        here = slice(start, start + block)
+        value = x_ref[:, here].astype(F32) + branch(start)
+        tiles = range(start // 128, (start + block) // 128)
+        mask = jnp.concatenate([values_ref[240 + 8 * t : 241 + 8 * t, :] for t in tiles], axis=1)
+        fine_ref[:, here] = (mask * value).astype(BF)
+    weights = wide(values_ref[192:240, :], 256)
     middle = pooled_cells([fine_ref[:, 256 * i : 256 * i + 256].astype(F32) * weights for i in range(4)], middle_pool_ref[...])
-    pooled_ref[...] = rim_ref[...]
     for i in range(4):
-        here = slice(128 * i + 128, 128 * i + 256)
-        pooled_ref[:, here] = (rim_ref[:, here].astype(F32) + middle[i * ROWS : (i + 1) * ROWS].astype(BF).astype(F32)).astype(BF)
+        pooled_ref[:, 128 * i : 128 * i + 128] = middle[i * ROWS : (i + 1) * ROWS].astype(BF)
 
 
 def mix_coarse(
-    own_ref, p1_ref, p2_ref, p3_ref, pooled_ref, small_mask_ref, fine_ref, mask_ref, gain_ref, shift_ref, up_ref,
-    down_ref, down_bias_ref, scale_ref, spread_cells_ref, pool_ref, out_ref, cat_ref,
+    own_ref, p1_ref, p2_ref, p3_ref, pooled_ref, fine_ref, mask_ref, weights_ref, values_ref, pool_ref, out_ref, cat_ref,
 ):
     gather_rows((own_ref, p1_ref, p2_ref, p3_ref), cat_ref)
     cells = cat_ref.shape[1]
-    branch = make_branch(1, cat_ref, gain_ref, shift_ref, up_ref, down_ref, down_bias_ref, cells)
-    value = pooled_ref[...].astype(F32) + wide(scale_ref[1], cells) * branch(0)
+    value = pooled_ref[...].astype(F32) + make_branch(cat_ref, weights_ref, values_ref, cells)(0)
     parts = []
     for i in range(GROUPS):
-        parts.append((small_mask_ref[8 * i : 8 * i + 1, :] * value[:, 128 * i : 128 * i + 128]).astype(BF))
+        parts.append((values_ref[192 + 8 * i : 193 + 8 * i, :] * value[:, 128 * i : 128 * i + 128]).astype(BF))
     spread = lax.dot_general(
         jnp.concatenate(parts, axis=0), pool_ref[...], (((1,), (1,)), ((), ())), preferred_element_type=F32
     )
-    weights = spread_cells_ref[...]
+    weights = jnp.concatenate([values_ref[240 + ROWS * j : 240 + ROWS * (j + 1), :] for j in range(3)], axis=1)
     for i in range(GROUPS):
         lanes = slice(i * FINE_IN, (i + 1) * FINE_IN)
         merged = fine_ref[:, lanes].astype(F32) + weights * spread[i * ROWS : (i + 1) * ROWS]
@@ -714,12 +745,13 @@
     )(wet_slots, device_of, features, pack)
     pool = jnp.asarray(POOL)
     arrived = lax.all_to_all(messages, "tile", 0, 0, tiled=True)
-    inner, fine_taps = pl.pallas_call(
+    inner, inner_middle, fine_taps = pl.pallas_call(
         lambda tab_ref, *refs: conv_inner(*refs),
         in_specs=[SMEM] + [VMEM] * 3,
-        out_specs=[VMEM] * 2,
-        out_shape=[shaped(ROWS, cells, dtype=F32), shaped(49, ROWS, 128, dtype=F32)],
+        out_specs=[VMEM] * 3,
+        out_shape=[shaped(ROWS, RIM, dtype=F32), shaped(ROWS, MIDDLE), shaped(28, ROWS, 128, dtype=F32)],
         scratch_shapes=[
+            pltpu.VMEM((49, ROWS, 128), F32),
             pltpu.VMEM((ROWS, 3584), F32),
             pltpu.VMEM((ROWS, 3584), F32),
             pltpu.VMEM((ROWS, 3072), F32),
@@ -732,42 +764,59 @@
         conv_border,
         in_specs=[SMEM] + [VMEM] * 3,
         out_specs=VMEM,
-        out_shape=shaped(ROWS, cells),
+        out_shape=shaped(ROWS, RIM),
         compiler_params=PARAMS,
         cost_estimate=takes(2),
         name="conv_border",
     )(table, arrived, inner, fine_taps)
 
+    pairs = lambda bit: [(i, i ^ bit) for i in range(4)]
+    middle_across = lax.ppermute(inner_middle, "chan", pairs(2))
+    middle_beside = lax.ppermute(inner_middle, "chan", pairs(1))
+    middle_across, _ = lax.optimization_barrier((middle_across, conv))
+    middle_pieces = (inner_middle, middle_beside, middle_across, lax.ppermute(middle_across, "chan", pairs(1)))
+
+    def beside_gather(own):
+        results = spread_params(own)
+        return *results, *pl.pallas_call(
+            mix_middle,
+            in_specs=[VMEM] * 8,
+            out_specs=[VMEM] * 2,
+            out_shape=[shaped(ROWS, MIDDLE), shaped(ROWS, 512)],
+            scratch_shapes=[pltpu.VMEM((4 * ROWS, MIDDLE), BF)],
+            compiler_params=PARAMS,
+            cost_estimate=takes(1),
+            name="mix_middle",
+        )(*middle_pieces, results[1], results[4], results[5], jnp.asarray(MIDDLE_POOL))
+
     def spread_params(own):
+        shapes = [
+            ((ROWS, RIM), BF), ((ROWS, MIDDLE), BF), ((8, RIM), F32), ((ROWS, 512), F32),
+            ((912, 256), BF), ((304, 128), F32), ((912, 256), BF), ((384, 128), F32),
+        ]
         return pl.pallas_call(
             params,
-            in_specs=[VMEM] * 12,
-            out_specs=[VMEM] * 10,
-            out_shape=[
-                shaped(*shape, dtype=dtype)
-                for shape, dtype in (
-                    ((ROWS, cells), BF), ((8, cells), F32), ((48, 128), F32), ((2, 192, 128), F32), ((2, 192, 128), F32),
-                    ((2, up_weight.shape[1], up_weight.shape[2] + 16), BF), ((2, ROWS, 128), F32), ((2, ROWS, 128), F32),
-                    ((ROWS, 640), F32), ((ROWS, FINE_IN), F32),
-                )
-            ],
+            in_specs=[VMEM] * 13,
+            out_specs=[VMEM] * len(shapes),
+            out_shape=[shaped(*shape, dtype=dtype) for shape, dtype in shapes],
             compiler_params=PARAMS,
             cost_estimate=takes(2),
             name="params",
         )(
-            own, features, land_mask, norm_gain, norm_bias, jnp.swapaxes(up_weight, 1, 2), up_bias, down_bias, layer_scale,
+            own, features, land_mask, norm_gain, norm_bias, jnp.swapaxes(up_weight, 1, 2), up_bias, down_weight, down_bias, layer_scale,
             pool_weight, spread_weight, pool,
         )
 
-    pieces, results = every_channel(conv, spread_params)
-    own_cells, own_mask, small_mask, gains, shifts, ups, down_biases, scales, pool_cells, spread_cells = results
-    rim, rim_pooled, messages, middle = pl.pallas_call(
+    pieces, results = every_channel(conv, beside_gather)
+    rim_cells, _, rim_mask, rim_weights, fine_weights, fine_values, coarse_weights, coarse_values, middle, middle_pooled = results
+    rim, messages, pooled = pl.pallas_call(
         make_mix_rim(count),
-        in_specs=[SMEM] + [VMEM] * 16,
-        out_specs=[VMEM] * 4,
-        out_shape=[shaped(ROWS, RIM), shaped(ROWS, 768), shaped(count, 16, 512), shaped(4 * ROWS, MIDDLE)],
+        in_specs=[SMEM] + [VMEM] * 13,
+        out_specs=[VMEM] * 3,
+        out_shape=[shaped(ROWS, RIM), shaped(count, 16, 512), shaped(ROWS, 768)],
         scratch_shapes=[
             pltpu.VMEM((4 * ROWS, RIM), BF),
+            pltpu.VMEM((ROWS, 768), BF),
             pltpu.VMEM((4, ROWS, 128), BF),
             pltpu.VMEM((2, 16, 128), BF),
         ],
@@ -775,21 +824,10 @@
         cost_estimate=takes(3),
         name="mix_rim",
     )(
-        table, *pieces, own_cells, own_mask, gains, shifts, ups, down_weight, down_biases, scales, pool_cells, pool,
-        jnp.asarray(RIM_POOL), jnp.asarray(SMALL_PACK),
+        table, *pieces, rim_cells, rim_mask, rim_weights, fine_weights, fine_values, pool, jnp.asarray(RIM_POOL),
+        jnp.asarray(SMALL_PACK), middle_pooled,
     )
     arrived = lax.all_to_all(messages, "tile", 0, 0, tiled=True)
-    middle, pooled = pl.pallas_call(
-        mix_middle,
-        in_specs=[VMEM] * 12,
-        out_specs=[VMEM] * 2,
-        out_shape=[shaped(ROWS, MIDDLE), shaped(ROWS, 768)],
-        compiler_params=PARAMS,
-        cost_estimate=takes(2),
-        name="mix_middle",
-    )(
-        middle, own_cells, own_mask, gains, shifts, ups, down_weight, down_biases, scales, pool_cells, jnp.asarray(MIDDLE_POOL), rim_pooled
-    )
     inner, taps = pl.pallas_call(
         conv_coarse,
         in_specs=[VMEM] * 3,
@@ -824,16 +862,14 @@
     pieces, (fine,) = every_channel(conv, back_in_rows)
     return pl.pallas_call(
         mix_coarse,
-        in_specs=[VMEM] * 16,
+        in_specs=[VMEM] * 10,
         out_specs=VMEM,
         out_shape=shaped(1, ROWS, cells),
         scratch_shapes=[pltpu.VMEM((4 * ROWS, 768), BF)],
         compiler_params=PARAMS,
         cost_estimate=takes(2),
         name="mix_coarse",
-    )(
-        *pieces, pooled, small_mask, fine, land_mask, gains, shifts, ups, down_weight, down_biases, scales, spread_cells, pool
-    )
+    )(*pieces, pooled, fine, land_mask, coarse_weights, coarse_values, pool)
 
 
 def solution(mesh):

time: 53 us -> 51.3 us (0.968)
  local copies, waits for them, and re-layouts: 6.97 us -> 1.17 us
  waiting for transfers between devices: 12.7 us -> 16.2 us
  starting transfers between devices: 14.7 us -> 15.7 us
    unnamed x78 -> x40, local copies, waits for them, and re-layouts: 6.97 us -> 1.17 us
    all_to_all x2, waiting for transfers between devices: 4.54 us -> 8.87 us  [per_device(): arrived = lax.all_to_all(messages, 'tile', 0, 0, tiled=True)]
    ppermute x0 -> x3, starting transfers between devices: none -> 1.8 us  [the longest x1 1.56 us: per_device(): middle_across = lax.ppermute(inner_middle, 'chan', pairs(2))]
    ppermute x2, waiting for transfers between devices: 5.39 us -> 4.34 us  [every_channel(): across = lax.ppermute(own, 'chan', pairs(2))]
    all_to_all x2, starting transfers between devices: 11.6 us -> 10.7 us  [per_device(): arrived = lax.all_to_all(messages, 'tile', 0, 0, tiled=True)]
  transfers between devices with their start and end apart: 8 -> 11, of which waited for: 5 -> 7; matrix products, arithmetic and copies ran while one was open for 0% -> 0% of each run, Pallas kernels for 15% -> 19%
where the time goes in v8:
time: 51.3 us; the launch traced here: 51 us
  Pallas kernels  17.7 us (35%)
  waiting for transfers between devices  16.2 us (32%)
  starting transfers between devices  15.7 us (31%)
  local copies, waits for them, and re-layouts  1.17 us (2%)
    all_to_all x2, starting transfers between devices, per_device(): arrived = lax.all_to_all(messages, 'tile', 0, 0, tiled=True)  10.7 us
    all_to_all x2, waiting for transfers between devices, per_device(): arrived = lax.all_to_all(messages, 'tile', 0, 0, tiled=True)  8.87 us
    ppermute x2, waiting for transfers between devices, every_channel(): across = lax.ppermute(own, 'chan', pairs(2))  4.34 us
    pallas_call x1, Pallas kernels, per_device(): pl.pallas_call(lambda tab_ref, *refs: conv_inner(*refs), in_specs=[SMEM]...  3.84 us
    pallas_call x1, Pallas kernels, per_device(): pl.pallas_call(make_mix_rim(count), in_specs=[SMEM] + [VMEM] * 13, out_sp...  3.21 us
    ppermute x2, starting transfers between devices, every_channel(): across = lax.ppermute(own, 'chan', pairs(2))  3.12 us
    ppermute x2, waiting for transfers between devices, every_channel(): diagonal = lax.ppermute(across, 'chan', pairs(1))  2.59 us
    pallas_call x1, Pallas kernels, per_device(): pl.pallas_call(conv_border, in_specs=[SMEM] + [VMEM] * 3, out_specs=VMEM,...  2.12 us
  transfers between devices with their start and end apart: 11, of which 7 were waited for; matrix products, arithmetic and copies ran while one was open for 0% of the time, Pallas kernels for 19%

profile of v8, /device:TPU:0, one launch (start us, length us, event | category | flops | bytes accessed | tf_op | source)
XLA Modules:
  0.0 51.0 jit_solution(14261219080318578864)
XLA Ops:
  0.0 0.1 strip_table.1.pack_ref
  0.1 0.6 %copy-done.11 = s32[8]{0:T(128)S(1)} copy-done((s32[8]{0:T(128)S(1)}, s32[8]{0:T(128)}, u32[]{:S(2)}) %copy-start.11) | copy-done | bytes 56
  0.7 0.0 copy-done.12
  0.7 0.3 copy-done.2
  1.0 1.6 %prep.1 = (bf16[8,16,896]{2,1,0:T(8,128)(2,1)}, s32[24]{0:T(128)S(1)}) custom-call(s32[8]{0:T(128)S(1)} %copy-done.11, s32[8]{0:T(128)S(1)} %copy-done.12, bf16[1,48,2304]{2,1,0:T(8,128)(2,1)S(1)} %copy-done.2, bf16[384,256]{1,0:T(8,128)(2,1)S(1)} %strip_table.1.pack_ref), custom_call_target="tpu_custom_call" | custom-call | flops 10000000000 | tf_op jit(solution)/shard_map/prep/pallas_call | solution.py:731
  2.6 7.3 %all-to-all-start = ((bf16[8,16,896]{2,1,0:T(8,128)(2,1)}), bf16[8,16,896]{2,1,0:T(8,128)(2,1)S(1)}, u32[]{:S(2)}, u32[]{:S(2)}) async-start(bf16[8,16,896]{2,1,0:T(8,128)(2,1)} %get-tuple-element.39), calls=%async_computation | async-start | bytes 458752 | tf_op jit(solution)/shard_map/all_to_all | solution.py:747
  10.0 3.8 %conv_inner.1 = (f32[48,1280]{1,0:T(8,128)S(1)}, bf16[48,1024]{1,0:T(8,128)(2,1)S(1)}, f32[28,48,128]{2,1,0:T(8,128)S(1)}) custom-call(s32[24]{0:T(128)S(1)} %get-tuple-element.38.tab_ref, bf16[1,48,2304]{2,1,0:T(8,128)(2,1)S(1)} %copy-done.2, f32[2,48,49]{2,1,0:T(8,128)S(1)} %copy-done.3, f32[2,48]{1,0:T(2,128)S(1)} %copy-done.10), custom_call_target="tpu_custom_call" | custom-call | flops 4000000000 | tf_op jit(solution)/shard_map/conv_inner/pallas_call | solution.py:748
  13.8 0.1 collective-permute-start.2
  13.9 1.6 %collective-permute-start.3 = (bf16[48,1024]{1,0:T(8,128)(2,1)S(1)}, bf16[48,1024]{1,0:T(8,128)(2,1)S(1)}, u32[]{:S(2)}, u32[]{:S(2)}) collective-permute-start(bf16[48,1024]{1,0:T(8,128)(2,1)S(1)} %get-tuple-element.50.own_ref), channel_id=1, source_target_pairs={{0,2},{1,3},{2,0},{3,1},{4,6},{5,7},{6,4},{7,5},{8,10},{9,11},{10,... | collective-permute-start | bytes 294920 | tf_op jit(solution)/shard_map/ppermute | solution.py:774
  15.4 0.1 copy.20.pool_weight_ref
  15.5 0.1 copy.21.spread_weight_ref
  15.6 2.7 %all-to-all-done.recv_ref = bf16[8,16,896]{2,1,0:T(8,128)(2,1)S(1)} async-done(((bf16[8,16,896]{2,1,0:T(8,128)(2,1)}), bf16[8,16,896]{2,1,0:T(8,128)(2,1)S(1)}, u32[]{:S(2)}, u32[]{:S(2)}) %all-to-all-start) | async-done | bytes 229408 | tf_op jit(solution)/shard_map/all_to_all | solution.py:747
  18.4 2.1 %conv_border.1.after_ref.own_ref = bf16[48,1280]{1,0:T(8,128)(2,1)S(1)} custom-call(s32[24]{0:T(128)S(1)} %get-tuple-element.38.tab_ref, bf16[8,16,896]{2,1,0:T(8,128)(2,1)S(1)} %all-to-all-done.recv_ref, f32[48,1280]{1,0:T(8,128)S(1)} %get-tuple-element.40.sum_ref, f32[28,48,128]{2,1,0:T(8,128)S(1)} %get-tuple-element.41.mirror_ref), custom_call_target="tpu_custom_call" | custom-call | flops 2000000000 | tf_op jit(solution)/shard_map/conv_border/pallas_call | solution.py:763
  20.5 0.1 collective-permute-start
  20.6 1.6 %collective-permute-start.1 = (bf16[48,1280]{1,0:T(8,128)(2,1)S(1)}, bf16[48,1280]{1,0:T(8,128)(2,1)S(1)}, u32[]{:S(2)}, u32[]{:S(2)}) collective-permute-start(bf16[48,1280]{1,0:T(8,128)(2,1)S(1)} %conv_border.1.after_ref.own_ref), channel_id=1, source_target_pairs={{0,2},{1,3},{2,0},{3,1},{4,6},{5,7},{6,4},{7,5},{8,10},{9,11},{10,... | collective-permute-start | bytes 368648 | tf_op jit(solution)/shard_map/ppermute | solution.py:714
  22.2 0.2 collective-permute-start.4
  22.4 0.7 %params.1 = (bf16[48,1280]{1,0:T(8,128)(2,1)S(1)}, bf16[48,1024]{1,0:T(8,128)(2,1)S(1)}, f32[8,1280]{1,0:T(8,128)S(1)}, f32[48,512]{1,0:T(8,128)S(1)}, bf16[912,...) custom-call(bf16[48,1280]{1,0:T(8,128)(2,1)S(1)} %conv_border.1.after_ref.o, ...), custom_call_target="tpu_custom_call" | custom-call | flops 2000000000 | tf_op jit(solution)/shard_map/params/pallas_call | solution.py:797
  23.1 0.3 collective-permute-done.4.p3_ref
  23.5 1.4 %mix_middle.1 = (bf16[48,1024]{1,0:T(8,128)(2,1)S(1)}, bf16[48,512]{1,0:T(8,128)(2,1)S(1)}) custom-call(bf16[48,1024]{1,0:T(8,128)(2,1)S(1)} %get-tuple-element.50.own_ref, bf16[48,1024]{1,0:T(8,128)(2,1)S(1)} %collective-permute-done.2.p1_ref, bf16[48,1024]{1,0:T(8,128)(2,1)S(1)} %collective-permute-done.3.p2_ref, ...), custom_call_target="tpu_custom_call" | custom-call | flops 1000000000 | tf_op jit(solution)/shard_map/mix_middle/pallas_call | solution.py:781
  24.9 1.5 %collective-permute-done.1.p2_ref = bf16[48,1280]{1,0:T(8,128)(2,1)S(1)} collective-permute-done((bf16[48,1280]{1,0:T(8,128)(2,1)S(1)}, bf16[48,1280]{1,0:T(8,128)(2,1)S(1)}, u32[]{:S(2)}, u32[]{:S(2)}) %collective-permute-start.1) | collective-permute-done | bytes 122912 | tf_op jit(solution)/shard_map/ppermute | solution.py:714
  26.4 1.3 %collective-permute-done.5.p3_ref = bf16[48,1280]{1,0:T(8,128)(2,1)S(1)} collective-permute-done((bf16[48,1280]{1,0:T(8,128)(2,1)S(1)}, bf16[48,1280]{1,0:T(8,128)(2,1)S(1)}, u32[]{:S(2)}, u32[]{:S(2)}) %collective-permute-start.5) | collective-permute-done | bytes 122912 | tf_op jit(solution)/shard_map/ppermute | solution.py:717
  27.7 3.2 %mix_rim.1 = (bf16[48,1280]{1,0:T(8,128)(2,1)S(1)}, bf16[8,16,512]{2,1,0:T(8,128)(2,1)}, bf16[48,768]{1,0:T(8,128)(2,1)S(1)}) custom-call(s32[24]{0:T(128)S(1)} %get-tuple-element.38.tab_ref, bf16[48,1280]{1,0:T(8,128)(2,1)S(1)} %conv_border.1.after_ref.own_ref, bf16[48,1280]{1,0:T(8,128)(2,1)S(1)} %collective-permute-done.p1_ref, ...), custom_call_target="tpu_custom_call" | custom-call | flops 3000000000 | tf_op jit(solution)/shard_map/mix_rim/pallas_call | solution.py:812
  30.9 3.4 %all-to-all-start.1 = ((bf16[8,16,512]{2,1,0:T(8,128)(2,1)}), bf16[8,16,512]{2,1,0:T(8,128)(2,1)S(1)}, u32[]{:S(2)}, u32[]{:S(2)}) async-start(bf16[8,16,512]{2,1,0:T(8,128)(2,1)} %get-tuple-element.61), calls=%async_computation.1 | async-start | bytes 262144 | tf_op jit(solution)/shard_map/all_to_all | solution.py:830
  34.3 1.4 %conv_coarse.1 = (f32[48,768]{1,0:T(8,128)S(1)}, f32[49,48,128]{2,1,0:T(8,128)S(1)}) custom-call(bf16[48,768]{1,0:T(8,128)(2,1)S(1)} %get-tuple-element.62.x_ref.pooled_ref, f32[2,48,49]{2,1,0:T(8,128)S(1)} %copy-done.3, f32[2,48]{1,0:T(2,128)S(1)} %copy-done.10), custom_call_target="tpu_custom_call" | custom-call | flops 2000000000 | tf_op jit(solution)/shard_map/conv_coarse/pallas_call | solution.py:831
  35.7 6.1 %all-to-all-done.1.recv_ref = bf16[8,16,512]{2,1,0:T(8,128)(2,1)S(1)} async-done(((bf16[8,16,512]{2,1,0:T(8,128)(2,1)}), bf16[8,16,512]{2,1,0:T(8,128)(2,1)S(1)}, u32[]{:S(2)}, u32[]{:S(2)}) %all-to-all-start.1) | async-done | bytes 131104 | tf_op jit(solution)/shard_map/all_to_all | solution.py:830
  41.8 1.3 %border_coarse.1.after_ref.own_ref = bf16[48,768]{1,0:T(8,128)(2,1)S(1)} custom-call(s32[24]{0:T(128)S(1)} %get-tuple-element.38.tab_ref, bf16[8,16,512]{2,1,0:T(8,128)(2,1)S(1)} %all-to-all-done.1.recv_ref, f32[48,768]{1,0:T(8,128)S(1)} %get-tuple-element.63.sum_ref, f32[49,48,128]{2,1,0:T(8,128)S(1)} %get-tuple-element.64.mirror_ref), custom_call_target="tpu_custom_call" | custom-call | flops 1000000000 | tf_op jit(solution)/shard_map/border_coarse/pallas_call | solution.py:841
  43.2 0.1 collective-permute-start.6
  43.2 1.6 %collective-permute-start.7 = (bf16[48,768]{1,0:T(8,128)(2,1)S(1)}, bf16[48,768]{1,0:T(8,128)(2,1)S(1)}, u32[]{:S(2)}, u32[]{:S(2)}) collective-permute-start(bf16[48,768]{1,0:T(8,128)(2,1)S(1)} %border_coarse.1.after_ref.own_ref), channel_id=1, source_target_pairs={{0,2},{1,3},{2,0},{3,1},{4,6},{5,7},{6,4},{7,5},{8,10},{9,11},{10,... | collective-permute-start | bytes 221192 | tf_op jit(solution)/shard_map/ppermute | solution.py:714
  44.8 0.2 in_rows.1.fine_ref
  45.0 2.9 %collective-permute-done.7.p2_ref = bf16[48,768]{1,0:T(8,128)(2,1)S(1)} collective-permute-done((bf16[48,768]{1,0:T(8,128)(2,1)S(1)}, bf16[48,768]{1,0:T(8,128)(2,1)S(1)}, u32[]{:S(2)}, u32[]{:S(2)}) %collective-permute-start.7) | collective-permute-done | bytes 73760 | tf_op jit(solution)/shard_map/ppermute | solution.py:714
  47.9 1.3 %collective-permute-done.8.p3_ref = bf16[48,768]{1,0:T(8,128)(2,1)S(1)} collective-permute-done((bf16[48,768]{1,0:T(8,128)(2,1)S(1)}, bf16[48,768]{1,0:T(8,128)(2,1)S(1)}, u32[]{:S(2)}, u32[]{:S(2)}) %collective-permute-start.8) | collective-permute-done | bytes 73760 | tf_op jit(solution)/shard_map/ppermute | solution.py:717
  49.2 1.8 %mix_coarse.1 = bf16[1,48,2304]{2,1,0:T(8,128)(2,1)} custom-call(bf16[48,768]{1,0:T(8,128)(2,1)S(1)} %border_coarse.1.after_ref.own_ref, bf16[48,768]{1,0:T(8,128)(2,1)S(1)} %collective-permute-done.6.p1_ref, bf16[48,768]{1,0:T(8,128)(2,1)S(1)} %collective-permute-done.7.p2_ref, bf16[48,768]{1,0:T(8,128)(2,1)S(1)} %collective-permute-done.8.p3_ref, ...), custom_call_target="tpu_custom_call" | custom-call | flops 2000000000 | tf_op jit(solution)/shard_map/mix_coarse/pallas_call | solution.py:863
  (41 shorter events, 0.1 us)
Async XLA Ops:
  0.0 0.7 %copy-start.11 = (s32[8]{0:T(128)S(1)}, s32[8]{0:T(128)}, u32[]{:S(2)}) copy-start(s32[8]{0:T(128)} %slots_ref.1) | copy-start | bytes 100
  0.0 0.7 %copy-start.12 = (s32[8]{0:T(128)S(1)}, s32[8]{0:T(128)}, u32[]{:S(2)}) copy-start(s32[8]{0:T(128)} %dev_ref.1) | copy-start | bytes 100
  0.0 1.0 %copy-start.2 = (bf16[1,48,2304]{2,1,0:T(8,128)(2,1)S(1)}, bf16[1,48,2304]{2,1,0:T(8,128)(2,1)}, u32[]{:S(2)}) copy-start(bf16[1,48,2304]{2,1,0:T(8,128)(2,1)} %x_ref.3) | copy-start | bytes 663556
  1.0 9.0 %copy-start.3 = (f32[2,48,49]{2,1,0:T(8,128)S(1)}, f32[2,48,49]{2,1,0:T(8,128)}, u32[]{:S(2)}) copy-start(f32[2,48,49]{2,1,0:T(8,128)} %weight_ref.1) | copy-start | bytes 56452
  1.0 9.0 %copy-start.10 = (f32[2,48]{1,0:T(2,128)S(1)}, f32[2,48]{1,0:T(2,128)}, u32[]{:S(2)}) copy-start(f32[2,48]{1,0:T(2,128)} %bias_ref.1) | copy-start | bytes 1156
  2.6 15.7 %all-to-all-start = ((bf16[8,16,896]{2,1,0:T(8,128)(2,1)}), bf16[8,16,896]{2,1,0:T(8,128)(2,1)S(1)}, u32[]{:S(2)}, u32[]{:S(2)}) async-start(bf16[8,16,896]{2,1,0:T(8,128)(2,1)} %get-tuple-element.39), calls=%async_computation | async-start | bytes 458752 | tf_op jit(solution)/shard_map/all_to_all | solution.py:747
  9.9 5.5 %copy-start.17 = (f32[48,4]{0,1:T(4,128)S(1)}, f32[48,4]{0,1:T(4,128)}, u32[]{:S(2)}) copy-start(f32[48,4]{0,1:T(4,128)} %param.32) | copy-start | bytes 2308
  9.9 5.6 %copy-start.18 = (f32[48,4]{0,1:T(4,128)S(1)}, f32[48,4]{0,1:T(4,128)}, u32[]{:S(2)}) copy-start(f32[48,4]{0,1:T(4,128)} %param.33) | copy-start | bytes 2308
  13.8 9.3 %collective-permute-start.2 = (bf16[48,1024]{1,0:T(8,128)(2,1)S(1)}, bf16[48,1024]{1,0:T(8,128)(2,1)S(1)}, u32[]{:S(2)}, u32[]{:S(2)}) collective-permute-start(bf16[48,1024]{1,0:T(8,128)(2,1)S(1)} %get-tuple-element.50.own_ref), channel_id=1, source_target_pairs={{0,1},{1,0},{2,3},{3,2},{4,5},{5,4},{6,7},{7,6},{8,9},{9,8},{10,11... | collective-permute-start | bytes 294920 | tf_op jit(solution)/shard_map/ppermute | solution.py:775
  13.9 8.3 %collective-permute-start.3 = (bf16[48,1024]{1,0:T(8,128)(2,1)S(1)}, bf16[48,1024]{1,0:T(8,128)(2,1)S(1)}, u32[]{:S(2)}, u32[]{:S(2)}) collective-permute-start(bf16[48,1024]{1,0:T(8,128)(2,1)S(1)} %get-tuple-element.50.own_ref), channel_id=1, source_target_pairs={{0,2},{1,3},{2,0},{3,1},{4,6},{5,7},{6,4},{7,5},{8,10},{9,11},{10,... | collective-permute-start | bytes 294920 | tf_op jit(solution)/shard_map/ppermute | solution.py:774
  18.4 4.0 %copy-start = (bf16[2,768,192]{1,2,0:T(8,128)(2,1)S(1)}, bf16[2,768,192]{1,2,0:T(8,128)(2,1)}, u32[]{:S(2)}) copy-start(bf16[2,768,192]{1,2,0:T(8,128)(2,1)} %param.27) | copy-start | bytes 1769476
  18.4 4.0 %copy-start.1 = (bf16[2,192,768]{2,1,0:T(8,128)(2,1)S(1)}, bf16[2,192,768]{2,1,0:T(8,128)(2,1)}, u32[]{:S(2)}) copy-start(bf16[2,192,768]{2,1,0:T(8,128)(2,1)} %down_ref.1) | copy-start | bytes 1769476
  18.4 4.0 %copy-start.4 = (s32[1,2304]{1,0:T(1,128)S(1)}, s32[1,2304]{1,0:T(1,128)}, u32[]{:S(2)}) copy-start(s32[1,2304]{1,0:T(1,128)} %mask_ref.3) | copy-start | bytes 27652
  18.4 4.0 %copy-start.5 = (f32[2,768]{1,0:T(2,128)S(1)}, f32[2,768]{1,0:T(2,128)}, u32[]{:S(2)}) copy-start(f32[2,768]{1,0:T(2,128)} %up_bias_ref.1) | copy-start | bytes 18436
  18.4 4.0 %copy-start.6 = (f32[2,192]{1,0:T(2,128)S(1)}, f32[2,192]{1,0:T(2,128)}, u32[]{:S(2)}) copy-start(f32[2,192]{1,0:T(2,128)} %gain_ref.1) | copy-start | bytes 4612
  18.4 4.0 %copy-start.7 = (f32[2,192]{1,0:T(2,128)S(1)}, f32[2,192]{1,0:T(2,128)}, u32[]{:S(2)}) copy-start(f32[2,192]{1,0:T(2,128)} %shift_ref.1) | copy-start | bytes 4612
  18.4 4.0 %copy-start.8 = (f32[2,192]{1,0:T(2,128)S(1)}, f32[2,192]{1,0:T(2,128)}, u32[]{:S(2)}) copy-start(f32[2,192]{1,0:T(2,128)} %down_bias_ref.1) | copy-start | bytes 4612
  18.4 4.0 %copy-start.9 = (f32[2,48]{1,0:T(2,128)S(1)}, f32[2,48]{1,0:T(2,128)}, u32[]{:S(2)}) copy-start(f32[2,48]{1,0:T(2,128)} %scale_ref.1) | copy-start | bytes 1156
  18.4 4.0 %copy-start.14 = (bf16[384,128]{1,0:T(8,128)(2,1)S(1)}, bf16[384,128]{1,0:T(8,128)(2,1)}, u32[]{:S(2)}) copy-start(bf16[384,128]{1,0:T(8,128)(2,1)} %constant.8.clone.pool_ref) | copy-start | bytes 294916
  20.5 5.8 %collective-permute-start = (bf16[48,1280]{1,0:T(8,128)(2,1)S(1)}, bf16[48,1280]{1,0:T(8,128)(2,1)S(1)}, u32[]{:S(2)}, u32[]{:S(2)}) collective-permute-start(bf16[48,1280]{1,0:T(8,128)(2,1)S(1)} %conv_border.1.after_ref.own_ref), channel_id=1, source_target_pairs={{0,1},{1,0},{2,3},{3,2},{4,5},{5,4},{6,7},{7,6},{8,9},{9,8},{10,11... | collective-permute-start | bytes 368648 | tf_op jit(solution)/shard_map/ppermute | solution.py:715
  20.6 5.7 %collective-permute-start.1 = (bf16[48,1280]{1,0:T(8,128)(2,1)S(1)}, bf16[48,1280]{1,0:T(8,128)(2,1)S(1)}, u32[]{:S(2)}, u32[]{:S(2)}) collective-permute-start(bf16[48,1280]{1,0:T(8,128)(2,1)S(1)} %conv_border.1.after_ref.own_ref), channel_id=1, source_target_pairs={{0,2},{1,3},{2,0},{3,1},{4,6},{5,7},{6,4},{7,5},{8,10},{9,11},{10,... | collective-permute-start | bytes 368648 | tf_op jit(solution)/shard_map/ppermute | solution.py:714
  22.2 1.3 %collective-permute-start.4 = (bf16[48,1024]{1,0:T(8,128)(2,1)S(1)}, bf16[48,1024]{1,0:T(8,128)(2,1)S(1)}, u32[]{:S(2)}, u32[]{:S(2)}) collective-permute-start(bf16[48,1024]{1,0:T(8,128)(2,1)S(1)} %collective-permute-done.3.p2_ref), channel_id=1, source_target_pairs={{0,1},{1,0},{2,3},{3,2},{4,5},{5,4},{6,7},{7,6},{8,9},{9,8},{10,11... | collective-permute-start | bytes 294920 | tf_op jit(solution)/shard_map/ppermute | solution.py:777
  22.4 1.1 %copy-start.15 = (bf16[256,128]{1,0:T(8,128)(2,1)S(1)}, bf16[256,128]{1,0:T(8,128)(2,1)}, u32[]{:S(2)}) copy-start(bf16[256,128]{1,0:T(8,128)(2,1)} %constant.9.clone.middle_pool_ref) | copy-start | bytes 196612
  23.5 4.2 %copy-start.13 = (bf16[768,384]{1,0:T(8,128)(2,1)S(1)}, bf16[768,384]{1,0:T(8,128)(2,1)}, u32[]{:S(2)}) copy-start(bf16[768,384]{1,0:T(8,128)(2,1)} %constant.11.clone.pack_ref) | copy-start | bytes 1769476
  23.5 4.2 %copy-start.16 = (bf16[128,128]{1,0:T(8,128)(2,1)S(1)}, bf16[128,128]{1,0:T(8,128)(2,1)}, u32[]{:S(2)}) copy-start(bf16[128,128]{1,0:T(8,128)(2,1)} %constant.10.clone.rim_pool_ref) | copy-start | bytes 98308
  26.4 1.3 %collective-permute-start.5 = (bf16[48,1280]{1,0:T(8,128)(2,1)S(1)}, bf16[48,1280]{1,0:T(8,128)(2,1)S(1)}, u32[]{:S(2)}, u32[]{:S(2)}) collective-permute-start(bf16[48,1280]{1,0:T(8,128)(2,1)S(1)} %collective-permute-done.1.p2_ref), channel_id=1, source_target_pairs={{0,1},{1,0},{2,3},{3,2},{4,5},{5,4},{6,7},{7,6},{8,9},{9,8},{10,11... | collective-permute-start | bytes 368648 | tf_op jit(solution)/shard_map/ppermute | solution.py:717
  30.9 10.9 %all-to-all-start.1 = ((bf16[8,16,512]{2,1,0:T(8,128)(2,1)}), bf16[8,16,512]{2,1,0:T(8,128)(2,1)S(1)}, u32[]{:S(2)}, u32[]{:S(2)}) async-start(bf16[8,16,512]{2,1,0:T(8,128)(2,1)} %get-tuple-element.61), calls=%async_computation.1 | async-start | bytes 262144 | tf_op jit(solution)/shard_map/all_to_all | solution.py:830
  43.2 4.8 %collective-permute-start.6 = (bf16[48,768]{1,0:T(8,128)(2,1)S(1)}, bf16[48,768]{1,0:T(8,128)(2,1)S(1)}, u32[]{:S(2)}, u32[]{:S(2)}) collective-permute-start(bf16[48,768]{1,0:T(8,128)(2,1)S(1)} %border_coarse.1.after_ref.own_ref), channel_id=1, source_target_pairs={{0,1},{1,0},{2,3},{3,2},{4,5},{5,4},{6,7},{7,6},{8,9},{9,8},{10,11... | collective-permute-start | bytes 221192 | tf_op jit(solution)/shard_map/ppermute | solution.py:715
  43.2 4.7 %collective-permute-start.7 = (bf16[48,768]{1,0:T(8,128)(2,1)S(1)}, bf16[48,768]{1,0:T(8,128)(2,1)S(1)}, u32[]{:S(2)}, u32[]{:S(2)}) collective-permute-start(bf16[48,768]{1,0:T(8,128)(2,1)S(1)} %border_coarse.1.after_ref.own_ref), channel_id=1, source_target_pairs={{0,2},{1,3},{2,0},{3,1},{4,6},{5,7},{6,4},{7,5},{8,10},{9,11},{10,... | collective-permute-start | bytes 221192 | tf_op jit(solution)/shard_map/ppermute | solution.py:714
  47.9 1.3 %collective-permute-start.8 = (bf16[48,768]{1,0:T(8,128)(2,1)S(1)}, bf16[48,768]{1,0:T(8,128)(2,1)S(1)}, u32[]{:S(2)}, u32[]{:S(2)}) collective-permute-start(bf16[48,768]{1,0:T(8,128)(2,1)S(1)} %collective-permute-done.7.p2_ref), channel_id=1, source_target_pairs={{0,1},{1,0},{2,3},{3,2},{4,5},{5,4},{6,7},{7,6},{8,9},{9,8},{10,11... | collective-permute-start | bytes 221192 | tf_op jit(solution)/shard_map/ppermute | solution.py:717

commit v9 on v8

--- a/solution.py
+++ b/solution.py
@@ -41,23 +41,7 @@
     return one_hot((384, 128), dense), one_hot((128, 128), rim), one_hot((256, 128), middle)
 
 
-def strip_pairs():
-    pack = []
-    for row in range(3):
-        for col in range(HALF):
-            pack.append((row * 32 + 3 + col, row * 24 + col))
-            pack.append(((21 + row) * 32 + 3 + col, 128 + row * 24 + col))
-    for row in range(HALF):
-        for j in range(3):
-            index = row * 3 + j
-            lane = 72 + index if row < 16 else index - 48
-            pack.append((row * 32 + 3 + j, lane if row < 16 else 256 + lane))
-            pack.append((row * 32 + 24 + j, 128 + lane if row < 16 else 256 + 64 + lane))
-    return pack
-
-
 POOL, RIM_POOL, MIDDLE_POOL = pool_tables()
-SMALL_PACK = one_hot((768, 384), strip_pairs())
 
 
 def dot(left, right):
@@ -331,27 +315,33 @@
     half, within = lane // 64, lane % 64
     low_half = tall(lane < 64)
 
+    group = lax.broadcasted_iota(jnp.int32, (ROWS, 128), 0) // 16
+
     def band_cells(band, offset):
         source, scale = band_source(tab_ref, band)
         main = jnp.concatenate([recv_ref[source, :, 256 * g + offset : 256 * g + offset + 128] for g in range(3)], axis=0)
-        rest = recv_ref[source, :, 768:896].astype(F32) * scale
-        rest = jnp.concatenate([rest, pltpu.roll(rest, 128 - 40, 1), pltpu.roll(rest, 128 - 80, 1)], axis=0)
-        return main.astype(F32) * scale, rest
-
-    def halo_rows(bands, folded, last):
-        left, middle, right = [band_cells(band, 0) for band in bands]
+        return main.astype(F32) * scale, recv_ref[source, :, 768:896].astype(F32) * scale
+
+    def halo_rows(bands, folded, last, rest_side):
+        sides = [band_cells(band, 0) for band in bands]
+        first_columns = jnp.where((lane + jnp.where(last, 16, 0)) % 48 < 24, 1, 0)
+        ends = jnp.where(tall(first_columns + jnp.where(folded, 1, 0) == 1), sides[2][0], sides[0][0])
+        rest_lane = lane_ids((16, 128)) % 40
+        rests = jnp.where(rest_lane < 20, sides[1][1], pltpu.roll(sides[rest_side][1], 20, 1))
+        rests = jnp.concatenate([rests] * 3, axis=0)
         tiles = []
         for first_row in (0, 2):
             row = first_row + half
+            inner = (within >= 3) & (within < 51)
             col = jnp.where(within < 3, 45 + within, jnp.where(within < 51, within - 3, within - 51))
             index = row * 48 + col
             index = jnp.where(folded, 143 - index, index)
             in_main = index - jnp.where(last, 16, 0)
             rest = (in_main < 0) | (in_main > 127)
-            in_rest = jnp.where(in_main < 0, in_main + 16, in_main - 128)
-            main_index, rest_index = tall(in_main & 127), tall(in_rest & 127)
-            picked = [jnp.where(tall(rest), lanes_from(r, rest_index), lanes_from(m, main_index)) for m, r in (left, middle, right)]
-            value = jnp.where(tall(within < 3), picked[0], jnp.where(tall(within < 51), picked[1], picked[2]))
+            in_rest = jnp.where(in_main < 0, in_main + 16, in_main - 128) + jnp.where(inner, 0, 20)
+            main_index, rest_index = tall(in_main & 127), (tall(in_rest) + 40 * group) & 127
+            value = jnp.where(tall(inner), lanes_from(sides[1][0], main_index), lanes_from(ends, main_index))
+            value = jnp.where(tall(rest), lanes_from(rests, rest_index), value)
             tiles.append(jnp.where(tall((within < 54) & (row < 3)), value, 0.0))
         return tiles
 
@@ -359,19 +349,19 @@
         return jnp.where(low_half, pltpu.roll(first, 64, 1), pltpu.roll(second, 64, 1))
 
     zeros = jnp.zeros((ROWS, 128), F32)
-    below = halo_rows((0, 1, 2), False, True)
+    below = halo_rows((0, 1, 2), False, True, 2)
     first_fix = row_sums(((0, 0, below[0]), (0, 1, joined(below[0], below[1])), (0, 2, below[1]), (1, 0, below[1])), mirror_ref)
     folded = tab_ref[8] == 2
-    above = halo_rows((5, 6, 7), folded, folded)
+    above = halo_rows((5, 6, 7), folded, folded, 0)
     edge = joined(zeros, above[0])
     last_fix = row_sums(((0, 6, edge), (1, 4, edge), (1, 5, above[0]), (1, 6, joined(above[0], above[1]))), mirror_ref)
 
-    left, right = band_cells(3, 128), band_cells(4, 128)
+    left, right = [(main, jnp.concatenate([rest] * 3, axis=0)) for main, rest in (band_cells(3, 128), band_cells(4, 128))]
     beside = []
     for j in range(3):
         which = jnp.where(half == 0, j, 2 - j)
         in_main = jnp.minimum(3 * within + which, 127)
-        main_index, rest_index = tall(in_main), tall(jnp.clip(3 * (within - 40) + 16 + which, 0, 127))
+        main_index, rest_index = tall(in_main), tall(jnp.clip(3 * (within - 40) + 16 + which, 0, 39)) + 40 * group
         picked = [
             jnp.where(tall(within < 40), lanes_from(main, main_index), lanes_from(rest, rest_index)) for main, rest in (left, right)
         ]
@@ -511,6 +501,7 @@
 def border_coarse(tab_ref, recv_ref, sum_ref, mirror_ref, out_ref):
     lane = lane_ids((8, 128))
     half, within, segment, inside = lane // 64, lane % 64, lane // 32, lane % 32
+    group = lax.broadcasted_iota(jnp.int32, (ROWS, 128), 0) // 16
 
     def band_main(band):
         source, scale = band_source(tab_ref, band)
@@ -518,8 +509,7 @@
 
     def band_rest(band):
         source, scale = band_source(tab_ref, band)
-        rest = recv_ref[source, :, 384:512].astype(F32) * scale
-        return jnp.concatenate([rest, pltpu.roll(rest, 128 - 24, 1), pltpu.roll(rest, 128 - 48, 1)], axis=0)
+        return jnp.concatenate([recv_ref[source, :, 384:512].astype(F32) * scale] * 3, axis=0)
 
     def halo_rows(bands, folded):
         col = jnp.where(inside < 3, 21 + inside, jnp.where(inside < 27, inside - 3, inside - 27))
@@ -543,7 +533,7 @@
     for j in range(3):
         which = jnp.where(half == 0, j, 2 - j)
         main_index = tall(jnp.minimum(72 + 3 * within + which, 127))
-        rest_index = tall(jnp.clip(3 * (within - 16) + which, 0, 127))
+        rest_index = tall(jnp.clip(3 * (within - 16) + which, 0, 23)) + 24 * group
         picked = [
             jnp.where(tall(within < 16), lanes_from(main, main_index), lanes_from(rest, rest_index)) for main, rest in sides
         ]
@@ -609,7 +599,7 @@
 def make_mix_rim(count):
     def mix_rim(
         tab_ref, own_ref, p1_ref, p2_ref, p3_ref, x_ref, mask_ref, pool_cells_ref, weights_ref, values_ref, pool_ref, rim_pool_ref,
-        pack_ref, middle_pooled_ref, fine_ref, msg_ref, all_pooled_ref, cat_ref, pooled_ref, mains_ref, rest_ref,
+        middle_pooled_ref, fine_ref, msg_ref, all_pooled_ref, cat_ref, pooled_ref, mains_ref, rest_ref,
     ):
         gather_rows((own_ref, p1_ref, p2_ref, p3_ref), cat_ref)
         block = RIM // 2
@@ -628,19 +618,26 @@
         for i in range(4):
             pooled_ref[:, 128 * i + 128 : 128 * i + 256] = rim[i * ROWS : (i + 1) * ROWS].astype(BF)
 
-        packed = dot(pooled_ref[...], pack_ref[...])
-        lane = lane_ids((ROWS, 128))
-        blocks = (packed[:, 0:128], packed[:, 128:256])
-        for r in range(2):
-            for c in range(2):
-                mains_ref[2 * r + c] = jnp.where(lane < 72, blocks[r], blocks[c]).astype(BF)
-        lane = lane_ids((16, 128))
+        groups = [pooled_ref[:, 128 * i : 128 * i + 128].astype(F32) for i in range(GROUPS)]
+        lane = lane_ids((8, 128))
+        index = lane // 24 * 32 + 3 + lane % 24
+        rows = [lanes_from(groups[0], tall(index & 127)), lanes_from(groups[5], tall((index + 32) & 127))]
+        cell = jnp.clip(lane - 72, 0, 47)
+        rest_cell = lane_ids((ROWS, 128)) - lax.broadcasted_iota(jnp.int32, (ROWS, 128), 0) // 16 * 24
+        rest_valid = (rest_cell >= 0) & (rest_cell < 24)
+        rest_cell = jnp.clip(rest_cell, 0, 23)
         for c in range(2):
-            rest = packed[:, 256:384]
-            rest = pltpu.roll(rest, 64, 1) if c else rest
-            parts = [rest[0:16], pltpu.roll(rest[16:32], 24, 1), pltpu.roll(rest[32:48], 48, 1)]
-            joined = jnp.where(lane < 24, parts[0], jnp.where(lane < 48, parts[1], parts[2]))
-            rest_ref[c] = jnp.where(lane < 72, joined, 0.0).astype(BF)
+            first = 24 if c else 3
+            index = tall(cell // 3 % 4 * 32 + first + cell % 3)
+            column = lanes_from(groups[0], index)
+            for i in range(1, 4):
+                column = jnp.where(tall(cell // 12 == i), lanes_from(groups[i], index), column)
+            for r in range(2):
+                mains_ref[2 * r + c] = jnp.where(tall(lane < 72), rows[r], column).astype(BF)
+            index = rest_cell // 3 % 4 * 32 + first + rest_cell % 3
+            rest = jnp.where(rest_cell < 12, lanes_from(groups[4], index), lanes_from(groups[5], index))
+            rest = jnp.where(rest_valid, rest, 0.0)
+            rest_ref[c] = (rest[0:16] + rest[16:32] + rest[32:48]).astype(BF)
 
         def fill(dev, carry):
             both = tab_ref[16 + dev]
@@ -709,11 +706,12 @@
 PARAMS = pltpu.CompilerParams(vmem_limit_bytes=24 * 1024 * 1024)
 
 
-def every_channel(own, beside_work=lambda own: ()):
+def every_channel(own, first_work, later_work=lambda *results: ()):
     pairs = lambda bit: [(i, i ^ bit) for i in range(4)]
     across = lax.ppermute(own, "chan", pairs(2))
-    beside = lax.ppermute(own, "chan", pairs(1))
-    across, *results = lax.optimization_barrier((across, *beside_work(own)))
+    near, *results = lax.optimization_barrier((own, *first_work(own)))
+    beside = lax.ppermute(near, "chan", pairs(1))
+    across, *results = lax.optimization_barrier((across, *results, *later_work(*results)))
     diagonal = lax.ppermute(across, "chan", pairs(1))
     return (own, beside, across, diagonal), results
 
@@ -776,9 +774,8 @@
     middle_across, _ = lax.optimization_barrier((middle_across, conv))
     middle_pieces = (inner_middle, middle_beside, middle_across, lax.ppermute(middle_across, "chan", pairs(1)))
 
-    def beside_gather(own):
-        results = spread_params(own)
-        return *results, *pl.pallas_call(
+    def mix_middle_cells(*results):
+        return pl.pallas_call(
             mix_middle,
             in_specs=[VMEM] * 8,
             out_specs=[VMEM] * 2,
@@ -807,11 +804,11 @@
             pool_weight, spread_weight, pool,
         )
 
-    pieces, results = every_channel(conv, beside_gather)
+    pieces, results = every_channel(conv, spread_params, mix_middle_cells)
     rim_cells, _, rim_mask, rim_weights, fine_weights, fine_values, coarse_weights, coarse_values, middle, middle_pooled = results
     rim, messages, pooled = pl.pallas_call(
         make_mix_rim(count),
-        in_specs=[SMEM] + [VMEM] * 13,
+        in_specs=[SMEM] + [VMEM] * 12,
         out_specs=[VMEM] * 3,
         out_shape=[shaped(ROWS, RIM), shaped(count, 16, 512), shaped(ROWS, 768)],
         scratch_shapes=[
@@ -825,7 +822,7 @@
         name="mix_rim",
     )(
         table, *pieces, rim_cells, rim_mask, rim_weights, fine_weights, fine_values, pool, jnp.asarray(RIM_POOL),
-        jnp.asarray(SMALL_PACK), middle_pooled,
+        middle_pooled,
     )
     arrived = lax.all_to_all(messages, "tile", 0, 0, tiled=True)
     inner, taps = pl.pallas_call(

time: 51.3 us -> 50.2 us (0.979)
  waiting for transfers between devices: 16.2 us -> 15 us
    all_to_all x2, starting transfers between devices: 10.7 us -> 11.4 us  [per_device(): arrived = lax.all_to_all(messages, 'tile', 0, 0, tiled=True)]
    ppermute x2, waiting for transfers between devices: 4.34 us -> 3.66 us  [every_channel(): across = lax.ppermute(own, 'chan', pairs(2))]
    ppermute x2, starting transfers between devices: 3.12 us -> 2.59 us  [every_channel(): across = lax.ppermute(own, 'chan', pairs(2))]
    unnamed x40 -> x38, local copies, waits for them, and re-layouts: 1.17 us -> 1.14 us
  transfers between devices with their start and end apart: 11 -> 11, of which waited for: 7 -> 6; matrix products, arithmetic and copies ran while one was open for 0% -> 0% of each run, Pallas kernels for 19% -> 19%
where the time goes in v9:
time: 50.2 us; the launch traced here: 49.9 us
  Pallas kernels  17.3 us (34%)
  starting transfers between devices  16.1 us (32%)
  waiting for transfers between devices  15 us (30%)
  local copies, waits for them, and re-layouts  1.14 us (2%)
    all_to_all x2, starting transfers between devices, per_device(): arrived = lax.all_to_all(messages, 'tile', 0, 0, tiled=True)  11.4 us
    all_to_all x2, waiting for transfers between devices, per_device(): arrived = lax.all_to_all(messages, 'tile', 0, 0, tiled=True)  8.78 us
    pallas_call x1, Pallas kernels, per_device(): pl.pallas_call(lambda tab_ref, *refs: conv_inner(*refs), in_specs=[SMEM]...  3.84 us
    ppermute x2, waiting for transfers between devices, every_channel(): across = lax.ppermute(own, 'chan', pairs(2))  3.66 us
    pallas_call x1, Pallas kernels, per_device(): pl.pallas_call(make_mix_rim(count), in_specs=[SMEM] + [VMEM] * 12, out_sp...  2.98 us
    ppermute x2, waiting for transfers between devices, every_channel(): diagonal = lax.ppermute(across, 'chan', pairs(1))  2.59 us
    ppermute x2, starting transfers between devices, every_channel(): across = lax.ppermute(own, 'chan', pairs(2))  2.59 us
    pallas_call x1, Pallas kernels, per_device(): pl.pallas_call(conv_border, in_specs=[SMEM] + [VMEM] * 3, out_specs=VMEM,...  1.92 us
  transfers between devices with their start and end apart: 11, of which 6 were waited for; matrix products, arithmetic and copies ran while one was open for 0% of the time, Pallas kernels for 19%

profile of v9, /device:TPU:0, one launch (start us, length us, event | category | flops | bytes accessed | tf_op | source)
XLA Modules:
  0.0 49.9 jit_solution(2119846973596049743)
XLA Ops:
  0.0 0.1 strip_table.1.pack_ref
  0.1 0.9 %copy-done.2 = bf16[1,48,2304]{2,1,0:T(8,128)(2,1)S(1)} copy-done((bf16[1,48,2304]{2,1,0:T(8,128)(2,1)S(1)}, bf16[1,48,2304]{2,1,0:T(8,128)(2,1)}, u32[]{:S(2)}) %copy-start.2) | copy-done | bytes 221208
  1.0 1.7 %prep.1 = (bf16[8,16,896]{2,1,0:T(8,128)(2,1)}, s32[24]{0:T(128)S(1)}) custom-call(s32[8]{0:T(128)S(1)} %copy-done.11, s32[8]{0:T(128)S(1)} %copy-done.12, bf16[1,48,2304]{2,1,0:T(8,128)(2,1)S(1)} %copy-done.2, bf16[384,256]{1,0:T(8,128)(2,1)S(1)} %strip_table.1.pack_ref), custom_call_target="tpu_custom_call" | custom-call | flops 10000000000 | tf_op jit(solution)/shard_map/prep/pallas_call | solution.py:729
  2.6 7.3 %all-to-all-start = ((bf16[8,16,896]{2,1,0:T(8,128)(2,1)}), bf16[8,16,896]{2,1,0:T(8,128)(2,1)S(1)}, u32[]{:S(2)}, u32[]{:S(2)}) async-start(bf16[8,16,896]{2,1,0:T(8,128)(2,1)} %get-tuple-element.50), calls=%async_computation | async-start | bytes 458752 | tf_op jit(solution)/shard_map/all_to_all | solution.py:745
  9.9 0.0 copy-start.17
  9.9 3.8 %conv_inner.1 = (f32[48,1280]{1,0:T(8,128)S(1)}, bf16[48,1024]{1,0:T(8,128)(2,1)S(1)}, f32[28,48,128]{2,1,0:T(8,128)S(1)}) custom-call(s32[24]{0:T(128)S(1)} %get-tuple-element.49.tab_ref, bf16[1,48,2304]{2,1,0:T(8,128)(2,1)S(1)} %copy-done.2, f32[2,48,49]{2,1,0:T(8,128)S(1)} %copy-done.3, f32[2,48]{1,0:T(2,128)S(1)} %copy-done.10), custom_call_target="tpu_custom_call" | custom-call | flops 4000000000 | tf_op jit(solution)/shard_map/conv_inner/pallas_call | solution.py:746
  13.8 1.6 %collective-permute-start.3 = (bf16[48,1024]{1,0:T(8,128)(2,1)S(1)}, bf16[48,1024]{1,0:T(8,128)(2,1)S(1)}, u32[]{:S(2)}, u32[]{:S(2)}) collective-permute-start(bf16[48,1024]{1,0:T(8,128)(2,1)S(1)} %get-tuple-element.70.own_ref), channel_id=1, source_target_pairs={{0,2},{1,3},{2,0},{3,1},{4,6},{5,7},{6,4},{7,5},{8,10},{9,11},{10,... | collective-permute-start | bytes 294920 | tf_op jit(solution)/shard_map/ppermute | solution.py:772
  15.4 0.1 copy.19.pool_weight_ref
  15.4 0.1 copy.20.spread_weight_ref
  15.5 2.8 %all-to-all-done.recv_ref = bf16[8,16,896]{2,1,0:T(8,128)(2,1)S(1)} async-done(((bf16[8,16,896]{2,1,0:T(8,128)(2,1)}), bf16[8,16,896]{2,1,0:T(8,128)(2,1)S(1)}, u32[]{:S(2)}, u32[]{:S(2)}) %all-to-all-start) | async-done | bytes 229408 | tf_op jit(solution)/shard_map/all_to_all | solution.py:745
  18.4 0.0 copy-start.7
  18.4 0.0 copy-start.13
  18.4 1.9 %conv_border.1.after_ref.own_ref = bf16[48,1280]{1,0:T(8,128)(2,1)S(1)} custom-call(s32[24]{0:T(128)S(1)} %get-tuple-element.49.tab_ref, bf16[8,16,896]{2,1,0:T(8,128)(2,1)S(1)} %all-to-all-done.recv_ref, f32[48,1280]{1,0:T(8,128)S(1)} %get-tuple-element.51.sum_ref, f32[28,48,128]{2,1,0:T(8,128)S(1)} %get-tuple-element.52.mirror_ref), custom_call_target="tpu_custom_call" | custom-call | flops 2000000000 | tf_op jit(solution)/shard_map/conv_border/pallas_call | solution.py:761
  20.3 1.6 %collective-permute-start.1 = (bf16[48,1280]{1,0:T(8,128)(2,1)S(1)}, bf16[48,1280]{1,0:T(8,128)(2,1)S(1)}, u32[]{:S(2)}, u32[]{:S(2)}) collective-permute-start(bf16[48,1280]{1,0:T(8,128)(2,1)S(1)} %conv_border.1.after_ref.own_ref), channel_id=1, source_target_pairs={{0,2},{1,3},{2,0},{3,1},{4,6},{5,7},{6,4},{7,5},{8,10},{9,11},{10,... | collective-permute-start | bytes 368648 | tf_op jit(solution)/shard_map/ppermute | solution.py:711
  22.0 0.0 copy-start.14
  22.0 0.7 %params.1 = (bf16[48,1280]{1,0:T(8,128)(2,1)S(1)}, bf16[48,1024]{1,0:T(8,128)(2,1)S(1)}, f32[8,1280]{1,0:T(8,128)S(1)}, f32[48,512]{1,0:T(8,128)S(1)}, bf16[912,...) custom-call(bf16[48,1280]{1,0:T(8,128)(2,1)S(1)} %conv_border.1.after_ref.o, ...), custom_call_target="tpu_custom_call" | custom-call | flops 2000000000 | tf_op jit(solution)/shard_map/params/pallas_call | solution.py:794
  22.7 0.0 copy-start.15
  22.7 0.6 %collective-permute-start = (bf16[48,1280]{1,0:T(8,128)(2,1)S(1)}, bf16[48,1280]{1,0:T(8,128)(2,1)S(1)}, u32[]{:S(2)}, u32[]{:S(2)}) collective-permute-start(bf16[48,1280]{1,0:T(8,128)(2,1)S(1)} %conv_border.1.after_ref.own_ref), channel_id=1, source_target_pairs={{0,1},{1,0},{2,3},{3,2},{4,5},{5,4},{6,7},{7,6},{8,9},{9,8},{10,11... | collective-permute-start | bytes 368648 | tf_op jit(solution)/shard_map/ppermute | solution.py:713
  23.3 1.4 %mix_middle.1 = (bf16[48,1024]{1,0:T(8,128)(2,1)S(1)}, bf16[48,512]{1,0:T(8,128)(2,1)S(1)}) custom-call(bf16[48,1024]{1,0:T(8,128)(2,1)S(1)} %get-tuple-element.70.own_ref, bf16[48,1024]{1,0:T(8,128)(2,1)S(1)} %collective-permute-done.2.p1_ref, bf16[48,1024]{1,0:T(8,128)(2,1)S(1)} %collective-permute-done.3.p2_ref, ...), custom_call_target="tpu_custom_call" | custom-call | flops 1000000000 | tf_op jit(solution)/shard_map/mix_middle/pallas_call | solution.py:778
  24.7 0.6 %collective-permute-done.1.p2_ref = bf16[48,1280]{1,0:T(8,128)(2,1)S(1)} collective-permute-done((bf16[48,1280]{1,0:T(8,128)(2,1)S(1)}, bf16[48,1280]{1,0:T(8,128)(2,1)S(1)}, u32[]{:S(2)}, u32[]{:S(2)}) %collective-permute-start.1) | collective-permute-done | bytes 122912 | tf_op jit(solution)/shard_map/ppermute | solution.py:711
  25.3 1.3 %collective-permute-done.5.p3_ref = bf16[48,1280]{1,0:T(8,128)(2,1)S(1)} collective-permute-done((bf16[48,1280]{1,0:T(8,128)(2,1)S(1)}, bf16[48,1280]{1,0:T(8,128)(2,1)S(1)}, u32[]{:S(2)}, u32[]{:S(2)}) %collective-permute-start.5) | collective-permute-done | bytes 122912 | tf_op jit(solution)/shard_map/ppermute | solution.py:715
  26.6 3.0 %mix_rim.1 = (bf16[48,1280]{1,0:T(8,128)(2,1)S(1)}, bf16[8,16,512]{2,1,0:T(8,128)(2,1)}, bf16[48,768]{1,0:T(8,128)(2,1)S(1)}) custom-call(s32[24]{0:T(128)S(1)} %get-tuple-element.49.tab_ref, bf16[48,1280]{1,0:T(8,128)(2,1)S(1)} %conv_border.1.after_ref.own_ref, bf16[48,1280]{1,0:T(8,128)(2,1)S(1)} %collective-permute-done.p1_ref, ...), custom_call_target="tpu_custom_call" | custom-call | flops 3000000000 | tf_op jit(solution)/shard_map/mix_rim/pallas_call | solution.py:809
  29.6 4.1 %all-to-all-start.1 = ((bf16[8,16,512]{2,1,0:T(8,128)(2,1)}), bf16[8,16,512]{2,1,0:T(8,128)(2,1)S(1)}, u32[]{:S(2)}, u32[]{:S(2)}) async-start(bf16[8,16,512]{2,1,0:T(8,128)(2,1)} %get-tuple-element.81), calls=%async_computation.1 | async-start | bytes 262144 | tf_op jit(solution)/shard_map/all_to_all | solution.py:827
  33.7 1.4 %conv_coarse.1 = (f32[48,768]{1,0:T(8,128)S(1)}, f32[49,48,128]{2,1,0:T(8,128)S(1)}) custom-call(bf16[48,768]{1,0:T(8,128)(2,1)S(1)} %get-tuple-element.82.x_ref.pooled_ref, f32[2,48,49]{2,1,0:T(8,128)S(1)} %copy-done.3, f32[2,48]{1,0:T(2,128)S(1)} %copy-done.10), custom_call_target="tpu_custom_call" | custom-call | flops 2000000000 | tf_op jit(solution)/shard_map/conv_coarse/pallas_call | solution.py:828
  35.0 6.0 %all-to-all-done.1.recv_ref = bf16[8,16,512]{2,1,0:T(8,128)(2,1)S(1)} async-done(((bf16[8,16,512]{2,1,0:T(8,128)(2,1)}), bf16[8,16,512]{2,1,0:T(8,128)(2,1)S(1)}, u32[]{:S(2)}, u32[]{:S(2)}) %all-to-all-start.1) | async-done | bytes 131104 | tf_op jit(solution)/shard_map/all_to_all | solution.py:827
  41.0 1.4 %border_coarse.1.after_ref.own_ref = bf16[48,768]{1,0:T(8,128)(2,1)S(1)} custom-call(s32[24]{0:T(128)S(1)} %get-tuple-element.49.tab_ref, bf16[8,16,512]{2,1,0:T(8,128)(2,1)S(1)} %all-to-all-done.1.recv_ref, f32[48,768]{1,0:T(8,128)S(1)} %get-tuple-element.83.sum_ref, f32[49,48,128]{2,1,0:T(8,128)S(1)} %get-tuple-element.84.mirror_ref), custom_call_target="tpu_custom_call" | custom-call | flops 1000000000 | tf_op jit(solution)/shard_map/border_coarse/pallas_call | solution.py:838
  42.4 1.0 %collective-permute-start.7 = (bf16[48,768]{1,0:T(8,128)(2,1)S(1)}, bf16[48,768]{1,0:T(8,128)(2,1)S(1)}, u32[]{:S(2)}, u32[]{:S(2)}) collective-permute-start(bf16[48,768]{1,0:T(8,128)(2,1)S(1)} %border_coarse.1.after_ref.own_ref), channel_id=1, source_target_pairs={{0,2},{1,3},{2,0},{3,1},{4,6},{5,7},{6,4},{7,5},{8,10},{9,11},{10,... | collective-permute-start | bytes 221192 | tf_op jit(solution)/shard_map/ppermute | solution.py:711
  43.4 0.2 in_rows.1.fine_ref
  43.7 0.1 collective-permute-start.6
  43.8 3.1 %collective-permute-done.7.p2_ref = bf16[48,768]{1,0:T(8,128)(2,1)S(1)} collective-permute-done((bf16[48,768]{1,0:T(8,128)(2,1)S(1)}, bf16[48,768]{1,0:T(8,128)(2,1)S(1)}, u32[]{:S(2)}, u32[]{:S(2)}) %collective-permute-start.7) | collective-permute-done | bytes 73760 | tf_op jit(solution)/shard_map/ppermute | solution.py:711
  46.8 1.3 %collective-permute-done.8.p3_ref = bf16[48,768]{1,0:T(8,128)(2,1)S(1)} collective-permute-done((bf16[48,768]{1,0:T(8,128)(2,1)S(1)}, bf16[48,768]{1,0:T(8,128)(2,1)S(1)}, u32[]{:S(2)}, u32[]{:S(2)}) %collective-permute-start.8) | collective-permute-done | bytes 73760 | tf_op jit(solution)/shard_map/ppermute | solution.py:715
  48.1 1.8 %mix_coarse.1 = bf16[1,48,2304]{2,1,0:T(8,128)(2,1)} custom-call(bf16[48,768]{1,0:T(8,128)(2,1)S(1)} %border_coarse.1.after_ref.own_ref, bf16[48,768]{1,0:T(8,128)(2,1)S(1)} %collective-permute-done.6.p1_ref, bf16[48,768]{1,0:T(8,128)(2,1)S(1)} %collective-permute-done.7.p2_ref, bf16[48,768]{1,0:T(8,128)(2,1)S(1)} %collective-permute-done.8.p3_ref, ...), custom_call_target="tpu_custom_call" | custom-call | flops 2000000000 | tf_op jit(solution)/shard_map/mix_coarse/pallas_call | solution.py:860
  (39 shorter events, 0.1 us)
Async XLA Ops:
  0.0 0.9 %copy-start.2 = (bf16[1,48,2304]{2,1,0:T(8,128)(2,1)S(1)}, bf16[1,48,2304]{2,1,0:T(8,128)(2,1)}, u32[]{:S(2)}) copy-start(bf16[1,48,2304]{2,1,0:T(8,128)(2,1)} %x_ref.3) | copy-start | bytes 663556
  0.0 0.9 %copy-start.12 = (s32[8]{0:T(128)S(1)}, s32[8]{0:T(128)}, u32[]{:S(2)}) copy-start(s32[8]{0:T(128)} %dev_ref.1) | copy-start | bytes 100
  0.0 0.9 %copy-start.11 = (s32[8]{0:T(128)S(1)}, s32[8]{0:T(128)}, u32[]{:S(2)}) copy-start(s32[8]{0:T(128)} %slots_ref.1) | copy-start | bytes 100
  0.9 9.0 %copy-start.3 = (f32[2,48,49]{2,1,0:T(8,128)S(1)}, f32[2,48,49]{2,1,0:T(8,128)}, u32[]{:S(2)}) copy-start(f32[2,48,49]{2,1,0:T(8,128)} %weight_ref.1) | copy-start | bytes 56452
  0.9 9.0 %copy-start.10 = (f32[2,48]{1,0:T(2,128)S(1)}, f32[2,48]{1,0:T(2,128)}, u32[]{:S(2)}) copy-start(f32[2,48]{1,0:T(2,128)} %bias_ref.1) | copy-start | bytes 1156
  2.6 15.7 %all-to-all-start = ((bf16[8,16,896]{2,1,0:T(8,128)(2,1)}), bf16[8,16,896]{2,1,0:T(8,128)(2,1)S(1)}, u32[]{:S(2)}, u32[]{:S(2)}) async-start(bf16[8,16,896]{2,1,0:T(8,128)(2,1)} %get-tuple-element.50), calls=%async_computation | async-start | bytes 458752 | tf_op jit(solution)/shard_map/all_to_all | solution.py:745
  9.9 5.4 %copy-start.16 = (f32[48,4]{0,1:T(4,128)S(1)}, f32[48,4]{0,1:T(4,128)}, u32[]{:S(2)}) copy-start(f32[48,4]{0,1:T(4,128)} %param.31) | copy-start | bytes 2308
  9.9 5.5 %copy-start.17 = (f32[48,4]{0,1:T(4,128)S(1)}, f32[48,4]{0,1:T(4,128)}, u32[]{:S(2)}) copy-start(f32[48,4]{0,1:T(4,128)} %param.32) | copy-start | bytes 2308
  13.8 8.1 %collective-permute-start.3 = (bf16[48,1024]{1,0:T(8,128)(2,1)S(1)}, bf16[48,1024]{1,0:T(8,128)(2,1)S(1)}, u32[]{:S(2)}, u32[]{:S(2)}) collective-permute-start(bf16[48,1024]{1,0:T(8,128)(2,1)S(1)} %get-tuple-element.70.own_ref), channel_id=1, source_target_pairs={{0,2},{1,3},{2,0},{3,1},{4,6},{5,7},{6,4},{7,5},{8,10},{9,11},{10,... | collective-permute-start | bytes 294920 | tf_op jit(solution)/shard_map/ppermute | solution.py:772
  15.3 7.9 %collective-permute-start.2 = (bf16[48,1024]{1,0:T(8,128)(2,1)S(1)}, bf16[48,1024]{1,0:T(8,128)(2,1)S(1)}, u32[]{:S(2)}, u32[]{:S(2)}) collective-permute-start(bf16[48,1024]{1,0:T(8,128)(2,1)S(1)} %get-tuple-element.70.own_ref), channel_id=1, source_target_pairs={{0,1},{1,0},{2,3},{3,2},{4,5},{5,4},{6,7},{7,6},{8,9},{9,8},{10,11... | collective-permute-start | bytes 294920 | tf_op jit(solution)/shard_map/ppermute | solution.py:773
  18.3 3.6 %copy-start = (bf16[2,768,192]{1,2,0:T(8,128)(2,1)S(1)}, bf16[2,768,192]{1,2,0:T(8,128)(2,1)}, u32[]{:S(2)}) copy-start(bf16[2,768,192]{1,2,0:T(8,128)(2,1)} %param.26) | copy-start | bytes 1769476
  18.3 3.6 %copy-start.1 = (bf16[2,192,768]{2,1,0:T(8,128)(2,1)S(1)}, bf16[2,192,768]{2,1,0:T(8,128)(2,1)}, u32[]{:S(2)}) copy-start(bf16[2,192,768]{2,1,0:T(8,128)(2,1)} %down_ref.1) | copy-start | bytes 1769476
  18.3 3.6 %copy-start.4 = (s32[1,2304]{1,0:T(1,128)S(1)}, s32[1,2304]{1,0:T(1,128)}, u32[]{:S(2)}) copy-start(s32[1,2304]{1,0:T(1,128)} %mask_ref.3) | copy-start | bytes 27652
  18.3 3.6 %copy-start.5 = (f32[2,768]{1,0:T(2,128)S(1)}, f32[2,768]{1,0:T(2,128)}, u32[]{:S(2)}) copy-start(f32[2,768]{1,0:T(2,128)} %up_bias_ref.1) | copy-start | bytes 18436
  18.4 3.6 %copy-start.6 = (f32[2,192]{1,0:T(2,128)S(1)}, f32[2,192]{1,0:T(2,128)}, u32[]{:S(2)}) copy-start(f32[2,192]{1,0:T(2,128)} %gain_ref.1) | copy-start | bytes 4612
  18.4 3.6 %copy-start.7 = (f32[2,192]{1,0:T(2,128)S(1)}, f32[2,192]{1,0:T(2,128)}, u32[]{:S(2)}) copy-start(f32[2,192]{1,0:T(2,128)} %shift_ref.1) | copy-start | bytes 4612
  18.4 3.6 %copy-start.8 = (f32[2,192]{1,0:T(2,128)S(1)}, f32[2,192]{1,0:T(2,128)}, u32[]{:S(2)}) copy-start(f32[2,192]{1,0:T(2,128)} %down_bias_ref.1) | copy-start | bytes 4612
  18.4 3.6 %copy-start.9 = (f32[2,48]{1,0:T(2,128)S(1)}, f32[2,48]{1,0:T(2,128)}, u32[]{:S(2)}) copy-start(f32[2,48]{1,0:T(2,128)} %scale_ref.1) | copy-start | bytes 1156
  18.4 3.6 %copy-start.13 = (bf16[384,128]{1,0:T(8,128)(2,1)S(1)}, bf16[384,128]{1,0:T(8,128)(2,1)}, u32[]{:S(2)}) copy-start(bf16[384,128]{1,0:T(8,128)(2,1)} %constant.6.clone.pool_ref) | copy-start | bytes 294916
  20.3 4.9 %collective-permute-start.1 = (bf16[48,1280]{1,0:T(8,128)(2,1)S(1)}, bf16[48,1280]{1,0:T(8,128)(2,1)S(1)}, u32[]{:S(2)}, u32[]{:S(2)}) collective-permute-start(bf16[48,1280]{1,0:T(8,128)(2,1)S(1)} %conv_border.1.after_ref.own_ref), channel_id=1, source_target_pairs={{0,2},{1,3},{2,0},{3,1},{4,6},{5,7},{6,4},{7,5},{8,10},{9,11},{10,... | collective-permute-start | bytes 368648 | tf_op jit(solution)/shard_map/ppermute | solution.py:711
  21.9 1.4 %collective-permute-start.4 = (bf16[48,1024]{1,0:T(8,128)(2,1)S(1)}, bf16[48,1024]{1,0:T(8,128)(2,1)S(1)}, u32[]{:S(2)}, u32[]{:S(2)}) collective-permute-start(bf16[48,1024]{1,0:T(8,128)(2,1)S(1)} %collective-permute-done.3.p2_ref), channel_id=1, source_target_pairs={{0,1},{1,0},{2,3},{3,2},{4,5},{5,4},{6,7},{7,6},{8,9},{9,8},{10,11... | collective-permute-start | bytes 294920 | tf_op jit(solution)/shard_map/ppermute | solution.py:775
  22.0 1.3 %copy-start.14 = (bf16[256,128]{1,0:T(8,128)(2,1)S(1)}, bf16[256,128]{1,0:T(8,128)(2,1)}, u32[]{:S(2)}) copy-start(bf16[256,128]{1,0:T(8,128)(2,1)} %constant.7.clone.middle_pool_ref) | copy-start | bytes 196612
  22.7 3.9 %copy-start.15 = (bf16[128,128]{1,0:T(8,128)(2,1)S(1)}, bf16[128,128]{1,0:T(8,128)(2,1)}, u32[]{:S(2)}) copy-start(bf16[128,128]{1,0:T(8,128)(2,1)} %constant.8.clone.rim_pool_ref) | copy-start | bytes 98308
  22.7 2.6 %collective-permute-start = (bf16[48,1280]{1,0:T(8,128)(2,1)S(1)}, bf16[48,1280]{1,0:T(8,128)(2,1)S(1)}, u32[]{:S(2)}, u32[]{:S(2)}) collective-permute-start(bf16[48,1280]{1,0:T(8,128)(2,1)S(1)} %conv_border.1.after_ref.own_ref), channel_id=1, source_target_pairs={{0,1},{1,0},{2,3},{3,2},{4,5},{5,4},{6,7},{7,6},{8,9},{9,8},{10,11... | collective-permute-start | bytes 368648 | tf_op jit(solution)/shard_map/ppermute | solution.py:713
  25.3 1.3 %collective-permute-start.5 = (bf16[48,1280]{1,0:T(8,128)(2,1)S(1)}, bf16[48,1280]{1,0:T(8,128)(2,1)S(1)}, u32[]{:S(2)}, u32[]{:S(2)}) collective-permute-start(bf16[48,1280]{1,0:T(8,128)(2,1)S(1)} %collective-permute-done.1.p2_ref), channel_id=1, source_target_pairs={{0,1},{1,0},{2,3},{3,2},{4,5},{5,4},{6,7},{7,6},{8,9},{9,8},{10,11... | collective-permute-start | bytes 368648 | tf_op jit(solution)/shard_map/ppermute | solution.py:715
  29.6 11.4 %all-to-all-start.1 = ((bf16[8,16,512]{2,1,0:T(8,128)(2,1)}), bf16[8,16,512]{2,1,0:T(8,128)(2,1)S(1)}, u32[]{:S(2)}, u32[]{:S(2)}) async-start(bf16[8,16,512]{2,1,0:T(8,128)(2,1)} %get-tuple-element.81), calls=%async_computation.1 | async-start | bytes 262144 | tf_op jit(solution)/shard_map/all_to_all | solution.py:827
  42.4 4.4 %collective-permute-start.7 = (bf16[48,768]{1,0:T(8,128)(2,1)S(1)}, bf16[48,768]{1,0:T(8,128)(2,1)S(1)}, u32[]{:S(2)}, u32[]{:S(2)}) collective-permute-start(bf16[48,768]{1,0:T(8,128)(2,1)S(1)} %border_coarse.1.after_ref.own_ref), channel_id=1, source_target_pairs={{0,2},{1,3},{2,0},{3,1},{4,6},{5,7},{6,4},{7,5},{8,10},{9,11},{10,... | collective-permute-start | bytes 221192 | tf_op jit(solution)/shard_map/ppermute | solution.py:711
  43.7 3.1 %collective-permute-start.6 = (bf16[48,768]{1,0:T(8,128)(2,1)S(1)}, bf16[48,768]{1,0:T(8,128)(2,1)S(1)}, u32[]{:S(2)}, u32[]{:S(2)}) collective-permute-start(bf16[48,768]{1,0:T(8,128)(2,1)S(1)} %border_coarse.1.after_ref.own_ref), channel_id=1, source_target_pairs={{0,1},{1,0},{2,3},{3,2},{4,5},{5,4},{6,7},{7,6},{8,9},{9,8},{10,11... | collective-permute-start | bytes 221192 | tf_op jit(solution)/shard_map/ppermute | solution.py:713
  46.8 1.3 %collective-permute-start.8 = (bf16[48,768]{1,0:T(8,128)(2,1)S(1)}, bf16[48,768]{1,0:T(8,128)(2,1)S(1)}, u32[]{:S(2)}, u32[]{:S(2)}) collective-permute-start(bf16[48,768]{1,0:T(8,128)(2,1)S(1)} %collective-permute-done.7.p2_ref), channel_id=1, source_target_pairs={{0,1},{1,0},{2,3},{3,2},{4,5},{5,4},{6,7},{7,6},{8,9},{9,8},{10,11... | collective-permute-start | bytes 221192 | tf_op jit(solution)/shard_map/ppermute | solution.py:715

commit v10 on v9

--- a/solution.py
+++ b/solution.py
@@ -41,7 +41,20 @@
     return one_hot((384, 128), dense), one_hot((128, 128), rim), one_hot((256, 128), middle)
 
 
+def coarse_spread_table():
+    pairs = []
+    for row in range(4):
+        for col in range(HALF):
+            if 4 <= col < 20:
+                lane = 32 + row * 16 + col - 4
+            else:
+                lane = row * 8 + (col if col < 4 else col - 16)
+            pairs += [(lane, (2 * row + u) * 48 + 2 * col + v) for u in range(2) for v in range(2)]
+    return one_hot((128, 384), pairs)
+
+
 POOL, RIM_POOL, MIDDLE_POOL = pool_tables()
+COARSE_SPREAD = coarse_spread_table()
 
 
 def dot(left, right):
@@ -420,7 +433,10 @@
     for i in range(GROUPS):
         masks.append(jnp.broadcast_to(mask_ref[:, i * FINE_IN : (i + 1) * FINE_IN].astype(F32), (8, FINE_IN)))
     counts = dot(jnp.concatenate(masks, axis=0).astype(BF), pool_ref[...])
-    coarse_values_ref[192:240, :] = jnp.where(counts > 0.5, 1.0, 0.0)
+    small_mask = jnp.where(counts > 0.5, 1.0, 0.0)
+    for m in range(5):
+        coarse_values_ref[192 + 8 * m : 200 + 8 * m, :] = coarse_tile(m, lambda i: small_mask[8 * i : 8 * i + 8], lambda value: value)
+    coarse_values_ref[232:240, :] = jnp.zeros((8, 128), F32)
     for m in range((RIM + MIDDLE) // 128):
         if m < 6:
             here = slice(128 * m, 128 * m + 128)
@@ -464,7 +480,7 @@
             out_ref[:, i * FINE_IN + 128 * m : i * FINE_IN + 128 * m + 128] = value.astype(BF)
 
 
-def conv_coarse(x_ref, weight_ref, bias_ref, sum_ref, wide_ref, pad_ref):
+def conv_coarse(x_ref, weight_ref, bias_ref, rim_ref, middle_ref, cells_ref, wide_ref, pad_ref, sum_ref):
     for tap in range(49):
         wide_ref[tap] = jnp.broadcast_to(weight_ref[1, :, tap : tap + 1], (ROWS, 128))
     pad_ref[0, :, 0:128] = jnp.zeros((ROWS, 128), F32)
@@ -496,6 +512,35 @@
         return carry
 
     lax.fori_loop(0, 6, group, 0)
+    for m in range(5):
+        here = slice(128 * m, 128 * m + 128)
+        cells_ref[:, here] = coarse_tile(m, lambda i: x_ref[:, 128 * i : 128 * i + 128].astype(F32)).astype(BF)
+        value = coarse_tile(m, lambda i: sum_ref[:, 128 * i : 128 * i + 128])
+        if m < 3:
+            rim_ref[:, here] = value
+        else:
+            middle_ref[:, 128 * m - 384 : 128 * m - 256] = value.astype(BF)
+
+
+def coarse_place(m):
+    lane = lane_ids((8, 128))
+    if m < 2:
+        return 20 * m + lane // 32, lane % 32 - 3
+    if m == 2:
+        col = lane % 8
+        return 4 + lane // 8, jnp.where(col < 4, col, col + 16)
+    return 4 + 8 * (m - 3) + lane // 16, 4 + lane % 16
+
+
+def coarse_tile(m, group, spread=tall):
+    if m < 2:
+        return group(5 * m)
+    row, col = coarse_place(m)
+    index, value = spread(row % 4 * 32 + 3 + col), None
+    for i in range(1, 5) if m == 2 else range(2 * m - 5, 2 * m - 3):
+        picked = lanes_from(group(i), index)
+        value = picked if value is None else jnp.where(spread(row // 4 == i), picked, value)
+    return value
 
 
 def border_coarse(tab_ref, recv_ref, sum_ref, mirror_ref, out_ref):
@@ -539,18 +584,16 @@
         ]
         beside.append(jnp.where(tall(within < HALF), jnp.where(tall(half == 0), picked[0], picked[1]), 0.0))
     column_fix = column_sums(beside, mirror_ref)
-    for m in range(GROUPS):
-        row, col = 4 * m + segment, inside - 3
+    for m in range(3):
+        row, col = coarse_place(m)
         index = tall(jnp.where(col < 12, row, 64 + row))
         value = sum_ref[:, 128 * m : 128 * m + 128]
         fix = jnp.zeros((ROWS, 128), F32)
         for q in range(3):
             fix = jnp.where(tall((col == q) | (col == 23 - q)), lanes_from(column_fix[q], index), fix)
         value = value + fix
-        if m == 0:
-            value = value + first_fix
-        if m == GROUPS - 1:
-            value = value + last_fix
+        if m < 2:
+            value = value + (first_fix, last_fix)[m]
         out_ref[:, 128 * m : 128 * m + 128] = value.astype(BF)
 
 
@@ -673,22 +716,39 @@
         pooled_ref[:, 128 * i : 128 * i + 128] = middle[i * ROWS : (i + 1) * ROWS].astype(BF)
 
 
+def coarse_cells(pieces, first, pooled_ref, weights_ref, values_ref, cat_ref):
+    gather_rows(pieces, cat_ref)
+    lanes = cat_ref.shape[1]
+    value = pooled_ref[:, 128 * first : 128 * first + lanes].astype(F32) + make_branch(cat_ref, weights_ref, values_ref, lanes)(0)
+    tiles = range(first, first + lanes // 128)
+    return jnp.concatenate([values_ref[192 + 8 * m : 193 + 8 * m, :] for m in tiles], axis=1) * value
+
+
+def mix_coarse_middle(own_ref, p1_ref, p2_ref, p3_ref, pooled_ref, weights_ref, values_ref, out_ref, cat_ref):
+    out_ref[...] = coarse_cells((own_ref, p1_ref, p2_ref, p3_ref), 3, pooled_ref, weights_ref, values_ref, cat_ref).astype(BF)
+
+
 def mix_coarse(
-    own_ref, p1_ref, p2_ref, p3_ref, pooled_ref, fine_ref, mask_ref, weights_ref, values_ref, pool_ref, out_ref, cat_ref,
+    own_ref, p1_ref, p2_ref, p3_ref, pooled_ref, middle_ref, fine_ref, mask_ref, weights_ref, values_ref, pool_ref, spread_ref, out_ref, cat_ref,
 ):
-    gather_rows((own_ref, p1_ref, p2_ref, p3_ref), cat_ref)
-    cells = cat_ref.shape[1]
-    value = pooled_ref[...].astype(F32) + make_branch(cat_ref, weights_ref, values_ref, cells)(0)
+    rim = coarse_cells((own_ref, p1_ref, p2_ref, p3_ref), 0, pooled_ref, weights_ref, values_ref, cat_ref)
+    ends = jnp.concatenate([rim[:, 0:128], rim[:, 128:256]], axis=0).astype(BF)
+    ends = lax.dot_general(ends, pool_ref[...], (((1,), (1,)), ((), ())), preferred_element_type=F32)
+    sides, lane = rim[:, 256:384], lane_ids((ROWS, 128))
     parts = []
-    for i in range(GROUPS):
-        parts.append((values_ref[192 + 8 * i : 193 + 8 * i, :] * value[:, 128 * i : 128 * i + 128]).astype(BF))
-    spread = lax.dot_general(
-        jnp.concatenate(parts, axis=0), pool_ref[...], (((1,), (1,)), ((), ())), preferred_element_type=F32
-    )
+    for i in range(4):
+        middle = middle_ref[:, 128 * (i // 2) : 128 * (i // 2) + 128].astype(F32)
+        side = pltpu.roll(sides, 128 - 32 * i, 1) if i else sides
+        parts.append(jnp.where(lane < 32, side, pltpu.roll(middle, 96 if i % 2 else 32, 1)).astype(BF))
+    inner = dot(jnp.concatenate(parts, axis=0), spread_ref[...])
     weights = jnp.concatenate([values_ref[240 + ROWS * j : 240 + ROWS * (j + 1), :] for j in range(3)], axis=1)
     for i in range(GROUPS):
         lanes = slice(i * FINE_IN, (i + 1) * FINE_IN)
-        merged = fine_ref[:, lanes].astype(F32) + weights * spread[i * ROWS : (i + 1) * ROWS]
+        if i % 5 == 0:
+            spread = ends[i // 5 * ROWS : (i // 5 + 1) * ROWS]
+        else:
+            spread = inner[(i - 1) * ROWS : i * ROWS]
+        merged = fine_ref[:, lanes].astype(F32) + weights * spread
         out_ref[0, :, lanes] = (mask_ref[:, lanes].astype(F32) * merged).astype(BF)
 
 
@@ -825,12 +885,12 @@
         middle_pooled,
     )
     arrived = lax.all_to_all(messages, "tile", 0, 0, tiled=True)
-    inner, taps = pl.pallas_call(
+    inner, middle_conv, pooled, taps = pl.pallas_call(
         conv_coarse,
         in_specs=[VMEM] * 3,
-        out_specs=[VMEM] * 2,
-        out_shape=[shaped(ROWS, 768, dtype=F32), shaped(49, ROWS, 128, dtype=F32)],
-        scratch_shapes=[pltpu.VMEM((4, ROWS, 1024), F32)],
+        out_specs=[VMEM] * 4,
+        out_shape=[shaped(ROWS, 384, dtype=F32), shaped(ROWS, 256), shaped(ROWS, 640), shaped(49, ROWS, 128, dtype=F32)],
+        scratch_shapes=[pltpu.VMEM((4, ROWS, 1024), F32), pltpu.VMEM((ROWS, 768), F32)],
         compiler_params=PARAMS,
         cost_estimate=takes(2),
         name="conv_coarse",
@@ -839,11 +899,15 @@
         border_coarse,
         in_specs=[SMEM] + [VMEM] * 3,
         out_specs=VMEM,
-        out_shape=shaped(ROWS, 768),
+        out_shape=shaped(ROWS, 384),
         compiler_params=PARAMS,
         cost_estimate=takes(1),
         name="border_coarse",
     )(table, arrived, inner, taps)
+    middle_across = lax.ppermute(middle_conv, "chan", pairs(2))
+    middle_beside = lax.ppermute(middle_conv, "chan", pairs(1))
+    middle_across, _ = lax.optimization_barrier((middle_across, conv))
+    coarse_pieces = (middle_conv, middle_beside, middle_across, lax.ppermute(middle_across, "chan", pairs(1)))
 
     def back_in_rows(own):
         return pl.pallas_call(
@@ -856,17 +920,29 @@
             name="in_rows",
         )(own, rim, middle)
 
-    pieces, (fine,) = every_channel(conv, back_in_rows)
+    def mix_coarse_cells(*results):
+        return pl.pallas_call(
+            mix_coarse_middle,
+            in_specs=[VMEM] * 7,
+            out_specs=[VMEM],
+            out_shape=[shaped(ROWS, 256)],
+            scratch_shapes=[pltpu.VMEM((4 * ROWS, 256), BF)],
+            compiler_params=PARAMS,
+            cost_estimate=takes(1),
+            name="mix_coarse_middle",
+        )(*coarse_pieces, pooled, coarse_weights, coarse_values)
+
+    pieces, (fine, coarse_middle) = every_channel(conv, back_in_rows, mix_coarse_cells)
     return pl.pallas_call(
         mix_coarse,
-        in_specs=[VMEM] * 10,
+        in_specs=[VMEM] * 12,
         out_specs=VMEM,
         out_shape=shaped(1, ROWS, cells),
-        scratch_shapes=[pltpu.VMEM((4 * ROWS, 768), BF)],
+        scratch_shapes=[pltpu.VMEM((4 * ROWS, 384), BF)],
         compiler_params=PARAMS,
         cost_estimate=takes(2),
         name="mix_coarse",
-    )(*pieces, pooled, fine, land_mask, coarse_weights, coarse_values, pool)
+    )(*pieces, pooled, coarse_middle, fine, land_mask, coarse_weights, coarse_values, pool, jnp.asarray(COARSE_SPREAD))
 
 
 def solution(mesh):

time: 50.2 us -> 49.5 us (0.986)
  waiting for transfers between devices: 15 us -> 12.4 us
  starting transfers between devices: 16.1 us -> 17.5 us
    ppermute x2, waiting for transfers between devices: 3.66 us -> 1.72 us  [every_channel(): across = lax.ppermute(own, 'chan', pairs(2))]
    all_to_all x2, waiting for transfers between devices: 8.78 us -> 7.76 us  [per_device(): arrived = lax.all_to_all(messages, 'tile', 0, 0, tiled=True)]
    ppermute x0 -> x2, starting transfers between devices: none -> 0.87 us  [the longest x1 0.87 us: per_device(): middle_across = lax.ppermute(middle_conv, 'chan', pairs(2))]
    pallas_call x2 -> x3, Pallas kernels: 3.15 us -> 3.64 us  [the longest x1 1.56 us: per_device(): pl.pallas_call(mix_coarse, in_specs=[VMEM] * 12, out_specs=VMEM, out_shap...]
    unnamed x38 -> x40, local copies, waits for them, and re-layouts: 1.14 us -> 1.14 us
  transfers between devices with their start and end apart: 11 -> 14, of which waited for: 6 -> 7; matrix products, arithmetic and copies ran while one was open for 0% -> 0% of each run, Pallas kernels for 19% -> 24%
where the time goes in v10:
time: 49.5 us; the launch traced here: 49.1 us
  Pallas kernels  17.8 us (36%)
  starting transfers between devices  17.5 us (35%)
  waiting for transfers between devices  12.4 us (25%)
  local copies, waits for them, and re-layouts  1.14 us (2%)
    all_to_all x2, starting transfers between devices, per_device(): arrived = lax.all_to_all(messages, 'tile', 0, 0, tiled=True)  11.4 us
    all_to_all x2, waiting for transfers between devices, per_device(): arrived = lax.all_to_all(messages, 'tile', 0, 0, tiled=True)  7.76 us
    pallas_call x1, Pallas kernels, per_device(): pl.pallas_call(lambda tab_ref, *refs: conv_inner(*refs), in_specs=[SMEM]...  3.84 us
    pallas_call x1, Pallas kernels, per_device(): pl.pallas_call(make_mix_rim(count), in_specs=[SMEM] + [VMEM] * 12, out_sp...  2.98 us
    ppermute x2, starting transfers between devices, every_channel(): across = lax.ppermute(own, 'chan', pairs(2))  2.59 us
    ppermute x2, waiting for transfers between devices, every_channel(): diagonal = lax.ppermute(across, 'chan', pairs(1))  2.54 us
    pallas_call x1, Pallas kernels, per_device(): pl.pallas_call(conv_border, in_specs=[SMEM] + [VMEM] * 3, out_specs=VMEM,...  1.92 us
    ppermute x2, waiting for transfers between devices, every_channel(): across = lax.ppermute(own, 'chan', pairs(2))  1.72 us
  transfers between devices with their start and end apart: 14, of which 7 were waited for; matrix products, arithmetic and copies ran while one was open for 0% of the time, Pallas kernels for 24%

profile of v10, /device:TPU:0, one launch (start us, length us, event | category | flops | bytes accessed | tf_op | source)
XLA Modules:
  0.0 49.1 jit_solution(10644719382532421431)
XLA Ops:
  0.0 0.1 strip_table.1.pack_ref
  0.1 0.9 %copy-done.2 = bf16[1,48,2304]{2,1,0:T(8,128)(2,1)S(1)} copy-done((bf16[1,48,2304]{2,1,0:T(8,128)(2,1)S(1)}, bf16[1,48,2304]{2,1,0:T(8,128)(2,1)}, u32[]{:S(2)}) %copy-start.2) | copy-done | bytes 221208
  1.0 1.7 %prep.1 = (bf16[8,16,896]{2,1,0:T(8,128)(2,1)}, s32[24]{0:T(128)S(1)}) custom-call(s32[8]{0:T(128)S(1)} %copy-done.11, s32[8]{0:T(128)S(1)} %copy-done.12, bf16[1,48,2304]{2,1,0:T(8,128)(2,1)S(1)} %copy-done.2, bf16[384,256]{1,0:T(8,128)(2,1)S(1)} %strip_table.1.pack_ref), custom_call_target="tpu_custom_call" | custom-call | flops 10000000000 | tf_op jit(solution)/shard_map/prep/pallas_call | solution.py:789
  2.6 7.3 %all-to-all-start = ((bf16[8,16,896]{2,1,0:T(8,128)(2,1)}), bf16[8,16,896]{2,1,0:T(8,128)(2,1)S(1)}, u32[]{:S(2)}, u32[]{:S(2)}) async-start(bf16[8,16,896]{2,1,0:T(8,128)(2,1)} %get-tuple-element.54), calls=%async_computation | async-start | bytes 458752 | tf_op jit(solution)/shard_map/all_to_all | solution.py:805
  10.0 3.8 %conv_inner.1 = (f32[48,1280]{1,0:T(8,128)S(1)}, bf16[48,1024]{1,0:T(8,128)(2,1)S(1)}, f32[28,48,128]{2,1,0:T(8,128)S(1)}) custom-call(s32[24]{0:T(128)S(1)} %get-tuple-element.53.tab_ref, bf16[1,48,2304]{2,1,0:T(8,128)(2,1)S(1)} %copy-done.2, f32[2,48,49]{2,1,0:T(8,128)S(1)} %copy-done.3, f32[2,48]{1,0:T(2,128)S(1)} %copy-done.10), custom_call_target="tpu_custom_call" | custom-call | flops 4000000000 | tf_op jit(solution)/shard_map/conv_inner/pallas_call | solution.py:806
  13.8 1.6 %collective-permute-start.3 = (bf16[48,1024]{1,0:T(8,128)(2,1)S(1)}, bf16[48,1024]{1,0:T(8,128)(2,1)S(1)}, u32[]{:S(2)}, u32[]{:S(2)}) collective-permute-start(bf16[48,1024]{1,0:T(8,128)(2,1)S(1)} %get-tuple-element.74.own_ref), channel_id=1, source_target_pairs={{0,2},{1,3},{2,0},{3,1},{4,6},{5,7},{6,4},{7,5},{8,10},{9,11},{10,... | collective-permute-start | bytes 294920 | tf_op jit(solution)/shard_map/ppermute | solution.py:832
  15.4 0.1 copy.20.pool_weight_ref
  15.5 0.1 copy.21.spread_weight_ref
  15.5 2.8 %all-to-all-done.recv_ref = bf16[8,16,896]{2,1,0:T(8,128)(2,1)S(1)} async-done(((bf16[8,16,896]{2,1,0:T(8,128)(2,1)}), bf16[8,16,896]{2,1,0:T(8,128)(2,1)S(1)}, u32[]{:S(2)}, u32[]{:S(2)}) %all-to-all-start) | async-done | bytes 229408 | tf_op jit(solution)/shard_map/all_to_all | solution.py:805
  18.4 0.0 copy-start.13
  18.4 1.9 %conv_border.1.after_ref.own_ref = bf16[48,1280]{1,0:T(8,128)(2,1)S(1)} custom-call(s32[24]{0:T(128)S(1)} %get-tuple-element.53.tab_ref, bf16[8,16,896]{2,1,0:T(8,128)(2,1)S(1)} %all-to-all-done.recv_ref, f32[48,1280]{1,0:T(8,128)S(1)} %get-tuple-element.55.sum_ref, f32[28,48,128]{2,1,0:T(8,128)S(1)} %get-tuple-element.56.mirror_ref), custom_call_target="tpu_custom_call" | custom-call | flops 2000000000 | tf_op jit(solution)/shard_map/conv_border/pallas_call | solution.py:821
  20.3 1.6 %collective-permute-start.1 = (bf16[48,1280]{1,0:T(8,128)(2,1)S(1)}, bf16[48,1280]{1,0:T(8,128)(2,1)S(1)}, u32[]{:S(2)}, u32[]{:S(2)}) collective-permute-start(bf16[48,1280]{1,0:T(8,128)(2,1)S(1)} %conv_border.1.after_ref.own_ref), channel_id=1, source_target_pairs={{0,2},{1,3},{2,0},{3,1},{4,6},{5,7},{6,4},{7,5},{8,10},{9,11},{10,... | collective-permute-start | bytes 368648 | tf_op jit(solution)/shard_map/ppermute | solution.py:771
  22.0 0.0 copy-start.15
  22.0 0.8 %params.1 = (bf16[48,1280]{1,0:T(8,128)(2,1)S(1)}, bf16[48,1024]{1,0:T(8,128)(2,1)S(1)}, f32[8,1280]{1,0:T(8,128)S(1)}, f32[48,512]{1,0:T(8,128)S(1)}, bf16[912,...) custom-call(bf16[48,1280]{1,0:T(8,128)(2,1)S(1)} %conv_border.1.after_ref.o, ...), custom_call_target="tpu_custom_call" | custom-call | flops 2000000000 | tf_op jit(solution)/shard_map/params/pallas_call | solution.py:854
  22.8 0.6 %collective-permute-start = (bf16[48,1280]{1,0:T(8,128)(2,1)S(1)}, bf16[48,1280]{1,0:T(8,128)(2,1)S(1)}, u32[]{:S(2)}, u32[]{:S(2)}) collective-permute-start(bf16[48,1280]{1,0:T(8,128)(2,1)S(1)} %conv_border.1.after_ref.own_ref), channel_id=1, source_target_pairs={{0,1},{1,0},{2,3},{3,2},{4,5},{5,4},{6,7},{7,6},{8,9},{9,8},{10,11... | collective-permute-start | bytes 368648 | tf_op jit(solution)/shard_map/ppermute | solution.py:773
  23.4 1.4 %mix_middle.1 = (bf16[48,1024]{1,0:T(8,128)(2,1)S(1)}, bf16[48,512]{1,0:T(8,128)(2,1)S(1)}) custom-call(bf16[48,1024]{1,0:T(8,128)(2,1)S(1)} %get-tuple-element.74.own_ref, bf16[48,1024]{1,0:T(8,128)(2,1)S(1)} %collective-permute-done.2.p1_ref, bf16[48,1024]{1,0:T(8,128)(2,1)S(1)} %collective-permute-done.3.p2_ref, ...), custom_call_target="tpu_custom_call" | custom-call | flops 1000000000 | tf_op jit(solution)/shard_map/mix_middle/pallas_call | solution.py:838
  24.8 0.5 %collective-permute-done.1.p2_ref = bf16[48,1280]{1,0:T(8,128)(2,1)S(1)} collective-permute-done((bf16[48,1280]{1,0:T(8,128)(2,1)S(1)}, bf16[48,1280]{1,0:T(8,128)(2,1)S(1)}, u32[]{:S(2)}, u32[]{:S(2)}) %collective-permute-start.1) | collective-permute-done | bytes 122912 | tf_op jit(solution)/shard_map/ppermute | solution.py:771
  25.3 1.3 %collective-permute-done.5.p3_ref = bf16[48,1280]{1,0:T(8,128)(2,1)S(1)} collective-permute-done((bf16[48,1280]{1,0:T(8,128)(2,1)S(1)}, bf16[48,1280]{1,0:T(8,128)(2,1)S(1)}, u32[]{:S(2)}, u32[]{:S(2)}) %collective-permute-start.5) | collective-permute-done | bytes 122912 | tf_op jit(solution)/shard_map/ppermute | solution.py:775
  26.6 3.0 %mix_rim.1 = (bf16[48,1280]{1,0:T(8,128)(2,1)S(1)}, bf16[8,16,512]{2,1,0:T(8,128)(2,1)}, bf16[48,768]{1,0:T(8,128)(2,1)S(1)}) custom-call(s32[24]{0:T(128)S(1)} %get-tuple-element.53.tab_ref, bf16[48,1280]{1,0:T(8,128)(2,1)S(1)} %conv_border.1.after_ref.own_ref, bf16[48,1280]{1,0:T(8,128)(2,1)S(1)} %collective-permute-done.p1_ref, ...), custom_call_target="tpu_custom_call" | custom-call | flops 3000000000 | tf_op jit(solution)/shard_map/mix_rim/pallas_call | solution.py:869
  29.6 4.1 %all-to-all-start.1 = ((bf16[8,16,512]{2,1,0:T(8,128)(2,1)}), bf16[8,16,512]{2,1,0:T(8,128)(2,1)S(1)}, u32[]{:S(2)}, u32[]{:S(2)}) async-start(bf16[8,16,512]{2,1,0:T(8,128)(2,1)} %get-tuple-element.85), calls=%async_computation.1 | async-start | bytes 262144 | tf_op jit(solution)/shard_map/all_to_all | solution.py:887
  33.7 1.5 %conv_coarse.1 = (f32[48,384]{1,0:T(8,128)S(1)}, bf16[48,256]{1,0:T(8,128)(2,1)S(1)}, bf16[48,640]{1,0:T(8,128)(2,1)S(1)}, f32[49,48,128]{2,1,0:T(8,128)S(1)}) custom-call(bf16[48,768]{1,0:T(8,128)(2,1)S(1)} %get-tuple-element.86.x_ref, f32[2,48,49]{2,1,0:T(8,128)S(1)} %copy-done.3, f32[2,48]{1,0:T(2,128)S(1)} %copy-done.10), custom_call_target="tpu_custom_call" | custom-call | flops 2000000000 | tf_op jit(solution)/shard_map/conv_coarse/pallas_call | solution.py:888
  35.2 0.9 %collective-permute-start.9 = (bf16[48,256]{1,0:T(8,128)(2,1)S(1)}, bf16[48,256]{1,0:T(8,128)(2,1)S(1)}, u32[]{:S(2)}, u32[]{:S(2)}) collective-permute-start(bf16[48,256]{1,0:T(8,128)(2,1)S(1)} %get-tuple-element.93.own_ref), channel_id=1, source_target_pairs={{0,2},{1,3},{2,0},{3,1},{4,6},{5,7},{6,4},{7,5},{8,10},{9,11},{10,... | collective-permute-start | bytes 73736 | tf_op jit(solution)/shard_map/ppermute | solution.py:907
  36.1 5.0 %all-to-all-done.1.recv_ref = bf16[8,16,512]{2,1,0:T(8,128)(2,1)S(1)} async-done(((bf16[8,16,512]{2,1,0:T(8,128)(2,1)}), bf16[8,16,512]{2,1,0:T(8,128)(2,1)S(1)}, u32[]{:S(2)}, u32[]{:S(2)}) %all-to-all-start.1) | async-done | bytes 131104 | tf_op jit(solution)/shard_map/all_to_all | solution.py:887
  41.0 1.3 %border_coarse.1.after_ref.own_ref = bf16[48,384]{1,0:T(8,128)(2,1)S(1)} custom-call(s32[24]{0:T(128)S(1)} %get-tuple-element.53.tab_ref, bf16[8,16,512]{2,1,0:T(8,128)(2,1)S(1)} %all-to-all-done.1.recv_ref, f32[48,384]{1,0:T(8,128)S(1)} %get-tuple-element.87.sum_ref, f32[49,48,128]{2,1,0:T(8,128)S(1)} %get-tuple-element.88.mirror_ref), custom_call_target="tpu_custom_call" | custom-call | flops 1000000000 | tf_op jit(solution)/shard_map/border_coarse/pallas_call | solution.py:898
  42.3 1.0 %collective-permute-start.7 = (bf16[48,384]{1,0:T(8,128)(2,1)S(1)}, bf16[48,384]{1,0:T(8,128)(2,1)S(1)}, u32[]{:S(2)}, u32[]{:S(2)}) collective-permute-start(bf16[48,384]{1,0:T(8,128)(2,1)S(1)} %border_coarse.1.after_ref.own_ref), channel_id=1, source_target_pairs={{0,2},{1,3},{2,0},{3,1},{4,6},{5,7},{6,4},{7,5},{8,10},{9,11},{10,... | collective-permute-start | bytes 110600 | tf_op jit(solution)/shard_map/ppermute | solution.py:771
  43.4 0.2 in_rows.1.fine_ref
  43.6 0.6 %collective-permute-start.6 = (bf16[48,384]{1,0:T(8,128)(2,1)S(1)}, bf16[48,384]{1,0:T(8,128)(2,1)S(1)}, u32[]{:S(2)}, u32[]{:S(2)}) collective-permute-start(bf16[48,384]{1,0:T(8,128)(2,1)S(1)} %border_coarse.1.after_ref.own_ref), channel_id=1, source_target_pairs={{0,1},{1,0},{2,3},{3,2},{4,5},{5,4},{6,7},{7,6},{8,9},{9,8},{10,11... | collective-permute-start | bytes 110600 | tf_op jit(solution)/shard_map/ppermute | solution.py:773
  44.2 0.4 collective-permute-done.10.p3_ref
  44.6 0.6 %mix_coarse_middle.1.middle_ref = bf16[48,256]{1,0:T(8,128)(2,1)S(1)} custom-call(bf16[48,256]{1,0:T(8,128)(2,1)S(1)} %get-tuple-element.93.own_ref, bf16[48,256]{1,0:T(8,128)(2,1)S(1)} %collective-permute-done.8.p1_ref, bf16[48,256]{1,0:T(8,128)(2,1)S(1)} %collective-permute-done.9.p2_ref, bf16[48,256]{1,0:T(8,128)(2,1)S(1)} %collective-permute-done.10.p3_ref, ...), custom_call_target="tpu_custom_call" | custom-call | flops 1000000000 | tf_op jit(solution)/shard_map/mix_coarse_middle/pallas_call | solution.py:924
  45.2 1.2 %collective-permute-done.7.p2_ref = bf16[48,384]{1,0:T(8,128)(2,1)S(1)} collective-permute-done((bf16[48,384]{1,0:T(8,128)(2,1)S(1)}, bf16[48,384]{1,0:T(8,128)(2,1)S(1)}, u32[]{:S(2)}, u32[]{:S(2)}) %collective-permute-start.7) | collective-permute-done | bytes 36896 | tf_op jit(solution)/shard_map/ppermute | solution.py:771
  46.4 1.2 %collective-permute-done.11.p3_ref = bf16[48,384]{1,0:T(8,128)(2,1)S(1)} collective-permute-done((bf16[48,384]{1,0:T(8,128)(2,1)S(1)}, bf16[48,384]{1,0:T(8,128)(2,1)S(1)}, u32[]{:S(2)}, u32[]{:S(2)}) %collective-permute-start.11) | collective-permute-done | bytes 36896 | tf_op jit(solution)/shard_map/ppermute | solution.py:775
  47.6 1.6 %mix_coarse.1 = bf16[1,48,2304]{2,1,0:T(8,128)(2,1)} custom-call(bf16[48,384]{1,0:T(8,128)(2,1)S(1)} %border_coarse.1.after_ref.own_ref, bf16[48,384]{1,0:T(8,128)(2,1)S(1)} %collective-permute-done.6.p1_ref, bf16[48,384]{1,0:T(8,128)(2,1)S(1)} %collective-permute-done.7.p2_ref, bf16[48,384]{1,0:T(8,128)(2,1)S(1)} %collective-permute-done.11.p3_ref, ...), custom_call_target="tpu_custom_call" | custom-call | flops 2000000000 | tf_op jit(solution)/shard_map/mix_coarse/pallas_call | solution.py:936
  (48 shorter events, 0.1 us)
Async XLA Ops:
  0.0 0.9 %copy-start.12 = (s32[8]{0:T(128)S(1)}, s32[8]{0:T(128)}, u32[]{:S(2)}) copy-start(s32[8]{0:T(128)} %dev_ref.1) | copy-start | bytes 100
  0.0 0.9 %copy-start.11 = (s32[8]{0:T(128)S(1)}, s32[8]{0:T(128)}, u32[]{:S(2)}) copy-start(s32[8]{0:T(128)} %slots_ref.1) | copy-start | bytes 100
  0.9 9.0 %copy-start.3 = (f32[2,48,49]{2,1,0:T(8,128)S(1)}, f32[2,48,49]{2,1,0:T(8,128)}, u32[]{:S(2)}) copy-start(f32[2,48,49]{2,1,0:T(8,128)} %weight_ref.1) | copy-start | bytes 56452
  0.9 9.0 %copy-start.10 = (f32[2,48]{1,0:T(2,128)S(1)}, f32[2,48]{1,0:T(2,128)}, u32[]{:S(2)}) copy-start(f32[2,48]{1,0:T(2,128)} %bias_ref.1) | copy-start | bytes 1156
  2.6 15.7 %all-to-all-start = ((bf16[8,16,896]{2,1,0:T(8,128)(2,1)}), bf16[8,16,896]{2,1,0:T(8,128)(2,1)S(1)}, u32[]{:S(2)}, u32[]{:S(2)}) async-start(bf16[8,16,896]{2,1,0:T(8,128)(2,1)} %get-tuple-element.54), calls=%async_computation | async-start | bytes 458752 | tf_op jit(solution)/shard_map/all_to_all | solution.py:805
  9.9 5.4 %copy-start.17 = (f32[48,4]{0,1:T(4,128)S(1)}, f32[48,4]{0,1:T(4,128)}, u32[]{:S(2)}) copy-start(f32[48,4]{0,1:T(4,128)} %param.32) | copy-start | bytes 2308
  9.9 5.5 %copy-start.18 = (f32[48,4]{0,1:T(4,128)S(1)}, f32[48,4]{0,1:T(4,128)}, u32[]{:S(2)}) copy-start(f32[48,4]{0,1:T(4,128)} %param.33) | copy-start | bytes 2308
  13.8 8.1 %collective-permute-start.3 = (bf16[48,1024]{1,0:T(8,128)(2,1)S(1)}, bf16[48,1024]{1,0:T(8,128)(2,1)S(1)}, u32[]{:S(2)}, u32[]{:S(2)}) collective-permute-start(bf16[48,1024]{1,0:T(8,128)(2,1)S(1)} %get-tuple-element.74.own_ref), channel_id=1, source_target_pairs={{0,2},{1,3},{2,0},{3,1},{4,6},{5,7},{6,4},{7,5},{8,10},{9,11},{10,... | collective-permute-start | bytes 294920 | tf_op jit(solution)/shard_map/ppermute | solution.py:832
  15.4 8.0 %collective-permute-start.2 = (bf16[48,1024]{1,0:T(8,128)(2,1)S(1)}, bf16[48,1024]{1,0:T(8,128)(2,1)S(1)}, u32[]{:S(2)}, u32[]{:S(2)}) collective-permute-start(bf16[48,1024]{1,0:T(8,128)(2,1)S(1)} %get-tuple-element.74.own_ref), channel_id=1, source_target_pairs={{0,1},{1,0},{2,3},{3,2},{4,5},{5,4},{6,7},{7,6},{8,9},{9,8},{10,11... | collective-permute-start | bytes 294920 | tf_op jit(solution)/shard_map/ppermute | solution.py:833
  18.4 3.6 %copy-start = (bf16[2,768,192]{1,2,0:T(8,128)(2,1)S(1)}, bf16[2,768,192]{1,2,0:T(8,128)(2,1)}, u32[]{:S(2)}) copy-start(bf16[2,768,192]{1,2,0:T(8,128)(2,1)} %param.27) | copy-start | bytes 1769476
  18.4 3.6 %copy-start.1 = (bf16[2,192,768]{2,1,0:T(8,128)(2,1)S(1)}, bf16[2,192,768]{2,1,0:T(8,128)(2,1)}, u32[]{:S(2)}) copy-start(bf16[2,192,768]{2,1,0:T(8,128)(2,1)} %down_ref.1) | copy-start | bytes 1769476
  18.4 3.6 %copy-start.4 = (s32[1,2304]{1,0:T(1,128)S(1)}, s32[1,2304]{1,0:T(1,128)}, u32[]{:S(2)}) copy-start(s32[1,2304]{1,0:T(1,128)} %mask_ref.3) | copy-start | bytes 27652
  18.4 3.6 %copy-start.5 = (f32[2,768]{1,0:T(2,128)S(1)}, f32[2,768]{1,0:T(2,128)}, u32[]{:S(2)}) copy-start(f32[2,768]{1,0:T(2,128)} %up_bias_ref.1) | copy-start | bytes 18436
  18.4 3.6 %copy-start.6 = (f32[2,192]{1,0:T(2,128)S(1)}, f32[2,192]{1,0:T(2,128)}, u32[]{:S(2)}) copy-start(f32[2,192]{1,0:T(2,128)} %gain_ref.1) | copy-start | bytes 4612
  18.4 3.6 %copy-start.7 = (f32[2,192]{1,0:T(2,128)S(1)}, f32[2,192]{1,0:T(2,128)}, u32[]{:S(2)}) copy-start(f32[2,192]{1,0:T(2,128)} %shift_ref.1) | copy-start | bytes 4612
  18.4 3.6 %copy-start.8 = (f32[2,192]{1,0:T(2,128)S(1)}, f32[2,192]{1,0:T(2,128)}, u32[]{:S(2)}) copy-start(f32[2,192]{1,0:T(2,128)} %down_bias_ref.1) | copy-start | bytes 4612
  18.4 3.6 %copy-start.9 = (f32[2,48]{1,0:T(2,128)S(1)}, f32[2,48]{1,0:T(2,128)}, u32[]{:S(2)}) copy-start(f32[2,48]{1,0:T(2,128)} %scale_ref.1) | copy-start | bytes 1156
  18.4 3.6 %copy-start.13 = (bf16[384,128]{1,0:T(8,128)(2,1)S(1)}, bf16[384,128]{1,0:T(8,128)(2,1)}, u32[]{:S(2)}) copy-start(bf16[384,128]{1,0:T(8,128)(2,1)} %constant.8.clone.pool_ref) | copy-start | bytes 294916
  20.3 4.9 %collective-permute-start.1 = (bf16[48,1280]{1,0:T(8,128)(2,1)S(1)}, bf16[48,1280]{1,0:T(8,128)(2,1)S(1)}, u32[]{:S(2)}, u32[]{:S(2)}) collective-permute-start(bf16[48,1280]{1,0:T(8,128)(2,1)S(1)} %conv_border.1.after_ref.own_ref), channel_id=1, source_target_pairs={{0,2},{1,3},{2,0},{3,1},{4,6},{5,7},{6,4},{7,5},{8,10},{9,11},{10,... | collective-permute-start | bytes 368648 | tf_op jit(solution)/shard_map/ppermute | solution.py:771
  21.9 1.5 %collective-permute-start.4 = (bf16[48,1024]{1,0:T(8,128)(2,1)S(1)}, bf16[48,1024]{1,0:T(8,128)(2,1)S(1)}, u32[]{:S(2)}, u32[]{:S(2)}) collective-permute-start(bf16[48,1024]{1,0:T(8,128)(2,1)S(1)} %collective-permute-done.3.p2_ref), channel_id=1, source_target_pairs={{0,1},{1,0},{2,3},{3,2},{4,5},{5,4},{6,7},{7,6},{8,9},{9,8},{10,11... | collective-permute-start | bytes 294920 | tf_op jit(solution)/shard_map/ppermute | solution.py:835
  22.0 1.4 %copy-start.15 = (bf16[256,128]{1,0:T(8,128)(2,1)S(1)}, bf16[256,128]{1,0:T(8,128)(2,1)}, u32[]{:S(2)}) copy-start(bf16[256,128]{1,0:T(8,128)(2,1)} %constant.9.clone.middle_pool_ref) | copy-start | bytes 196612
  22.8 3.8 %copy-start.16 = (bf16[128,128]{1,0:T(8,128)(2,1)S(1)}, bf16[128,128]{1,0:T(8,128)(2,1)}, u32[]{:S(2)}) copy-start(bf16[128,128]{1,0:T(8,128)(2,1)} %constant.10.clone.rim_pool_ref) | copy-start | bytes 98308
  22.8 2.5 %collective-permute-start = (bf16[48,1280]{1,0:T(8,128)(2,1)S(1)}, bf16[48,1280]{1,0:T(8,128)(2,1)S(1)}, u32[]{:S(2)}, u32[]{:S(2)}) collective-permute-start(bf16[48,1280]{1,0:T(8,128)(2,1)S(1)} %conv_border.1.after_ref.own_ref), channel_id=1, source_target_pairs={{0,1},{1,0},{2,3},{3,2},{4,5},{5,4},{6,7},{7,6},{8,9},{9,8},{10,11... | collective-permute-start | bytes 368648 | tf_op jit(solution)/shard_map/ppermute | solution.py:773
  25.3 1.3 %collective-permute-start.5 = (bf16[48,1280]{1,0:T(8,128)(2,1)S(1)}, bf16[48,1280]{1,0:T(8,128)(2,1)S(1)}, u32[]{:S(2)}, u32[]{:S(2)}) collective-permute-start(bf16[48,1280]{1,0:T(8,128)(2,1)S(1)} %collective-permute-done.1.p2_ref), channel_id=1, source_target_pairs={{0,1},{1,0},{2,3},{3,2},{4,5},{5,4},{6,7},{7,6},{8,9},{9,8},{10,11... | collective-permute-start | bytes 368648 | tf_op jit(solution)/shard_map/ppermute | solution.py:775
  29.6 11.4 %all-to-all-start.1 = ((bf16[8,16,512]{2,1,0:T(8,128)(2,1)}), bf16[8,16,512]{2,1,0:T(8,128)(2,1)S(1)}, u32[]{:S(2)}, u32[]{:S(2)}) async-start(bf16[8,16,512]{2,1,0:T(8,128)(2,1)} %get-tuple-element.85), calls=%async_computation.1 | async-start | bytes 262144 | tf_op jit(solution)/shard_map/all_to_all | solution.py:887
  35.2 8.2 %collective-permute-start.9 = (bf16[48,256]{1,0:T(8,128)(2,1)S(1)}, bf16[48,256]{1,0:T(8,128)(2,1)S(1)}, u32[]{:S(2)}, u32[]{:S(2)}) collective-permute-start(bf16[48,256]{1,0:T(8,128)(2,1)S(1)} %get-tuple-element.93.own_ref), channel_id=1, source_target_pairs={{0,2},{1,3},{2,0},{3,1},{4,6},{5,7},{6,4},{7,5},{8,10},{9,11},{10,... | collective-permute-start | bytes 73736 | tf_op jit(solution)/shard_map/ppermute | solution.py:907
  36.1 8.1 %collective-permute-start.8 = (bf16[48,256]{1,0:T(8,128)(2,1)S(1)}, bf16[48,256]{1,0:T(8,128)(2,1)S(1)}, u32[]{:S(2)}, u32[]{:S(2)}) collective-permute-start(bf16[48,256]{1,0:T(8,128)(2,1)S(1)} %get-tuple-element.93.own_ref), channel_id=1, source_target_pairs={{0,1},{1,0},{2,3},{3,2},{4,5},{5,4},{6,7},{7,6},{8,9},{9,8},{10,11... | collective-permute-start | bytes 73736 | tf_op jit(solution)/shard_map/ppermute | solution.py:908
  42.3 4.0 %collective-permute-start.7 = (bf16[48,384]{1,0:T(8,128)(2,1)S(1)}, bf16[48,384]{1,0:T(8,128)(2,1)S(1)}, u32[]{:S(2)}, u32[]{:S(2)}) collective-permute-start(bf16[48,384]{1,0:T(8,128)(2,1)S(1)} %border_coarse.1.after_ref.own_ref), channel_id=1, source_target_pairs={{0,2},{1,3},{2,0},{3,1},{4,6},{5,7},{6,4},{7,5},{8,10},{9,11},{10,... | collective-permute-start | bytes 110600 | tf_op jit(solution)/shard_map/ppermute | solution.py:771
  43.4 1.2 %collective-permute-start.10 = (bf16[48,256]{1,0:T(8,128)(2,1)S(1)}, bf16[48,256]{1,0:T(8,128)(2,1)S(1)}, u32[]{:S(2)}, u32[]{:S(2)}) collective-permute-start(bf16[48,256]{1,0:T(8,128)(2,1)S(1)} %collective-permute-done.9.p2_ref), channel_id=1, source_target_pairs={{0,1},{1,0},{2,3},{3,2},{4,5},{5,4},{6,7},{7,6},{8,9},{9,8},{10,11... | collective-permute-start | bytes 73736 | tf_op jit(solution)/shard_map/ppermute | solution.py:910
  43.6 2.7 %collective-permute-start.6 = (bf16[48,384]{1,0:T(8,128)(2,1)S(1)}, bf16[48,384]{1,0:T(8,128)(2,1)S(1)}, u32[]{:S(2)}, u32[]{:S(2)}) collective-permute-start(bf16[48,384]{1,0:T(8,128)(2,1)S(1)} %border_coarse.1.after_ref.own_ref), channel_id=1, source_target_pairs={{0,1},{1,0},{2,3},{3,2},{4,5},{5,4},{6,7},{7,6},{8,9},{9,8},{10,11... | collective-permute-start | bytes 110600 | tf_op jit(solution)/shard_map/ppermute | solution.py:773
  44.6 3.0 %copy-start.14 = (bf16[128,384]{1,0:T(8,128)(2,1)S(1)}, bf16[128,384]{1,0:T(8,128)(2,1)}, u32[]{:S(2)}) copy-start(bf16[128,384]{1,0:T(8,128)(2,1)} %constant.11.clone.spread_ref) | copy-start | bytes 294916
  46.4 1.2 %collective-permute-start.11 = (bf16[48,384]{1,0:T(8,128)(2,1)S(1)}, bf16[48,384]{1,0:T(8,128)(2,1)S(1)}, u32[]{:S(2)}, u32[]{:S(2)}) collective-permute-start(bf16[48,384]{1,0:T(8,128)(2,1)S(1)} %collective-permute-done.7.p2_ref), channel_id=1, source_target_pairs={{0,1},{1,0},{2,3},{3,2},{4,5},{5,4},{6,7},{7,6},{8,9},{9,8},{10,11... | collective-permute-start | bytes 110600 | tf_op jit(solution)/shard_map/ppermute | solution.py:775
  (1 other events, 0.9 us)

commit v11 on v10

--- a/solution.py
+++ b/solution.py
@@ -13,8 +13,8 @@
 GROUPS = 6
 ROWS = 48
 FINE_IN = 8 * TILE
-RIM = 1280
-MIDDLE = 1024
+RIM = 896
+MIDDLE = 1664
 BANDS = ((-1, -1), (-1, 0), (-1, 1), (0, -1), (0, 1), (1, -1), (1, 0), (1, 1))
 norm_eps = 1e-06
 BF = jnp.bfloat16
@@ -28,17 +28,8 @@
     return table.astype(ml_dtypes.bfloat16)
 
 
-def pool_tables():
-    dense, rim, middle = [], [], []
-    for row in range(8):
-        for col in range(48):
-            target = (row // 2) * 32 + 3 + col // 2
-            dense.append((row * 48 + col, target))
-            if 8 <= col < 40:
-                middle.append((row * 32 + col - 8, target))
-            else:
-                rim.append((row * 16 + (col if col < 8 else col - 32), target))
-    return one_hot((384, 128), dense), one_hot((128, 128), rim), one_hot((256, 128), middle)
+def pool_table():
+    return one_hot((384, 128), [(row * 48 + col, (row // 2) * 32 + 3 + col // 2) for row in range(8) for col in range(48)])
 
 
 def coarse_spread_table():
@@ -53,7 +44,7 @@
     return one_hot((128, 384), pairs)
 
 
-POOL, RIM_POOL, MIDDLE_POOL = pool_tables()
+POOL = pool_table()
 COARSE_SPREAD = coarse_spread_table()
 
 
@@ -254,25 +245,56 @@
             middle_ref[:, 128 * m - RIM : 128 * m - RIM + 128] = value.astype(BF)
 
 
-def place_of(m):
+def place_of(m, lane=None, ops=jnp):
+    lane = lane_ids((8, 128)) if lane is None else lane
+    if m < 4:
+        return (2 * m if m < 2 else 40 + 2 * m) + lane // 64, ops.minimum(lane % 64, 47)
+    if m < 7:
+        col = lane % 8
+        return ops.minimum(16 * m - 60 + lane // 8, 43), ops.where(col < 4, col, col + 40)
+    cell = ops.minimum(128 * m - RIM + lane, 1599)
+    return 4 + cell // 40, 4 + cell % 40
+
+
+def pairs_of(m):
+    return np.unique(place_of(m, np.arange(128), np)[0] // 2).tolist()
+
+
+def sources_of(m):
+    row, col = place_of(m, np.arange(128), np)
+    return np.unique((row * 48 + col) // 128).tolist()
+
+
+def lane_of(row, col, ops=jnp):
+    ends = (row < 4) | (row >= 44)
+    end = ops.where(row < 4, row, row - 40)
+    side = (col < 4) | (col >= 44)
+    cell = (row - 4) * 40 + col - 4
+    tile = ops.where(ends, end // 2, ops.where(side, 4 + (row - 4) // 16, 7 + cell // 128))
+    side_lane = (row - 4) % 16 * 8 + ops.where(col < 4, col, col - 40)
+    return tile, ops.where(ends, end % 2 * 64 + col, ops.where(side, side_lane, cell % 128)) & 127
+
+
+def collected(tiles, row, col, static_row, static_col, pick):
+    tile, index = lane_of(row, col)
+    value = None
+    for m in np.unique(lane_of(static_row, static_col, np)[0]).tolist():
+        if not pick(m):
+            continue
+        part = jnp.where(tall(tile == m), lanes_from(tiles(m), tall(index)), 0.0 if value is None else value)
+        value = part
+    return jnp.zeros((ROWS, 128), F32) if value is None else value
+
+
+def coarse_from(i, sums, pick):
+    def place(lane, ops):
+        return 2 * (4 * i + lane // 32), 2 * ops.clip(lane % 32 - 3, 0, 23)
+
     lane = lane_ids((8, 128))
-    if m < 6:
-        cell = 128 * (m % 3) + lane
-        return cell // 48 + (40 if m >= 3 else 0), cell % 48
-    if m < 10:
-        col = lane % 16
-        return 8 * (m - 5) + lane // 16, jnp.where(col < 8, col, col + 32)
-    return 8 + 4 * (m - 10) + lane // 32, 8 + lane % 32
-
-
-def pairs_of(m):
-    if m < 6:
-        first = 128 * (m % 3)
-        start = 20 if m >= 3 else 0
-        return range(start + first // 96, start + (first + 127) // 96 + 1)
-    if m < 10:
-        return range(4 * (m - 5), 4 * (m - 5) + 4)
-    return range(4 + 2 * (m - 10), 6 + 2 * (m - 10))
+    inside = lane % 32
+    row, col = place(lane, jnp)
+    value = collected(sums, row, col, *place(np.arange(128), np), pick)
+    return jnp.where(tall((inside >= 3) & (inside < 27)), value, 0.0)
 
 
 def column_sums(beside, mirror_ref):
@@ -398,7 +420,7 @@
 
 def params(
     after_ref, x_ref, mask_ref, gain_ref, shift_ref, up_ref, up_bias_ref, down_ref, down_bias_ref, scale_ref, pool_weight_ref, spread_weight_ref,
-    pool_ref, rim_cells_ref, middle_cells_ref, rim_mask_ref, rim_weights_ref, *level_refs,
+    pool_ref, rim_cells_ref, middle_cells_ref, rim_mask_ref, rim_weights_ref, middle_weights_ref, *level_refs,
 ):
     me = lax.axis_index("chan")
     lane = lane_ids((192, 128))
@@ -421,13 +443,14 @@
         values_ref[0:192, :] = jnp.where(lane < 2, norm, jnp.where(lane == 2, own, scale))
     fine_values_ref, coarse_values_ref = level_refs[1], level_refs[3]
     lane = lane_ids((ROWS, FINE_IN))
-    rim_weights_ref[:, 0:384] = cell_weights(pool_weight_ref, lane // 48, lane % 48)
     spread = cell_weights(spread_weight_ref, lane // 48, lane % 48)
     for j in range(3):
         coarse_values_ref[240 + ROWS * j : 240 + ROWS * (j + 1), :] = spread[:, 128 * j : 128 * j + 128]
     lane = lane_ids((ROWS, 128))
-    rim_weights_ref[:, 384:512] = cell_weights(pool_weight_ref, lane // 16, lane)
-    fine_values_ref[192:240, :] = cell_weights(pool_weight_ref, lane // 32, lane)
+    rim_weights_ref[:, 0:128] = cell_weights(pool_weight_ref, lane // 64, lane)
+    rim_weights_ref[:, 128:256] = cell_weights(pool_weight_ref, lane // 8, lane)
+    lane = lane_ids((ROWS, MIDDLE))
+    middle_weights_ref[...] = cell_weights(pool_weight_ref, lane // 40, lane)
 
     masks = []
     for i in range(GROUPS):
@@ -438,46 +461,35 @@
         coarse_values_ref[192 + 8 * m : 200 + 8 * m, :] = coarse_tile(m, lambda i: small_mask[8 * i : 8 * i + 8], lambda value: value)
     coarse_values_ref[232:240, :] = jnp.zeros((8, 128), F32)
     for m in range((RIM + MIDDLE) // 128):
-        if m < 6:
-            here = slice(128 * m, 128 * m + 128)
-            source = 128 * (m if m < 3 else m + 12)
-            rim_cells_ref[:, here] = x_ref[0, :, source : source + 128]
-            rim_mask_ref[:, here] = jnp.broadcast_to(mask_ref[:, source : source + 128].astype(F32), (8, 128))
-            continue
         row, col = place_of(m)
         cell = row * 48 + col
-        first, final = (8 * (m - 5) * 48, 8 * (m - 4) * 48 - 1) if m < 10 else ((4 * m - 32) * 48 + 8, (4 * m - 29) * 48 + 39)
         index, value, mask = cell % 128, None, None
-        for tile in range(first // 128, final // 128 + 1):
+        for tile in sources_of(m):
             lanes = slice(128 * tile, 128 * tile + 128)
             part = lanes_from(x_ref[0, :, lanes].astype(F32), tall(index))
             mask_part = lanes_from(jnp.broadcast_to(mask_ref[:, lanes].astype(F32), (8, 128)), index)
             value = part if value is None else jnp.where(tall(cell // 128 == tile), part, value)
             mask = mask_part if mask is None else jnp.where(cell // 128 == tile, mask_part, mask)
-        if m < 10:
+        if m < RIM // 128:
             rim_cells_ref[:, 128 * m : 128 * m + 128] = value.astype(BF)
             rim_mask_ref[:, 128 * m : 128 * m + 128] = mask
         else:
-            middle_cells_ref[:, 128 * m - RIM : 128 * m - RIM + 128] = value.astype(BF)
-            fine_values_ref[240 + 8 * (m - 10) : 248 + 8 * (m - 10), :] = mask
+            t = m - RIM // 128
+            middle_cells_ref[:, 128 * t : 128 * t + 128] = value.astype(BF)
+            fine_values_ref[192 + 8 * t : 200 + 8 * t, :] = mask
 
 
 def in_rows(rim_ref, middle_ref, out_ref):
-    out_ref[:, 0:FINE_IN] = rim_ref[:, 0:FINE_IN]
-    out_ref[:, 5 * FINE_IN :] = rim_ref[:, FINE_IN : 2 * FINE_IN]
-    for i in range(1, 5):
-        rim = rim_ref[:, 768 + 128 * (i - 1) : 768 + 128 * i].astype(F32)
-        middle = [middle_ref[:, 256 * (i - 1) + 128 * h : 256 * (i - 1) + 128 * h + 128].astype(F32) for h in range(2)]
-        for m in range(3):
-            cell = 128 * m + lane_ids((8, 128))
-            row, col = cell // 48, cell % 48
-            value = lanes_from(rim, tall((row * 16 + jnp.where(col < 8, col, col - 32)) & 127))
-            in_middle = (col >= 8) & (col < 40)
-            index = tall((row % 4 * 32 + col - 8) & 127)
-            for h in range(2):
-                if 192 * h < 128 * m + 128 and 192 * h + 192 > 128 * m:
-                    value = jnp.where(tall(in_middle & (row // 4 == h)), lanes_from(middle[h], index), value)
-            out_ref[:, i * FINE_IN + 128 * m : i * FINE_IN + 128 * m + 128] = value.astype(BF)
+    rim_tiles = RIM // 128
+
+    def tiles(m):
+        ref, t = (rim_ref, m) if m < rim_tiles else (middle_ref, m - rim_tiles)
+        return ref[:, 128 * t : 128 * t + 128].astype(F32)
+
+    for t in range(TILE * TILE // 128):
+        cell, static = 128 * t + lane_ids((8, 128)), 128 * t + np.arange(128)
+        value = collected(tiles, cell // 48, cell % 48, static // 48, static % 48, lambda m: True)
+        out_ref[:, 128 * t : 128 * t + 128] = value.astype(BF)
 
 
 def conv_coarse(x_ref, weight_ref, bias_ref, rim_ref, middle_ref, cells_ref, wide_ref, pad_ref, sum_ref):
@@ -633,35 +645,31 @@
     return result
 
 
-def pooled_cells(products, table):
-    highs = [product.astype(BF) for product in products]
-    lows = [(product - high.astype(F32)).astype(BF) for product, high in zip(products, highs)]
-    return dot(jnp.concatenate(highs, axis=0), table) + dot(jnp.concatenate(lows, axis=0), table)
-
-
 def make_mix_rim(count):
     def mix_rim(
-        tab_ref, own_ref, p1_ref, p2_ref, p3_ref, x_ref, mask_ref, pool_cells_ref, weights_ref, values_ref, pool_ref, rim_pool_ref,
-        middle_pooled_ref, fine_ref, msg_ref, all_pooled_ref, cat_ref, pooled_ref, mains_ref, rest_ref,
+        tab_ref, own_ref, p1_ref, p2_ref, p3_ref, x_ref, mask_ref, pool_cells_ref, weights_ref, values_ref,
+        middle_pooled_ref, fine_ref, msg_ref, all_pooled_ref, cat_ref, mains_ref, rest_ref,
     ):
         gather_rows((own_ref, p1_ref, p2_ref, p3_ref), cat_ref)
-        block = RIM // 2
+        block = RIM
         branch = make_branch(cat_ref, weights_ref, values_ref, block)
         for start in range(0, RIM, block):
             here = slice(start, start + block)
             value = x_ref[:, here].astype(F32) + branch(start)
             fine_ref[:, here] = (mask_ref[0:1, here] * value).astype(BF)
 
-        weights = pool_cells_ref[:, 0:384]
-        whole = pooled_cells([fine_ref[:, start : start + 384].astype(F32) * weights for start in (0, 384)], pool_ref[...])
-        weights = pool_cells_ref[:, 384:512]
-        rim = pooled_cells([fine_ref[:, 768 + 128 * i : 896 + 128 * i].astype(F32) * weights for i in range(4)], rim_pool_ref[...])
-        pooled_ref[:, 0:128] = whole[0:ROWS].astype(BF)
-        pooled_ref[:, 640:768] = whole[ROWS : 2 * ROWS].astype(BF)
-        for i in range(4):
-            pooled_ref[:, 128 * i + 128 : 128 * i + 256] = rim[i * ROWS : (i + 1) * ROWS].astype(BF)
-
-        groups = [pooled_ref[:, 128 * i : 128 * i + 128].astype(F32) for i in range(GROUPS)]
+        sums = []
+        for m in range(RIM // 128):
+            weights, step = (pool_cells_ref[:, 0:128], 64) if m < 4 else (pool_cells_ref[:, 128:256], 8)
+            product = fine_ref[:, 128 * m : 128 * m + 128].astype(F32) * weights
+            product = product + lane_shifted(product, 1)
+            sums.append(product + lane_shifted(product, step))
+        for i in range(GROUPS):
+            here = slice(128 * i, 128 * i + 128)
+            value = coarse_from(i, lambda m: sums[m], lambda m: m < RIM // 128)
+            all_pooled_ref[:, here] = (value + middle_pooled_ref[:, here].astype(F32)).astype(BF)
+
+        groups = [all_pooled_ref[:, 128 * i : 128 * i + 128].astype(F32) for i in range(GROUPS)]
         lane = lane_ids((8, 128))
         index = lane // 24 * 32 + 3 + lane % 24
         rows = [lanes_from(groups[0], tall(index & 127)), lanes_from(groups[5], tall((index + 32) & 127))]
@@ -690,30 +698,24 @@
             return carry
 
         scan_tiles(count, fill, jnp.int32(0))
-        all_pooled_ref[...] = pooled_ref[...]
-        for i in range(4):
-            here = slice(128 * i + 128, 128 * i + 256)
-            all_pooled_ref[:, here] = (pooled_ref[:, here].astype(F32) + middle_pooled_ref[:, 128 * i : 128 * i + 128].astype(F32)).astype(BF)
 
     return mix_rim
 
 
 def mix_middle(
-    own_ref, p1_ref, p2_ref, p3_ref, x_ref, weights_ref, values_ref, middle_pool_ref, fine_ref, pooled_ref, cat_ref
+    own_ref, p1_ref, p2_ref, p3_ref, x_ref, pool_cells_ref, weights_ref, values_ref, fine_ref, pooled_ref, cat_ref
 ):
     gather_rows((own_ref, p1_ref, p2_ref, p3_ref), cat_ref)
-    block = MIDDLE // 2
-    branch = make_branch(cat_ref, weights_ref, values_ref, block)
-    for start in range(0, MIDDLE, block):
-        here = slice(start, start + block)
-        value = x_ref[:, here].astype(F32) + branch(start)
-        tiles = range(start // 128, (start + block) // 128)
-        mask = jnp.concatenate([values_ref[240 + 8 * t : 241 + 8 * t, :] for t in tiles], axis=1)
-        fine_ref[:, here] = (mask * value).astype(BF)
-    weights = wide(values_ref[192:240, :], 256)
-    middle = pooled_cells([fine_ref[:, 256 * i : 256 * i + 256].astype(F32) * weights for i in range(4)], middle_pool_ref[...])
-    for i in range(4):
-        pooled_ref[:, 128 * i : 128 * i + 128] = middle[i * ROWS : (i + 1) * ROWS].astype(BF)
+    value = x_ref[...].astype(F32) + make_branch(cat_ref, weights_ref, values_ref, MIDDLE)(0)
+    mask = jnp.concatenate([values_ref[192 + 8 * t : 193 + 8 * t, :] for t in range(MIDDLE // 128)], axis=1)
+    fine_ref[...] = (mask * value).astype(BF)
+    sums = fine_ref[...].astype(F32) * pool_cells_ref[...]
+    sums = sums + lane_shifted(sums, 1)
+    sums = sums + lane_shifted(sums, 40)
+    first = RIM // 128
+    for i in range(GROUPS):
+        value = coarse_from(i, lambda m: sums[:, 128 * (m - first) : 128 * (m - first) + 128], lambda m: m >= first)
+        pooled_ref[:, 128 * i : 128 * i + 128] = value.astype(BF)
 
 
 def coarse_cells(pieces, first, pooled_ref, weights_ref, values_ref, cat_ref):
@@ -839,17 +841,17 @@
             mix_middle,
             in_specs=[VMEM] * 8,
             out_specs=[VMEM] * 2,
-            out_shape=[shaped(ROWS, MIDDLE), shaped(ROWS, 512)],
+            out_shape=[shaped(ROWS, MIDDLE), shaped(ROWS, 768)],
             scratch_shapes=[pltpu.VMEM((4 * ROWS, MIDDLE), BF)],
             compiler_params=PARAMS,
             cost_estimate=takes(1),
             name="mix_middle",
-        )(*middle_pieces, results[1], results[4], results[5], jnp.asarray(MIDDLE_POOL))
+        )(*middle_pieces, results[1], results[4], results[5], results[6])
 
     def spread_params(own):
         shapes = [
-            ((ROWS, RIM), BF), ((ROWS, MIDDLE), BF), ((8, RIM), F32), ((ROWS, 512), F32),
-            ((912, 256), BF), ((304, 128), F32), ((912, 256), BF), ((384, 128), F32),
+            ((ROWS, RIM), BF), ((ROWS, MIDDLE), BF), ((8, RIM), F32), ((ROWS, 256), F32), ((ROWS, MIDDLE), F32),
+            ((912, 256), BF), ((296, 128), F32), ((912, 256), BF), ((384, 128), F32),
         ]
         return pl.pallas_call(
             params,
@@ -865,15 +867,14 @@
         )
 
     pieces, results = every_channel(conv, spread_params, mix_middle_cells)
-    rim_cells, _, rim_mask, rim_weights, fine_weights, fine_values, coarse_weights, coarse_values, middle, middle_pooled = results
+    rim_cells, _, rim_mask, rim_weights, _, fine_weights, fine_values, coarse_weights, coarse_values, middle, middle_pooled = results
     rim, messages, pooled = pl.pallas_call(
         make_mix_rim(count),
-        in_specs=[SMEM] + [VMEM] * 12,
+        in_specs=[SMEM] + [VMEM] * 10,
         out_specs=[VMEM] * 3,
         out_shape=[shaped(ROWS, RIM), shaped(count, 16, 512), shaped(ROWS, 768)],
         scratch_shapes=[
             pltpu.VMEM((4 * ROWS, RIM), BF),
-            pltpu.VMEM((ROWS, 768), BF),
             pltpu.VMEM((4, ROWS, 128), BF),
             pltpu.VMEM((2, 16, 128), BF),
         ],
@@ -881,8 +882,7 @@
         cost_estimate=takes(3),
         name="mix_rim",
     )(
-        table, *pieces, rim_cells, rim_mask, rim_weights, fine_weights, fine_values, pool, jnp.asarray(RIM_POOL),
-        middle_pooled,
+        table, *pieces, rim_cells, rim_mask, rim_weights, fine_weights, fine_values, middle_pooled,
     )
     arrived = lax.all_to_all(messages, "tile", 0, 0, tiled=True)
     inner, middle_conv, pooled, taps = pl.pallas_call(

time: 49.5 us -> 49 us (0.990)
  waiting for transfers between devices: 12.4 us -> 10.8 us
  Pallas kernels: 17.8 us -> 18.6 us
    ppermute x2, waiting for transfers between devices: 1.72 us -> 0.87 us  [every_channel(): across = lax.ppermute(own, 'chan', pairs(2))]
    pallas_call x1, Pallas kernels: 1.4 us -> 2.16 us  [mix_middle_cells(): pl.pallas_call(mix_middle, in_specs=[VMEM] * 8, out_specs=[VMEM] * 2, out...]
    all_to_all x2, starting transfers between devices: 11.4 us -> 10.7 us  [per_device(): arrived = lax.all_to_all(messages, 'tile', 0, 0, tiled=True)]
    ppermute x1, starting transfers between devices: 0.87 us -> 1.52 us  [per_device(): middle_across = lax.ppermute(middle_conv, 'chan', pairs(2))]
    all_to_all x2, waiting for transfers between devices: 7.76 us -> 7.25 us  [per_device(): arrived = lax.all_to_all(messages, 'tile', 0, 0, tiled=True)]
    unnamed x40 -> x36, local copies, waits for them, and re-layouts: 1.14 us -> 1.13 us
  transfers between devices with their start and end apart: 14 -> 14, of which waited for: 7 -> 6; matrix products, arithmetic and copies ran while one was open for 0% -> 0% of each run, Pallas kernels for 24% -> 26%
where the time goes in v11:
time: 49 us; the launch traced here: 48.7 us
  Pallas kernels  18.6 us (38%)
  starting transfers between devices  17.9 us (37%)
  waiting for transfers between devices  10.8 us (22%)
  local copies, waits for them, and re-layouts  1.13 us (2%)
    all_to_all x2, starting transfers between devices, per_device(): arrived = lax.all_to_all(messages, 'tile', 0, 0, tiled=True)  10.7 us
    all_to_all x2, waiting for transfers between devices, per_device(): arrived = lax.all_to_all(messages, 'tile', 0, 0, tiled=True)  7.25 us
    pallas_call x1, Pallas kernels, per_device(): pl.pallas_call(lambda tab_ref, *refs: conv_inner(*refs), in_specs=[SMEM]...  3.87 us
    ppermute x2, starting transfers between devices, every_channel(): across = lax.ppermute(own, 'chan', pairs(2))  2.91 us
    pallas_call x1, Pallas kernels, per_device(): pl.pallas_call(make_mix_rim(count), in_specs=[SMEM] + [VMEM] * 10, out_sp...  2.74 us
    ppermute x2, waiting for transfers between devices, every_channel(): diagonal = lax.ppermute(across, 'chan', pairs(1))  2.46 us
    pallas_call x1, Pallas kernels, mix_middle_cells(): pl.pallas_call(mix_middle, in_specs=[VMEM] * 8, out_specs=[VMEM] * 2, out...  2.16 us
    pallas_call x1, Pallas kernels, per_device(): pl.pallas_call(conv_border, in_specs=[SMEM] + [VMEM] * 3, out_specs=VMEM,...  1.84 us
  transfers between devices with their start and end apart: 14, of which 6 were waited for; matrix products, arithmetic and copies ran while one was open for 0% of the time, Pallas kernels for 26%

profile of v11, /device:TPU:0, one launch (start us, length us, event | category | flops | bytes accessed | tf_op | source)
XLA Modules:
  0.0 48.7 jit_solution(18186519612423158674)
XLA Ops:
  0.0 0.1 strip_table.1.pack_ref
  0.1 0.9 %copy-done.2 = bf16[1,48,2304]{2,1,0:T(8,128)(2,1)S(1)} copy-done((bf16[1,48,2304]{2,1,0:T(8,128)(2,1)S(1)}, bf16[1,48,2304]{2,1,0:T(8,128)(2,1)}, u32[]{:S(2)}) %copy-start.2) | copy-done | bytes 221208
  1.0 1.7 %prep.1 = (bf16[8,16,896]{2,1,0:T(8,128)(2,1)}, s32[24]{0:T(128)S(1)}) custom-call(s32[8]{0:T(128)S(1)} %copy-done.11, s32[8]{0:T(128)S(1)} %copy-done.12, bf16[1,48,2304]{2,1,0:T(8,128)(2,1)S(1)} %copy-done.2, bf16[384,256]{1,0:T(8,128)(2,1)S(1)} %strip_table.1.pack_ref), custom_call_target="tpu_custom_call" | custom-call | flops 10000000000 | tf_op jit(solution)/shard_map/prep/pallas_call | solution.py:791
  2.6 7.3 %all-to-all-start = ((bf16[8,16,896]{2,1,0:T(8,128)(2,1)}), bf16[8,16,896]{2,1,0:T(8,128)(2,1)S(1)}, u32[]{:S(2)}, u32[]{:S(2)}) async-start(bf16[8,16,896]{2,1,0:T(8,128)(2,1)} %get-tuple-element.56), calls=%async_computation | async-start | bytes 458752 | tf_op jit(solution)/shard_map/all_to_all | solution.py:807
  9.9 0.0 copy-start.16
  9.9 3.9 %conv_inner.1 = (f32[48,896]{1,0:T(8,128)S(1)}, bf16[48,1664]{1,0:T(8,128)(2,1)S(1)}, f32[28,48,128]{2,1,0:T(8,128)S(1)}) custom-call(s32[24]{0:T(128)S(1)} %get-tuple-element.55.tab_ref, bf16[1,48,2304]{2,1,0:T(8,128)(2,1)S(1)} %copy-done.2, f32[2,48,49]{2,1,0:T(8,128)S(1)} %copy-done.3, f32[2,48]{1,0:T(2,128)S(1)} %copy-done.10), custom_call_target="tpu_custom_call" | custom-call | flops 4000000000 | tf_op jit(solution)/shard_map/conv_inner/pallas_call | solution.py:808
  13.8 1.6 %collective-permute-start.3 = (bf16[48,1664]{1,0:T(8,128)(2,1)S(1)}, bf16[48,1664]{1,0:T(8,128)(2,1)S(1)}, u32[]{:S(2)}, u32[]{:S(2)}) collective-permute-start(bf16[48,1664]{1,0:T(8,128)(2,1)S(1)} %get-tuple-element.78.own_ref), channel_id=1, source_target_pairs={{0,2},{1,3},{2,0},{3,1},{4,6},{5,7},{6,4},{7,5},{8,10},{9,11},{10,... | collective-permute-start | bytes 479240 | tf_op jit(solution)/shard_map/ppermute | solution.py:834
  15.4 0.1 copy.18.pool_weight_ref
  15.5 0.1 copy.19.spread_weight_ref
  15.6 2.8 %all-to-all-done.recv_ref = bf16[8,16,896]{2,1,0:T(8,128)(2,1)S(1)} async-done(((bf16[8,16,896]{2,1,0:T(8,128)(2,1)}), bf16[8,16,896]{2,1,0:T(8,128)(2,1)S(1)}, u32[]{:S(2)}, u32[]{:S(2)}) %all-to-all-start) | async-done | bytes 229408 | tf_op jit(solution)/shard_map/all_to_all | solution.py:807
  18.4 0.0 copy-start.13
  18.4 1.8 %conv_border.1.after_ref.own_ref = bf16[48,896]{1,0:T(8,128)(2,1)S(1)} custom-call(s32[24]{0:T(128)S(1)} %get-tuple-element.55.tab_ref, bf16[8,16,896]{2,1,0:T(8,128)(2,1)S(1)} %all-to-all-done.recv_ref, f32[48,896]{1,0:T(8,128)S(1)} %get-tuple-element.57.sum_ref, f32[28,48,128]{2,1,0:T(8,128)S(1)} %get-tuple-element.58.mirror_ref), custom_call_target="tpu_custom_call" | custom-call | flops 2000000000 | tf_op jit(solution)/shard_map/conv_border/pallas_call | solution.py:823
  20.3 1.6 %collective-permute-start.1 = (bf16[48,896]{1,0:T(8,128)(2,1)S(1)}, bf16[48,896]{1,0:T(8,128)(2,1)S(1)}, u32[]{:S(2)}, u32[]{:S(2)}) collective-permute-start(bf16[48,896]{1,0:T(8,128)(2,1)S(1)} %conv_border.1.after_ref.own_ref), channel_id=1, source_target_pairs={{0,2},{1,3},{2,0},{3,1},{4,6},{5,7},{6,4},{7,5},{8,10},{9,11},{10,... | collective-permute-start | bytes 258056 | tf_op jit(solution)/shard_map/ppermute | solution.py:773
  21.9 0.9 %params.1 = (bf16[48,896]{1,0:T(8,128)(2,1)S(1)}, bf16[48,1664]{1,0:T(8,128)(2,1)S(1)}, f32[8,896]{1,0:T(8,128)S(1)}, f32[48,256]{1,0:T(8,128)S(1)}, f32[48,1664...) custom-call(bf16[48,896]{1,0:T(8,128)(2,1)S(1)} %conv_border.1.after, ...), custom_call_target="tpu_custom_call" | custom-call | flops 2000000000 | tf_op jit(solution)/shard_map/params/pallas_call | solution.py:856
  22.8 0.6 %collective-permute-start = (bf16[48,896]{1,0:T(8,128)(2,1)S(1)}, bf16[48,896]{1,0:T(8,128)(2,1)S(1)}, u32[]{:S(2)}, u32[]{:S(2)}) collective-permute-start(bf16[48,896]{1,0:T(8,128)(2,1)S(1)} %conv_border.1.after_ref.own_ref), channel_id=1, source_target_pairs={{0,1},{1,0},{2,3},{3,2},{4,5},{5,4},{6,7},{7,6},{8,9},{9,8},{10,11... | collective-permute-start | bytes 258056 | tf_op jit(solution)/shard_map/ppermute | solution.py:775
  23.4 2.2 %mix_middle.1 = (bf16[48,1664]{1,0:T(8,128)(2,1)S(1)}, bf16[48,768]{1,0:T(8,128)(2,1)S(1)}) custom-call(bf16[48,1664]{1,0:T(8,128)(2,1)S(1)} %get-tuple-element.78.own_ref, bf16[48,1664]{1,0:T(8,128)(2,1)S(1)} %collective-permute-done.2.p1_ref, bf16[48,1664]{1,0:T(8,128)(2,1)S(1)} %collective-permute-done.3.p2_ref, ...), custom_call_target="tpu_custom_call" | custom-call | flops 1000000000 | tf_op jit(solution)/shard_map/mix_middle/pallas_call | solution.py:840
  25.6 0.1 collective-permute-start.5
  25.7 1.2 %collective-permute-done.5.p3_ref = bf16[48,896]{1,0:T(8,128)(2,1)S(1)} collective-permute-done((bf16[48,896]{1,0:T(8,128)(2,1)S(1)}, bf16[48,896]{1,0:T(8,128)(2,1)S(1)}, u32[]{:S(2)}, u32[]{:S(2)}) %collective-permute-start.5) | collective-permute-done | bytes 86048 | tf_op jit(solution)/shard_map/ppermute | solution.py:777
  26.9 2.7 %mix_rim.1 = (bf16[48,896]{1,0:T(8,128)(2,1)S(1)}, bf16[8,16,512]{2,1,0:T(8,128)(2,1)}, bf16[48,768]{1,0:T(8,128)(2,1)S(1)}) custom-call(s32[24]{0:T(128)S(1)} %get-tuple-element.55.tab_ref, bf16[48,896]{1,0:T(8,128)(2,1)S(1)} %conv_border.1.after_ref.own_ref, bf16[48,896]{1,0:T(8,128)(2,1)S(1)} %collective-permute-done.p1_ref, ...), custom_call_target="tpu_custom_call" | custom-call | flops 3000000000 | tf_op jit(solution)/shard_map/mix_rim/pallas_call | solution.py:871
  29.6 3.4 %all-to-all-start.1 = ((bf16[8,16,512]{2,1,0:T(8,128)(2,1)}), bf16[8,16,512]{2,1,0:T(8,128)(2,1)S(1)}, u32[]{:S(2)}, u32[]{:S(2)}) async-start(bf16[8,16,512]{2,1,0:T(8,128)(2,1)} %get-tuple-element.89), calls=%async_computation.1 | async-start | bytes 262144 | tf_op jit(solution)/shard_map/all_to_all | solution.py:887
  33.0 1.5 %conv_coarse.1 = (f32[48,384]{1,0:T(8,128)S(1)}, bf16[48,256]{1,0:T(8,128)(2,1)S(1)}, bf16[48,640]{1,0:T(8,128)(2,1)S(1)}, f32[49,48,128]{2,1,0:T(8,128)S(1)}) custom-call(bf16[48,768]{1,0:T(8,128)(2,1)S(1)} %get-tuple-element.90.x_ref, f32[2,48,49]{2,1,0:T(8,128)S(1)} %copy-done.3, f32[2,48]{1,0:T(2,128)S(1)} %copy-done.10), custom_call_target="tpu_custom_call" | custom-call | flops 2000000000 | tf_op jit(solution)/shard_map/conv_coarse/pallas_call | solution.py:888
  34.5 1.5 %collective-permute-start.9 = (bf16[48,256]{1,0:T(8,128)(2,1)S(1)}, bf16[48,256]{1,0:T(8,128)(2,1)S(1)}, u32[]{:S(2)}, u32[]{:S(2)}) collective-permute-start(bf16[48,256]{1,0:T(8,128)(2,1)S(1)} %get-tuple-element.97.own_ref), channel_id=1, source_target_pairs={{0,2},{1,3},{2,0},{3,1},{4,6},{5,7},{6,4},{7,5},{8,10},{9,11},{10,... | collective-permute-start | bytes 73736 | tf_op jit(solution)/shard_map/ppermute | solution.py:907
  36.1 4.5 %all-to-all-done.1.recv_ref = bf16[8,16,512]{2,1,0:T(8,128)(2,1)S(1)} async-done(((bf16[8,16,512]{2,1,0:T(8,128)(2,1)}), bf16[8,16,512]{2,1,0:T(8,128)(2,1)S(1)}, u32[]{:S(2)}, u32[]{:S(2)}) %all-to-all-start.1) | async-done | bytes 131104 | tf_op jit(solution)/shard_map/all_to_all | solution.py:887
  40.5 1.3 %border_coarse.1.after_ref.own_ref = bf16[48,384]{1,0:T(8,128)(2,1)S(1)} custom-call(s32[24]{0:T(128)S(1)} %get-tuple-element.55.tab_ref, bf16[8,16,512]{2,1,0:T(8,128)(2,1)S(1)} %all-to-all-done.1.recv_ref, f32[48,384]{1,0:T(8,128)S(1)} %get-tuple-element.91.sum_ref, f32[49,48,128]{2,1,0:T(8,128)S(1)} %get-tuple-element.92.mirror_ref), custom_call_target="tpu_custom_call" | custom-call | flops 1000000000 | tf_op jit(solution)/shard_map/border_coarse/pallas_call | solution.py:898
  41.9 1.4 %collective-permute-start.7 = (bf16[48,384]{1,0:T(8,128)(2,1)S(1)}, bf16[48,384]{1,0:T(8,128)(2,1)S(1)}, u32[]{:S(2)}, u32[]{:S(2)}) collective-permute-start(bf16[48,384]{1,0:T(8,128)(2,1)S(1)} %border_coarse.1.after_ref.own_ref), channel_id=1, source_target_pairs={{0,2},{1,3},{2,0},{3,1},{4,6},{5,7},{6,4},{7,5},{8,10},{9,11},{10,... | collective-permute-start | bytes 110600 | tf_op jit(solution)/shard_map/ppermute | solution.py:773
  43.2 0.4 in_rows.1.fine_ref
  43.7 0.6 %collective-permute-start.6 = (bf16[48,384]{1,0:T(8,128)(2,1)S(1)}, bf16[48,384]{1,0:T(8,128)(2,1)S(1)}, u32[]{:S(2)}, u32[]{:S(2)}) collective-permute-start(bf16[48,384]{1,0:T(8,128)(2,1)S(1)} %border_coarse.1.after_ref.own_ref), channel_id=1, source_target_pairs={{0,1},{1,0},{2,3},{3,2},{4,5},{5,4},{6,7},{7,6},{8,9},{9,8},{10,11... | collective-permute-start | bytes 110600 | tf_op jit(solution)/shard_map/ppermute | solution.py:775
  44.2 0.2 collective-permute-done.10.p3_ref
  44.4 0.6 %mix_coarse_middle.1.middle_ref = bf16[48,256]{1,0:T(8,128)(2,1)S(1)} custom-call(bf16[48,256]{1,0:T(8,128)(2,1)S(1)} %get-tuple-element.97.own_ref, bf16[48,256]{1,0:T(8,128)(2,1)S(1)} %collective-permute-done.8.p1_ref, bf16[48,256]{1,0:T(8,128)(2,1)S(1)} %collective-permute-done.9.p2_ref, bf16[48,256]{1,0:T(8,128)(2,1)S(1)} %collective-permute-done.10.p3_ref, ...), custom_call_target="tpu_custom_call" | custom-call | flops 1000000000 | tf_op jit(solution)/shard_map/mix_coarse_middle/pallas_call | solution.py:924
  45.0 0.9 %collective-permute-done.7.p2_ref = bf16[48,384]{1,0:T(8,128)(2,1)S(1)} collective-permute-done((bf16[48,384]{1,0:T(8,128)(2,1)S(1)}, bf16[48,384]{1,0:T(8,128)(2,1)S(1)}, u32[]{:S(2)}, u32[]{:S(2)}) %collective-permute-start.7) | collective-permute-done | bytes 36896 | tf_op jit(solution)/shard_map/ppermute | solution.py:773
  45.9 1.2 %collective-permute-done.11.p3_ref = bf16[48,384]{1,0:T(8,128)(2,1)S(1)} collective-permute-done((bf16[48,384]{1,0:T(8,128)(2,1)S(1)}, bf16[48,384]{1,0:T(8,128)(2,1)S(1)}, u32[]{:S(2)}, u32[]{:S(2)}) %collective-permute-start.11) | collective-permute-done | bytes 36896 | tf_op jit(solution)/shard_map/ppermute | solution.py:777
  47.1 1.6 %mix_coarse.1 = bf16[1,48,2304]{2,1,0:T(8,128)(2,1)} custom-call(bf16[48,384]{1,0:T(8,128)(2,1)S(1)} %border_coarse.1.after_ref.own_ref, bf16[48,384]{1,0:T(8,128)(2,1)S(1)} %collective-permute-done.6.p1_ref, bf16[48,384]{1,0:T(8,128)(2,1)S(1)} %collective-permute-done.7.p2_ref, bf16[48,384]{1,0:T(8,128)(2,1)S(1)} %collective-permute-done.11.p3_ref, ...), custom_call_target="tpu_custom_call" | custom-call | flops 2000000000 | tf_op jit(solution)/shard_map/mix_coarse/pallas_call | solution.py:936
  (44 shorter events, 0.1 us)
Async XLA Ops:
  0.0 0.9 %copy-start.2 = (bf16[1,48,2304]{2,1,0:T(8,128)(2,1)S(1)}, bf16[1,48,2304]{2,1,0:T(8,128)(2,1)}, u32[]{:S(2)}) copy-start(bf16[1,48,2304]{2,1,0:T(8,128)(2,1)} %x_ref.3) | copy-start | bytes 663556
  0.0 0.9 %copy-start.11 = (s32[8]{0:T(128)S(1)}, s32[8]{0:T(128)}, u32[]{:S(2)}) copy-start(s32[8]{0:T(128)} %slots_ref.1) | copy-start | bytes 100
  0.0 0.9 %copy-start.12 = (s32[8]{0:T(128)S(1)}, s32[8]{0:T(128)}, u32[]{:S(2)}) copy-start(s32[8]{0:T(128)} %dev_ref.1) | copy-start | bytes 100
  0.9 9.0 %copy-start.3 = (f32[2,48,49]{2,1,0:T(8,128)S(1)}, f32[2,48,49]{2,1,0:T(8,128)}, u32[]{:S(2)}) copy-start(f32[2,48,49]{2,1,0:T(8,128)} %weight_ref.1) | copy-start | bytes 56452
  0.9 9.0 %copy-start.10 = (f32[2,48]{1,0:T(2,128)S(1)}, f32[2,48]{1,0:T(2,128)}, u32[]{:S(2)}) copy-start(f32[2,48]{1,0:T(2,128)} %bias_ref.1) | copy-start | bytes 1156
  2.6 15.7 %all-to-all-start = ((bf16[8,16,896]{2,1,0:T(8,128)(2,1)}), bf16[8,16,896]{2,1,0:T(8,128)(2,1)S(1)}, u32[]{:S(2)}, u32[]{:S(2)}) async-start(bf16[8,16,896]{2,1,0:T(8,128)(2,1)} %get-tuple-element.56), calls=%async_computation | async-start | bytes 458752 | tf_op jit(solution)/shard_map/all_to_all | solution.py:807
  9.9 5.5 %copy-start.15 = (f32[48,4]{0,1:T(4,128)S(1)}, f32[48,4]{0,1:T(4,128)}, u32[]{:S(2)}) copy-start(f32[48,4]{0,1:T(4,128)} %param.30) | copy-start | bytes 2308
  9.9 5.5 %copy-start.16 = (f32[48,4]{0,1:T(4,128)S(1)}, f32[48,4]{0,1:T(4,128)}, u32[]{:S(2)}) copy-start(f32[48,4]{0,1:T(4,128)} %param.31) | copy-start | bytes 2308
  13.8 8.0 %collective-permute-start.3 = (bf16[48,1664]{1,0:T(8,128)(2,1)S(1)}, bf16[48,1664]{1,0:T(8,128)(2,1)S(1)}, u32[]{:S(2)}, u32[]{:S(2)}) collective-permute-start(bf16[48,1664]{1,0:T(8,128)(2,1)S(1)} %get-tuple-element.78.own_ref), channel_id=1, source_target_pairs={{0,2},{1,3},{2,0},{3,1},{4,6},{5,7},{6,4},{7,5},{8,10},{9,11},{10,... | collective-permute-start | bytes 479240 | tf_op jit(solution)/shard_map/ppermute | solution.py:834
  15.4 8.0 %collective-permute-start.2 = (bf16[48,1664]{1,0:T(8,128)(2,1)S(1)}, bf16[48,1664]{1,0:T(8,128)(2,1)S(1)}, u32[]{:S(2)}, u32[]{:S(2)}) collective-permute-start(bf16[48,1664]{1,0:T(8,128)(2,1)S(1)} %get-tuple-element.78.own_ref), channel_id=1, source_target_pairs={{0,1},{1,0},{2,3},{3,2},{4,5},{5,4},{6,7},{7,6},{8,9},{9,8},{10,11... | collective-permute-start | bytes 479240 | tf_op jit(solution)/shard_map/ppermute | solution.py:835
  18.3 3.5 %copy-start = (bf16[2,768,192]{1,2,0:T(8,128)(2,1)S(1)}, bf16[2,768,192]{1,2,0:T(8,128)(2,1)}, u32[]{:S(2)}) copy-start(bf16[2,768,192]{1,2,0:T(8,128)(2,1)} %param.25) | copy-start | bytes 1769476
  18.3 3.5 %copy-start.1 = (bf16[2,192,768]{2,1,0:T(8,128)(2,1)S(1)}, bf16[2,192,768]{2,1,0:T(8,128)(2,1)}, u32[]{:S(2)}) copy-start(bf16[2,192,768]{2,1,0:T(8,128)(2,1)} %down_ref.1) | copy-start | bytes 1769476
  18.3 3.5 %copy-start.4 = (s32[1,2304]{1,0:T(1,128)S(1)}, s32[1,2304]{1,0:T(1,128)}, u32[]{:S(2)}) copy-start(s32[1,2304]{1,0:T(1,128)} %mask_ref.3) | copy-start | bytes 27652
  18.3 3.5 %copy-start.5 = (f32[2,768]{1,0:T(2,128)S(1)}, f32[2,768]{1,0:T(2,128)}, u32[]{:S(2)}) copy-start(f32[2,768]{1,0:T(2,128)} %up_bias_ref.1) | copy-start | bytes 18436
  18.4 3.5 %copy-start.6 = (f32[2,192]{1,0:T(2,128)S(1)}, f32[2,192]{1,0:T(2,128)}, u32[]{:S(2)}) copy-start(f32[2,192]{1,0:T(2,128)} %gain_ref.1) | copy-start | bytes 4612
  18.4 3.5 %copy-start.7 = (f32[2,192]{1,0:T(2,128)S(1)}, f32[2,192]{1,0:T(2,128)}, u32[]{:S(2)}) copy-start(f32[2,192]{1,0:T(2,128)} %shift_ref.1) | copy-start | bytes 4612
  18.4 3.5 %copy-start.8 = (f32[2,192]{1,0:T(2,128)S(1)}, f32[2,192]{1,0:T(2,128)}, u32[]{:S(2)}) copy-start(f32[2,192]{1,0:T(2,128)} %down_bias_ref.1) | copy-start | bytes 4612
  18.4 3.5 %copy-start.9 = (f32[2,48]{1,0:T(2,128)S(1)}, f32[2,48]{1,0:T(2,128)}, u32[]{:S(2)}) copy-start(f32[2,48]{1,0:T(2,128)} %scale_ref.1) | copy-start | bytes 1156
  18.4 3.5 %copy-start.13 = (bf16[384,128]{1,0:T(8,128)(2,1)S(1)}, bf16[384,128]{1,0:T(8,128)(2,1)}, u32[]{:S(2)}) copy-start(bf16[384,128]{1,0:T(8,128)(2,1)} %constant.4.clone.pool_ref) | copy-start | bytes 294916
  20.3 5.3 %collective-permute-start.1 = (bf16[48,896]{1,0:T(8,128)(2,1)S(1)}, bf16[48,896]{1,0:T(8,128)(2,1)S(1)}, u32[]{:S(2)}, u32[]{:S(2)}) collective-permute-start(bf16[48,896]{1,0:T(8,128)(2,1)S(1)} %conv_border.1.after_ref.own_ref), channel_id=1, source_target_pairs={{0,2},{1,3},{2,0},{3,1},{4,6},{5,7},{6,4},{7,5},{8,10},{9,11},{10,... | collective-permute-start | bytes 258056 | tf_op jit(solution)/shard_map/ppermute | solution.py:773
  21.8 1.6 %collective-permute-start.4 = (bf16[48,1664]{1,0:T(8,128)(2,1)S(1)}, bf16[48,1664]{1,0:T(8,128)(2,1)S(1)}, u32[]{:S(2)}, u32[]{:S(2)}) collective-permute-start(bf16[48,1664]{1,0:T(8,128)(2,1)S(1)} %collective-permute-done.3.p2_ref), channel_id=1, source_target_pairs={{0,1},{1,0},{2,3},{3,2},{4,5},{5,4},{6,7},{7,6},{8,9},{9,8},{10,11... | collective-permute-start | bytes 479240 | tf_op jit(solution)/shard_map/ppermute | solution.py:837
  22.8 2.8 %collective-permute-start = (bf16[48,896]{1,0:T(8,128)(2,1)S(1)}, bf16[48,896]{1,0:T(8,128)(2,1)S(1)}, u32[]{:S(2)}, u32[]{:S(2)}) collective-permute-start(bf16[48,896]{1,0:T(8,128)(2,1)S(1)} %conv_border.1.after_ref.own_ref), channel_id=1, source_target_pairs={{0,1},{1,0},{2,3},{3,2},{4,5},{5,4},{6,7},{7,6},{8,9},{9,8},{10,11... | collective-permute-start | bytes 258056 | tf_op jit(solution)/shard_map/ppermute | solution.py:775
  25.6 1.3 %collective-permute-start.5 = (bf16[48,896]{1,0:T(8,128)(2,1)S(1)}, bf16[48,896]{1,0:T(8,128)(2,1)S(1)}, u32[]{:S(2)}, u32[]{:S(2)}) collective-permute-start(bf16[48,896]{1,0:T(8,128)(2,1)S(1)} %collective-permute-done.1.p2_ref), channel_id=1, source_target_pairs={{0,1},{1,0},{2,3},{3,2},{4,5},{5,4},{6,7},{7,6},{8,9},{9,8},{10,11... | collective-permute-start | bytes 258056 | tf_op jit(solution)/shard_map/ppermute | solution.py:777
  29.6 10.9 %all-to-all-start.1 = ((bf16[8,16,512]{2,1,0:T(8,128)(2,1)}), bf16[8,16,512]{2,1,0:T(8,128)(2,1)S(1)}, u32[]{:S(2)}, u32[]{:S(2)}) async-start(bf16[8,16,512]{2,1,0:T(8,128)(2,1)} %get-tuple-element.89), calls=%async_computation.1 | async-start | bytes 262144 | tf_op jit(solution)/shard_map/all_to_all | solution.py:887
  34.5 8.7 %collective-permute-start.9 = (bf16[48,256]{1,0:T(8,128)(2,1)S(1)}, bf16[48,256]{1,0:T(8,128)(2,1)S(1)}, u32[]{:S(2)}, u32[]{:S(2)}) collective-permute-start(bf16[48,256]{1,0:T(8,128)(2,1)S(1)} %get-tuple-element.97.own_ref), channel_id=1, source_target_pairs={{0,2},{1,3},{2,0},{3,1},{4,6},{5,7},{6,4},{7,5},{8,10},{9,11},{10,... | collective-permute-start | bytes 73736 | tf_op jit(solution)/shard_map/ppermute | solution.py:907
  36.1 8.2 %collective-permute-start.8 = (bf16[48,256]{1,0:T(8,128)(2,1)S(1)}, bf16[48,256]{1,0:T(8,128)(2,1)S(1)}, u32[]{:S(2)}, u32[]{:S(2)}) collective-permute-start(bf16[48,256]{1,0:T(8,128)(2,1)S(1)} %get-tuple-element.97.own_ref), channel_id=1, source_target_pairs={{0,1},{1,0},{2,3},{3,2},{4,5},{5,4},{6,7},{7,6},{8,9},{9,8},{10,11... | collective-permute-start | bytes 73736 | tf_op jit(solution)/shard_map/ppermute | solution.py:908
  41.9 4.0 %collective-permute-start.7 = (bf16[48,384]{1,0:T(8,128)(2,1)S(1)}, bf16[48,384]{1,0:T(8,128)(2,1)S(1)}, u32[]{:S(2)}, u32[]{:S(2)}) collective-permute-start(bf16[48,384]{1,0:T(8,128)(2,1)S(1)} %border_coarse.1.after_ref.own_ref), channel_id=1, source_target_pairs={{0,2},{1,3},{2,0},{3,1},{4,6},{5,7},{6,4},{7,5},{8,10},{9,11},{10,... | collective-permute-start | bytes 110600 | tf_op jit(solution)/shard_map/ppermute | solution.py:773
  43.2 1.2 %collective-permute-start.10 = (bf16[48,256]{1,0:T(8,128)(2,1)S(1)}, bf16[48,256]{1,0:T(8,128)(2,1)S(1)}, u32[]{:S(2)}, u32[]{:S(2)}) collective-permute-start(bf16[48,256]{1,0:T(8,128)(2,1)S(1)} %collective-permute-done.9.p2_ref), channel_id=1, source_target_pairs={{0,1},{1,0},{2,3},{3,2},{4,5},{5,4},{6,7},{7,6},{8,9},{9,8},{10,11... | collective-permute-start | bytes 73736 | tf_op jit(solution)/shard_map/ppermute | solution.py:910
  43.7 2.2 %collective-permute-start.6 = (bf16[48,384]{1,0:T(8,128)(2,1)S(1)}, bf16[48,384]{1,0:T(8,128)(2,1)S(1)}, u32[]{:S(2)}, u32[]{:S(2)}) collective-permute-start(bf16[48,384]{1,0:T(8,128)(2,1)S(1)} %border_coarse.1.after_ref.own_ref), channel_id=1, source_target_pairs={{0,1},{1,0},{2,3},{3,2},{4,5},{5,4},{6,7},{7,6},{8,9},{9,8},{10,11... | collective-permute-start | bytes 110600 | tf_op jit(solution)/shard_map/ppermute | solution.py:775
  44.4 2.7 %copy-start.14 = (bf16[128,384]{1,0:T(8,128)(2,1)S(1)}, bf16[128,384]{1,0:T(8,128)(2,1)}, u32[]{:S(2)}) copy-start(bf16[128,384]{1,0:T(8,128)(2,1)} %constant.5.clone.spread_ref) | copy-start | bytes 294916
  45.9 1.2 %collective-permute-start.11 = (bf16[48,384]{1,0:T(8,128)(2,1)S(1)}, bf16[48,384]{1,0:T(8,128)(2,1)S(1)}, u32[]{:S(2)}, u32[]{:S(2)}) collective-permute-start(bf16[48,384]{1,0:T(8,128)(2,1)S(1)} %collective-permute-done.7.p2_ref), channel_id=1, source_target_pairs={{0,1},{1,0},{2,3},{3,2},{4,5},{5,4},{6,7},{7,6},{8,9},{9,8},{10,11... | collective-permute-start | bytes 110600 | tf_op jit(solution)/shard_map/ppermute | solution.py:777

commit v12 on v11

--- a/solution.py
+++ b/solution.py
@@ -768,13 +768,18 @@
 PARAMS = pltpu.CompilerParams(vmem_limit_bytes=24 * 1024 * 1024)
 
 
-def every_channel(own, first_work, later_work=lambda *results: ()):
+def every_channel(own, first_work, later_work, direct):
     pairs = lambda bit: [(i, i ^ bit) for i in range(4)]
     across = lax.ppermute(own, "chan", pairs(2))
+    if direct:
+        diagonal = lax.ppermute(own, "chan", pairs(3))
     near, *results = lax.optimization_barrier((own, *first_work(own)))
     beside = lax.ppermute(near, "chan", pairs(1))
-    across, *results = lax.optimization_barrier((across, *results, *later_work(*results)))
-    diagonal = lax.ppermute(across, "chan", pairs(1))
+    if direct:
+        across, diagonal, *results = lax.optimization_barrier((across, diagonal, *results, *later_work(*results)))
+    else:
+        across, *results = lax.optimization_barrier((across, *results, *later_work(*results)))
+        diagonal = lax.ppermute(across, "chan", pairs(1))
     return (own, beside, across, diagonal), results
 
 
@@ -866,7 +871,7 @@
             pool_weight, spread_weight, pool,
         )
 
-    pieces, results = every_channel(conv, spread_params, mix_middle_cells)
+    pieces, results = every_channel(conv, spread_params, mix_middle_cells, True)
     rim_cells, _, rim_mask, rim_weights, _, fine_weights, fine_values, coarse_weights, coarse_values, middle, middle_pooled = results
     rim, messages, pooled = pl.pallas_call(
         make_mix_rim(count),
@@ -932,7 +937,7 @@
             name="mix_coarse_middle",
         )(*coarse_pieces, pooled, coarse_weights, coarse_values)
 
-    pieces, (fine, coarse_middle) = every_channel(conv, back_in_rows, mix_coarse_cells)
+    pieces, (fine, coarse_middle) = every_channel(conv, back_in_rows, mix_coarse_cells, True)
     return pl.pallas_call(
         mix_coarse,
         in_specs=[VMEM] * 12,

time: 49 us -> 48.2 us (0.984)
  waiting for transfers between devices: 10.8 us -> 10.1 us
    ppermute x2, starting transfers between devices: 0.01 us -> 1.61 us  [per_device(): lax.ppermute(middle_across, 'chan', pairs(1))]
    ppermute x2, starting transfers between devices: 1.12 us -> 0.16 us  [every_channel(): beside = lax.ppermute(near, 'chan', pairs(1))]
    ppermute x1, starting transfers between devices: 1.52 us -> 0.68 us  [per_device(): middle_across = lax.ppermute(middle_conv, 'chan', pairs(2))]
    ppermute x2, waiting for transfers between devices: 2.46 us -> 1.69 us  [every_channel(): diagonal = lax.ppermute(own, 'chan', pairs(3))]
    ppermute x2, waiting for transfers between devices: 0.87 us -> 0.37 us  [every_channel(): across = lax.ppermute(own, 'chan', pairs(2))]
where the time goes in v12:
time: 48.2 us; the launch traced here: 47.9 us
  Pallas kernels  18.6 us (39%)
  starting transfers between devices  17.9 us (37%)
  waiting for transfers between devices  10.1 us (21%)
  local copies, waits for them, and re-layouts  1.13 us (2%)
    all_to_all x2, starting transfers between devices, per_device(): arrived = lax.all_to_all(messages, 'tile', 0, 0, tiled=True)  10.7 us
    all_to_all x2, waiting for transfers between devices, per_device(): arrived = lax.all_to_all(messages, 'tile', 0, 0, tiled=True)  7.65 us
    pallas_call x1, Pallas kernels, per_device(): pl.pallas_call(lambda tab_ref, *refs: conv_inner(*refs), in_specs=[SMEM]...  3.87 us
    ppermute x2, starting transfers between devices, every_channel(): across = lax.ppermute(own, 'chan', pairs(2))  2.8 us
    pallas_call x1, Pallas kernels, per_device(): pl.pallas_call(make_mix_rim(count), in_specs=[SMEM] + [VMEM] * 10, out_sp...  2.74 us
    pallas_call x1, Pallas kernels, mix_middle_cells(): pl.pallas_call(mix_middle, in_specs=[VMEM] * 8, out_specs=[VMEM] * 2, out...  2.16 us
    pallas_call x1, Pallas kernels, per_device(): pl.pallas_call(conv_border, in_specs=[SMEM] + [VMEM] * 3, out_specs=VMEM,...  1.84 us
    ppermute x2, waiting for transfers between devices, every_channel(): diagonal = lax.ppermute(own, 'chan', pairs(3))  1.69 us
  transfers between devices with their start and end apart: 14, of which 6 were waited for; matrix products, arithmetic and copies ran while one was open for 0% of the time, Pallas kernels for 26%

profile of v12, /device:TPU:0, one launch (start us, length us, event | category | flops | bytes accessed | tf_op | source)
XLA Modules:
  0.0 47.9 jit_solution(102425864343523905)
XLA Ops:
  0.0 0.1 strip_table.1.pack_ref
  0.1 0.9 %copy-done.2 = bf16[1,48,2304]{2,1,0:T(8,128)(2,1)S(1)} copy-done((bf16[1,48,2304]{2,1,0:T(8,128)(2,1)S(1)}, bf16[1,48,2304]{2,1,0:T(8,128)(2,1)}, u32[]{:S(2)}) %copy-start.2) | copy-done | bytes 221208
  1.0 1.7 %prep.1 = (bf16[8,16,896]{2,1,0:T(8,128)(2,1)}, s32[24]{0:T(128)S(1)}) custom-call(s32[8]{0:T(128)S(1)} %copy-done.11, s32[8]{0:T(128)S(1)} %copy-done.12, bf16[1,48,2304]{2,1,0:T(8,128)(2,1)S(1)} %copy-done.2, bf16[384,256]{1,0:T(8,128)(2,1)S(1)} %strip_table.1.pack_ref), custom_call_target="tpu_custom_call" | custom-call | flops 10000000000 | tf_op jit(solution)/shard_map/prep/pallas_call | solution.py:796
  2.6 7.3 %all-to-all-start = ((bf16[8,16,896]{2,1,0:T(8,128)(2,1)}), bf16[8,16,896]{2,1,0:T(8,128)(2,1)S(1)}, u32[]{:S(2)}, u32[]{:S(2)}) async-start(bf16[8,16,896]{2,1,0:T(8,128)(2,1)} %get-tuple-element.58), calls=%async_computation | async-start | bytes 458752 | tf_op jit(solution)/shard_map/all_to_all | solution.py:812
  9.9 3.9 %conv_inner.1 = (f32[48,896]{1,0:T(8,128)S(1)}, bf16[48,1664]{1,0:T(8,128)(2,1)S(1)}, f32[28,48,128]{2,1,0:T(8,128)S(1)}) custom-call(s32[24]{0:T(128)S(1)} %get-tuple-element.57.tab_ref, bf16[1,48,2304]{2,1,0:T(8,128)(2,1)S(1)} %copy-done.2, f32[2,48,49]{2,1,0:T(8,128)S(1)} %copy-done.3, f32[2,48]{1,0:T(2,128)S(1)} %copy-done.10), custom_call_target="tpu_custom_call" | custom-call | flops 4000000000 | tf_op jit(solution)/shard_map/conv_inner/pallas_call | solution.py:813
  13.8 1.6 %collective-permute-start.4 = (bf16[48,1664]{1,0:T(8,128)(2,1)S(1)}, bf16[48,1664]{1,0:T(8,128)(2,1)S(1)}, u32[]{:S(2)}, u32[]{:S(2)}) collective-permute-start(bf16[48,1664]{1,0:T(8,128)(2,1)S(1)} %get-tuple-element.80.own_ref), channel_id=1, source_target_pairs={{0,2},{1,3},{2,0},{3,1},{4,6},{5,7},{6,4},{7,5},{8,10},{9,11},{10,... | collective-permute-start | bytes 479240 | tf_op jit(solution)/shard_map/ppermute | solution.py:839
  15.4 0.1 copy.18.pool_weight_ref
  15.5 0.1 copy.19.spread_weight_ref
  15.6 2.8 %all-to-all-done.recv_ref = bf16[8,16,896]{2,1,0:T(8,128)(2,1)S(1)} async-done(((bf16[8,16,896]{2,1,0:T(8,128)(2,1)}), bf16[8,16,896]{2,1,0:T(8,128)(2,1)S(1)}, u32[]{:S(2)}, u32[]{:S(2)}) %all-to-all-start) | async-done | bytes 229408 | tf_op jit(solution)/shard_map/all_to_all | solution.py:812
  18.4 1.8 %conv_border.1.after_ref.own_ref = bf16[48,896]{1,0:T(8,128)(2,1)S(1)} custom-call(s32[24]{0:T(128)S(1)} %get-tuple-element.57.tab_ref, bf16[8,16,896]{2,1,0:T(8,128)(2,1)S(1)} %all-to-all-done.recv_ref, f32[48,896]{1,0:T(8,128)S(1)} %get-tuple-element.59.sum_ref, f32[28,48,128]{2,1,0:T(8,128)S(1)} %get-tuple-element.60.mirror_ref), custom_call_target="tpu_custom_call" | custom-call | flops 2000000000 | tf_op jit(solution)/shard_map/conv_border/pallas_call | solution.py:828
  20.3 1.6 %collective-permute-start.1 = (bf16[48,896]{1,0:T(8,128)(2,1)S(1)}, bf16[48,896]{1,0:T(8,128)(2,1)S(1)}, u32[]{:S(2)}, u32[]{:S(2)}) collective-permute-start(bf16[48,896]{1,0:T(8,128)(2,1)S(1)} %conv_border.1.after_ref.own_ref), channel_id=1, source_target_pairs={{0,2},{1,3},{2,0},{3,1},{4,6},{5,7},{6,4},{7,5},{8,10},{9,11},{10,... | collective-permute-start | bytes 258056 | tf_op jit(solution)/shard_map/ppermute | solution.py:773
  21.8 0.6 %collective-permute-start.5 = (bf16[48,1664]{1,0:T(8,128)(2,1)S(1)}, bf16[48,1664]{1,0:T(8,128)(2,1)S(1)}, u32[]{:S(2)}, u32[]{:S(2)}) collective-permute-start(bf16[48,1664]{1,0:T(8,128)(2,1)S(1)} %collective-permute-done.4.p2_ref), channel_id=1, source_target_pairs={{0,1},{1,0},{2,3},{3,2},{4,5},{5,4},{6,7},{7,6},{8,9},{9,8},{10,11... | collective-permute-start | bytes 479240 | tf_op jit(solution)/shard_map/ppermute | solution.py:842
  22.5 0.9 %params.1 = (bf16[48,896]{1,0:T(8,128)(2,1)S(1)}, bf16[48,1664]{1,0:T(8,128)(2,1)S(1)}, f32[8,896]{1,0:T(8,128)S(1)}, f32[48,256]{1,0:T(8,128)S(1)}, f32[48,1664...) custom-call(bf16[48,896]{1,0:T(8,128)(2,1)S(1)} %conv_border.1.after, ...), custom_call_target="tpu_custom_call" | custom-call | flops 2000000000 | tf_op jit(solution)/shard_map/params/pallas_call | solution.py:861
  23.5 0.1 collective-permute-start
  23.6 2.2 %mix_middle.1 = (bf16[48,1664]{1,0:T(8,128)(2,1)S(1)}, bf16[48,768]{1,0:T(8,128)(2,1)S(1)}) custom-call(bf16[48,1664]{1,0:T(8,128)(2,1)S(1)} %get-tuple-element.80.own_ref, bf16[48,1664]{1,0:T(8,128)(2,1)S(1)} %collective-permute-done.3.p1_ref, bf16[48,1664]{1,0:T(8,128)(2,1)S(1)} %collective-permute-done.4.p2_ref, ...), custom_call_target="tpu_custom_call" | custom-call | flops 1000000000 | tf_op jit(solution)/shard_map/mix_middle/pallas_call | solution.py:845
  25.7 0.9 %collective-permute-done.2.p3_ref = bf16[48,896]{1,0:T(8,128)(2,1)S(1)} collective-permute-done((bf16[48,896]{1,0:T(8,128)(2,1)S(1)}, bf16[48,896]{1,0:T(8,128)(2,1)S(1)}, u32[]{:S(2)}, u32[]{:S(2)}) %collective-permute-start.2) | collective-permute-done | bytes 86048 | tf_op jit(solution)/shard_map/ppermute | solution.py:775
  26.6 2.7 %mix_rim.1 = (bf16[48,896]{1,0:T(8,128)(2,1)S(1)}, bf16[8,16,512]{2,1,0:T(8,128)(2,1)}, bf16[48,768]{1,0:T(8,128)(2,1)S(1)}) custom-call(s32[24]{0:T(128)S(1)} %get-tuple-element.57.tab_ref, bf16[48,896]{1,0:T(8,128)(2,1)S(1)} %conv_border.1.after_ref.own_ref, bf16[48,896]{1,0:T(8,128)(2,1)S(1)} %collective-permute-done.p1_ref, ...), custom_call_target="tpu_custom_call" | custom-call | flops 3000000000 | tf_op jit(solution)/shard_map/mix_rim/pallas_call | solution.py:876
  29.4 3.4 %all-to-all-start.1 = ((bf16[8,16,512]{2,1,0:T(8,128)(2,1)}), bf16[8,16,512]{2,1,0:T(8,128)(2,1)S(1)}, u32[]{:S(2)}, u32[]{:S(2)}) async-start(bf16[8,16,512]{2,1,0:T(8,128)(2,1)} %get-tuple-element.92), calls=%async_computation.1 | async-start | bytes 262144 | tf_op jit(solution)/shard_map/all_to_all | solution.py:892
  32.8 1.5 %conv_coarse.1 = (f32[48,384]{1,0:T(8,128)S(1)}, bf16[48,256]{1,0:T(8,128)(2,1)S(1)}, bf16[48,640]{1,0:T(8,128)(2,1)S(1)}, f32[49,48,128]{2,1,0:T(8,128)S(1)}) custom-call(bf16[48,768]{1,0:T(8,128)(2,1)S(1)} %get-tuple-element.93.x_ref, f32[2,48,49]{2,1,0:T(8,128)S(1)} %copy-done.3, f32[2,48]{1,0:T(2,128)S(1)} %copy-done.10), custom_call_target="tpu_custom_call" | custom-call | flops 2000000000 | tf_op jit(solution)/shard_map/conv_coarse/pallas_call | solution.py:893
  34.3 0.7 %collective-permute-start.10 = (bf16[48,256]{1,0:T(8,128)(2,1)S(1)}, bf16[48,256]{1,0:T(8,128)(2,1)S(1)}, u32[]{:S(2)}, u32[]{:S(2)}) collective-permute-start(bf16[48,256]{1,0:T(8,128)(2,1)S(1)} %get-tuple-element.100.own_ref), channel_id=1, source_target_pairs={{0,2},{1,3},{2,0},{3,1},{4,6},{5,7},{6,4},{7,5},{8,10},{9,11},{10,... | collective-permute-start | bytes 73736 | tf_op jit(solution)/shard_map/ppermute | solution.py:912
  34.9 0.4 collective-permute-start.9
  35.3 4.9 %all-to-all-done.1.recv_ref = bf16[8,16,512]{2,1,0:T(8,128)(2,1)S(1)} async-done(((bf16[8,16,512]{2,1,0:T(8,128)(2,1)}), bf16[8,16,512]{2,1,0:T(8,128)(2,1)S(1)}, u32[]{:S(2)}, u32[]{:S(2)}) %all-to-all-start.1) | async-done | bytes 131104 | tf_op jit(solution)/shard_map/all_to_all | solution.py:892
  40.2 1.3 %border_coarse.1.after_ref.own_ref = bf16[48,384]{1,0:T(8,128)(2,1)S(1)} custom-call(s32[24]{0:T(128)S(1)} %get-tuple-element.57.tab_ref, bf16[8,16,512]{2,1,0:T(8,128)(2,1)S(1)} %all-to-all-done.1.recv_ref, f32[48,384]{1,0:T(8,128)S(1)} %get-tuple-element.94.sum_ref, f32[49,48,128]{2,1,0:T(8,128)S(1)} %get-tuple-element.95.mirror_ref), custom_call_target="tpu_custom_call" | custom-call | flops 1000000000 | tf_op jit(solution)/shard_map/border_coarse/pallas_call | solution.py:903
  41.5 1.2 %collective-permute-start.7 = (bf16[48,384]{1,0:T(8,128)(2,1)S(1)}, bf16[48,384]{1,0:T(8,128)(2,1)S(1)}, u32[]{:S(2)}, u32[]{:S(2)}) collective-permute-start(bf16[48,384]{1,0:T(8,128)(2,1)S(1)} %border_coarse.1.after_ref.own_ref), channel_id=1, source_target_pairs={{0,2},{1,3},{2,0},{3,1},{4,6},{5,7},{6,4},{7,5},{8,10},{9,11},{10,... | collective-permute-start | bytes 110600 | tf_op jit(solution)/shard_map/ppermute | solution.py:773
  42.8 1.0 %collective-permute-start.11 = (bf16[48,256]{1,0:T(8,128)(2,1)S(1)}, bf16[48,256]{1,0:T(8,128)(2,1)S(1)}, u32[]{:S(2)}, u32[]{:S(2)}) collective-permute-start(bf16[48,256]{1,0:T(8,128)(2,1)S(1)} %collective-permute-done.10.p2_ref), channel_id=1, source_target_pairs={{0,1},{1,0},{2,3},{3,2},{4,5},{5,4},{6,7},{7,6},{8,9},{9,8},{10,11... | collective-permute-start | bytes 73736 | tf_op jit(solution)/shard_map/ppermute | solution.py:915
  43.8 0.4 in_rows.1.fine_ref
  44.2 0.1 collective-permute-start.6
  44.3 0.3 collective-permute-done.11.p3_ref
  44.6 0.6 %mix_coarse_middle.1.middle_ref = bf16[48,256]{1,0:T(8,128)(2,1)S(1)} custom-call(bf16[48,256]{1,0:T(8,128)(2,1)S(1)} %get-tuple-element.100.own_ref, bf16[48,256]{1,0:T(8,128)(2,1)S(1)} %collective-permute-done.9.p1_ref, bf16[48,256]{1,0:T(8,128)(2,1)S(1)} %collective-permute-done.10.p2_ref, bf16[48,256]{1,0:T(8,128)(2,1)S(1)} %collective-permute-done.11.p3_ref, ...), custom_call_target="tpu_custom_call" | custom-call | flops 1000000000 | tf_op jit(solution)/shard_map/mix_coarse_middle/pallas_call | solution.py:929
  45.2 0.4 collective-permute-done.7.p2_ref
  45.6 0.8 %collective-permute-done.8.p3_ref = bf16[48,384]{1,0:T(8,128)(2,1)S(1)} collective-permute-done((bf16[48,384]{1,0:T(8,128)(2,1)S(1)}, bf16[48,384]{1,0:T(8,128)(2,1)S(1)}, u32[]{:S(2)}, u32[]{:S(2)}) %collective-permute-start.8) | collective-permute-done | bytes 36896 | tf_op jit(solution)/shard_map/ppermute | solution.py:775
  46.4 1.6 %mix_coarse.1 = bf16[1,48,2304]{2,1,0:T(8,128)(2,1)} custom-call(bf16[48,384]{1,0:T(8,128)(2,1)S(1)} %border_coarse.1.after_ref.own_ref, bf16[48,384]{1,0:T(8,128)(2,1)S(1)} %collective-permute-done.6.p1_ref, bf16[48,384]{1,0:T(8,128)(2,1)S(1)} %collective-permute-done.7.p2_ref, bf16[48,384]{1,0:T(8,128)(2,1)S(1)} %collective-permute-done.8.p3_ref, ...), custom_call_target="tpu_custom_call" | custom-call | flops 2000000000 | tf_op jit(solution)/shard_map/mix_coarse/pallas_call | solution.py:941
  (44 shorter events, 0.1 us)
Async XLA Ops:
  0.0 0.9 %copy-start.2 = (bf16[1,48,2304]{2,1,0:T(8,128)(2,1)S(1)}, bf16[1,48,2304]{2,1,0:T(8,128)(2,1)}, u32[]{:S(2)}) copy-start(bf16[1,48,2304]{2,1,0:T(8,128)(2,1)} %x_ref.3) | copy-start | bytes 663556
  0.0 0.9 %copy-start.11 = (s32[8]{0:T(128)S(1)}, s32[8]{0:T(128)}, u32[]{:S(2)}) copy-start(s32[8]{0:T(128)} %slots_ref.1) | copy-start | bytes 100
  0.0 0.9 %copy-start.12 = (s32[8]{0:T(128)S(1)}, s32[8]{0:T(128)}, u32[]{:S(2)}) copy-start(s32[8]{0:T(128)} %dev_ref.1) | copy-start | bytes 100
  0.9 9.0 %copy-start.3 = (f32[2,48,49]{2,1,0:T(8,128)S(1)}, f32[2,48,49]{2,1,0:T(8,128)}, u32[]{:S(2)}) copy-start(f32[2,48,49]{2,1,0:T(8,128)} %weight_ref.1) | copy-start | bytes 56452
  0.9 9.0 %copy-start.10 = (f32[2,48]{1,0:T(2,128)S(1)}, f32[2,48]{1,0:T(2,128)}, u32[]{:S(2)}) copy-start(f32[2,48]{1,0:T(2,128)} %bias_ref.1) | copy-start | bytes 1156
  2.6 15.7 %all-to-all-start = ((bf16[8,16,896]{2,1,0:T(8,128)(2,1)}), bf16[8,16,896]{2,1,0:T(8,128)(2,1)S(1)}, u32[]{:S(2)}, u32[]{:S(2)}) async-start(bf16[8,16,896]{2,1,0:T(8,128)(2,1)} %get-tuple-element.58), calls=%async_computation | async-start | bytes 458752 | tf_op jit(solution)/shard_map/all_to_all | solution.py:812
  9.9 5.5 %copy-start.15 = (f32[48,4]{0,1:T(4,128)S(1)}, f32[48,4]{0,1:T(4,128)}, u32[]{:S(2)}) copy-start(f32[48,4]{0,1:T(4,128)} %param.30) | copy-start | bytes 2308
  9.9 5.5 %copy-start.16 = (f32[48,4]{0,1:T(4,128)S(1)}, f32[48,4]{0,1:T(4,128)}, u32[]{:S(2)}) copy-start(f32[48,4]{0,1:T(4,128)} %param.31) | copy-start | bytes 2308
  13.8 8.0 %collective-permute-start.4 = (bf16[48,1664]{1,0:T(8,128)(2,1)S(1)}, bf16[48,1664]{1,0:T(8,128)(2,1)S(1)}, u32[]{:S(2)}, u32[]{:S(2)}) collective-permute-start(bf16[48,1664]{1,0:T(8,128)(2,1)S(1)} %get-tuple-element.80.own_ref), channel_id=1, source_target_pairs={{0,2},{1,3},{2,0},{3,1},{4,6},{5,7},{6,4},{7,5},{8,10},{9,11},{10,... | collective-permute-start | bytes 479240 | tf_op jit(solution)/shard_map/ppermute | solution.py:839
  15.4 8.2 %collective-permute-start.3 = (bf16[48,1664]{1,0:T(8,128)(2,1)S(1)}, bf16[48,1664]{1,0:T(8,128)(2,1)S(1)}, u32[]{:S(2)}, u32[]{:S(2)}) collective-permute-start(bf16[48,1664]{1,0:T(8,128)(2,1)S(1)} %get-tuple-element.80.own_ref), channel_id=1, source_target_pairs={{0,1},{1,0},{2,3},{3,2},{4,5},{5,4},{6,7},{7,6},{8,9},{9,8},{10,11... | collective-permute-start | bytes 479240 | tf_op jit(solution)/shard_map/ppermute | solution.py:840
  18.3 4.1 %copy-start = (bf16[2,768,192]{1,2,0:T(8,128)(2,1)S(1)}, bf16[2,768,192]{1,2,0:T(8,128)(2,1)}, u32[]{:S(2)}) copy-start(bf16[2,768,192]{1,2,0:T(8,128)(2,1)} %param.25) | copy-start | bytes 1769476
  18.3 4.1 %copy-start.1 = (bf16[2,192,768]{2,1,0:T(8,128)(2,1)S(1)}, bf16[2,192,768]{2,1,0:T(8,128)(2,1)}, u32[]{:S(2)}) copy-start(bf16[2,192,768]{2,1,0:T(8,128)(2,1)} %down_ref.1) | copy-start | bytes 1769476
  18.3 4.1 %copy-start.4 = (s32[1,2304]{1,0:T(1,128)S(1)}, s32[1,2304]{1,0:T(1,128)}, u32[]{:S(2)}) copy-start(s32[1,2304]{1,0:T(1,128)} %mask_ref.3) | copy-start | bytes 27652
  18.3 4.1 %copy-start.5 = (f32[2,768]{1,0:T(2,128)S(1)}, f32[2,768]{1,0:T(2,128)}, u32[]{:S(2)}) copy-start(f32[2,768]{1,0:T(2,128)} %up_bias_ref.1) | copy-start | bytes 18436
  18.4 4.1 %copy-start.6 = (f32[2,192]{1,0:T(2,128)S(1)}, f32[2,192]{1,0:T(2,128)}, u32[]{:S(2)}) copy-start(f32[2,192]{1,0:T(2,128)} %gain_ref.1) | copy-start | bytes 4612
  18.4 4.1 %copy-start.7 = (f32[2,192]{1,0:T(2,128)S(1)}, f32[2,192]{1,0:T(2,128)}, u32[]{:S(2)}) copy-start(f32[2,192]{1,0:T(2,128)} %shift_ref.1) | copy-start | bytes 4612
  18.4 4.1 %copy-start.8 = (f32[2,192]{1,0:T(2,128)S(1)}, f32[2,192]{1,0:T(2,128)}, u32[]{:S(2)}) copy-start(f32[2,192]{1,0:T(2,128)} %down_bias_ref.1) | copy-start | bytes 4612
  18.4 4.1 %copy-start.9 = (f32[2,48]{1,0:T(2,128)S(1)}, f32[2,48]{1,0:T(2,128)}, u32[]{:S(2)}) copy-start(f32[2,48]{1,0:T(2,128)} %scale_ref.1) | copy-start | bytes 1156
  18.4 4.1 %copy-start.13 = (bf16[384,128]{1,0:T(8,128)(2,1)S(1)}, bf16[384,128]{1,0:T(8,128)(2,1)}, u32[]{:S(2)}) copy-start(bf16[384,128]{1,0:T(8,128)(2,1)} %constant.4.clone.pool_ref) | copy-start | bytes 294916
  20.3 5.5 %collective-permute-start.1 = (bf16[48,896]{1,0:T(8,128)(2,1)S(1)}, bf16[48,896]{1,0:T(8,128)(2,1)S(1)}, u32[]{:S(2)}, u32[]{:S(2)}) collective-permute-start(bf16[48,896]{1,0:T(8,128)(2,1)S(1)} %conv_border.1.after_ref.own_ref), channel_id=1, source_target_pairs={{0,2},{1,3},{2,0},{3,1},{4,6},{5,7},{6,4},{7,5},{8,10},{9,11},{10,... | collective-permute-start | bytes 258056 | tf_op jit(solution)/shard_map/ppermute | solution.py:773
  21.8 4.8 %collective-permute-start.2 = (bf16[48,896]{1,0:T(8,128)(2,1)S(1)}, bf16[48,896]{1,0:T(8,128)(2,1)S(1)}, u32[]{:S(2)}, u32[]{:S(2)}) collective-permute-start(bf16[48,896]{1,0:T(8,128)(2,1)S(1)} %conv_border.1.after_ref.own_ref), channel_id=1, source_target_pairs={{0,3},{1,2},{2,1},{3,0},{4,7},{5,6},{6,5},{7,4},{8,11},{9,10},{10,... | collective-permute-start | bytes 258056 | tf_op jit(solution)/shard_map/ppermute | solution.py:775
  21.8 1.7 %collective-permute-start.5 = (bf16[48,1664]{1,0:T(8,128)(2,1)S(1)}, bf16[48,1664]{1,0:T(8,128)(2,1)S(1)}, u32[]{:S(2)}, u32[]{:S(2)}) collective-permute-start(bf16[48,1664]{1,0:T(8,128)(2,1)S(1)} %collective-permute-done.4.p2_ref), channel_id=1, source_target_pairs={{0,1},{1,0},{2,3},{3,2},{4,5},{5,4},{6,7},{7,6},{8,9},{9,8},{10,11... | collective-permute-start | bytes 479240 | tf_op jit(solution)/shard_map/ppermute | solution.py:842
  23.5 3.2 %collective-permute-start = (bf16[48,896]{1,0:T(8,128)(2,1)S(1)}, bf16[48,896]{1,0:T(8,128)(2,1)S(1)}, u32[]{:S(2)}, u32[]{:S(2)}) collective-permute-start(bf16[48,896]{1,0:T(8,128)(2,1)S(1)} %conv_border.1.after_ref.own_ref), channel_id=1, source_target_pairs={{0,1},{1,0},{2,3},{3,2},{4,5},{5,4},{6,7},{7,6},{8,9},{9,8},{10,11... | collective-permute-start | bytes 258056 | tf_op jit(solution)/shard_map/ppermute | solution.py:777
  29.4 10.9 %all-to-all-start.1 = ((bf16[8,16,512]{2,1,0:T(8,128)(2,1)}), bf16[8,16,512]{2,1,0:T(8,128)(2,1)S(1)}, u32[]{:S(2)}, u32[]{:S(2)}) async-start(bf16[8,16,512]{2,1,0:T(8,128)(2,1)} %get-tuple-element.92), calls=%async_computation.1 | async-start | bytes 262144 | tf_op jit(solution)/shard_map/all_to_all | solution.py:892
  34.3 8.5 %collective-permute-start.10 = (bf16[48,256]{1,0:T(8,128)(2,1)S(1)}, bf16[48,256]{1,0:T(8,128)(2,1)S(1)}, u32[]{:S(2)}, u32[]{:S(2)}) collective-permute-start(bf16[48,256]{1,0:T(8,128)(2,1)S(1)} %get-tuple-element.100.own_ref), channel_id=1, source_target_pairs={{0,2},{1,3},{2,0},{3,1},{4,6},{5,7},{6,4},{7,5},{8,10},{9,11},{10,... | collective-permute-start | bytes 73736 | tf_op jit(solution)/shard_map/ppermute | solution.py:912
  34.9 9.3 %collective-permute-start.9 = (bf16[48,256]{1,0:T(8,128)(2,1)S(1)}, bf16[48,256]{1,0:T(8,128)(2,1)S(1)}, u32[]{:S(2)}, u32[]{:S(2)}) collective-permute-start(bf16[48,256]{1,0:T(8,128)(2,1)S(1)} %get-tuple-element.100.own_ref), channel_id=1, source_target_pairs={{0,1},{1,0},{2,3},{3,2},{4,5},{5,4},{6,7},{7,6},{8,9},{9,8},{10,11... | collective-permute-start | bytes 73736 | tf_op jit(solution)/shard_map/ppermute | solution.py:913
  41.5 4.0 %collective-permute-start.7 = (bf16[48,384]{1,0:T(8,128)(2,1)S(1)}, bf16[48,384]{1,0:T(8,128)(2,1)S(1)}, u32[]{:S(2)}, u32[]{:S(2)}) collective-permute-start(bf16[48,384]{1,0:T(8,128)(2,1)S(1)} %border_coarse.1.after_ref.own_ref), channel_id=1, source_target_pairs={{0,2},{1,3},{2,0},{3,1},{4,6},{5,7},{6,4},{7,5},{8,10},{9,11},{10,... | collective-permute-start | bytes 110600 | tf_op jit(solution)/shard_map/ppermute | solution.py:773
  42.8 3.6 %collective-permute-start.8 = (bf16[48,384]{1,0:T(8,128)(2,1)S(1)}, bf16[48,384]{1,0:T(8,128)(2,1)S(1)}, u32[]{:S(2)}, u32[]{:S(2)}) collective-permute-start(bf16[48,384]{1,0:T(8,128)(2,1)S(1)} %border_coarse.1.after_ref.own_ref), channel_id=1, source_target_pairs={{0,3},{1,2},{2,1},{3,0},{4,7},{5,6},{6,5},{7,4},{8,11},{9,10},{10,... | collective-permute-start | bytes 110600 | tf_op jit(solution)/shard_map/ppermute | solution.py:775
  42.8 1.8 %collective-permute-start.11 = (bf16[48,256]{1,0:T(8,128)(2,1)S(1)}, bf16[48,256]{1,0:T(8,128)(2,1)S(1)}, u32[]{:S(2)}, u32[]{:S(2)}) collective-permute-start(bf16[48,256]{1,0:T(8,128)(2,1)S(1)} %collective-permute-done.10.p2_ref), channel_id=1, source_target_pairs={{0,1},{1,0},{2,3},{3,2},{4,5},{5,4},{6,7},{7,6},{8,9},{9,8},{10,11... | collective-permute-start | bytes 73736 | tf_op jit(solution)/shard_map/ppermute | solution.py:915
  44.2 2.2 %collective-permute-start.6 = (bf16[48,384]{1,0:T(8,128)(2,1)S(1)}, bf16[48,384]{1,0:T(8,128)(2,1)S(1)}, u32[]{:S(2)}, u32[]{:S(2)}) collective-permute-start(bf16[48,384]{1,0:T(8,128)(2,1)S(1)} %border_coarse.1.after_ref.own_ref), channel_id=1, source_target_pairs={{0,1},{1,0},{2,3},{3,2},{4,5},{5,4},{6,7},{7,6},{8,9},{9,8},{10,11... | collective-permute-start | bytes 110600 | tf_op jit(solution)/shard_map/ppermute | solution.py:777
  44.6 1.8 %copy-start.14 = (bf16[128,384]{1,0:T(8,128)(2,1)S(1)}, bf16[128,384]{1,0:T(8,128)(2,1)}, u32[]{:S(2)}) copy-start(bf16[128,384]{1,0:T(8,128)(2,1)} %constant.5.clone.spread_ref) | copy-start | bytes 294916

commit v13 on v12

--- a/solution.py
+++ b/solution.py
@@ -442,14 +442,14 @@
         norm = jnp.where(lane == 0, columns(gain_ref[row, :]), columns(shift_ref[row, :]))
         values_ref[0:192, :] = jnp.where(lane < 2, norm, jnp.where(lane == 2, own, scale))
     fine_values_ref, coarse_values_ref = level_refs[1], level_refs[3]
-    lane = lane_ids((ROWS, FINE_IN))
+    lane = lane_ids((8, FINE_IN))
     spread = cell_weights(spread_weight_ref, lane // 48, lane % 48)
     for j in range(3):
         coarse_values_ref[240 + ROWS * j : 240 + ROWS * (j + 1), :] = spread[:, 128 * j : 128 * j + 128]
-    lane = lane_ids((ROWS, 128))
+    lane = lane_ids((8, 128))
     rim_weights_ref[:, 0:128] = cell_weights(pool_weight_ref, lane // 64, lane)
     rim_weights_ref[:, 128:256] = cell_weights(pool_weight_ref, lane // 8, lane)
-    lane = lane_ids((ROWS, MIDDLE))
+    lane = lane_ids((8, MIDDLE))
     middle_weights_ref[...] = cell_weights(pool_weight_ref, lane // 40, lane)
 
     masks = []
@@ -638,8 +638,8 @@
 
 
 def cell_weights(weight_ref, row, col):
-    kind = 2 * (row % 2) + col % 2
-    result = jnp.zeros(row.shape, F32)
+    kind = tall(2 * (row % 2) + col % 2)
+    result = jnp.zeros(kind.shape, F32)
     for k in range(4):
         result = jnp.where(kind == k, weight_ref[:, k : k + 1], result)
     return result

time: 48.2 us -> 48.2 us (level)
  no operation moved by 1% of the time
where the time goes in v13:
time: 48.2 us; the launch traced here: 47.9 us
  Pallas kernels  18.6 us (39%)
  starting transfers between devices  17.9 us (37%)
  waiting for transfers between devices  10.1 us (21%)
  local copies, waits for them, and re-layouts  1.13 us (2%)
    all_to_all x2, starting transfers between devices, per_device(): arrived = lax.all_to_all(messages, 'tile', 0, 0, tiled=True)  10.7 us
    all_to_all x2, waiting for transfers between devices, per_device(): arrived = lax.all_to_all(messages, 'tile', 0, 0, tiled=True)  7.65 us
    pallas_call x1, Pallas kernels, per_device(): pl.pallas_call(lambda tab_ref, *refs: conv_inner(*refs), in_specs=[SMEM]...  3.87 us
    ppermute x2, starting transfers between devices, every_channel(): across = lax.ppermute(own, 'chan', pairs(2))  2.8 us
    pallas_call x1, Pallas kernels, per_device(): pl.pallas_call(make_mix_rim(count), in_specs=[SMEM] + [VMEM] * 10, out_sp...  2.74 us
    pallas_call x1, Pallas kernels, mix_middle_cells(): pl.pallas_call(mix_middle, in_specs=[VMEM] * 8, out_specs=[VMEM] * 2, out...  2.16 us
    pallas_call x1, Pallas kernels, per_device(): pl.pallas_call(conv_border, in_specs=[SMEM] + [VMEM] * 3, out_specs=VMEM,...  1.84 us
    ppermute x2, waiting for transfers between devices, every_channel(): diagonal = lax.ppermute(own, 'chan', pairs(3))  1.69 us
  transfers between devices with their start and end apart: 14, of which 6 were waited for; matrix products, arithmetic and copies ran while one was open for 0% of the time, Pallas kernels for 26%

profile of v13, /device:TPU:0, one launch (start us, length us, event | category | flops | bytes accessed | tf_op | source)
XLA Modules:
  0.0 47.9 jit_solution(102425864343523905)
XLA Ops:
  0.0 0.1 strip_table.1.pack_ref
  0.1 0.9 %copy-done.2 = bf16[1,48,2304]{2,1,0:T(8,128)(2,1)S(1)} copy-done((bf16[1,48,2304]{2,1,0:T(8,128)(2,1)S(1)}, bf16[1,48,2304]{2,1,0:T(8,128)(2,1)}, u32[]{:S(2)}) %copy-start.2) | copy-done | bytes 221208
  1.0 1.7 %prep.1 = (bf16[8,16,896]{2,1,0:T(8,128)(2,1)}, s32[24]{0:T(128)S(1)}) custom-call(s32[8]{0:T(128)S(1)} %copy-done.11, s32[8]{0:T(128)S(1)} %copy-done.12, bf16[1,48,2304]{2,1,0:T(8,128)(2,1)S(1)} %copy-done.2, bf16[384,256]{1,0:T(8,128)(2,1)S(1)} %strip_table.1.pack_ref), custom_call_target="tpu_custom_call" | custom-call | flops 10000000000 | tf_op jit(solution)/shard_map/prep/pallas_call | solution.py:796
  2.6 7.3 %all-to-all-start = ((bf16[8,16,896]{2,1,0:T(8,128)(2,1)}), bf16[8,16,896]{2,1,0:T(8,128)(2,1)S(1)}, u32[]{:S(2)}, u32[]{:S(2)}) async-start(bf16[8,16,896]{2,1,0:T(8,128)(2,1)} %get-tuple-element.58), calls=%async_computation | async-start | bytes 458752 | tf_op jit(solution)/shard_map/all_to_all | solution.py:812
  9.9 3.9 %conv_inner.1 = (f32[48,896]{1,0:T(8,128)S(1)}, bf16[48,1664]{1,0:T(8,128)(2,1)S(1)}, f32[28,48,128]{2,1,0:T(8,128)S(1)}) custom-call(s32[24]{0:T(128)S(1)} %get-tuple-element.57.tab_ref, bf16[1,48,2304]{2,1,0:T(8,128)(2,1)S(1)} %copy-done.2, f32[2,48,49]{2,1,0:T(8,128)S(1)} %copy-done.3, f32[2,48]{1,0:T(2,128)S(1)} %copy-done.10), custom_call_target="tpu_custom_call" | custom-call | flops 4000000000 | tf_op jit(solution)/shard_map/conv_inner/pallas_call | solution.py:813
  13.8 1.6 %collective-permute-start.4 = (bf16[48,1664]{1,0:T(8,128)(2,1)S(1)}, bf16[48,1664]{1,0:T(8,128)(2,1)S(1)}, u32[]{:S(2)}, u32[]{:S(2)}) collective-permute-start(bf16[48,1664]{1,0:T(8,128)(2,1)S(1)} %get-tuple-element.80.own_ref), channel_id=1, source_target_pairs={{0,2},{1,3},{2,0},{3,1},{4,6},{5,7},{6,4},{7,5},{8,10},{9,11},{10,... | collective-permute-start | bytes 479240 | tf_op jit(solution)/shard_map/ppermute | solution.py:839
  15.4 0.1 copy.18.pool_weight_ref
  15.5 0.1 copy.19.spread_weight_ref
  15.6 2.8 %all-to-all-done.recv_ref = bf16[8,16,896]{2,1,0:T(8,128)(2,1)S(1)} async-done(((bf16[8,16,896]{2,1,0:T(8,128)(2,1)}), bf16[8,16,896]{2,1,0:T(8,128)(2,1)S(1)}, u32[]{:S(2)}, u32[]{:S(2)}) %all-to-all-start) | async-done | bytes 229408 | tf_op jit(solution)/shard_map/all_to_all | solution.py:812
  18.4 1.8 %conv_border.1.after_ref.own_ref = bf16[48,896]{1,0:T(8,128)(2,1)S(1)} custom-call(s32[24]{0:T(128)S(1)} %get-tuple-element.57.tab_ref, bf16[8,16,896]{2,1,0:T(8,128)(2,1)S(1)} %all-to-all-done.recv_ref, f32[48,896]{1,0:T(8,128)S(1)} %get-tuple-element.59.sum_ref, f32[28,48,128]{2,1,0:T(8,128)S(1)} %get-tuple-element.60.mirror_ref), custom_call_target="tpu_custom_call" | custom-call | flops 2000000000 | tf_op jit(solution)/shard_map/conv_border/pallas_call | solution.py:828
  20.3 1.6 %collective-permute-start.1 = (bf16[48,896]{1,0:T(8,128)(2,1)S(1)}, bf16[48,896]{1,0:T(8,128)(2,1)S(1)}, u32[]{:S(2)}, u32[]{:S(2)}) collective-permute-start(bf16[48,896]{1,0:T(8,128)(2,1)S(1)} %conv_border.1.after_ref.own_ref), channel_id=1, source_target_pairs={{0,2},{1,3},{2,0},{3,1},{4,6},{5,7},{6,4},{7,5},{8,10},{9,11},{10,... | collective-permute-start | bytes 258056 | tf_op jit(solution)/shard_map/ppermute | solution.py:773
  21.8 0.6 %collective-permute-start.5 = (bf16[48,1664]{1,0:T(8,128)(2,1)S(1)}, bf16[48,1664]{1,0:T(8,128)(2,1)S(1)}, u32[]{:S(2)}, u32[]{:S(2)}) collective-permute-start(bf16[48,1664]{1,0:T(8,128)(2,1)S(1)} %collective-permute-done.4.p2_ref), channel_id=1, source_target_pairs={{0,1},{1,0},{2,3},{3,2},{4,5},{5,4},{6,7},{7,6},{8,9},{9,8},{10,11... | collective-permute-start | bytes 479240 | tf_op jit(solution)/shard_map/ppermute | solution.py:842
  22.5 0.9 %params.1 = (bf16[48,896]{1,0:T(8,128)(2,1)S(1)}, bf16[48,1664]{1,0:T(8,128)(2,1)S(1)}, f32[8,896]{1,0:T(8,128)S(1)}, f32[48,256]{1,0:T(8,128)S(1)}, f32[48,1664...) custom-call(bf16[48,896]{1,0:T(8,128)(2,1)S(1)} %conv_border.1.after, ...), custom_call_target="tpu_custom_call" | custom-call | flops 2000000000 | tf_op jit(solution)/shard_map/params/pallas_call | solution.py:861
  23.5 0.1 collective-permute-start
  23.6 2.2 %mix_middle.1 = (bf16[48,1664]{1,0:T(8,128)(2,1)S(1)}, bf16[48,768]{1,0:T(8,128)(2,1)S(1)}) custom-call(bf16[48,1664]{1,0:T(8,128)(2,1)S(1)} %get-tuple-element.80.own_ref, bf16[48,1664]{1,0:T(8,128)(2,1)S(1)} %collective-permute-done.3.p1_ref, bf16[48,1664]{1,0:T(8,128)(2,1)S(1)} %collective-permute-done.4.p2_ref, ...), custom_call_target="tpu_custom_call" | custom-call | flops 1000000000 | tf_op jit(solution)/shard_map/mix_middle/pallas_call | solution.py:845
  25.7 0.9 %collective-permute-done.2.p3_ref = bf16[48,896]{1,0:T(8,128)(2,1)S(1)} collective-permute-done((bf16[48,896]{1,0:T(8,128)(2,1)S(1)}, bf16[48,896]{1,0:T(8,128)(2,1)S(1)}, u32[]{:S(2)}, u32[]{:S(2)}) %collective-permute-start.2) | collective-permute-done | bytes 86048 | tf_op jit(solution)/shard_map/ppermute | solution.py:775
  26.6 2.7 %mix_rim.1 = (bf16[48,896]{1,0:T(8,128)(2,1)S(1)}, bf16[8,16,512]{2,1,0:T(8,128)(2,1)}, bf16[48,768]{1,0:T(8,128)(2,1)S(1)}) custom-call(s32[24]{0:T(128)S(1)} %get-tuple-element.57.tab_ref, bf16[48,896]{1,0:T(8,128)(2,1)S(1)} %conv_border.1.after_ref.own_ref, bf16[48,896]{1,0:T(8,128)(2,1)S(1)} %collective-permute-done.p1_ref, ...), custom_call_target="tpu_custom_call" | custom-call | flops 3000000000 | tf_op jit(solution)/shard_map/mix_rim/pallas_call | solution.py:876
  29.4 3.4 %all-to-all-start.1 = ((bf16[8,16,512]{2,1,0:T(8,128)(2,1)}), bf16[8,16,512]{2,1,0:T(8,128)(2,1)S(1)}, u32[]{:S(2)}, u32[]{:S(2)}) async-start(bf16[8,16,512]{2,1,0:T(8,128)(2,1)} %get-tuple-element.92), calls=%async_computation.1 | async-start | bytes 262144 | tf_op jit(solution)/shard_map/all_to_all | solution.py:892
  32.8 1.5 %conv_coarse.1 = (f32[48,384]{1,0:T(8,128)S(1)}, bf16[48,256]{1,0:T(8,128)(2,1)S(1)}, bf16[48,640]{1,0:T(8,128)(2,1)S(1)}, f32[49,48,128]{2,1,0:T(8,128)S(1)}) custom-call(bf16[48,768]{1,0:T(8,128)(2,1)S(1)} %get-tuple-element.93.x_ref, f32[2,48,49]{2,1,0:T(8,128)S(1)} %copy-done.3, f32[2,48]{1,0:T(2,128)S(1)} %copy-done.10), custom_call_target="tpu_custom_call" | custom-call | flops 2000000000 | tf_op jit(solution)/shard_map/conv_coarse/pallas_call | solution.py:893
  34.3 0.7 %collective-permute-start.10 = (bf16[48,256]{1,0:T(8,128)(2,1)S(1)}, bf16[48,256]{1,0:T(8,128)(2,1)S(1)}, u32[]{:S(2)}, u32[]{:S(2)}) collective-permute-start(bf16[48,256]{1,0:T(8,128)(2,1)S(1)} %get-tuple-element.100.own_ref), channel_id=1, source_target_pairs={{0,2},{1,3},{2,0},{3,1},{4,6},{5,7},{6,4},{7,5},{8,10},{9,11},{10,... | collective-permute-start | bytes 73736 | tf_op jit(solution)/shard_map/ppermute | solution.py:912
  34.9 0.4 collective-permute-start.9
  35.3 4.9 %all-to-all-done.1.recv_ref = bf16[8,16,512]{2,1,0:T(8,128)(2,1)S(1)} async-done(((bf16[8,16,512]{2,1,0:T(8,128)(2,1)}), bf16[8,16,512]{2,1,0:T(8,128)(2,1)S(1)}, u32[]{:S(2)}, u32[]{:S(2)}) %all-to-all-start.1) | async-done | bytes 131104 | tf_op jit(solution)/shard_map/all_to_all | solution.py:892
  40.2 1.3 %border_coarse.1.after_ref.own_ref = bf16[48,384]{1,0:T(8,128)(2,1)S(1)} custom-call(s32[24]{0:T(128)S(1)} %get-tuple-element.57.tab_ref, bf16[8,16,512]{2,1,0:T(8,128)(2,1)S(1)} %all-to-all-done.1.recv_ref, f32[48,384]{1,0:T(8,128)S(1)} %get-tuple-element.94.sum_ref, f32[49,48,128]{2,1,0:T(8,128)S(1)} %get-tuple-element.95.mirror_ref), custom_call_target="tpu_custom_call" | custom-call | flops 1000000000 | tf_op jit(solution)/shard_map/border_coarse/pallas_call | solution.py:903
  41.5 1.2 %collective-permute-start.7 = (bf16[48,384]{1,0:T(8,128)(2,1)S(1)}, bf16[48,384]{1,0:T(8,128)(2,1)S(1)}, u32[]{:S(2)}, u32[]{:S(2)}) collective-permute-start(bf16[48,384]{1,0:T(8,128)(2,1)S(1)} %border_coarse.1.after_ref.own_ref), channel_id=1, source_target_pairs={{0,2},{1,3},{2,0},{3,1},{4,6},{5,7},{6,4},{7,5},{8,10},{9,11},{10,... | collective-permute-start | bytes 110600 | tf_op jit(solution)/shard_map/ppermute | solution.py:773
  42.8 1.0 %collective-permute-start.11 = (bf16[48,256]{1,0:T(8,128)(2,1)S(1)}, bf16[48,256]{1,0:T(8,128)(2,1)S(1)}, u32[]{:S(2)}, u32[]{:S(2)}) collective-permute-start(bf16[48,256]{1,0:T(8,128)(2,1)S(1)} %collective-permute-done.10.p2_ref), channel_id=1, source_target_pairs={{0,1},{1,0},{2,3},{3,2},{4,5},{5,4},{6,7},{7,6},{8,9},{9,8},{10,11... | collective-permute-start | bytes 73736 | tf_op jit(solution)/shard_map/ppermute | solution.py:915
  43.8 0.4 in_rows.1.fine_ref
  44.2 0.1 collective-permute-start.6
  44.3 0.3 collective-permute-done.11.p3_ref
  44.6 0.6 %mix_coarse_middle.1.middle_ref = bf16[48,256]{1,0:T(8,128)(2,1)S(1)} custom-call(bf16[48,256]{1,0:T(8,128)(2,1)S(1)} %get-tuple-element.100.own_ref, bf16[48,256]{1,0:T(8,128)(2,1)S(1)} %collective-permute-done.9.p1_ref, bf16[48,256]{1,0:T(8,128)(2,1)S(1)} %collective-permute-done.10.p2_ref, bf16[48,256]{1,0:T(8,128)(2,1)S(1)} %collective-permute-done.11.p3_ref, ...), custom_call_target="tpu_custom_call" | custom-call | flops 1000000000 | tf_op jit(solution)/shard_map/mix_coarse_middle/pallas_call | solution.py:929
  45.2 0.4 collective-permute-done.7.p2_ref
  45.6 0.8 %collective-permute-done.8.p3_ref = bf16[48,384]{1,0:T(8,128)(2,1)S(1)} collective-permute-done((bf16[48,384]{1,0:T(8,128)(2,1)S(1)}, bf16[48,384]{1,0:T(8,128)(2,1)S(1)}, u32[]{:S(2)}, u32[]{:S(2)}) %collective-permute-start.8) | collective-permute-done | bytes 36896 | tf_op jit(solution)/shard_map/ppermute | solution.py:775
  46.4 1.6 %mix_coarse.1 = bf16[1,48,2304]{2,1,0:T(8,128)(2,1)} custom-call(bf16[48,384]{1,0:T(8,128)(2,1)S(1)} %border_coarse.1.after_ref.own_ref, bf16[48,384]{1,0:T(8,128)(2,1)S(1)} %collective-permute-done.6.p1_ref, bf16[48,384]{1,0:T(8,128)(2,1)S(1)} %collective-permute-done.7.p2_ref, bf16[48,384]{1,0:T(8,128)(2,1)S(1)} %collective-permute-done.8.p3_ref, ...), custom_call_target="tpu_custom_call" | custom-call | flops 2000000000 | tf_op jit(solution)/shard_map/mix_coarse/pallas_call | solution.py:941
  (44 shorter events, 0.1 us)
Async XLA Ops:
  0.0 0.9 %copy-start.2 = (bf16[1,48,2304]{2,1,0:T(8,128)(2,1)S(1)}, bf16[1,48,2304]{2,1,0:T(8,128)(2,1)}, u32[]{:S(2)}) copy-start(bf16[1,48,2304]{2,1,0:T(8,128)(2,1)} %x_ref.3) | copy-start | bytes 663556
  0.0 0.9 %copy-start.11 = (s32[8]{0:T(128)S(1)}, s32[8]{0:T(128)}, u32[]{:S(2)}) copy-start(s32[8]{0:T(128)} %slots_ref.1) | copy-start | bytes 100
  0.0 0.9 %copy-start.12 = (s32[8]{0:T(128)S(1)}, s32[8]{0:T(128)}, u32[]{:S(2)}) copy-start(s32[8]{0:T(128)} %dev_ref.1) | copy-start | bytes 100
  0.9 9.0 %copy-start.3 = (f32[2,48,49]{2,1,0:T(8,128)S(1)}, f32[2,48,49]{2,1,0:T(8,128)}, u32[]{:S(2)}) copy-start(f32[2,48,49]{2,1,0:T(8,128)} %weight_ref.1) | copy-start | bytes 56452
  0.9 9.0 %copy-start.10 = (f32[2,48]{1,0:T(2,128)S(1)}, f32[2,48]{1,0:T(2,128)}, u32[]{:S(2)}) copy-start(f32[2,48]{1,0:T(2,128)} %bias_ref.1) | copy-start | bytes 1156
  2.6 15.7 %all-to-all-start = ((bf16[8,16,896]{2,1,0:T(8,128)(2,1)}), bf16[8,16,896]{2,1,0:T(8,128)(2,1)S(1)}, u32[]{:S(2)}, u32[]{:S(2)}) async-start(bf16[8,16,896]{2,1,0:T(8,128)(2,1)} %get-tuple-element.58), calls=%async_computation | async-start | bytes 458752 | tf_op jit(solution)/shard_map/all_to_all | solution.py:812
  9.9 5.5 %copy-start.15 = (f32[48,4]{0,1:T(4,128)S(1)}, f32[48,4]{0,1:T(4,128)}, u32[]{:S(2)}) copy-start(f32[48,4]{0,1:T(4,128)} %param.30) | copy-start | bytes 2308
  9.9 5.5 %copy-start.16 = (f32[48,4]{0,1:T(4,128)S(1)}, f32[48,4]{0,1:T(4,128)}, u32[]{:S(2)}) copy-start(f32[48,4]{0,1:T(4,128)} %param.31) | copy-start | bytes 2308
  13.8 8.0 %collective-permute-start.4 = (bf16[48,1664]{1,0:T(8,128)(2,1)S(1)}, bf16[48,1664]{1,0:T(8,128)(2,1)S(1)}, u32[]{:S(2)}, u32[]{:S(2)}) collective-permute-start(bf16[48,1664]{1,0:T(8,128)(2,1)S(1)} %get-tuple-element.80.own_ref), channel_id=1, source_target_pairs={{0,2},{1,3},{2,0},{3,1},{4,6},{5,7},{6,4},{7,5},{8,10},{9,11},{10,... | collective-permute-start | bytes 479240 | tf_op jit(solution)/shard_map/ppermute | solution.py:839
  15.4 8.2 %collective-permute-start.3 = (bf16[48,1664]{1,0:T(8,128)(2,1)S(1)}, bf16[48,1664]{1,0:T(8,128)(2,1)S(1)}, u32[]{:S(2)}, u32[]{:S(2)}) collective-permute-start(bf16[48,1664]{1,0:T(8,128)(2,1)S(1)} %get-tuple-element.80.own_ref), channel_id=1, source_target_pairs={{0,1},{1,0},{2,3},{3,2},{4,5},{5,4},{6,7},{7,6},{8,9},{9,8},{10,11... | collective-permute-start | bytes 479240 | tf_op jit(solution)/shard_map/ppermute | solution.py:840
  18.3 4.1 %copy-start = (bf16[2,768,192]{1,2,0:T(8,128)(2,1)S(1)}, bf16[2,768,192]{1,2,0:T(8,128)(2,1)}, u32[]{:S(2)}) copy-start(bf16[2,768,192]{1,2,0:T(8,128)(2,1)} %param.25) | copy-start | bytes 1769476
  18.3 4.1 %copy-start.1 = (bf16[2,192,768]{2,1,0:T(8,128)(2,1)S(1)}, bf16[2,192,768]{2,1,0:T(8,128)(2,1)}, u32[]{:S(2)}) copy-start(bf16[2,192,768]{2,1,0:T(8,128)(2,1)} %down_ref.1) | copy-start | bytes 1769476
  18.3 4.1 %copy-start.4 = (s32[1,2304]{1,0:T(1,128)S(1)}, s32[1,2304]{1,0:T(1,128)}, u32[]{:S(2)}) copy-start(s32[1,2304]{1,0:T(1,128)} %mask_ref.3) | copy-start | bytes 27652
  18.3 4.1 %copy-start.5 = (f32[2,768]{1,0:T(2,128)S(1)}, f32[2,768]{1,0:T(2,128)}, u32[]{:S(2)}) copy-start(f32[2,768]{1,0:T(2,128)} %up_bias_ref.1) | copy-start | bytes 18436
  18.4 4.1 %copy-start.6 = (f32[2,192]{1,0:T(2,128)S(1)}, f32[2,192]{1,0:T(2,128)}, u32[]{:S(2)}) copy-start(f32[2,192]{1,0:T(2,128)} %gain_ref.1) | copy-start | bytes 4612
  18.4 4.1 %copy-start.7 = (f32[2,192]{1,0:T(2,128)S(1)}, f32[2,192]{1,0:T(2,128)}, u32[]{:S(2)}) copy-start(f32[2,192]{1,0:T(2,128)} %shift_ref.1) | copy-start | bytes 4612
  18.4 4.1 %copy-start.8 = (f32[2,192]{1,0:T(2,128)S(1)}, f32[2,192]{1,0:T(2,128)}, u32[]{:S(2)}) copy-start(f32[2,192]{1,0:T(2,128)} %down_bias_ref.1) | copy-start | bytes 4612
  18.4 4.1 %copy-start.9 = (f32[2,48]{1,0:T(2,128)S(1)}, f32[2,48]{1,0:T(2,128)}, u32[]{:S(2)}) copy-start(f32[2,48]{1,0:T(2,128)} %scale_ref.1) | copy-start | bytes 1156
  18.4 4.1 %copy-start.13 = (bf16[384,128]{1,0:T(8,128)(2,1)S(1)}, bf16[384,128]{1,0:T(8,128)(2,1)}, u32[]{:S(2)}) copy-start(bf16[384,128]{1,0:T(8,128)(2,1)} %constant.4.clone.pool_ref) | copy-start | bytes 294916
  20.3 5.5 %collective-permute-start.1 = (bf16[48,896]{1,0:T(8,128)(2,1)S(1)}, bf16[48,896]{1,0:T(8,128)(2,1)S(1)}, u32[]{:S(2)}, u32[]{:S(2)}) collective-permute-start(bf16[48,896]{1,0:T(8,128)(2,1)S(1)} %conv_border.1.after_ref.own_ref), channel_id=1, source_target_pairs={{0,2},{1,3},{2,0},{3,1},{4,6},{5,7},{6,4},{7,5},{8,10},{9,11},{10,... | collective-permute-start | bytes 258056 | tf_op jit(solution)/shard_map/ppermute | solution.py:773
  21.8 4.8 %collective-permute-start.2 = (bf16[48,896]{1,0:T(8,128)(2,1)S(1)}, bf16[48,896]{1,0:T(8,128)(2,1)S(1)}, u32[]{:S(2)}, u32[]{:S(2)}) collective-permute-start(bf16[48,896]{1,0:T(8,128)(2,1)S(1)} %conv_border.1.after_ref.own_ref), channel_id=1, source_target_pairs={{0,3},{1,2},{2,1},{3,0},{4,7},{5,6},{6,5},{7,4},{8,11},{9,10},{10,... | collective-permute-start | bytes 258056 | tf_op jit(solution)/shard_map/ppermute | solution.py:775
  21.8 1.7 %collective-permute-start.5 = (bf16[48,1664]{1,0:T(8,128)(2,1)S(1)}, bf16[48,1664]{1,0:T(8,128)(2,1)S(1)}, u32[]{:S(2)}, u32[]{:S(2)}) collective-permute-start(bf16[48,1664]{1,0:T(8,128)(2,1)S(1)} %collective-permute-done.4.p2_ref), channel_id=1, source_target_pairs={{0,1},{1,0},{2,3},{3,2},{4,5},{5,4},{6,7},{7,6},{8,9},{9,8},{10,11... | collective-permute-start | bytes 479240 | tf_op jit(solution)/shard_map/ppermute | solution.py:842
  23.5 3.2 %collective-permute-start = (bf16[48,896]{1,0:T(8,128)(2,1)S(1)}, bf16[48,896]{1,0:T(8,128)(2,1)S(1)}, u32[]{:S(2)}, u32[]{:S(2)}) collective-permute-start(bf16[48,896]{1,0:T(8,128)(2,1)S(1)} %conv_border.1.after_ref.own_ref), channel_id=1, source_target_pairs={{0,1},{1,0},{2,3},{3,2},{4,5},{5,4},{6,7},{7,6},{8,9},{9,8},{10,11... | collective-permute-start | bytes 258056 | tf_op jit(solution)/shard_map/ppermute | solution.py:777
  29.4 10.9 %all-to-all-start.1 = ((bf16[8,16,512]{2,1,0:T(8,128)(2,1)}), bf16[8,16,512]{2,1,0:T(8,128)(2,1)S(1)}, u32[]{:S(2)}, u32[]{:S(2)}) async-start(bf16[8,16,512]{2,1,0:T(8,128)(2,1)} %get-tuple-element.92), calls=%async_computation.1 | async-start | bytes 262144 | tf_op jit(solution)/shard_map/all_to_all | solution.py:892
  34.3 8.5 %collective-permute-start.10 = (bf16[48,256]{1,0:T(8,128)(2,1)S(1)}, bf16[48,256]{1,0:T(8,128)(2,1)S(1)}, u32[]{:S(2)}, u32[]{:S(2)}) collective-permute-start(bf16[48,256]{1,0:T(8,128)(2,1)S(1)} %get-tuple-element.100.own_ref), channel_id=1, source_target_pairs={{0,2},{1,3},{2,0},{3,1},{4,6},{5,7},{6,4},{7,5},{8,10},{9,11},{10,... | collective-permute-start | bytes 73736 | tf_op jit(solution)/shard_map/ppermute | solution.py:912
  34.9 9.3 %collective-permute-start.9 = (bf16[48,256]{1,0:T(8,128)(2,1)S(1)}, bf16[48,256]{1,0:T(8,128)(2,1)S(1)}, u32[]{:S(2)}, u32[]{:S(2)}) collective-permute-start(bf16[48,256]{1,0:T(8,128)(2,1)S(1)} %get-tuple-element.100.own_ref), channel_id=1, source_target_pairs={{0,1},{1,0},{2,3},{3,2},{4,5},{5,4},{6,7},{7,6},{8,9},{9,8},{10,11... | collective-permute-start | bytes 73736 | tf_op jit(solution)/shard_map/ppermute | solution.py:913
  41.5 4.0 %collective-permute-start.7 = (bf16[48,384]{1,0:T(8,128)(2,1)S(1)}, bf16[48,384]{1,0:T(8,128)(2,1)S(1)}, u32[]{:S(2)}, u32[]{:S(2)}) collective-permute-start(bf16[48,384]{1,0:T(8,128)(2,1)S(1)} %border_coarse.1.after_ref.own_ref), channel_id=1, source_target_pairs={{0,2},{1,3},{2,0},{3,1},{4,6},{5,7},{6,4},{7,5},{8,10},{9,11},{10,... | collective-permute-start | bytes 110600 | tf_op jit(solution)/shard_map/ppermute | solution.py:773
  42.8 3.6 %collective-permute-start.8 = (bf16[48,384]{1,0:T(8,128)(2,1)S(1)}, bf16[48,384]{1,0:T(8,128)(2,1)S(1)}, u32[]{:S(2)}, u32[]{:S(2)}) collective-permute-start(bf16[48,384]{1,0:T(8,128)(2,1)S(1)} %border_coarse.1.after_ref.own_ref), channel_id=1, source_target_pairs={{0,3},{1,2},{2,1},{3,0},{4,7},{5,6},{6,5},{7,4},{8,11},{9,10},{10,... | collective-permute-start | bytes 110600 | tf_op jit(solution)/shard_map/ppermute | solution.py:775
  42.8 1.8 %collective-permute-start.11 = (bf16[48,256]{1,0:T(8,128)(2,1)S(1)}, bf16[48,256]{1,0:T(8,128)(2,1)S(1)}, u32[]{:S(2)}, u32[]{:S(2)}) collective-permute-start(bf16[48,256]{1,0:T(8,128)(2,1)S(1)} %collective-permute-done.10.p2_ref), channel_id=1, source_target_pairs={{0,1},{1,0},{2,3},{3,2},{4,5},{5,4},{6,7},{7,6},{8,9},{9,8},{10,11... | collective-permute-start | bytes 73736 | tf_op jit(solution)/shard_map/ppermute | solution.py:915
  44.2 2.2 %collective-permute-start.6 = (bf16[48,384]{1,0:T(8,128)(2,1)S(1)}, bf16[48,384]{1,0:T(8,128)(2,1)S(1)}, u32[]{:S(2)}, u32[]{:S(2)}) collective-permute-start(bf16[48,384]{1,0:T(8,128)(2,1)S(1)} %border_coarse.1.after_ref.own_ref), channel_id=1, source_target_pairs={{0,1},{1,0},{2,3},{3,2},{4,5},{5,4},{6,7},{7,6},{8,9},{9,8},{10,11... | collective-permute-start | bytes 110600 | tf_op jit(solution)/shard_map/ppermute | solution.py:777
  44.6 1.8 %copy-start.14 = (bf16[128,384]{1,0:T(8,128)(2,1)S(1)}, bf16[128,384]{1,0:T(8,128)(2,1)}, u32[]{:S(2)}) copy-start(bf16[128,384]{1,0:T(8,128)(2,1)} %constant.5.clone.spread_ref) | copy-start | bytes 294916
